TPU v7x, 256 devices: a whole 4x4x8 slice. The times are simulated.
256 devices in a mesh: blk: 16 (over x, y_lo, core), group: 16 (over y_hi, z).
Axes of the slice: x: 4, y: 4 (y_hi: 2, y_lo: 2; y = y_hi * 2 + y_lo), z: 8, core: 2. Of those that a mesh axis runs over, the one named last changes fastest.
Arguments:
- image_emb: float32 [65536, 1152], P(('blk', 'group')), may hold values from -0.2 to 0.2
- text_emb: float32 [65536, 1152], P(('blk', 'group')), may hold values from -0.2 to 0.2
- log_scale: float32 [], replicated, may hold values from 2 to 2.6
- bias: float32 [], replicated, may hold values from -8 to -5
Outputs:
- loss: float32 [], replicated
- grad_image: float32 [65536, 1152], P(('blk', 'group'))
- grad_text: float32 [65536, 1152], P(('blk', 'group'))
- grad_log_scale: float32 [], replicated
- grad_bias: float32 [], replicated
All inputs are finite; a program needn't handle non-finite values.
Results may differ from a plain program's by a relative error of at most 0.0028.
Values may be sent and summed in bfloat16 or wider, within the bound.
No kernel may reach another device: no remote copies, remote signals or barrier semaphores. Data moves between devices by JAX's collectives and lax.ppermute only.
A program may use at most 128 MiB of HBM per device.

v0:
```python
import jax
import jax.numpy as jnp
from jax import lax
from jax.sharding import PartitionSpec as P


def normalize(emb):
    squares = jnp.sum(emb * emb, axis=1, keepdims=True)
    inverse = lax.rsqrt(squares + 1e-06)
    return (emb * inverse, inverse)


def backnorm(hat, inverse, upstream):
    along = jnp.sum(hat * upstream, axis=1, keepdims=True)
    return inverse * (upstream - hat * along)


def block_grad(image_rows, text_rows, image_ids, text_ids, scale, bias):
    sim = lax.dot_general(
        image_rows, text_rows, (((1,), (1,)), ((), ())), preferred_element_type=jnp.float32
    )
    scaled = scale * sim
    logits = scaled + bias
    positive = image_ids[:, None] == text_ids[None, :]
    grad = jax.nn.sigmoid(logits) - positive.astype(jnp.float32)
    return (logits, positive, scaled, grad)


def pair_block(image_rows, text_rows, image_ids, text_ids, scale, bias):
    logits, positive, scaled, grad = block_grad(
        image_rows, text_rows, image_ids, text_ids, scale, bias
    )
    sign = jnp.where(positive, 1.0, -1.0).astype(jnp.float32)
    loss_part = jnp.sum(jax.nn.softplus(-sign * logits))
    scale_part = jnp.sum(grad * scaled)
    bias_part = jnp.sum(grad)
    return (grad.astype(jnp.bfloat16), loss_part, scale_part, bias_part)


def shards(image_emb, text_emb, log_scale, bias):
    rows = image_emb.shape[0]
    blocks = lax.axis_size("blk")
    groups = lax.axis_size("group")
    here_blk = lax.axis_index("blk")
    image_hat, image_inv = normalize(image_emb)
    text_hat, text_inv = normalize(text_emb)
    image_norm = image_hat.astype(jnp.bfloat16)
    text_norm = text_hat.astype(jnp.bfloat16)
    scale = jnp.exp(log_scale)
    local_ids = here_blk * rows + jnp.arange(rows, dtype=jnp.int32)
    set_ids = jnp.arange(blocks * rows, dtype=jnp.int32)
    text_all = lax.all_gather(text_norm, "blk", axis=0, tiled=True)
    grad_q, loss_part, scale_part, bias_part = pair_block(
        image_norm, text_all, local_ids, set_ids, scale, bias
    )
    dimage = scale * jnp.dot(grad_q, text_all, preferred_element_type=jnp.float32)
    dtext = lax.psum_scatter(
        scale
        * lax.dot_general(
            grad_q, image_norm, (((0,), (0,)), ((), ())), preferred_element_type=jnp.float32
        ),
        "blk",
        scatter_dimension=0,
        tiled=True,
    )
    loss_sum, scale_sum, bias_sum = lax.psum((loss_part, scale_part, bias_part), ("blk", "group"))
    total_rows = rows * blocks * groups
    grad_image = backnorm(image_hat, image_inv, dimage)
    grad_text = backnorm(text_hat, text_inv, dtext)
    return (
        loss_sum / total_rows,
        grad_image,
        grad_text,
        scale_sum / total_rows,
        bias_sum / total_rows,
    )


def solution(mesh):
    in_specs = (P(("blk", "group"), None), P(("blk", "group"), None), P(), P())
    out_specs = (P(), P(("blk", "group"), None), P(("blk", "group"), None), P(), P())
    return jax.shard_map(shards, mesh=mesh, in_specs=in_specs, out_specs=out_specs, check_vma=False)
```

profile of v0, /device:TPU:1, one launch (start us, length us, event | category | flops | bytes accessed | tf_op | source)
XLA Modules:
  0.0 315.7 jit_solution(1374390409106807606)
XLA Ops:
  7.2 0.0 copy-start.1
  7.2 0.0 all-gather.2.cloned.1.call-start
  7.2 1.5 multiply_reduce_fusion.3
  8.7 2.2 multiply_convert_fusion
  11.0 0.0 all-gather.2.cloned.1.call-update
  11.0 0.0 reduce-scatter.2.cloned.1.call-start
  12.4 0.0 copy-done.1
  12.4 0.2 multiply_reduce_fusion.4
  12.6 62.4 %all-gather.2.cloned.1.call-done = bf16[4096,1152]{1,0:T(8,128)(2,1)} async-done(((bf16[256,1152]{1,0:T(8,128)(2,1)}), bf16[4096,1152]{1,0:T(8,128)(2,1)}) %all-gather.2.cloned.1.call-update) | async-done | bytes 9437200 | tf_op jit(solution)/shard_map/all_gather | solution.py:52
  75.0 9.8 %fusion.3 = (f32[]{:T(128)}, f32[]{:T(128)}, f32[]{:T(128)}, f32[256,4096]{1,0:T(8,128)S(1)}) fusion(s32[256]{0:T(256)S(1)} %iota_add_fusion, f32[]{:T(128)S(6)} %copy.10, bf16[4096,1152]{1,0:T(8,128)(2,1)} %all-gather.2.cloned.1.call-done, f32[256,1152]{1,0:T(8,128)S(1)} %copy-done.1, f32[256]{0:T(256)S(1)} %add_rsqrt_fusion.1, f32[]{:T(128)S(6)} %exp.10), kind=kOutput, calls=%fused_computation.21 | convolution fusion | flops 2438529024 | bytes 14813204 | tf_op jit(solution)/shard_map/dot_general | solution.py:19
  84.7 0.0 copy-start.2
  84.7 2.0 copy-done.2
  86.8 8.5 %convolution_multiply_fusion = f32[4096,1152]{1,0:T(8,128)} fusion(f32[]{:T(128)S(6)} %exp.10, f32[256,1152]{1,0:T(8,128)S(1)} %copy-done.1, f32[256]{0:T(256)S(1)} %add_rsqrt_fusion.1, f32[256,4096]{1,0:T(8,128)S(1)} %get-tuple-element.11, f32[]{:T(128)S(6)} %copy.10, s32[256]{0:T(256)S(1)} %iota_add_fusion), kind=kOutput, calls=%fused_computation | convolution fusion | flops 2429616128 | bytes 24250376 | tf_op jit(solution)/shard_map/dot_general | solution.py:59
  95.3 0.0 reduce-scatter.2.cloned.1.call-update
  95.3 93.9 %all-reduce = (f32[]{:T(128)}, f32[]{:T(128)}, f32[]{:T(128)}) all-reduce(f32[]{:T(128)} %get-tuple-element.7, f32[]{:T(128)} %get-tuple-element.6, f32[]{:T(128)} %get-tuple-element.5), channel_id=1, replica_groups=mesh['blk'=16,'group'=16] {'blk','group'}, use_global_device_ids=true, to_apply=%region_3.4 | all-reduce | flops 3 | bytes 24 | tf_op jit(solution)/shard_map/psum | solution.py:66
  191.2 8.3 %multiply_reduce_fusion.2 = (f32[256]{0:T(256)S(1)}, f32[256,1152]{1,0:T(8,128)S(1)}) fusion(f32[256,1152]{1,0:T(8,128)S(1)} %copy-done.1, f32[256]{0:T(256)S(1)} %add_rsqrt_fusion.1, bf16[4096,1152]{1,0:T(8,128)(2,1)} %all-gather.2.cloned.1.call-done, s32[256]{0:T(256)S(1)} %iota_add_fusion, f32[256,4096]{1,0:T(8,128)} %copy-done.2, f32[]{:T(128)S(6)} %copy.10, ...), kind=kOutput, calls=%fused_computation.11 | convolution fusion | flops 2425487104 | bytes 15993864 | tf_op jit(solution)/shard_map/dot_general | solution.py:56
  199.5 0.0 copy-start
  199.5 1.3 subtract_multiply_fusion.1
  200.8 100.6 %reduce-scatter.2.cloned.1.call-done = f32[256,1152]{1,0:T(8,128)} async-done(((f32[4096,1152]{1,0:T(8,128)}), f32[256,1152]{1,0:T(8,128)}) %reduce-scatter.2.cloned.1.call-update) | async-done | bytes 1179664 | tf_op jit(solution)/shard_map/reduce_scatter | solution.py:57
  301.3 0.0 copy-done
  301.3 1.6 multiply_reduce_fusion.1
  302.9 2.5 subtract_multiply_fusion
  (3 shorter events, 0.0 us)
Async XLA Ops:
  7.2 5.2 %copy-start.1 = (f32[256,1152]{1,0:T(8,128)S(1)}, f32[256,1152]{1,0:T(8,128)}, u32[]{:S(2)}) copy-start(f32[256,1152]{1,0:T(8,128)} %param.4) | copy-start | bytes 3538948
  7.2 67.8 %all-gather.2.cloned.1.call-start = ((), (), s32[]{:S(2)}) async-start(), calls=%async_computation.1 | async-start | bytes 10027008 | tf_op jit(solution)/shard_map/all_gather | solution.py:52
  11.0 290.3 %reduce-scatter.2.cloned.1.call-start = ((), (), s32[]{:S(2)}) async-start(), calls=%async_computation.2 | async-start | bytes 20054016 | tf_op jit(solution)/shard_map/reduce_scatter | solution.py:57
  84.7 2.0 copy-start.2
  199.5 101.9 %copy-start = (f32[256,1152]{1,0:T(8,128)S(1)}, f32[256,1152]{1,0:T(8,128)}, u32[]{:S(2)}) copy-start(f32[256,1152]{1,0:T(8,128)} %param.5) | copy-start | bytes 3538948
Sparse Core Ops, SparseCore 0:
  11.1 63.7 all-gather.1
  95.5 205.8 reduce-scatter.1
where the time goes:
time: 316 us
  waiting for transfers between devices  163 us (52%)
  blocking collectives  93.9 us (30%)
  matrix products  26.6 us (8%)
  between operations  20.8 us (7%)
  other arithmetic  9.3 us (3%)
    reduce_scatter x1, waiting for transfers between devices, shards(): lax.psum_scatter(scale * lax.dot_general(grad_q, image_norm, (((0,), (0,)...  101 us
    psum x1, blocking collectives, shards(): lax.psum((loss_part, scale_part, bias_part), ('blk', 'group'))  93.9 us
    all_gather x1, waiting for transfers between devices, shards(): text_all = lax.all_gather(text_norm, 'blk', axis=0, tiled=True)  62.4 us
    dot_general x1, matrix products, block_grad(): lax.dot_general(image_rows, text_rows, (((1,), (1,)), ((), ())), preferre...  9.78 us
    dot_general x1, matrix products, shards(): lax.dot_general(grad_q, image_norm, (((0,), (0,)), ((), ())), preferred_e...  8.53 us
    dot_general x1, matrix products, shards(): jnp.dot(grad_q, text_all, preferred_element_type=jnp.float32)  8.3 us
  transfers between devices with their start and end apart: 2, of which 2 were waited for; matrix products, arithmetic and copies ran while one was open for 3% of the time, Pallas kernels for 0%

commit v1 on v0

v1 whole, which is shorter than its diff:
```python
import jax
import jax.numpy as jnp
from jax import lax
from jax.experimental import pallas as pl
from jax.experimental.pallas import tpu as pltpu
from jax.sharding import PartitionSpec as P

F32 = jnp.float32
BF16 = jnp.bfloat16
VMEM = pl.BlockSpec(memory_space=pltpu.VMEM)
SMEM = pl.BlockSpec(memory_space=pltpu.SMEM)


def params(mib):
    return pltpu.CompilerParams(vmem_limit_bytes=mib * 1024 * 1024)


def unit_rows(emb):
    inverse = lax.rsqrt(jnp.sum(emb * emb, axis=1, keepdims=True) + 1e-06)
    return emb * inverse, inverse


def normalize_kernel(image_ref, text_ref, image_out, text_out):
    image_out[...] = unit_rows(image_ref[...])[0].astype(BF16)
    text_out[...] = unit_rows(text_ref[...])[0].astype(BF16)


def normalize(image_emb, text_emb):
    rows, width = image_emb.shape
    return pl.pallas_call(
        normalize_kernel,
        out_shape=(jax.ShapeDtypeStruct((rows, width), BF16),) * 2,
        in_specs=[VMEM] * 2,
        out_specs=(VMEM,) * 2,
        compiler_params=params(16),
        cost_estimate=pl.CostEstimate(
            flops=8 * rows * width, bytes_accessed=12 * rows * width, transcendentals=rows
        ),
        name="normalize",
    )(image_emb, text_emb)


def cut(block, at):
    rows, width = block.shape

    def kernel(block_ref, out_ref):
        out_ref[...] = block_ref[pl.ds(at, rows // 2), :]

    return pl.pallas_call(
        kernel,
        out_shape=jax.ShapeDtypeStruct((rows // 2, width), block.dtype),
        in_specs=[VMEM],
        out_specs=VMEM,
        compiler_params=params(16),
        cost_estimate=pl.CostEstimate(flops=0, bytes_accessed=rows * width, transcendentals=0),
        name="cut",
    )(block)


def sim_tile(image_rows, text_rows):
    return lax.dot_general(
        image_rows, text_rows, (((1,), (1,)), ((), ())), preferred_element_type=F32
    )


def pair_tile(sim, scale, bias, diagonal):
    scaled = scale * sim
    logits = scaled + bias
    rows, columns = sim.shape
    if diagonal:
        positive = lax.broadcasted_iota(jnp.int32, (rows, columns), 0) == (
            lax.broadcasted_iota(jnp.int32, (rows, columns), 1)
        )
        logits = jnp.where(positive, -logits, logits)
    odds = jnp.exp(logits)
    total = 1.0 + odds
    inverse = pl.reciprocal(total, approx=True)
    inverse = inverse * (2.0 - total * inverse)
    grad = odds * inverse
    if diagonal:
        grad = jnp.where(positive, -grad, grad)
    lost = (odds - (total - 1.0)) * inverse
    part = rows // 8
    product = total[:part]
    for i in range(1, 8):
        product = product * total[i * part : (i + 1) * part]

    def fold(values):
        return jnp.sum(values.reshape(values.shape[0] // 8, 8, columns), axis=0)

    loss = fold(jnp.log(product)) + fold(lost)
    return grad.astype(BF16), loss, fold(grad * scaled), fold(grad)


def write_sums(sums_ref, loss, scaled, grad):
    row = lax.broadcasted_iota(jnp.int32, sums_ref.shape, 0)
    sums_ref[...] = jnp.where(
        row == 0, jnp.sum(loss), jnp.where(row == 1, jnp.sum(scaled), jnp.sum(grad))
    )


def write_copies(out, sums):
    for i in range(out.shape[0] // 8):
        out[pl.ds(i * 8, 8), :] = sums


def near_kernel(
    scalars, own_i, left_i, right_i, own_t, core_t, y_t, yc_t,
    own_out, left_top_out, left_bot_out, right_top_out, right_bot_out,
    images, texts, grads, sums_ref,
):
    rows = own_i.shape[0]
    half = rows // 2
    scale, bias = scalars[0], scalars[1]
    for i, src in enumerate((own_i, left_i, right_i)):
        images[pl.ds(i * rows, rows), :] = src[...]
    for i, src in enumerate((own_t, core_t, y_t, yc_t)):
        texts[pl.ds(i * rows, rows), :] = src[...]
    loss = scaled = grad = jnp.zeros((8, rows), F32)
    tiles = [(b, t) for b in range(3) for t in range(4)]

    def sim_of(k):
        b, t = tiles[k]
        return sim_tile(images[pl.ds(b * rows, rows), :], texts[pl.ds(t * rows, rows), :])

    sim = sim_of(0)
    for k, (b, t) in enumerate(tiles):
        sim_next = sim_of(k + 1) if k + 1 < len(tiles) else None
        grad_q, loss_now, scaled_now, grad_now = pair_tile(sim, scale, bias, k == 0)
        grads[pl.ds(b * rows, rows), pl.ds(t * rows, rows)] = grad_q
        loss, scaled, grad = loss + loss_now, scaled + scaled_now, grad + grad_now
        sim = sim_next
        if t == 3:
            partial = jnp.dot(
                grads[pl.ds(b * rows, rows), :], texts[...], preferred_element_type=F32
            )
            if b == 0:
                own_out[...] = partial
            elif b == 1:
                left_top_out[...] = partial[:half].astype(BF16)
                left_bot_out[...] = partial[half:]
            else:
                right_top_out[...] = partial[:half]
                right_bot_out[...] = partial[half:].astype(BF16)
    write_sums(sums_ref, loss, scaled, grad)


def text_grad(grads, near_images, far_grads, far_images, at):
    return lax.dot_general(
        grads[:, at], near_images[...], (((0,), (0,)), ((), ())), preferred_element_type=F32
    ) + lax.dot_general(
        far_grads[:, at], far_images[...], (((0,), (0,)), ((), ())), preferred_element_type=F32
    )


def far_kernel(
    scalars, top_i, bot_i, near_images, texts, near_grads, near_sums,
    far_top, far_bot, y_out, yc_out, images, grads, sums_ref,
):
    half = top_i.shape[0]
    rows = 2 * half
    scale, bias = scalars[0], scalars[1]
    images[pl.ds(0, half), :] = top_i[...]
    images[pl.ds(half, half), :] = bot_i[...]
    loss = scaled = grad = jnp.zeros((8, rows), F32)

    def sim_of(t):
        return sim_tile(images[...], texts[pl.ds(t * rows, rows), :])

    sim = sim_of(0)
    for t in range(4):
        sim_next = sim_of(t + 1) if t < 3 else None
        grad_q, loss_now, scaled_now, grad_now = pair_tile(sim, scale, bias, False)
        grads[:, pl.ds(t * rows, rows)] = grad_q
        loss, scaled, grad = loss + loss_now, scaled + scaled_now, grad + grad_now
        sim = sim_next
    partial = jnp.dot(grads[...], texts[...], preferred_element_type=F32)
    far_top[...] = partial[:half].astype(BF16)
    far_bot[...] = partial[half:].astype(BF16)
    yc_out[...] = text_grad(near_grads, near_images, grads, images, pl.ds(3 * rows, rows)).astype(BF16)
    y_out[...] = text_grad(near_grads, near_images, grads, images, pl.ds(2 * rows, rows))
    write_sums(sums_ref, loss, scaled, grad)
    sums_ref[...] += near_sums[...]


def text_kernel(
    near_grads, far_grads, near_images, far_images, own_p, top_p, bot_p, sums,
    own_out, core_out, own_sum, sums_out,
):
    rows = far_images.shape[0]
    half = rows // 2
    for t, out in ((1, core_out), (0, own_out)):
        out[...] = text_grad(
            near_grads, near_images, far_grads, far_images, pl.ds(t * rows, rows)
        ).astype(out.dtype)
    own_sum[:half, :] = own_p[:half, :] + top_p[...].astype(F32)
    own_sum[half:, :] = own_p[half:, :] + bot_p[...].astype(F32)
    write_copies(sums_out, sums[...])


def near_part(scalars, images, texts):
    rows, width = texts[0].shape
    half = rows // 2
    shape = jax.ShapeDtypeStruct
    return pl.pallas_call(
        near_kernel,
        out_shape=(
            shape((rows, width), F32),
            shape((half, width), BF16),
            shape((half, width), F32),
            shape((half, width), F32),
            shape((half, width), BF16),
            shape((3 * rows, width), BF16),
            shape((4 * rows, width), BF16),
            shape((3 * rows, 4 * rows), BF16),
            shape((8, 128), F32),
        ),
        in_specs=[SMEM] + [VMEM] * 7,
        out_specs=(VMEM,) * 9,
        compiler_params=params(32),
        cost_estimate=pl.CostEstimate(
            flops=2 * 2 * 12 * rows * rows * width,
            bytes_accessed=24 * rows * width,
            transcendentals=3 * 12 * rows * rows,
        ),
        name="near",
    )(scalars, *images, *texts)


def far_part(scalars, far_images, near_images, texts, near_grads, near_sums):
    half, width = far_images[0].shape
    rows = 2 * half
    shape = jax.ShapeDtypeStruct
    return pl.pallas_call(
        far_kernel,
        out_shape=(
            shape((half, width), BF16),
            shape((half, width), BF16),
            shape((rows, width), F32),
            shape((rows, width), BF16),
            shape((rows, width), BF16),
            shape((rows, 4 * rows), BF16),
            shape((8, 128), F32),
        ),
        in_specs=[SMEM] + [VMEM] * 6,
        out_specs=(VMEM,) * 7,
        compiler_params=params(32),
        cost_estimate=pl.CostEstimate(
            flops=rows * rows * width,
            bytes_accessed=2 * rows * width,
            transcendentals=rows * rows,
        ),
        name="far",
    )(scalars, *far_images, near_images, texts, near_grads, near_sums)


def text_part(near_grads, far_grads, near_images, far_images, own_p, top_p, bot_p, sums, copies):
    rows, width = far_images.shape
    shape = jax.ShapeDtypeStruct
    return pl.pallas_call(
        text_kernel,
        out_shape=(
            shape((rows, width), F32), shape((rows, width), BF16), shape((rows, width), F32),
            shape((copies * 8, 128), F32),
        ),
        in_specs=[VMEM] * 8,
        out_specs=(VMEM,) * 4,
        compiler_params=params(32),
        cost_estimate=pl.CostEstimate(
            flops=rows * rows * width, bytes_accessed=rows * width, transcendentals=0
        ),
        name="text",
    )(near_grads, far_grads, near_images, far_images, own_p, top_p, bot_p, sums)


def relay_y_kernel(own, passing, out):
    out[...] = (own[...] + passing[...].astype(F32)).astype(BF16)


def relay_y(own, passing):
    return pl.pallas_call(
        relay_y_kernel,
        out_shape=jax.ShapeDtypeStruct(passing.shape, BF16),
        in_specs=[VMEM] * 2,
        out_specs=VMEM,
        compiler_params=params(16),
        cost_estimate=pl.CostEstimate(flops=passing.size, bytes_accessed=passing.size, transcendentals=0),
        name="relay_y",
    )(own, passing)


def relay_kernel(top, top_passing, bot, bot_passing, own_p, arrived, top_out, bot_out, own_out, sums_out):
    top_out[...] = (top[...] + top_passing[...].astype(F32)).astype(BF16)
    bot_out[...] = (bot[...] + bot_passing[...].astype(F32)).astype(BF16)
    own_out[...] = own_p[...]
    sums = arrived[pl.ds(0, 8), :]
    for i in range(1, arrived.shape[0] // 8):
        sums += arrived[pl.ds(i * 8, 8), :]
    write_copies(sums_out, sums)


def relay(top, top_passing, bot, bot_passing, own_p, arrived, copies):
    shape = jax.ShapeDtypeStruct
    return pl.pallas_call(
        relay_kernel,
        out_shape=(
            shape(top.shape, BF16), shape(bot.shape, BF16), shape(own_p.shape, F32),
            shape((copies * 8, 128), F32),
        ),
        in_specs=[VMEM] * 6,
        out_specs=(VMEM,) * 4,
        compiler_params=params(16),
        cost_estimate=pl.CostEstimate(flops=top.size, bytes_accessed=top.size, transcendentals=0),
        name="relay",
    )(top, top_passing, bot, bot_passing, own_p, arrived)


def backnorm(emb, upstream, scale):
    hat, inverse = unit_rows(emb)
    along = jnp.sum(hat * upstream, axis=1, keepdims=True)
    return (scale * inverse) * (upstream - hat * along)


def image_end_kernel(scalars, emb, own, top, bot, out):
    half = emb.shape[0] // 2
    for at, part in ((0, top), (half, bot)):
        at = pl.ds(at, half)
        out[at, :] = backnorm(emb[at, :], own[at, :] + part[...].astype(F32), scalars[0])


def text_end_kernel(scalars, emb, own, one, two, out):
    upstream = own[...] + one[...].astype(F32) + two[...].astype(F32)
    out[...] = backnorm(emb[...], upstream, scalars[0])


def end_part(kernel, name, scalars, emb, *parts):
    rows, width = emb.shape
    return pl.pallas_call(
        kernel,
        out_shape=jax.ShapeDtypeStruct((rows, width), F32),
        in_specs=[SMEM] + [VMEM] * (1 + len(parts)),
        out_specs=VMEM,
        compiler_params=params(24),
        cost_estimate=pl.CostEstimate(
            flops=10 * rows * width, bytes_accessed=16 * rows * width, transcendentals=rows
        ),
        name=name,
    )(scalars, emb, *parts)


def shards(image_emb, text_emb, log_scale, bias):
    rows = image_emb.shape[0]
    blocks = lax.axis_size("blk")
    groups = lax.axis_size("group")
    ahead = [(i, (i + 4) % blocks) for i in range(blocks)]
    back = [(i, (i - 4) % blocks) for i in range(blocks)]
    across_y = [(i, i ^ 2) for i in range(blocks)]
    across_core = [(i, i ^ 1) for i in range(blocks)]

    def send(value, perm):
        return lax.ppermute(value, "blk", perm)

    scale = jnp.exp(log_scale)
    scalars = jnp.stack([scale, bias])
    own_i, own_t = normalize(image_emb, text_emb)
    left_i = send(own_i, ahead)
    right_i = send(own_i, back)
    y_t = send(own_t, across_y)
    core_t = send(own_t, across_core)
    yc_t = send(y_t, across_core)
    top_i = send(cut(left_i, 0), ahead)
    bot_i = send(cut(right_i, rows // 2), back)

    (
        own_p, left_top_p, left_bot_p, right_top_p, right_bot_p,
        near_images, texts, near_grads, near_sums,
    ) = near_part(scalars, (own_i, left_i, right_i), (own_t, core_t, y_t, yc_t))
    from_left_bot = send(right_bot_p, ahead)
    from_right_top = send(left_top_p, back)

    far_top, far_bot, y_q, yc_q, far_images, far_grads, sums = far_part(
        scalars, (top_i, bot_i), near_images, texts, near_grads, near_sums
    )
    relay_top = send(far_top, ahead)
    relay_bot = send(far_bot, back)
    from_y = send(relay_y(y_q, send(yc_q, across_core)), across_y)
    own_q, core_q, own_p, sums = text_part(
        near_grads, far_grads, near_images, far_images, own_p, from_right_top, from_left_bot, sums, blocks
    )
    from_core = send(core_q, across_core)
    sums = lax.all_to_all(sums, "blk", split_axis=0, concat_axis=0, tiled=True)
    top_sum, bot_sum, own_p, sums = relay(
        right_top_p, relay_top, left_bot_p, relay_bot, own_p, sums, groups
    )
    from_left_top = send(top_sum, ahead)
    from_right_bot = send(bot_sum, back)
    sums = lax.all_to_all(sums, "group", split_axis=0, concat_axis=0, tiled=True)
    sums = jnp.sum(sums.reshape(groups, 8, 128), axis=0)

    grad_text = end_part(text_end_kernel, "text_end", scalars, text_emb, own_q, from_core, from_y)
    grad_image = end_part(
        image_end_kernel, "image_end", scalars, image_emb,
        own_p, from_left_top, from_right_bot,
    )
    totals = sums[:, 0] / (rows * blocks * groups)
    return (totals[0], grad_image, grad_text, totals[1], totals[2])


def solution(mesh):
    in_specs = (P(("blk", "group"), None), P(("blk", "group"), None), P(), P())
    out_specs = (P(), P(("blk", "group"), None), P(("blk", "group"), None), P(), P())
    return jax.shard_map(shards, mesh=mesh, in_specs=in_specs, out_specs=out_specs, check_vma=False)
```

time: 316 us -> 106 us (0.34)
  the two profiles are of different devices: /device:TPU:1 before, /device:TPU:32 now
where the time goes in v1:
time: 106 us; the launch traced here: 105 us
  starting transfers between devices  35.5 us (33%)
  waiting for transfers between devices  31.3 us (30%)
  Pallas kernels  19.6 us (18%)
  local copies, waits for them, and re-layouts  16 us (15%)
  between operations  2.11 us (2%)
    ppermute x16, starting transfers between devices, send(): return lax.ppermute(value, 'blk', perm)  18.9 us
    ppermute x16, waiting for transfers between devices, send(): return lax.ppermute(value, 'blk', perm)  16.5 us
    unnamed x38, local copies, waits for them, and re-layouts  15.5 us
    all_to_all x1, starting transfers between devices, shards(): lax.all_to_all(sums, 'group', split_axis=0, concat_axis=0, tiled=True)  10.9 us
    all_to_all x1, waiting for transfers between devices, shards(): sums = lax.all_to_all(sums, 'blk', split_axis=0, concat_axis=0, tiled=True)  9.08 us
    pallas_call x1, Pallas kernels, near_part(): pl.pallas_call(near_kernel, out_shape=(shape((rows, width), F32), shape((...  7 us
    all_to_all x1, waiting for transfers between devices, shards(): lax.all_to_all(sums, 'group', split_axis=0, concat_axis=0, tiled=True)  5.71 us
    all_to_all x1, starting transfers between devices, shards(): sums = lax.all_to_all(sums, 'blk', split_axis=0, concat_axis=0, tiled=True)  5.63 us
  transfers between devices with their start and end apart: 18, of which 6 were waited for; matrix products, arithmetic and copies ran while one was open for 1% of the time, Pallas kernels for 12%

profile of v1, /device:TPU:32, one launch (start us, length us, event | category | flops | bytes accessed | tf_op | source)
XLA Modules:
  0.0 104.6 jit_solution(13996702992113218498)
XLA Ops:
  0.6 0.0 copy-start
  0.6 1.3 %copy-done = f32[256,1152]{1,0:T(8,128)S(1)} copy-done((f32[256,1152]{1,0:T(8,128)S(1)}, f32[256,1152]{1,0:T(8,128)}, u32[]{:S(2)}) %copy-start) | copy-done | bytes 1179672
  1.9 1.3 %copy-done.2 = f32[256,1152]{1,0:T(8,128)S(1)} copy-done((f32[256,1152]{1,0:T(8,128)S(1)}, f32[256,1152]{1,0:T(8,128)}, u32[]{:S(2)}) %copy-start.2) | copy-done | bytes 1179672
  3.2 0.3 normalize.1
  3.5 1.7 %collective-permute-start.3 = (bf16[256,1152]{1,0:T(8,128)(2,1)S(1)}, bf16[256,1152]{1,0:T(8,128)(2,1)S(1)}, u32[]{:S(2)}, u32[]{:S(2)}) collective-permute-start(bf16[256,1152]{1,0:T(8,128)(2,1)S(1)} %get-tuple-element.32.own_t), channel_id=1, source_target_pairs={{0,32},{16,48},{32,0},{48,16},{64,96},{80,112},{96,64},{112,80},{1... | collective-permute-start | bytes 1769480 | tf_op jit(solution)/shard_map/ppermute | solution.py:361
  5.1 1.5 %collective-permute-start = (bf16[256,1152]{1,0:T(8,128)(2,1)S(1)}, bf16[256,1152]{1,0:T(8,128)(2,1)S(1)}, u32[]{:S(2)}, u32[]{:S(2)}) collective-permute-start(bf16[256,1152]{1,0:T(8,128)(2,1)S(1)} %get-tuple-element.31.own_i), channel_id=1, source_target_pairs={{0,64},{16,80},{32,96},{48,112},{64,128},{80,144},{96,160},{112,17... | collective-permute-start | bytes 1769480 | tf_op jit(solution)/shard_map/ppermute | solution.py:361
  6.6 1.7 %collective-permute-start.1 = (bf16[256,1152]{1,0:T(8,128)(2,1)S(1)}, bf16[256,1152]{1,0:T(8,128)(2,1)S(1)}, u32[]{:S(2)}, u32[]{:S(2)}) collective-permute-start(bf16[256,1152]{1,0:T(8,128)(2,1)S(1)} %get-tuple-element.31.own_i), channel_id=1, source_target_pairs={{0,192},{16,208},{32,224},{48,240},{64,0},{80,16},{96,32},{112,48}... | collective-permute-start | bytes 1769480 | tf_op jit(solution)/shard_map/ppermute | solution.py:361
  8.4 10.3 %collective-permute-done.3.y_t = bf16[256,1152]{1,0:T(8,128)(2,1)S(1)} collective-permute-done((bf16[256,1152]{1,0:T(8,128)(2,1)S(1)}, bf16[256,1152]{1,0:T(8,128)(2,1)S(1)}, u32[]{:S(2)}, u32[]{:S(2)}) %collective-permute-start.3) | collective-permute-done | bytes 589856 | tf_op jit(solution)/shard_map/ppermute | solution.py:361
  20.0 0.1 pad_maximum_fusion.scalars
  20.0 1.1 %collective-permute-done.left_i.block_ref = bf16[256,1152]{1,0:T(8,128)(2,1)S(1)} collective-permute-done((bf16[256,1152]{1,0:T(8,128)(2,1)S(1)}, bf16[256,1152]{1,0:T(8,128)(2,1)S(1)}, u32[]{:S(2)}, u32[]{:S(2)}) %collective-permute-start) | collective-permute-done | bytes 589856 | tf_op jit(solution)/shard_map/ppermute | solution.py:361
  21.2 0.5 collective-permute-start.5
  21.7 3.1 %collective-permute-start.6 = (bf16[128,1152]{1,0:T(8,128)(2,1)S(1)}, bf16[128,1152]{1,0:T(8,128)(2,1)S(1)}, u32[]{:S(2)}, u32[]{:S(2)}) collective-permute-start(bf16[128,1152]{1,0:T(8,128)(2,1)S(1)} %cut.3), channel_id=1, source_target_pairs={{0,192},{16,208},{32,224},{48,240},{64,0},{80,16},{96,32},{112,48}... | collective-permute-start | bytes 884744 | tf_op jit(solution)/shard_map/ppermute | solution.py:361
  24.8 7.0 %near.1 = (f32[256,1152]{1,0:T(8,128)S(1)}, bf16[128,1152]{1,0:T(8,128)(2,1)S(1)}, f32[128,1152]{1,0:T(8,128)S(1)}, f32[128,1152]{1,0:T(8,128)S(1)}, bf16[128,11...) custom-call(f32[2]{0:T(128)S(1)} %pad_maximum_fusion.scalars, ...), custom_call_target="tpu_custom_call" | custom-call | flops 3623878656 | bytes 7077888 | tf_op jit(solution)/shard_map/near/pallas_call | solution.py:205
  31.8 0.0 copy-start.6
  31.8 0.8 copy-done.6
  32.6 0.8 copy-done.8
  33.4 4.1 %far.1 = (bf16[128,1152]{1,0:T(8,128)(2,1)}, bf16[128,1152]{1,0:T(8,128)(2,1)}, f32[256,1152]{1,0:T(8,128)S(1)}, bf16[256,1152]{1,0:T(8,128)(2,1)S(1)}, bf16[256...) custom-call(f32[2]{0:T(128)S(1)} %pad_maximum_fusion.scalars, ...), custom_call_target="tpu_custom_call" | custom-call | flops 75497472 | bytes 589824 | tf_op jit(solution)/shard_map/far/pallas_call | solution.py:234
  37.5 0.1 collective-permute-start.14
  37.6 0.1 collective-permute-start.10
  37.7 3.2 %collective-permute-start.9 = (bf16[128,1152]{1,0:T(8,128)(2,1)S(1)}, bf16[128,1152]{1,0:T(8,128)(2,1)S(1)}, u32[]{:S(2)}, u32[]{:S(2)}) collective-permute-start(bf16[128,1152]{1,0:T(8,128)(2,1)S(1)} %get-tuple-element.44), channel_id=1, source_target_pairs={{0,192},{16,208},{32,224},{48,240},{64,0},{80,16},{96,32},{112,48}... | collective-permute-start | bytes 884744 | tf_op jit(solution)/shard_map/ppermute | solution.py:361
  41.0 3.2 %collective-permute-start.8 = (bf16[128,1152]{1,0:T(8,128)(2,1)}, bf16[128,1152]{1,0:T(8,128)(2,1)S(1)}, u32[]{:S(2)}, u32[]{:S(2)}) collective-permute-start(bf16[128,1152]{1,0:T(8,128)(2,1)} %get-tuple-element.40), channel_id=1, source_target_pairs={{0,192},{16,208},{32,224},{48,240},{64,0},{80,16},{96,32},{112,48}... | collective-permute-start | bytes 884744 | tf_op jit(solution)/shard_map/ppermute | solution.py:361
  44.2 4.5 %collective-permute-done.10.bot_p = bf16[128,1152]{1,0:T(8,128)(2,1)S(1)} collective-permute-done((bf16[128,1152]{1,0:T(8,128)(2,1)S(1)}, bf16[128,1152]{1,0:T(8,128)(2,1)S(1)}, u32[]{:S(2)}, u32[]{:S(2)}) %collective-permute-start.10) | collective-permute-done | bytes 294944 | tf_op jit(solution)/shard_map/ppermute | solution.py:361
  48.7 2.3 %text.1 = (f32[256,1152]{1,0:T(8,128)S(1)}, bf16[256,1152]{1,0:T(8,128)(2,1)}, f32[256,1152]{1,0:T(8,128)S(1)}, f32[128,128]{1,0:T(8,128)}) custom-call(bf16[768,1024]{1,0:T(8,128)(2,1)S(1)} %get-tuple-element.36.near_grads, bf16[256,1024]{1,0:T(8,128)(2,1)S(1)} %get-tuple-element.41.far_grads, bf16[768,1152]{1,0:T(8,128)(2,1)S(1)} %get-tuple-element.34.near_images, ...), custom_call_target="tpu_custom_call" | custom-call | flops 75497472 | bytes 294912 | tf_op jit(solution)/shard_map/text/pallas_call | solution.py:260
  51.0 1.0 relay_y.1
  52.0 0.5 collective-permute-start.15
  52.5 5.6 %all-to-all-start = ((f32[16,8,128]{2,1,0:T(8,128)}), f32[16,8,128]{2,1,0:T(8,128)S(1)}, u32[]{:S(2)}, u32[]{:S(2)}) async-start(f32[16,8,128]{2,1,0:T(8,128)} %bitcast.2), calls=%async_computation | async-start | bytes 131072 | tf_op jit(solution)/shard_map/all_to_all | solution.py:391
  58.1 0.7 copy-done.10
  58.8 0.7 copy-done.12
  59.6 9.1 %all-to-all-done = f32[16,8,128]{2,1,0:T(8,128)S(1)} async-done(((f32[16,8,128]{2,1,0:T(8,128)}), f32[16,8,128]{2,1,0:T(8,128)S(1)}, u32[]{:S(2)}, u32[]{:S(2)}) %all-to-all-start) | async-done | bytes 65568 | tf_op jit(solution)/shard_map/all_to_all | solution.py:391
  68.6 0.6 copy-done.14
  69.3 1.1 %copy-done.7 = f32[128,1152]{1,0:T(8,128)S(1)} copy-done((f32[128,1152]{1,0:T(8,128)S(1)}, f32[128,1152]{1,0:T(8,128)}, u32[]{:S(2)}) %copy-start.7) | copy-done | bytes 589848
  70.3 1.1 %copy-done.9 = f32[128,1152]{1,0:T(8,128)S(1)} copy-done((f32[128,1152]{1,0:T(8,128)S(1)}, f32[128,1152]{1,0:T(8,128)}, u32[]{:S(2)}) %copy-start.9) | copy-done | bytes 589848
  71.4 1.0 copy-done.11
  72.4 1.0 copy-done.13
  73.3 0.8 copy-done.15
  74.2 0.2 relay.1
  74.4 1.0 copy-done.4
  75.4 0.7 copy-done.17
  76.1 0.7 copy-done.18
  76.8 0.6 copy-done.16
  77.4 10.9 %all-to-all-start.1 = ((f32[16,8,128]{2,1,0:T(8,128)}), f32[16,8,128]{2,1,0:T(8,128)S(1)}, u32[]{:S(2)}, u32[]{:S(2)}) async-start(f32[16,8,128]{2,1,0:T(8,128)} %bitcast.10), calls=%async_computation.1 | async-start | bytes 131072 | tf_op jit(solution)/shard_map/all_to_all | solution.py:397
  88.4 3.3 %collective-permute-start.12 = (bf16[128,1152]{1,0:T(8,128)(2,1)}, bf16[128,1152]{1,0:T(8,128)(2,1)S(1)}, u32[]{:S(2)}, u32[]{:S(2)}) collective-permute-start(bf16[128,1152]{1,0:T(8,128)(2,1)} %copy-done.17), channel_id=1, source_target_pairs={{0,192},{16,208},{32,224},{48,240},{64,0},{80,16},{96,32},{112,48}... | collective-permute-start | bytes 884744 | tf_op jit(solution)/shard_map/ppermute | solution.py:361
  91.7 5.7 %all-to-all-done.1 = f32[16,8,128]{2,1,0:T(8,128)S(1)} async-done(((f32[16,8,128]{2,1,0:T(8,128)}), f32[16,8,128]{2,1,0:T(8,128)S(1)}, u32[]{:S(2)}, u32[]{:S(2)}) %all-to-all-start.1) | async-done | bytes 65568 | tf_op jit(solution)/shard_map/all_to_all | solution.py:397
  97.4 0.5 fusion
  98.0 0.6 collective-permute-done.11.top
  98.6 1.3 %copy-done.5 = f32[256,1152]{1,0:T(8,128)S(1)} copy-done((f32[256,1152]{1,0:T(8,128)S(1)}, f32[256,1152]{1,0:T(8,128)}, u32[]{:S(2)}) %copy-start.5) | copy-done | bytes 1179672
  99.8 2.0 %image_end.1 = f32[256,1152]{1,0:T(8,128)} custom-call(f32[2]{0:T(128)S(1)} %pad_maximum_fusion.scalars, f32[256,1152]{1,0:T(8,128)S(1)} %copy-done.3, f32[256,1152]{1,0:T(8,128)S(1)} %copy-done.5, bf16[128,1152]{1,0:T(8,128)(2,1)S(1)} %collective-permute-done.11.top, bf16[128,1152]{1,0:T(8,128)(2,1)S(1)} %collective-permute-done.12.bot), custom_call_target="tpu_custom_call" | custom-call | flops 2949120 | bytes 4718592 | tf_op jit(solution)/shard_map/image_end/pallas_call | solution.py:338
  101.8 2.8 %text_end.1 = f32[256,1152]{1,0:T(8,128)} custom-call(f32[2]{0:T(128)S(1)} %pad_maximum_fusion.scalars, f32[256,1152]{1,0:T(8,128)S(1)} %copy-done.1, f32[256,1152]{1,0:T(8,128)S(1)} %get-tuple-element.53.own, bf16[256,1152]{1,0:T(8,128)(2,1)} %collective-permute-done.13.one, bf16[256,1152]{1,0:T(8,128)(2,1)} %collective-permute-done.15.two), custom_call_target="tpu_custom_call" | custom-call | flops 2949120 | bytes 4718592 | tf_op jit(solution)/shard_map/text_end/pallas_call | solution.py:338
  (40 shorter events, 0.1 us)
Async XLA Ops:
  0.6 1.3 %copy-start = (f32[256,1152]{1,0:T(8,128)S(1)}, f32[256,1152]{1,0:T(8,128)}, u32[]{:S(2)}) copy-start(f32[256,1152]{1,0:T(8,128)} %emb.3) | copy-start | bytes 3538948
  1.9 1.3 %copy-start.2 = (f32[256,1152]{1,0:T(8,128)S(1)}, f32[256,1152]{1,0:T(8,128)}, u32[]{:S(2)}) copy-start(f32[256,1152]{1,0:T(8,128)} %emb.2) | copy-start | bytes 3538948
  3.5 15.2 %collective-permute-start.3 = (bf16[256,1152]{1,0:T(8,128)(2,1)S(1)}, bf16[256,1152]{1,0:T(8,128)(2,1)S(1)}, u32[]{:S(2)}, u32[]{:S(2)}) collective-permute-start(bf16[256,1152]{1,0:T(8,128)(2,1)S(1)} %get-tuple-element.32.own_t), channel_id=1, source_target_pairs={{0,32},{16,48},{32,0},{48,16},{64,96},{80,112},{96,64},{112,80},{1... | collective-permute-start | bytes 1769480 | tf_op jit(solution)/shard_map/ppermute | solution.py:361
  5.1 16.0 %collective-permute-start = (bf16[256,1152]{1,0:T(8,128)(2,1)S(1)}, bf16[256,1152]{1,0:T(8,128)(2,1)S(1)}, u32[]{:S(2)}, u32[]{:S(2)}) collective-permute-start(bf16[256,1152]{1,0:T(8,128)(2,1)S(1)} %get-tuple-element.31.own_i), channel_id=1, source_target_pairs={{0,64},{16,80},{32,96},{48,112},{64,128},{80,144},{96,160},{112,17... | collective-permute-start | bytes 1769480 | tf_op jit(solution)/shard_map/ppermute | solution.py:361
  6.6 15.0 %collective-permute-start.1 = (bf16[256,1152]{1,0:T(8,128)(2,1)S(1)}, bf16[256,1152]{1,0:T(8,128)(2,1)S(1)}, u32[]{:S(2)}, u32[]{:S(2)}) collective-permute-start(bf16[256,1152]{1,0:T(8,128)(2,1)S(1)} %get-tuple-element.31.own_i), channel_id=1, source_target_pairs={{0,192},{16,208},{32,224},{48,240},{64,0},{80,16},{96,32},{112,48}... | collective-permute-start | bytes 1769480 | tf_op jit(solution)/shard_map/ppermute | solution.py:361
  8.4 16.4 %collective-permute-start.2 = (bf16[256,1152]{1,0:T(8,128)(2,1)S(1)}, bf16[256,1152]{1,0:T(8,128)(2,1)S(1)}, u32[]{:S(2)}, u32[]{:S(2)}) collective-permute-start(bf16[256,1152]{1,0:T(8,128)(2,1)S(1)} %get-tuple-element.32.own_t), channel_id=1, source_target_pairs={{0,16},{16,0},{32,48},{48,32},{64,80},{80,64},{96,112},{112,96},{1... | collective-permute-start | bytes 1769480 | tf_op jit(solution)/shard_map/ppermute | solution.py:361
  18.6 6.1 %collective-permute-start.4 = (bf16[256,1152]{1,0:T(8,128)(2,1)S(1)}, bf16[256,1152]{1,0:T(8,128)(2,1)}, u32[]{:S(2)}, u32[]{:S(2)}) collective-permute-start(bf16[256,1152]{1,0:T(8,128)(2,1)S(1)} %collective-permute-done.3.y_t), channel_id=1, source_target_pairs={{0,16},{16,0},{32,48},{48,32},{64,80},{80,64},{96,112},{112,96},{1... | collective-permute-start | bytes 1769480 | tf_op jit(solution)/shard_map/ppermute | solution.py:361
  21.2 12.2 %collective-permute-start.5 = (bf16[128,1152]{1,0:T(8,128)(2,1)S(1)}, bf16[128,1152]{1,0:T(8,128)(2,1)S(1)}, u32[]{:S(2)}, u32[]{:S(2)}) collective-permute-start(bf16[128,1152]{1,0:T(8,128)(2,1)S(1)} %cut.2), channel_id=1, source_target_pairs={{0,64},{16,80},{32,96},{48,112},{64,128},{80,144},{96,160},{112,17... | collective-permute-start | bytes 884744 | tf_op jit(solution)/shard_map/ppermute | solution.py:361
  21.7 11.7 %collective-permute-start.6 = (bf16[128,1152]{1,0:T(8,128)(2,1)S(1)}, bf16[128,1152]{1,0:T(8,128)(2,1)S(1)}, u32[]{:S(2)}, u32[]{:S(2)}) collective-permute-start(bf16[128,1152]{1,0:T(8,128)(2,1)S(1)} %cut.3), channel_id=1, source_target_pairs={{0,192},{16,208},{32,224},{48,240},{64,0},{80,16},{96,32},{112,48}... | collective-permute-start | bytes 884744 | tf_op jit(solution)/shard_map/ppermute | solution.py:361
  31.8 0.8 copy-start.6
  32.6 0.8 copy-start.8
  37.5 13.5 %collective-permute-start.14 = (bf16[256,1152]{1,0:T(8,128)(2,1)S(1)}, bf16[256,1152]{1,0:T(8,128)(2,1)S(1)}, u32[]{:S(2)}, u32[]{:S(2)}) collective-permute-start(bf16[256,1152]{1,0:T(8,128)(2,1)S(1)} %get-tuple-element.56), channel_id=1, source_target_pairs={{0,16},{16,0},{32,48},{48,32},{64,80},{80,64},{96,112},{112,96},{1... | collective-permute-start | bytes 1769480 | tf_op jit(solution)/shard_map/ppermute | solution.py:361
  37.6 11.1 %collective-permute-start.10 = (bf16[128,1152]{1,0:T(8,128)(2,1)S(1)}, bf16[128,1152]{1,0:T(8,128)(2,1)S(1)}, u32[]{:S(2)}, u32[]{:S(2)}) collective-permute-start(bf16[128,1152]{1,0:T(8,128)(2,1)S(1)} %get-tuple-element.45), channel_id=1, source_target_pairs={{0,64},{16,80},{32,96},{48,112},{64,128},{80,144},{96,160},{112,17... | collective-permute-start | bytes 884744 | tf_op jit(solution)/shard_map/ppermute | solution.py:361
  37.7 11.0 %collective-permute-start.9 = (bf16[128,1152]{1,0:T(8,128)(2,1)S(1)}, bf16[128,1152]{1,0:T(8,128)(2,1)S(1)}, u32[]{:S(2)}, u32[]{:S(2)}) collective-permute-start(bf16[128,1152]{1,0:T(8,128)(2,1)S(1)} %get-tuple-element.44), channel_id=1, source_target_pairs={{0,192},{16,208},{32,224},{48,240},{64,0},{80,16},{96,32},{112,48}... | collective-permute-start | bytes 884744 | tf_op jit(solution)/shard_map/ppermute | solution.py:361
  41.0 17.1 %collective-permute-start.7 = (bf16[128,1152]{1,0:T(8,128)(2,1)}, bf16[128,1152]{1,0:T(8,128)(2,1)S(1)}, u32[]{:S(2)}, u32[]{:S(2)}) collective-permute-start(bf16[128,1152]{1,0:T(8,128)(2,1)} %get-tuple-element.38), channel_id=1, source_target_pairs={{0,64},{16,80},{32,96},{48,112},{64,128},{80,144},{96,160},{112,17... | collective-permute-start | bytes 884744 | tf_op jit(solution)/shard_map/ppermute | solution.py:361
  41.0 17.9 %collective-permute-start.8 = (bf16[128,1152]{1,0:T(8,128)(2,1)}, bf16[128,1152]{1,0:T(8,128)(2,1)S(1)}, u32[]{:S(2)}, u32[]{:S(2)}) collective-permute-start(bf16[128,1152]{1,0:T(8,128)(2,1)} %get-tuple-element.40), channel_id=1, source_target_pairs={{0,192},{16,208},{32,224},{48,240},{64,0},{80,16},{96,32},{112,48}... | collective-permute-start | bytes 884744 | tf_op jit(solution)/shard_map/ppermute | solution.py:361
  51.0 50.8 %collective-permute-start.13 = (bf16[256,1152]{1,0:T(8,128)(2,1)}, bf16[256,1152]{1,0:T(8,128)(2,1)}, u32[]{:S(2)}, u32[]{:S(2)}) collective-permute-start(bf16[256,1152]{1,0:T(8,128)(2,1)} %get-tuple-element.54), channel_id=1, source_target_pairs={{0,16},{16,0},{32,48},{48,32},{64,80},{80,64},{96,112},{112,96},{1... | collective-permute-start | bytes 1769480 | tf_op jit(solution)/shard_map/ppermute | solution.py:361
  52.0 49.9 %collective-permute-start.15 = (bf16[256,1152]{1,0:T(8,128)(2,1)}, bf16[256,1152]{1,0:T(8,128)(2,1)}, u32[]{:S(2)}, u32[]{:S(2)}) collective-permute-start(bf16[256,1152]{1,0:T(8,128)(2,1)} %relay_y.1), channel_id=1, source_target_pairs={{0,32},{16,48},{32,0},{48,16},{64,96},{80,112},{96,64},{112,80},{1... | collective-permute-start | bytes 1769480 | tf_op jit(solution)/shard_map/ppermute | solution.py:361
  52.5 16.2 %all-to-all-start = ((f32[16,8,128]{2,1,0:T(8,128)}), f32[16,8,128]{2,1,0:T(8,128)S(1)}, u32[]{:S(2)}, u32[]{:S(2)}) async-start(f32[16,8,128]{2,1,0:T(8,128)} %bitcast.2), calls=%async_computation | async-start | bytes 131072 | tf_op jit(solution)/shard_map/all_to_all | solution.py:391
  58.1 0.7 copy-start.10
  58.8 0.7 copy-start.12
  68.6 0.6 copy-start.14
  69.3 1.1 %copy-start.7 = (f32[128,1152]{1,0:T(8,128)S(1)}, f32[128,1152]{1,0:T(8,128)}, u32[]{:S(2)}) copy-start(f32[128,1152]{1,0:T(8,128)} %copy-done.6) | copy-start | bytes 1769476
  70.3 1.1 %copy-start.9 = (f32[128,1152]{1,0:T(8,128)S(1)}, f32[128,1152]{1,0:T(8,128)}, u32[]{:S(2)}) copy-start(f32[128,1152]{1,0:T(8,128)} %copy-done.8) | copy-start | bytes 1769476
  71.4 1.0 copy-start.11
  72.4 1.0 copy-start.13
  73.3 0.8 copy-start.15
  74.2 24.4 %copy-start.3 = (f32[256,1152]{1,0:T(8,128)S(1)}, f32[256,1152]{1,0:T(8,128)}, u32[]{:S(2)}) copy-start(f32[256,1152]{1,0:T(8,128)} %emb.2) | copy-start | bytes 3538948
  74.4 1.0 copy-start.4
  75.4 0.7 copy-start.17
  76.1 0.7 copy-start.18
  76.8 0.6 copy-start.16
  77.4 20.0 %all-to-all-start.1 = ((f32[16,8,128]{2,1,0:T(8,128)}), f32[16,8,128]{2,1,0:T(8,128)S(1)}, u32[]{:S(2)}, u32[]{:S(2)}) async-start(f32[16,8,128]{2,1,0:T(8,128)} %bitcast.10), calls=%async_computation.1 | async-start | bytes 131072 | tf_op jit(solution)/shard_map/all_to_all | solution.py:397
  88.4 10.2 %collective-permute-start.11 = (bf16[128,1152]{1,0:T(8,128)(2,1)}, bf16[128,1152]{1,0:T(8,128)(2,1)S(1)}, u32[]{:S(2)}, u32[]{:S(2)}) collective-permute-start(bf16[128,1152]{1,0:T(8,128)(2,1)} %copy-done.18), channel_id=1, source_target_pairs={{0,64},{16,80},{32,96},{48,112},{64,128},{80,144},{96,160},{112,17... | collective-permute-start | bytes 884744 | tf_op jit(solution)/shard_map/ppermute | solution.py:361
  88.4 10.2 %collective-permute-start.12 = (bf16[128,1152]{1,0:T(8,128)(2,1)}, bf16[128,1152]{1,0:T(8,128)(2,1)S(1)}, u32[]{:S(2)}, u32[]{:S(2)}) collective-permute-start(bf16[128,1152]{1,0:T(8,128)(2,1)} %copy-done.17), channel_id=1, source_target_pairs={{0,192},{16,208},{32,224},{48,240},{64,0},{80,16},{96,32},{112,48}... | collective-permute-start | bytes 884744 | tf_op jit(solution)/shard_map/ppermute | solution.py:361
  98.6 1.3 %copy-start.5 = (f32[256,1152]{1,0:T(8,128)S(1)}, f32[256,1152]{1,0:T(8,128)}, u32[]{:S(2)}) copy-start(f32[256,1152]{1,0:T(8,128)} %copy-done.4) | copy-start | bytes 3538948
  99.8 2.0 %copy-start.1 = (f32[256,1152]{1,0:T(8,128)S(1)}, f32[256,1152]{1,0:T(8,128)}, u32[]{:S(2)}) copy-start(f32[256,1152]{1,0:T(8,128)} %emb.3) | copy-start | bytes 3538948

commit v2 on v1

--- a/solution.py
+++ b/solution.py
@@ -7,6 +7,7 @@
 
 F32 = jnp.float32
 BF16 = jnp.bfloat16
+HBM = pl.BlockSpec(memory_space=pltpu.HBM)
 VMEM = pl.BlockSpec(memory_space=pltpu.VMEM)
 SMEM = pl.BlockSpec(memory_space=pltpu.SMEM)
 
@@ -20,9 +21,22 @@
     return emb * inverse, inverse
 
 
-def normalize_kernel(image_ref, text_ref, image_out, text_out):
-    image_out[...] = unit_rows(image_ref[...])[0].astype(BF16)
-    text_out[...] = unit_rows(text_ref[...])[0].astype(BF16)
+def normalize_kernel(image_ref, text_ref, image_out, text_out, images, texts, sems):
+    rows = image_ref.shape[0]
+    step = rows // 4
+    pairs = [
+        (src.at[pl.ds(i * step, step)], dst.at[pl.ds(i * step, step)])
+        for src, dst in ((image_ref, images), (text_ref, texts))
+        for i in range(4)
+    ]
+    copies = [pltpu.make_async_copy(src, dst, sems.at[i]) for i, (src, dst) in enumerate(pairs)]
+    for copy in copies:
+        copy.start()
+    for k, (emb, out) in enumerate(((images, image_out), (texts, text_out))):
+        for i in range(4):
+            copies[4 * k + i].wait()
+            at = pl.ds(i * step, step)
+            out[at, :] = unit_rows(emb[at, :])[0].astype(BF16)
 
 
 def normalize(image_emb, text_emb):
@@ -30,8 +44,13 @@
     return pl.pallas_call(
         normalize_kernel,
         out_shape=(jax.ShapeDtypeStruct((rows, width), BF16),) * 2,
-        in_specs=[VMEM] * 2,
+        in_specs=[HBM] * 2,
         out_specs=(VMEM,) * 2,
+        scratch_shapes=[
+            pltpu.VMEM((rows, width), F32),
+            pltpu.VMEM((rows, width), F32),
+            pltpu.SemaphoreType.DMA((8,)),
+        ],
         compiler_params=params(16),
         cost_estimate=pl.CostEstimate(
             flops=8 * rows * width, bytes_accessed=12 * rows * width, transcendentals=rows
@@ -99,11 +118,6 @@
     )
 
 
-def write_copies(out, sums):
-    for i in range(out.shape[0] // 8):
-        out[pl.ds(i * 8, 8), :] = sums
-
-
 def near_kernel(
     scalars, own_i, left_i, right_i, own_t, core_t, y_t, yc_t,
     own_out, left_top_out, left_bot_out, right_top_out, right_bot_out,
@@ -183,19 +197,12 @@
     sums_ref[...] += near_sums[...]
 
 
-def text_kernel(
-    near_grads, far_grads, near_images, far_images, own_p, top_p, bot_p, sums,
-    own_out, core_out, own_sum, sums_out,
-):
+def text_kernel(near_grads, far_grads, near_images, far_images, own_out, core_out):
     rows = far_images.shape[0]
-    half = rows // 2
     for t, out in ((1, core_out), (0, own_out)):
         out[...] = text_grad(
             near_grads, near_images, far_grads, far_images, pl.ds(t * rows, rows)
         ).astype(out.dtype)
-    own_sum[:half, :] = own_p[:half, :] + top_p[...].astype(F32)
-    own_sum[half:, :] = own_p[half:, :] + bot_p[...].astype(F32)
-    write_copies(sums_out, sums[...])
 
 
 def near_part(scalars, images, texts):
@@ -254,65 +261,65 @@
     )(scalars, *far_images, near_images, texts, near_grads, near_sums)
 
 
-def text_part(near_grads, far_grads, near_images, far_images, own_p, top_p, bot_p, sums, copies):
+def text_part(near_grads, far_grads, near_images, far_images):
     rows, width = far_images.shape
     shape = jax.ShapeDtypeStruct
     return pl.pallas_call(
         text_kernel,
-        out_shape=(
-            shape((rows, width), F32), shape((rows, width), BF16), shape((rows, width), F32),
-            shape((copies * 8, 128), F32),
-        ),
-        in_specs=[VMEM] * 8,
-        out_specs=(VMEM,) * 4,
+        out_shape=(shape((rows, width), F32), shape((rows, width), BF16)),
+        in_specs=[VMEM] * 4,
+        out_specs=(VMEM,) * 2,
         compiler_params=params(32),
         cost_estimate=pl.CostEstimate(
             flops=rows * rows * width, bytes_accessed=rows * width, transcendentals=0
         ),
         name="text",
-    )(near_grads, far_grads, near_images, far_images, own_p, top_p, bot_p, sums)
-
-
-def relay_y_kernel(own, passing, out):
+    )(near_grads, far_grads, near_images, far_images)
+
+
+def relay_y_kernel(own, passing, sums, out, sums_out):
     out[...] = (own[...] + passing[...].astype(F32)).astype(BF16)
-
-
-def relay_y(own, passing):
+    sums_out[...] = sums[...]
+
+
+def relay_y(own, passing, sums):
     return pl.pallas_call(
         relay_y_kernel,
-        out_shape=jax.ShapeDtypeStruct(passing.shape, BF16),
-        in_specs=[VMEM] * 2,
-        out_specs=VMEM,
+        out_shape=(jax.ShapeDtypeStruct(passing.shape, BF16), jax.ShapeDtypeStruct(sums.shape, F32)),
+        in_specs=[VMEM] * 3,
+        out_specs=(VMEM,) * 2,
         compiler_params=params(16),
         cost_estimate=pl.CostEstimate(flops=passing.size, bytes_accessed=passing.size, transcendentals=0),
         name="relay_y",
-    )(own, passing)
-
-
-def relay_kernel(top, top_passing, bot, bot_passing, own_p, arrived, top_out, bot_out, own_out, sums_out):
+    )(own, passing, sums)
+
+
+def relay_kernel(
+    top, top_passing, bot, bot_passing, own_p, top_p, bot_p, sums,
+    top_out, bot_out, own_out, sums_out,
+):
+    half = top.shape[0]
     top_out[...] = (top[...] + top_passing[...].astype(F32)).astype(BF16)
     bot_out[...] = (bot[...] + bot_passing[...].astype(F32)).astype(BF16)
-    own_out[...] = own_p[...]
-    sums = arrived[pl.ds(0, 8), :]
-    for i in range(1, arrived.shape[0] // 8):
-        sums += arrived[pl.ds(i * 8, 8), :]
-    write_copies(sums_out, sums)
-
-
-def relay(top, top_passing, bot, bot_passing, own_p, arrived, copies):
+    own_out[:half, :] = own_p[:half, :] + top_p[...].astype(F32)
+    own_out[half:, :] = own_p[half:, :] + bot_p[...].astype(F32)
+    sums_out[...] = sums[...]
+
+
+def relay(top, top_passing, bot, bot_passing, own_p, top_p, bot_p, sums):
     shape = jax.ShapeDtypeStruct
     return pl.pallas_call(
         relay_kernel,
         out_shape=(
             shape(top.shape, BF16), shape(bot.shape, BF16), shape(own_p.shape, F32),
-            shape((copies * 8, 128), F32),
-        ),
-        in_specs=[VMEM] * 6,
+            shape(sums.shape, F32),
+        ),
+        in_specs=[VMEM] * 8,
         out_specs=(VMEM,) * 4,
         compiler_params=params(16),
         cost_estimate=pl.CostEstimate(flops=top.size, bytes_accessed=top.size, transcendentals=0),
         name="relay",
-    )(top, top_passing, bot, bot_passing, own_p, arrived)
+    )(top, top_passing, bot, bot_passing, own_p, top_p, bot_p, sums)
 
 
 def backnorm(emb, upstream, scale):
@@ -321,16 +328,36 @@
     return (scale * inverse) * (upstream - hat * along)
 
 
-def image_end_kernel(scalars, emb, own, top, bot, out):
-    half = emb.shape[0] // 2
-    for at, part in ((0, top), (half, bot)):
-        at = pl.ds(at, half)
-        out[at, :] = backnorm(emb[at, :], own[at, :] + part[...].astype(F32), scalars[0])
-
-
-def text_end_kernel(scalars, emb, own, one, two, out):
-    upstream = own[...] + one[...].astype(F32) + two[...].astype(F32)
-    out[...] = backnorm(emb[...], upstream, scalars[0])
+def write_rows(out, values, slots, sems, i):
+    rows = values.shape[0]
+    at = pl.ds(i * rows, rows)
+    slots[at, :] = values
+    copy = pltpu.make_async_copy(slots.at[at], out.at[at], sems.at[i])
+    copy.start()
+    return copy
+
+
+def image_end_kernel(scalars, emb, own, top, bot, out, slots, sems):
+    step = emb.shape[0] // 4
+    copies = []
+    for i in range(4):
+        at = pl.ds(i * step, step)
+        part = (top, bot)[i // 2][pl.ds(i % 2 * step, step), :]
+        values = backnorm(emb[at, :], own[at, :] + part.astype(F32), scalars[0])
+        copies.append(write_rows(out, values, slots, sems, i))
+    for copy in copies:
+        copy.wait()
+
+
+def text_end_kernel(scalars, emb, own, one, two, out, slots, sems):
+    step = emb.shape[0] // 4
+    copies = []
+    for i in range(4):
+        at = pl.ds(i * step, step)
+        upstream = own[at, :] + one[at, :].astype(F32) + two[at, :].astype(F32)
+        copies.append(write_rows(out, backnorm(emb[at, :], upstream, scalars[0]), slots, sems, i))
+    for copy in copies:
+        copy.wait()
 
 
 def end_part(kernel, name, scalars, emb, *parts):
@@ -339,10 +366,11 @@
         kernel,
         out_shape=jax.ShapeDtypeStruct((rows, width), F32),
         in_specs=[SMEM] + [VMEM] * (1 + len(parts)),
-        out_specs=VMEM,
+        out_specs=HBM,
+        scratch_shapes=[pltpu.VMEM((rows, width), F32), pltpu.SemaphoreType.DMA((4,))],
         compiler_params=params(24),
         cost_estimate=pl.CostEstimate(
-            flops=10 * rows * width, bytes_accessed=16 * rows * width, transcendentals=rows
+            flops=rows * width, bytes_accessed=rows * width, transcendentals=rows
         ),
         name=name,
     )(scalars, emb, *parts)
@@ -383,19 +411,18 @@
     )
     relay_top = send(far_top, ahead)
     relay_bot = send(far_bot, back)
-    from_y = send(relay_y(y_q, send(yc_q, across_core)), across_y)
-    own_q, core_q, own_p, sums = text_part(
-        near_grads, far_grads, near_images, far_images, own_p, from_right_top, from_left_bot, sums, blocks
-    )
+    mate_y = send(yc_q, across_core)
+    own_q, core_q = text_part(near_grads, far_grads, near_images, far_images)
+    y_sum, sums = relay_y(y_q, mate_y, sums)
+    from_y = send(y_sum, across_y)
     from_core = send(core_q, across_core)
-    sums = lax.all_to_all(sums, "blk", split_axis=0, concat_axis=0, tiled=True)
+    sums = lax.psum(sums, "blk")
     top_sum, bot_sum, own_p, sums = relay(
-        right_top_p, relay_top, left_bot_p, relay_bot, own_p, sums, groups
+        right_top_p, relay_top, left_bot_p, relay_bot, own_p, from_right_top, from_left_bot, sums
     )
     from_left_top = send(top_sum, ahead)
     from_right_bot = send(bot_sum, back)
-    sums = lax.all_to_all(sums, "group", split_axis=0, concat_axis=0, tiled=True)
-    sums = jnp.sum(sums.reshape(groups, 8, 128), axis=0)
+    sums = lax.psum(sums, "group")
 
     grad_text = end_part(text_end_kernel, "text_end", scalars, text_emb, own_q, from_core, from_y)
     grad_image = end_part(

time: 106 us -> 153 us (1.44)
  the two profiles are of different devices: /device:TPU:32 before, /device:TPU:0 now
where the time goes in v2:
time: 153 us; the launch traced here: 152 us
  blocking collectives  79.3 us (52%)
  Pallas kernels  21.7 us (14%)
  local copies, waits for them, and re-layouts  18.8 us (12%)
  starting transfers between devices  17.3 us (11%)
  waiting for transfers between devices  12.9 us (8%)
  between operations  2.29 us (1%)
    psum x1, blocking collectives, shards(): sums = lax.psum(sums, 'group')  44.8 us
    psum x1, blocking collectives, shards(): sums = lax.psum(sums, 'blk')  34.5 us
    unnamed x44, local copies, waits for them, and re-layouts  18.3 us
    ppermute x16, starting transfers between devices, send(): return lax.ppermute(value, 'blk', perm)  17.3 us
    ppermute x16, waiting for transfers between devices, send(): return lax.ppermute(value, 'blk', perm)  12.9 us
    pallas_call x1, Pallas kernels, near_part(): pl.pallas_call(near_kernel, out_shape=(shape((rows, width), F32), shape((...  7.72 us
    pallas_call x2, Pallas kernels, end_part(): pl.pallas_call(kernel, out_shape=jax.ShapeDtypeStruct((rows, width), F32)...  4.6 us
    pallas_call x1, Pallas kernels, far_part(): pl.pallas_call(far_kernel, out_shape=(shape((half, width), BF16), shape((...  4.11 us
  transfers between devices with their start and end apart: 16, of which 3 were waited for; matrix products, arithmetic and copies ran while one was open for 0% of the time, Pallas kernels for 9%

profile of v2, /device:TPU:0, one launch (start us, length us, event | category | flops | bytes accessed | tf_op | source)
XLA Modules:
  0.0 152.4 jit_solution(2524209333375210375)
XLA Ops:
  0.6 0.0 copy-start
  0.6 1.3 copy-done
  1.9 1.3 copy-done.2
  3.2 1.4 normalize.1
  4.6 0.1 collective-permute-start.3
  4.7 1.3 collective-permute-start
  6.0 2.0 %collective-permute-start.1 = (bf16[256,1152]{1,0:T(8,128)(2,1)S(1)}, bf16[256,1152]{1,0:T(8,128)(2,1)S(1)}, u32[]{:S(2)}, u32[]{:S(2)}) collective-permute-start(bf16[256,1152]{1,0:T(8,128)(2,1)S(1)} %get-tuple-element.31.own_i), channel_id=1, source_target_pairs={{0,192},{16,208},{32,224},{48,240},{64,0},{80,16},{96,32},{112,48}... | collective-permute-start | bytes 1769480 | tf_op jit(solution)/shard_map/ppermute | solution.py:389
  8.0 0.0 collective-permute-start.2
  8.0 9.8 %collective-permute-done.3.y_t = bf16[256,1152]{1,0:T(8,128)(2,1)S(1)} collective-permute-done((bf16[256,1152]{1,0:T(8,128)(2,1)S(1)}, bf16[256,1152]{1,0:T(8,128)(2,1)S(1)}, u32[]{:S(2)}, u32[]{:S(2)}) %collective-permute-start.3) | collective-permute-done | bytes 589856 | tf_op jit(solution)/shard_map/ppermute | solution.py:389
  19.2 0.1 pad_maximum_fusion.scalars
  19.3 1.2 collective-permute-done.left_i.block_ref
  20.6 0.5 collective-permute-start.5
  21.1 3.1 %collective-permute-start.6 = (bf16[128,1152]{1,0:T(8,128)(2,1)S(1)}, bf16[128,1152]{1,0:T(8,128)(2,1)S(1)}, u32[]{:S(2)}, u32[]{:S(2)}) collective-permute-start(bf16[128,1152]{1,0:T(8,128)(2,1)S(1)} %cut.3), channel_id=1, source_target_pairs={{0,192},{16,208},{32,224},{48,240},{64,0},{80,16},{96,32},{112,48}... | collective-permute-start | bytes 884744 | tf_op jit(solution)/shard_map/ppermute | solution.py:389
  24.2 0.8 copy-done.20
  25.0 1.1 copy-done.19
  26.1 1.1 copy-done.21
  27.1 7.7 %near.1 = (f32[256,1152]{1,0:T(8,128)S(1)}, bf16[128,1152]{1,0:T(8,128)(2,1)}, f32[128,1152]{1,0:T(8,128)S(1)}, f32[128,1152]{1,0:T(8,128)S(1)}, bf16[128,1152]{...) custom-call(f32[2]{0:T(128)S(1)} %pad_maximum_fusion.scalars, ...), custom_call_target="tpu_custom_call" | custom-call | flops 3623878656 | bytes 7077888 | tf_op jit(solution)/shard_map/near/pallas_call | solution.py:212
  34.9 0.8 copy-done.6
  35.7 0.8 copy-done.8
  36.5 4.1 %far.1 = (bf16[128,1152]{1,0:T(8,128)(2,1)S(1)}, bf16[128,1152]{1,0:T(8,128)(2,1)}, f32[256,1152]{1,0:T(8,128)S(1)}, bf16[256,1152]{1,0:T(8,128)(2,1)S(1)}, bf16...) custom-call(f32[2]{0:T(128)S(1)} %pad_maximum_fusion.scalars, ...), custom_call_target="tpu_custom_call" | custom-call | flops 75497472 | bytes 589824 | tf_op jit(solution)/shard_map/far/pallas_call | solution.py:241
  40.6 0.1 collective-permute-start.11
  40.7 0.1 collective-permute-start.7
  40.8 3.2 %collective-permute-start.8 = (bf16[128,1152]{1,0:T(8,128)(2,1)}, bf16[128,1152]{1,0:T(8,128)(2,1)S(1)}, u32[]{:S(2)}, u32[]{:S(2)}) collective-permute-start(bf16[128,1152]{1,0:T(8,128)(2,1)} %get-tuple-element.40), channel_id=1, source_target_pairs={{0,192},{16,208},{32,224},{48,240},{64,0},{80,16},{96,32},{112,48}... | collective-permute-start | bytes 884744 | tf_op jit(solution)/shard_map/ppermute | solution.py:389
  44.0 3.2 %collective-permute-start.9 = (bf16[128,1152]{1,0:T(8,128)(2,1)}, bf16[128,1152]{1,0:T(8,128)(2,1)S(1)}, u32[]{:S(2)}, u32[]{:S(2)}) collective-permute-start(bf16[128,1152]{1,0:T(8,128)(2,1)} %get-tuple-element.42), channel_id=1, source_target_pairs={{0,192},{16,208},{32,224},{48,240},{64,0},{80,16},{96,32},{112,48}... | collective-permute-start | bytes 884744 | tf_op jit(solution)/shard_map/ppermute | solution.py:389
  47.3 1.8 %text.1 = (f32[256,1152]{1,0:T(8,128)S(1)}, bf16[256,1152]{1,0:T(8,128)(2,1)}) custom-call(bf16[768,1024]{1,0:T(8,128)(2,1)S(1)} %get-tuple-element.36.near_grads, bf16[256,1024]{1,0:T(8,128)(2,1)S(1)} %get-tuple-element.52.far_grads, bf16[768,1152]{1,0:T(8,128)(2,1)S(1)} %get-tuple-element.34.near_images, bf16[256,1152]{1,0:T(8,128)(2,1)S(1)} %get-tuple-element.53.far_images), custom_call_target="tpu_custom_call" | custom-call | flops 75497472 | bytes 294912 | tf_op jit(solution)/shard_map/text/pallas_call | solution.py:267
  49.0 1.0 relay_y.1
  50.0 1.8 %collective-permute-done.7.top_passing = bf16[128,1152]{1,0:T(8,128)(2,1)S(1)} collective-permute-done((bf16[128,1152]{1,0:T(8,128)(2,1)S(1)}, bf16[128,1152]{1,0:T(8,128)(2,1)S(1)}, u32[]{:S(2)}, u32[]{:S(2)}) %collective-permute-start.7) | collective-permute-done | bytes 294944 | tf_op jit(solution)/shard_map/ppermute | solution.py:389
  51.8 0.7 copy-done.10
  52.5 0.5 collective-permute-start.15
  53.0 34.5 %psum.14.sums = f32[8,128]{1,0:T(8,128)S(1)} all-reduce(f32[8,128]{1,0:T(8,128)S(1)} %get-tuple-element.47), channel_id=1, replica_groups=mesh['blk'=16,'group'=16] {'blk'}, use_global_device_ids=true, to_apply=%region_0.0 | all-reduce | flops 1024 | bytes 8192 | tf_op jit(solution)/shard_map/psum | solution.py:419
  87.5 0.7 copy-done.12
  88.3 0.7 copy-done.14
  89.0 0.7 copy-done.16
  89.7 1.1 copy-done.7
  90.8 1.1 copy-done.9
  91.9 1.0 copy-done.11
  92.8 1.0 copy-done.13
  93.8 1.0 copy-done.15
  94.7 1.0 copy-done.17
  95.7 1.0 relay.1
  96.7 1.0 copy-done.4
  97.7 3.2 %collective-permute-start.13 = (bf16[128,1152]{1,0:T(8,128)(2,1)}, bf16[128,1152]{1,0:T(8,128)(2,1)S(1)}, u32[]{:S(2)}, u32[]{:S(2)}) collective-permute-start(bf16[128,1152]{1,0:T(8,128)(2,1)} %get-tuple-element.51), channel_id=1, source_target_pairs={{0,192},{16,208},{32,224},{48,240},{64,0},{80,16},{96,32},{112,48}... | collective-permute-start | bytes 884744 | tf_op jit(solution)/shard_map/ppermute | solution.py:389
  101.0 44.8 %psum.15 = f32[8,128]{1,0:T(8,128)S(1)} all-reduce(f32[8,128]{1,0:T(8,128)S(1)} %get-tuple-element.48), channel_id=1, replica_groups=mesh['blk'=16,'group'=16] {'group'}, use_global_device_ids=true, to_apply=%region_1.0 | all-reduce | flops 1024 | bytes 8192 | tf_op jit(solution)/shard_map/psum | solution.py:425
  145.8 0.5 fusion
  146.3 0.0 copy-start.5
  146.3 1.3 copy-done.5
  147.6 1.9 %image_end.1 = f32[256,1152]{1,0:T(8,128)} custom-call(f32[2]{0:T(128)S(1)} %pad_maximum_fusion.scalars, f32[256,1152]{1,0:T(8,128)S(1)} %copy-done.3, f32[256,1152]{1,0:T(8,128)S(1)} %copy-done.5, bf16[128,1152]{1,0:T(8,128)(2,1)S(1)} %collective-permute-done.12.top, bf16[128,1152]{1,0:T(8,128)(2,1)S(1)} %collective-permute-done.13.bot), custom_call_target="tpu_custom_call" | custom-call | flops 294912 | bytes 294912 | tf_op jit(solution)/shard_map/image_end/pallas_call | solution.py:365
  149.5 2.7 %text_end.1 = f32[256,1152]{1,0:T(8,128)} custom-call(f32[2]{0:T(128)S(1)} %pad_maximum_fusion.scalars, f32[256,1152]{1,0:T(8,128)S(1)} %copy-done.1, f32[256,1152]{1,0:T(8,128)S(1)} %get-tuple-element.54.own, bf16[256,1152]{1,0:T(8,128)(2,1)} %collective-permute-done.14.one, bf16[256,1152]{1,0:T(8,128)(2,1)} %collective-permute-done.15.two), custom_call_target="tpu_custom_call" | custom-call | flops 294912 | bytes 294912 | tf_op jit(solution)/shard_map/text_end/pallas_call | solution.py:365
  (43 shorter events, 0.1 us)
Async XLA Ops:
  0.6 1.3 copy-start
  1.9 1.3 copy-start.2
  4.6 13.3 %collective-permute-start.3 = (bf16[256,1152]{1,0:T(8,128)(2,1)S(1)}, bf16[256,1152]{1,0:T(8,128)(2,1)S(1)}, u32[]{:S(2)}, u32[]{:S(2)}) collective-permute-start(bf16[256,1152]{1,0:T(8,128)(2,1)S(1)} %get-tuple-element.32.own_t), channel_id=1, source_target_pairs={{0,32},{16,48},{32,0},{48,16},{64,96},{80,112},{96,64},{112,80},{1... | collective-permute-start | bytes 1769480 | tf_op jit(solution)/shard_map/ppermute | solution.py:389
  4.7 15.8 %collective-permute-start = (bf16[256,1152]{1,0:T(8,128)(2,1)S(1)}, bf16[256,1152]{1,0:T(8,128)(2,1)S(1)}, u32[]{:S(2)}, u32[]{:S(2)}) collective-permute-start(bf16[256,1152]{1,0:T(8,128)(2,1)S(1)} %get-tuple-element.31.own_i), channel_id=1, source_target_pairs={{0,64},{16,80},{32,96},{48,112},{64,128},{80,144},{96,160},{112,17... | collective-permute-start | bytes 1769480 | tf_op jit(solution)/shard_map/ppermute | solution.py:389
  6.0 15.0 %collective-permute-start.1 = (bf16[256,1152]{1,0:T(8,128)(2,1)S(1)}, bf16[256,1152]{1,0:T(8,128)(2,1)S(1)}, u32[]{:S(2)}, u32[]{:S(2)}) collective-permute-start(bf16[256,1152]{1,0:T(8,128)(2,1)S(1)} %get-tuple-element.31.own_i), channel_id=1, source_target_pairs={{0,192},{16,208},{32,224},{48,240},{64,0},{80,16},{96,32},{112,48}... | collective-permute-start | bytes 1769480 | tf_op jit(solution)/shard_map/ppermute | solution.py:389
  8.0 16.1 %collective-permute-start.2 = (bf16[256,1152]{1,0:T(8,128)(2,1)S(1)}, bf16[256,1152]{1,0:T(8,128)(2,1)S(1)}, u32[]{:S(2)}, u32[]{:S(2)}) collective-permute-start(bf16[256,1152]{1,0:T(8,128)(2,1)S(1)} %get-tuple-element.32.own_t), channel_id=1, source_target_pairs={{0,16},{16,0},{32,48},{48,32},{64,80},{80,64},{96,112},{112,96},{1... | collective-permute-start | bytes 1769480 | tf_op jit(solution)/shard_map/ppermute | solution.py:389
  17.9 6.3 %copy-start.18 = (bf16[256,1152]{1,0:T(8,128)(2,1)}, bf16[256,1152]{1,0:T(8,128)(2,1)S(1)}, u32[]{:S(2)}) copy-start(bf16[256,1152]{1,0:T(8,128)(2,1)S(1)} %collective-permute-done.3.y_t) | copy-start | bytes 1769476
  17.9 7.1 %collective-permute-start.4 = (bf16[256,1152]{1,0:T(8,128)(2,1)S(1)}, bf16[256,1152]{1,0:T(8,128)(2,1)}, u32[]{:S(2)}, u32[]{:S(2)}) collective-permute-start(bf16[256,1152]{1,0:T(8,128)(2,1)S(1)} %collective-permute-done.3.y_t), channel_id=1, source_target_pairs={{0,16},{16,0},{32,48},{48,32},{64,80},{80,64},{96,112},{112,96},{1... | collective-permute-start | bytes 1769480 | tf_op jit(solution)/shard_map/ppermute | solution.py:389
  20.6 15.9 %collective-permute-start.5 = (bf16[128,1152]{1,0:T(8,128)(2,1)S(1)}, bf16[128,1152]{1,0:T(8,128)(2,1)S(1)}, u32[]{:S(2)}, u32[]{:S(2)}) collective-permute-start(bf16[128,1152]{1,0:T(8,128)(2,1)S(1)} %cut.2), channel_id=1, source_target_pairs={{0,64},{16,80},{32,96},{48,112},{64,128},{80,144},{96,160},{112,17... | collective-permute-start | bytes 884744 | tf_op jit(solution)/shard_map/ppermute | solution.py:389
  21.1 15.4 %collective-permute-start.6 = (bf16[128,1152]{1,0:T(8,128)(2,1)S(1)}, bf16[128,1152]{1,0:T(8,128)(2,1)S(1)}, u32[]{:S(2)}, u32[]{:S(2)}) collective-permute-start(bf16[128,1152]{1,0:T(8,128)(2,1)S(1)} %cut.3), channel_id=1, source_target_pairs={{0,192},{16,208},{32,224},{48,240},{64,0},{80,16},{96,32},{112,48}... | collective-permute-start | bytes 884744 | tf_op jit(solution)/shard_map/ppermute | solution.py:389
  24.2 0.8 copy-start.20
  25.0 1.1 copy-start.19
  26.1 1.1 copy-start.21
  34.9 0.8 copy-start.6
  35.7 0.8 copy-start.8
  40.6 8.4 %collective-permute-start.11 = (bf16[256,1152]{1,0:T(8,128)(2,1)S(1)}, bf16[256,1152]{1,0:T(8,128)(2,1)S(1)}, u32[]{:S(2)}, u32[]{:S(2)}) collective-permute-start(bf16[256,1152]{1,0:T(8,128)(2,1)S(1)} %get-tuple-element.45), channel_id=1, source_target_pairs={{0,16},{16,0},{32,48},{48,32},{64,80},{80,64},{96,112},{112,96},{1... | collective-permute-start | bytes 1769480 | tf_op jit(solution)/shard_map/ppermute | solution.py:389
  40.7 11.1 %collective-permute-start.7 = (bf16[128,1152]{1,0:T(8,128)(2,1)S(1)}, bf16[128,1152]{1,0:T(8,128)(2,1)S(1)}, u32[]{:S(2)}, u32[]{:S(2)}) collective-permute-start(bf16[128,1152]{1,0:T(8,128)(2,1)S(1)} %get-tuple-element.38), channel_id=1, source_target_pairs={{0,64},{16,80},{32,96},{48,112},{64,128},{80,144},{96,160},{112,17... | collective-permute-start | bytes 884744 | tf_op jit(solution)/shard_map/ppermute | solution.py:389
  40.8 46.7 %collective-permute-start.8 = (bf16[128,1152]{1,0:T(8,128)(2,1)}, bf16[128,1152]{1,0:T(8,128)(2,1)S(1)}, u32[]{:S(2)}, u32[]{:S(2)}) collective-permute-start(bf16[128,1152]{1,0:T(8,128)(2,1)} %get-tuple-element.40), channel_id=1, source_target_pairs={{0,192},{16,208},{32,224},{48,240},{64,0},{80,16},{96,32},{112,48}... | collective-permute-start | bytes 884744 | tf_op jit(solution)/shard_map/ppermute | solution.py:389
  44.0 44.2 %collective-permute-start.10 = (bf16[128,1152]{1,0:T(8,128)(2,1)}, bf16[128,1152]{1,0:T(8,128)(2,1)S(1)}, u32[]{:S(2)}, u32[]{:S(2)}) collective-permute-start(bf16[128,1152]{1,0:T(8,128)(2,1)} %get-tuple-element.43), channel_id=1, source_target_pairs={{0,64},{16,80},{32,96},{48,112},{64,128},{80,144},{96,160},{112,17... | collective-permute-start | bytes 884744 | tf_op jit(solution)/shard_map/ppermute | solution.py:389
  44.0 45.0 %collective-permute-start.9 = (bf16[128,1152]{1,0:T(8,128)(2,1)}, bf16[128,1152]{1,0:T(8,128)(2,1)S(1)}, u32[]{:S(2)}, u32[]{:S(2)}) collective-permute-start(bf16[128,1152]{1,0:T(8,128)(2,1)} %get-tuple-element.42), channel_id=1, source_target_pairs={{0,192},{16,208},{32,224},{48,240},{64,0},{80,16},{96,32},{112,48}... | collective-permute-start | bytes 884744 | tf_op jit(solution)/shard_map/ppermute | solution.py:389
  49.0 100.4 %collective-permute-start.14 = (bf16[256,1152]{1,0:T(8,128)(2,1)}, bf16[256,1152]{1,0:T(8,128)(2,1)}, u32[]{:S(2)}, u32[]{:S(2)}) collective-permute-start(bf16[256,1152]{1,0:T(8,128)(2,1)} %get-tuple-element.55), channel_id=1, source_target_pairs={{0,16},{16,0},{32,48},{48,32},{64,80},{80,64},{96,112},{112,96},{1... | collective-permute-start | bytes 1769480 | tf_op jit(solution)/shard_map/ppermute | solution.py:389
  51.8 0.7 copy-start.10
  52.5 97.0 %collective-permute-start.15 = (bf16[256,1152]{1,0:T(8,128)(2,1)}, bf16[256,1152]{1,0:T(8,128)(2,1)}, u32[]{:S(2)}, u32[]{:S(2)}) collective-permute-start(bf16[256,1152]{1,0:T(8,128)(2,1)} %get-tuple-element.56), channel_id=1, source_target_pairs={{0,32},{16,48},{32,0},{48,16},{64,96},{80,112},{96,64},{112,80},{1... | collective-permute-start | bytes 1769480 | tf_op jit(solution)/shard_map/ppermute | solution.py:389
  87.5 0.7 copy-start.12
  88.3 0.7 copy-start.14
  89.0 0.7 copy-start.16
  89.7 1.1 copy-start.7
  90.8 1.1 copy-start.9
  91.9 1.0 copy-start.11
  92.8 1.0 copy-start.13
  93.8 1.0 copy-start.15
  94.7 1.0 copy-start.17
  95.7 50.6 %copy-start.3 = (f32[256,1152]{1,0:T(8,128)S(1)}, f32[256,1152]{1,0:T(8,128)}, u32[]{:S(2)}) copy-start(f32[256,1152]{1,0:T(8,128)} %emb.2) | copy-start | bytes 3538948
  96.7 1.0 copy-start.4
  97.7 48.6 %collective-permute-start.12 = (bf16[128,1152]{1,0:T(8,128)(2,1)}, bf16[128,1152]{1,0:T(8,128)(2,1)S(1)}, u32[]{:S(2)}, u32[]{:S(2)}) collective-permute-start(bf16[128,1152]{1,0:T(8,128)(2,1)} %get-tuple-element.50), channel_id=1, source_target_pairs={{0,64},{16,80},{32,96},{48,112},{64,128},{80,144},{96,160},{112,17... | collective-permute-start | bytes 884744 | tf_op jit(solution)/shard_map/ppermute | solution.py:389
  97.7 48.6 %collective-permute-start.13 = (bf16[128,1152]{1,0:T(8,128)(2,1)}, bf16[128,1152]{1,0:T(8,128)(2,1)S(1)}, u32[]{:S(2)}, u32[]{:S(2)}) collective-permute-start(bf16[128,1152]{1,0:T(8,128)(2,1)} %get-tuple-element.51), channel_id=1, source_target_pairs={{0,192},{16,208},{32,224},{48,240},{64,0},{80,16},{96,32},{112,48}... | collective-permute-start | bytes 884744 | tf_op jit(solution)/shard_map/ppermute | solution.py:389
  146.3 1.3 copy-start.5
  147.6 1.9 %copy-start.1 = (f32[256,1152]{1,0:T(8,128)S(1)}, f32[256,1152]{1,0:T(8,128)}, u32[]{:S(2)}) copy-start(f32[256,1152]{1,0:T(8,128)} %emb.3) | copy-start | bytes 3538948

commit v3 on v1

--- a/solution.py
+++ b/solution.py
@@ -7,6 +7,7 @@
 
 F32 = jnp.float32
 BF16 = jnp.bfloat16
+HBM = pl.BlockSpec(memory_space=pltpu.HBM)
 VMEM = pl.BlockSpec(memory_space=pltpu.VMEM)
 SMEM = pl.BlockSpec(memory_space=pltpu.SMEM)
 
@@ -20,24 +21,27 @@
     return emb * inverse, inverse
 
 
-def normalize_kernel(image_ref, text_ref, image_out, text_out):
-    image_out[...] = unit_rows(image_ref[...])[0].astype(BF16)
-    text_out[...] = unit_rows(text_ref[...])[0].astype(BF16)
-
-
-def normalize(image_emb, text_emb):
-    rows, width = image_emb.shape
+def normalize_kernel(emb_ref, *refs):
+    norm_ref, token = refs[-2:]
+    norm_ref[...] = unit_rows(emb_ref[...])[0].astype(BF16)
+    token[...] = jnp.zeros(token.shape, F32)
+
+
+def normalize(emb, *after):
+    rows, width = emb.shape
     return pl.pallas_call(
         normalize_kernel,
-        out_shape=(jax.ShapeDtypeStruct((rows, width), BF16),) * 2,
-        in_specs=[VMEM] * 2,
+        out_shape=(
+            jax.ShapeDtypeStruct((rows, width), BF16), jax.ShapeDtypeStruct((8, 128), F32)
+        ),
+        in_specs=[VMEM] * (1 + len(after)),
         out_specs=(VMEM,) * 2,
         compiler_params=params(16),
         cost_estimate=pl.CostEstimate(
-            flops=8 * rows * width, bytes_accessed=12 * rows * width, transcendentals=rows
+            flops=4 * rows * width, bytes_accessed=6 * rows * width, transcendentals=rows
         ),
         name="normalize",
-    )(image_emb, text_emb)
+    )(emb, *after)
 
 
 def cut(block, at):
@@ -93,15 +97,10 @@
 
 
 def write_sums(sums_ref, loss, scaled, grad):
-    row = lax.broadcasted_iota(jnp.int32, sums_ref.shape, 0)
+    column = lax.broadcasted_iota(jnp.int32, sums_ref.shape, 1)
     sums_ref[...] = jnp.where(
-        row == 0, jnp.sum(loss), jnp.where(row == 1, jnp.sum(scaled), jnp.sum(grad))
-    )
-
-
-def write_copies(out, sums):
-    for i in range(out.shape[0] // 8):
-        out[pl.ds(i * 8, 8), :] = sums
+        column == 0, jnp.sum(loss), jnp.where(column == 1, jnp.sum(scaled), jnp.sum(grad))
+    )
 
 
 def near_kernel(
@@ -153,10 +152,7 @@
     )
 
 
-def far_kernel(
-    scalars, top_i, bot_i, near_images, texts, near_grads, near_sums,
-    far_top, far_bot, y_out, yc_out, images, grads, sums_ref,
-):
+def far_kernel(scalars, top_i, bot_i, texts, near_sums, images, grads, sums_ref):
     half = top_i.shape[0]
     rows = 2 * half
     scale, bias = scalars[0], scalars[1]
@@ -174,28 +170,35 @@
         grads[:, pl.ds(t * rows, rows)] = grad_q
         loss, scaled, grad = loss + loss_now, scaled + scaled_now, grad + grad_now
         sim = sim_next
-    partial = jnp.dot(grads[...], texts[...], preferred_element_type=F32)
+    write_sums(sums_ref, loss, scaled, grad)
+    sums_ref[...] += near_sums[...]
+
+
+def far_grad_kernel(far_images, far_grads, near_images, texts, near_grads, far_top, far_bot, y_out, yc_out):
+    rows = far_images.shape[0]
+    half = rows // 2
+    partial = jnp.dot(far_grads[...], texts[...], preferred_element_type=F32)
     far_top[...] = partial[:half].astype(BF16)
     far_bot[...] = partial[half:].astype(BF16)
-    yc_out[...] = text_grad(near_grads, near_images, grads, images, pl.ds(3 * rows, rows)).astype(BF16)
-    y_out[...] = text_grad(near_grads, near_images, grads, images, pl.ds(2 * rows, rows))
-    write_sums(sums_ref, loss, scaled, grad)
-    sums_ref[...] += near_sums[...]
+    for t, out in ((3, yc_out), (2, y_out)):
+        out[...] = text_grad(
+            near_grads, near_images, far_grads, far_images, pl.ds(t * rows, rows)
+        ).astype(out.dtype)
 
 
 def text_kernel(
-    near_grads, far_grads, near_images, far_images, own_p, top_p, bot_p, sums,
-    own_out, core_out, own_sum, sums_out,
+    near_grads, far_grads, near_images, far_images, own_p, top_p, bot_p,
+    own_out, core_out, own_sum, token,
 ):
     rows = far_images.shape[0]
-    half = rows // 2
     for t, out in ((1, core_out), (0, own_out)):
         out[...] = text_grad(
             near_grads, near_images, far_grads, far_images, pl.ds(t * rows, rows)
         ).astype(out.dtype)
+    half = rows // 2
     own_sum[:half, :] = own_p[:half, :] + top_p[...].astype(F32)
     own_sum[half:, :] = own_p[half:, :] + bot_p[...].astype(F32)
-    write_copies(sums_out, sums[...])
+    token[...] = jnp.zeros(token.shape, F32)
 
 
 def near_part(scalars, images, texts):
@@ -217,9 +220,9 @@
         ),
         in_specs=[SMEM] + [VMEM] * 7,
         out_specs=(VMEM,) * 9,
-        compiler_params=params(32),
-        cost_estimate=pl.CostEstimate(
-            flops=2 * 2 * 12 * rows * rows * width,
+        compiler_params=params(16),
+        cost_estimate=pl.CostEstimate(
+            flops=8 * 2 * 2 * 12 * rows * rows * width,
             bytes_accessed=24 * rows * width,
             transcendentals=3 * 12 * rows * rows,
         ),
@@ -227,92 +230,99 @@
     )(scalars, *images, *texts)
 
 
-def far_part(scalars, far_images, near_images, texts, near_grads, near_sums):
+def far_part(scalars, far_images, texts, near_sums):
     half, width = far_images[0].shape
     rows = 2 * half
     shape = jax.ShapeDtypeStruct
     return pl.pallas_call(
         far_kernel,
         out_shape=(
-            shape((half, width), BF16),
-            shape((half, width), BF16),
-            shape((rows, width), F32),
-            shape((rows, width), BF16),
-            shape((rows, width), BF16),
-            shape((rows, 4 * rows), BF16),
-            shape((8, 128), F32),
-        ),
-        in_specs=[SMEM] + [VMEM] * 6,
-        out_specs=(VMEM,) * 7,
-        compiler_params=params(32),
-        cost_estimate=pl.CostEstimate(
-            flops=rows * rows * width,
-            bytes_accessed=2 * rows * width,
-            transcendentals=rows * rows,
+            shape((rows, width), BF16), shape((rows, 4 * rows), BF16), shape((8, 128), F32)
+        ),
+        in_specs=[SMEM] + [VMEM] * 4,
+        out_specs=(VMEM,) * 3,
+        compiler_params=params(16),
+        cost_estimate=pl.CostEstimate(
+            flops=rows * rows * width, bytes_accessed=2 * rows * width, transcendentals=rows * rows
         ),
         name="far",
-    )(scalars, *far_images, near_images, texts, near_grads, near_sums)
-
-
-def text_part(near_grads, far_grads, near_images, far_images, own_p, top_p, bot_p, sums, copies):
+    )(scalars, *far_images, texts, near_sums)
+
+
+def far_grad_part(far_images, far_grads, near_images, texts, near_grads):
     rows, width = far_images.shape
     shape = jax.ShapeDtypeStruct
     return pl.pallas_call(
+        far_grad_kernel,
+        out_shape=(shape((rows // 2, width), BF16),) * 2
+        + (shape((rows, width), F32), shape((rows, width), BF16)),
+        in_specs=[VMEM] * 5,
+        out_specs=(VMEM,) * 4,
+        compiler_params=params(16),
+        cost_estimate=pl.CostEstimate(
+            flops=rows * rows * width, bytes_accessed=2 * rows * width, transcendentals=0
+        ),
+        name="far_grad",
+    )(far_images, far_grads, near_images, texts, near_grads)
+
+
+def text_part(near_grads, far_grads, near_images, far_images, own_p, top_p, bot_p):
+    rows, width = far_images.shape
+    shape = jax.ShapeDtypeStruct
+    return pl.pallas_call(
         text_kernel,
         out_shape=(
             shape((rows, width), F32), shape((rows, width), BF16), shape((rows, width), F32),
-            shape((copies * 8, 128), F32),
-        ),
-        in_specs=[VMEM] * 8,
+            shape((8, 128), F32),
+        ),
+        in_specs=[VMEM] * 7,
         out_specs=(VMEM,) * 4,
-        compiler_params=params(32),
-        cost_estimate=pl.CostEstimate(
-            flops=rows * rows * width, bytes_accessed=rows * width, transcendentals=0
+        compiler_params=params(16),
+        cost_estimate=pl.CostEstimate(
+            flops=64 * rows * rows * width, bytes_accessed=rows * width, transcendentals=0
         ),
         name="text",
-    )(near_grads, far_grads, near_images, far_images, own_p, top_p, bot_p, sums)
-
-
-def relay_y_kernel(own, passing, out):
+    )(near_grads, far_grads, near_images, far_images, own_p, top_p, bot_p)
+
+
+def relay_y_kernel(own, passing, after, sums, arrived, out, sums_out):
     out[...] = (own[...] + passing[...].astype(F32)).astype(BF16)
-
-
-def relay_y(own, passing):
+    sums_out[...] = sums[...] + arrived[...]
+
+
+def relay_y(own, passing, after, sums, arrived):
     return pl.pallas_call(
         relay_y_kernel,
-        out_shape=jax.ShapeDtypeStruct(passing.shape, BF16),
-        in_specs=[VMEM] * 2,
-        out_specs=VMEM,
+        out_shape=(
+            jax.ShapeDtypeStruct(passing.shape, BF16), jax.ShapeDtypeStruct(after.shape, F32)
+        ),
+        in_specs=[VMEM] * 5,
+        out_specs=(VMEM,) * 2,
         compiler_params=params(16),
         cost_estimate=pl.CostEstimate(flops=passing.size, bytes_accessed=passing.size, transcendentals=0),
         name="relay_y",
-    )(own, passing)
-
-
-def relay_kernel(top, top_passing, bot, bot_passing, own_p, arrived, top_out, bot_out, own_out, sums_out):
+    )(own, passing, after, sums, arrived)
+
+
+def relay_kernel(
+    top, top_passing, bot, bot_passing, sums, arrived, top_out, bot_out, sums_out
+):
     top_out[...] = (top[...] + top_passing[...].astype(F32)).astype(BF16)
     bot_out[...] = (bot[...] + bot_passing[...].astype(F32)).astype(BF16)
-    own_out[...] = own_p[...]
-    sums = arrived[pl.ds(0, 8), :]
-    for i in range(1, arrived.shape[0] // 8):
-        sums += arrived[pl.ds(i * 8, 8), :]
-    write_copies(sums_out, sums)
-
-
-def relay(top, top_passing, bot, bot_passing, own_p, arrived, copies):
+    sums_out[...] = sums[...] + arrived[...]
+
+
+def relay(top, top_passing, bot, bot_passing, sums, arrived):
     shape = jax.ShapeDtypeStruct
     return pl.pallas_call(
         relay_kernel,
-        out_shape=(
-            shape(top.shape, BF16), shape(bot.shape, BF16), shape(own_p.shape, F32),
-            shape((copies * 8, 128), F32),
-        ),
+        out_shape=(shape(top.shape, BF16), shape(bot.shape, BF16), shape(sums.shape, F32)),
         in_specs=[VMEM] * 6,
-        out_specs=(VMEM,) * 4,
+        out_specs=(VMEM,) * 3,
         compiler_params=params(16),
         cost_estimate=pl.CostEstimate(flops=top.size, bytes_accessed=top.size, transcendentals=0),
         name="relay",
-    )(top, top_passing, bot, bot_passing, own_p, arrived)
+    )(top, top_passing, bot, bot_passing, sums, arrived)
 
 
 def backnorm(emb, upstream, scale):
@@ -321,28 +331,53 @@
     return (scale * inverse) * (upstream - hat * along)
 
 
-def image_end_kernel(scalars, emb, own, top, bot, out):
-    half = emb.shape[0] // 2
-    for at, part in ((0, top), (half, bot)):
-        at = pl.ds(at, half)
-        out[at, :] = backnorm(emb[at, :], own[at, :] + part[...].astype(F32), scalars[0])
-
-
-def text_end_kernel(scalars, emb, own, one, two, out):
-    upstream = own[...] + one[...].astype(F32) + two[...].astype(F32)
-    out[...] = backnorm(emb[...], upstream, scalars[0])
-
-
-def end_part(kernel, name, scalars, emb, *parts):
+def write_rows(out, values, slots, sems, i):
+    rows = values.shape[0]
+    at = pl.ds(i * rows, rows)
+    slots[at, :] = values
+    copy = pltpu.make_async_copy(slots.at[at], out.at[at], sems.at[i])
+    copy.start()
+    return copy
+
+
+def text_end_kernel(scalars, emb, own, one, two, after, out, token, slots, sems):
+    step = emb.shape[0] // 4
+    copies = []
+    for i in range(4):
+        at = pl.ds(i * step, step)
+        upstream = own[at, :] + one[at, :].astype(F32) + two[at, :].astype(F32)
+        copies.append(write_rows(out, backnorm(emb[at, :], upstream, scalars[0]), slots, sems, i))
+    token[...] = after[...]
+    for copy in copies:
+        copy.wait()
+
+
+def image_end_kernel(scalars, emb, own, top, bot, after, out, token, slots, sems):
+    step = emb.shape[0] // 4
+    copies = []
+    for i in range(4):
+        at = pl.ds(i * step, step)
+        part = (top, bot)[i // 2][pl.ds(i % 2 * step, step), :]
+        values = backnorm(emb[at, :], own[at, :] + part.astype(F32), scalars[0])
+        copies.append(write_rows(out, values, slots, sems, i))
+    token[...] = after[...]
+    for copy in copies:
+        copy.wait()
+
+
+def end_part(kernel, name, cost, scalars, emb, *parts):
     rows, width = emb.shape
     return pl.pallas_call(
         kernel,
-        out_shape=jax.ShapeDtypeStruct((rows, width), F32),
+        out_shape=(
+            jax.ShapeDtypeStruct((rows, width), F32), jax.ShapeDtypeStruct((8, 128), F32)
+        ),
         in_specs=[SMEM] + [VMEM] * (1 + len(parts)),
-        out_specs=VMEM,
+        out_specs=(HBM, VMEM),
+        scratch_shapes=[pltpu.VMEM((rows, width), F32), pltpu.SemaphoreType.DMA((4,))],
         compiler_params=params(24),
         cost_estimate=pl.CostEstimate(
-            flops=10 * rows * width, bytes_accessed=16 * rows * width, transcendentals=rows
+            flops=cost * rows * width, bytes_accessed=rows * width, transcendentals=rows
         ),
         name=name,
     )(scalars, emb, *parts)
@@ -362,7 +397,8 @@
 
     scale = jnp.exp(log_scale)
     scalars = jnp.stack([scale, bias])
-    own_i, own_t = normalize(image_emb, text_emb)
+    own_i, token = normalize(image_emb)
+    own_t, _ = normalize(text_emb, token)
     left_i = send(own_i, ahead)
     right_i = send(own_i, back)
     y_t = send(own_t, across_y)
@@ -378,31 +414,49 @@
     from_left_bot = send(right_bot_p, ahead)
     from_right_top = send(left_top_p, back)
 
-    far_top, far_bot, y_q, yc_q, far_images, far_grads, sums = far_part(
-        scalars, (top_i, bot_i), near_images, texts, near_grads, near_sums
+    far_images, far_grads, sums = far_part(scalars, (top_i, bot_i), texts, near_sums)
+
+    def pair_group(value, k):
+        return lax.ppermute(value, "group", [(i, i ^ k) for i in range(groups)])
+
+    def pair_blk(value, k):
+        return send(value, [(i, i ^ k) for i in range(blocks)])
+
+    sums_1 = sums + pair_group(sums, 1)
+    far_top, far_bot, y_q, yc_q = far_grad_part(
+        far_images, far_grads, near_images, texts, near_grads
     )
     relay_top = send(far_top, ahead)
     relay_bot = send(far_bot, back)
-    from_y = send(relay_y(y_q, send(yc_q, across_core)), across_y)
-    own_q, core_q, own_p, sums = text_part(
-        near_grads, far_grads, near_images, far_images, own_p, from_right_top, from_left_bot, sums, blocks
-    )
+    mate_y = send(yc_q, across_core)
+    own_q, core_q, own_p, token = text_part(
+        near_grads, far_grads, near_images, far_images, own_p, from_right_top, from_left_bot
+    )
+    y_sum, sums_2 = relay_y(y_q, mate_y, token, sums_1, pair_group(sums_1, 2))
+    from_y = send(y_sum, across_y)
     from_core = send(core_q, across_core)
-    sums = lax.all_to_all(sums, "blk", split_axis=0, concat_axis=0, tiled=True)
-    top_sum, bot_sum, own_p, sums = relay(
-        right_top_p, relay_top, left_bot_p, relay_bot, own_p, sums, groups
+    sums_3 = sums_2 + pair_group(sums_2, 4)
+    top_sum, bot_sum, sums_4 = relay(
+        right_top_p, relay_top, left_bot_p, relay_bot, sums_3, pair_group(sums_3, 8)
     )
     from_left_top = send(top_sum, ahead)
     from_right_bot = send(bot_sum, back)
-    sums = lax.all_to_all(sums, "group", split_axis=0, concat_axis=0, tiled=True)
-    sums = jnp.sum(sums.reshape(groups, 8, 128), axis=0)
-
-    grad_text = end_part(text_end_kernel, "text_end", scalars, text_emb, own_q, from_core, from_y)
-    grad_image = end_part(
-        image_end_kernel, "image_end", scalars, image_emb,
-        own_p, from_left_top, from_right_bot,
-    )
-    totals = sums[:, 0] / (rows * blocks * groups)
+
+    def over_blk(_, value):
+        for k in (1, 2, 4, 8):
+            value = value + pair_blk(value, k)
+        return value
+
+    sums_8 = lax.fori_loop(0, (scale > 0.0).astype(jnp.int32), over_blk, sums_4)
+
+    grad_text, token = end_part(
+        text_end_kernel, "text_end", 8, scalars, text_emb, own_q, from_core, from_y, sums_8
+    )
+    grad_image, _ = end_part(
+        image_end_kernel, "image_end", 8, scalars, image_emb,
+        own_p, from_left_top, from_right_bot, token,
+    )
+    totals = sums_8[0] / (rows * blocks * groups)
     return (totals[0], grad_image, grad_text, totals[1], totals[2])
 
 

time: 106 us -> 95.6 us (0.902); the launches traced: 105 us -> 95.3 us
  local copies, waits for them, and re-layouts: 16 us -> 4.18 us
  starting transfers between devices: 35.5 us -> 29.3 us
  waiting for transfers between devices: 31.3 us -> 36.4 us
  Pallas kernels: 19.6 us -> 23 us
    all_to_all x2 -> x0, starting transfers between devices: 16.5 us -> none  [the longest x1 10.9 us: shards(): lax.all_to_all(sums, 'group', split_axis=0, concat_axis=0, tiled=True)]
    all_to_all x2 -> x0, waiting for transfers between devices: 14.8 us -> none  [the longest x1 9.08 us: shards(): sums = lax.all_to_all(sums, 'blk', split_axis=0, concat_axis=0, tiled=True)]
    ppermute x0 -> x4, starting transfers between devices: none -> 12.1 us  [pair_group(): return lax.ppermute(value, 'group', [(i, i ^ k) for i in range(groups)])]
    unnamed x38 -> x14, local copies, waits for them, and re-layouts: 15.5 us -> 3.58 us
    ppermute x0 -> x4, waiting for transfers between devices: none -> 11.7 us  [pair_group(): return lax.ppermute(value, 'group', [(i, i ^ k) for i in range(groups)])]
    ppermute x16 -> x20, waiting for transfers between devices: 16.5 us -> 24.7 us  [send(): return lax.ppermute(value, 'blk', perm)]
    ppermute x16 -> x20, starting transfers between devices: 18.9 us -> 17.2 us  [send(): return lax.ppermute(value, 'blk', perm)]
    pallas_call x1, Pallas kernels: 0.19 us -> 1.91 us  [relay(): pl.pallas_call(relay_kernel, out_shape=(shape(top.shape, BF16), shape(bot...]
  transfers between devices with their start and end apart: 18 -> 24, of which waited for: 6 -> 9; matrix products, arithmetic and copies ran while one was open for 1% -> 1% of each run, Pallas kernels for 12% -> 20%
where the time goes in v3:
time: 95.6 us; the launch traced here: 95.3 us
  waiting for transfers between devices  36.4 us (38%)
  starting transfers between devices  29.3 us (31%)
  Pallas kernels  23 us (24%)
  local copies, waits for them, and re-layouts  4.18 us (4%)
  between operations  2.33 us (2%)
    ppermute x20, waiting for transfers between devices, send(): return lax.ppermute(value, 'blk', perm)  24.7 us
    ppermute x20, starting transfers between devices, send(): return lax.ppermute(value, 'blk', perm)  17.2 us
    ppermute x4, starting transfers between devices, pair_group(): return lax.ppermute(value, 'group', [(i, i ^ k) for i in range(groups)])  12.1 us
    ppermute x4, waiting for transfers between devices, pair_group(): return lax.ppermute(value, 'group', [(i, i ^ k) for i in range(groups)])  11.7 us
    pallas_call x1, Pallas kernels, near_part(): pl.pallas_call(near_kernel, out_shape=(shape((rows, width), F32), shape((...  7.36 us
    pallas_call x2, Pallas kernels, end_part(): pl.pallas_call(kernel, out_shape=(jax.ShapeDtypeStruct((rows, width), F32...  5.79 us
    unnamed x14, local copies, waits for them, and re-layouts  3.58 us
    pallas_call x1, Pallas kernels, far_grad_part(): pl.pallas_call(far_grad_kernel, out_shape=(shape((rows // 2, width), BF16...  2.24 us
  transfers between devices with their start and end apart: 24, of which 9 were waited for; matrix products, arithmetic and copies ran while one was open for 1% of the time, Pallas kernels for 20%

profile of v3, /device:TPU:32, one launch (start us, length us, event | category | flops | bytes accessed | tf_op | source)
XLA Modules:
  0.0 95.3 jit_solution(13612040489359074891)
XLA Ops:
  0.6 0.0 copy-start.1
  0.7 1.4 %copy-done.1 = f32[256,1152]{1,0:T(8,128)S(1)} copy-done((f32[256,1152]{1,0:T(8,128)S(1)}, f32[256,1152]{1,0:T(8,128)}, u32[]{:S(2)}) %copy-start.1) | copy-done | bytes 1179672
  2.0 0.2 normalize.2
  2.2 0.1 copy-done
  2.3 0.7 normalize.3
  3.0 1.6 %collective-permute-start.7 = (bf16[256,1152]{1,0:T(8,128)(2,1)S(1)}, bf16[256,1152]{1,0:T(8,128)(2,1)}, u32[]{:S(2)}, u32[]{:S(2)}) collective-permute-start(bf16[256,1152]{1,0:T(8,128)(2,1)S(1)} %get-tuple-element.56.own_t), channel_id=1, source_target_pairs={{0,32},{16,48},{32,0},{48,16},{64,96},{80,112},{96,64},{112,80},{1... | collective-permute-start | bytes 1769480 | tf_op jit(solution)/shard_map/ppermute | solution.py:396
  4.5 1.5 %collective-permute-start.4 = (bf16[256,1152]{1,0:T(8,128)(2,1)S(1)}, bf16[256,1152]{1,0:T(8,128)(2,1)S(1)}, u32[]{:S(2)}, u32[]{:S(2)}) collective-permute-start(bf16[256,1152]{1,0:T(8,128)(2,1)S(1)} %get-tuple-element.54.own_i), channel_id=1, source_target_pairs={{0,64},{16,80},{32,96},{48,112},{64,128},{80,144},{96,160},{112,17... | collective-permute-start | bytes 1769480 | tf_op jit(solution)/shard_map/ppermute | solution.py:396
  6.0 1.7 %collective-permute-start.5 = (bf16[256,1152]{1,0:T(8,128)(2,1)S(1)}, bf16[256,1152]{1,0:T(8,128)(2,1)S(1)}, u32[]{:S(2)}, u32[]{:S(2)}) collective-permute-start(bf16[256,1152]{1,0:T(8,128)(2,1)S(1)} %get-tuple-element.54.own_i), channel_id=1, source_target_pairs={{0,192},{16,208},{32,224},{48,240},{64,0},{80,16},{96,32},{112,48}... | collective-permute-start | bytes 1769480 | tf_op jit(solution)/shard_map/ppermute | solution.py:396
  7.8 0.0 collective-permute-start.6
  7.8 10.4 %collective-permute-done.7.y_t = bf16[256,1152]{1,0:T(8,128)(2,1)} collective-permute-done((bf16[256,1152]{1,0:T(8,128)(2,1)S(1)}, bf16[256,1152]{1,0:T(8,128)(2,1)}, u32[]{:S(2)}, u32[]{:S(2)}) %collective-permute-start.7) | collective-permute-done | bytes 589856 | tf_op jit(solution)/shard_map/ppermute | solution.py:396
  19.5 0.1 pad_maximum_fusion.scalars
  19.6 1.0 %collective-permute-done.4.left_i.block_ref = bf16[256,1152]{1,0:T(8,128)(2,1)S(1)} collective-permute-done((bf16[256,1152]{1,0:T(8,128)(2,1)S(1)}, bf16[256,1152]{1,0:T(8,128)(2,1)S(1)}, u32[]{:S(2)}, u32[]{:S(2)}) %collective-permute-start.4) | collective-permute-done | bytes 589856 | tf_op jit(solution)/shard_map/ppermute | solution.py:396
  20.6 0.6 collective-permute-start.9
  21.2 2.8 %collective-permute-start.10 = (bf16[128,1152]{1,0:T(8,128)(2,1)S(1)}, bf16[128,1152]{1,0:T(8,128)(2,1)S(1)}, u32[]{:S(2)}, u32[]{:S(2)}) collective-permute-start(bf16[128,1152]{1,0:T(8,128)(2,1)S(1)} %cut.3), channel_id=1, source_target_pairs={{0,192},{16,208},{32,224},{48,240},{64,0},{80,16},{96,32},{112,48}... | collective-permute-start | bytes 884744 | tf_op jit(solution)/shard_map/ppermute | solution.py:396
  24.0 7.4 %near.1 = (f32[256,1152]{1,0:T(8,128)S(1)}, bf16[128,1152]{1,0:T(8,128)(2,1)S(1)}, f32[128,1152]{1,0:T(8,128)S(1)}, f32[128,1152]{1,0:T(8,128)S(1)}, bf16[128,11...) custom-call(f32[2]{0:T(128)S(1)} %pad_maximum_fusion.scalars, ...), custom_call_target="tpu_custom_call" | custom-call | flops 28991029248 | bytes 7077888 | tf_op jit(solution)/shard_map/near/pallas_call | solution.py:208
  31.4 0.0 copy-start.3
  31.4 0.0 copy-start.5
  31.4 0.6 collective-permute-start.14
  32.0 1.5 %collective-permute-start.15 = (bf16[128,1152]{1,0:T(8,128)(2,1)S(1)}, bf16[128,1152]{1,0:T(8,128)(2,1)S(1)}, u32[]{:S(2)}, u32[]{:S(2)}) collective-permute-start(bf16[128,1152]{1,0:T(8,128)(2,1)S(1)} %get-tuple-element.71), channel_id=1, source_target_pairs={{0,64},{16,80},{32,96},{48,112},{64,128},{80,144},{96,160},{112,17... | collective-permute-start | bytes 884744 | tf_op jit(solution)/shard_map/ppermute | solution.py:396
  33.5 2.1 %far.1 = (bf16[256,1152]{1,0:T(8,128)(2,1)S(1)}, bf16[256,1024]{1,0:T(8,128)(2,1)S(1)}, f32[8,128]{1,0:T(8,128)S(1)}) custom-call(f32[2]{0:T(128)S(1)} %pad_maximum_fusion.scalars, bf16[128,1152]{1,0:T(8,128)(2,1)S(1)} %collective-permute-done.9.top_i, bf16[128,1152]{1,0:T(8,128)(2,1)S(1)} %collective-permute-done.10.bot_i, ...), custom_call_target="tpu_custom_call" | custom-call | flops 75497472 | bytes 589824 | tf_op jit(solution)/shard_map/far/pallas_call | solution.py:237
  35.6 2.2 %far_grad.1 = (bf16[128,1152]{1,0:T(8,128)(2,1)}, bf16[128,1152]{1,0:T(8,128)(2,1)}, f32[256,1152]{1,0:T(8,128)S(1)}, bf16[256,1152]{1,0:T(8,128)(2,1)S(1)}) custom-call(bf16[256,1152]{1,0:T(8,128)(2,1)S(1)} %get-tuple-element.60.far_images, bf16[256,1024]{1,0:T(8,128)(2,1)S(1)} %get-tuple-element.61.far_grads, ...), custom_call_target="tpu_custom_call" | custom-call | flops 75497472 | bytes 589824 | tf_op jit(solution)/shard_map/far_grad/pallas_call | solution.py:255
  37.8 0.1 collective-permute-start.13
  37.9 0.2 collective-permute-start.16
  38.1 0.0 collective-permute-start.11
  38.2 3.5 %collective-permute-done.16 = f32[8,128]{1,0:T(8,128)S(1)} collective-permute-done((f32[8,128]{1,0:T(8,128)S(1)}, f32[8,128]{1,0:T(8,128)S(1)}, u32[]{:S(2)}, u32[]{:S(2)}) %collective-permute-start.16) | collective-permute-done | bytes 4128 | tf_op jit(solution)/shard_map/ppermute | solution.py:420
  41.6 1.8 %collective-permute-start.12 = (bf16[128,1152]{1,0:T(8,128)(2,1)}, bf16[128,1152]{1,0:T(8,128)(2,1)}, u32[]{:S(2)}, u32[]{:S(2)}) collective-permute-start(bf16[128,1152]{1,0:T(8,128)(2,1)} %get-tuple-element.66), channel_id=1, source_target_pairs={{0,192},{16,208},{32,224},{48,240},{64,0},{80,16},{96,32},{112,48}... | collective-permute-start | bytes 884744 | tf_op jit(solution)/shard_map/ppermute | solution.py:396
  43.4 3.3 %collective-permute-start.17 = (f32[8,128]{1,0:T(8,128)S(1)}, f32[8,128]{1,0:T(8,128)S(1)}, u32[]{:S(2)}, u32[]{:S(2)}) collective-permute-start(f32[8,128]{1,0:T(8,128)S(1)} %add.21.sums), channel_id=1, source_target_pairs={{0,2},{1,3},{2,0},{3,1},{4,6},{5,7},{6,4},{7,5},{8,10},{9,11},{10,... | collective-permute-start | bytes 12296 | tf_op jit(solution)/shard_map/ppermute | solution.py:420
  46.7 1.7 %text.1 = (f32[256,1152]{1,0:T(8,128)S(1)}, bf16[256,1152]{1,0:T(8,128)(2,1)}, f32[256,1152]{1,0:T(8,128)S(1)}, f32[8,128]{1,0:T(8,128)S(1)}) custom-call(bf16[768,1024]{1,0:T(8,128)(2,1)S(1)} %get-tuple-element.63.near_grads, bf16[256,1024]{1,0:T(8,128)(2,1)S(1)} %get-tuple-element.61.far_grads, bf16[768,1152]{1,0:T(8,128)(2,1)S(1)} %get-tuple-element.62.near_images, ...), custom_call_target="tpu_custom_call" | custom-call | flops 4831838208 | bytes 294912 | tf_op jit(solution)/shard_map/text/pallas_call | solution.py:272
  48.5 0.0 collective-permute-start.22
  48.5 0.9 relay_y.1
  49.4 1.6 %collective-permute-start.23 = (bf16[256,1152]{1,0:T(8,128)(2,1)}, bf16[256,1152]{1,0:T(8,128)(2,1)}, u32[]{:S(2)}, u32[]{:S(2)}) collective-permute-start(bf16[256,1152]{1,0:T(8,128)(2,1)} %get-tuple-element.82), channel_id=1, source_target_pairs={{0,32},{16,48},{32,0},{48,16},{64,96},{80,112},{96,64},{112,80},{1... | collective-permute-start | bytes 1769480 | tf_op jit(solution)/shard_map/ppermute | solution.py:396
  51.0 5.7 %collective-permute-start.18 = (f32[8,128]{1,0:T(8,128)S(1)}, f32[8,128]{1,0:T(8,128)S(1)}, u32[]{:S(2)}, u32[]{:S(2)}) collective-permute-start(f32[8,128]{1,0:T(8,128)S(1)} %get-tuple-element.74), channel_id=1, source_target_pairs={{0,4},{1,5},{2,6},{3,7},{4,0},{5,1},{6,2},{7,3},{8,12},{9,13},{10,... | collective-permute-start | bytes 12296 | tf_op jit(solution)/shard_map/ppermute | solution.py:420
  56.7 1.8 %collective-permute-done.18 = f32[8,128]{1,0:T(8,128)S(1)} collective-permute-done((f32[8,128]{1,0:T(8,128)S(1)}, f32[8,128]{1,0:T(8,128)S(1)}, u32[]{:S(2)}, u32[]{:S(2)}) %collective-permute-start.18) | collective-permute-done | bytes 4128 | tf_op jit(solution)/shard_map/ppermute | solution.py:420
  58.5 2.9 %collective-permute-start.19 = (f32[8,128]{1,0:T(8,128)S(1)}, f32[8,128]{1,0:T(8,128)S(1)}, u32[]{:S(2)}, u32[]{:S(2)}) collective-permute-start(f32[8,128]{1,0:T(8,128)S(1)} %add.22.sums), channel_id=1, source_target_pairs={{0,8},{1,9},{2,10},{3,11},{4,12},{5,13},{6,14},{7,15},{8,0},{9,1},... | collective-permute-start | bytes 12296 | tf_op jit(solution)/shard_map/ppermute | solution.py:420
  61.4 6.5 %collective-permute-done.19.arrived = f32[8,128]{1,0:T(8,128)S(1)} collective-permute-done((f32[8,128]{1,0:T(8,128)S(1)}, f32[8,128]{1,0:T(8,128)S(1)}, u32[]{:S(2)}, u32[]{:S(2)}) %collective-permute-start.19) | collective-permute-done | bytes 4128 | tf_op jit(solution)/shard_map/ppermute | solution.py:420
  67.9 1.1 %copy-done.4 = f32[128,1152]{1,0:T(8,128)S(1)} copy-done((f32[128,1152]{1,0:T(8,128)S(1)}, f32[128,1152]{1,0:T(8,128)}, u32[]{:S(2)}) %copy-start.4) | copy-done | bytes 589848
  69.0 1.1 %copy-done.6 = f32[128,1152]{1,0:T(8,128)S(1)} copy-done((f32[128,1152]{1,0:T(8,128)S(1)}, f32[128,1152]{1,0:T(8,128)}, u32[]{:S(2)}) %copy-start.6) | copy-done | bytes 589848
  70.0 1.9 %relay.1 = (bf16[128,1152]{1,0:T(8,128)(2,1)}, bf16[128,1152]{1,0:T(8,128)(2,1)}, f32[8,128]{1,0:T(8,128)S(1)}) custom-call(f32[128,1152]{1,0:T(8,128)S(1)} %copy-done.6, bf16[128,1152]{1,0:T(8,128)(2,1)} %collective-permute-done.11.top_passing, f32[128,1152]{1,0:T(8,128)S(1)} %copy-done.4, bf16[128,1152]{1,0:T(8,128)(2,1)} %collective-permute-done.12.bot_passing, ...), custom_call_target="tpu_custom_call" | custom-call | flops 147456 | bytes 147456 | tf_op jit(solution)/shard_map/relay/pallas_call | solution.py:317
  71.9 3.2 %collective-permute-start.21 = (bf16[128,1152]{1,0:T(8,128)(2,1)}, bf16[128,1152]{1,0:T(8,128)(2,1)}, u32[]{:S(2)}, u32[]{:S(2)}) collective-permute-start(bf16[128,1152]{1,0:T(8,128)(2,1)} %get-tuple-element.79), channel_id=1, source_target_pairs={{0,192},{16,208},{32,224},{48,240},{64,0},{80,16},{96,32},{112,48}... | collective-permute-start | bytes 884744 | tf_op jit(solution)/shard_map/ppermute | solution.py:396
  75.2 13.5 %while.10 = (s32[]{:T(128)}, f32[8,128]{1,0:T(8,128)S(1)}, s32[]{:T(128)}, s32[]{:T(128)}) while((s32[]{:T(128)}, f32[8,128]{1,0:T(8,128)S(1)}, s32[]{:T(128)}, s32[]{:T(128)}) %tuple.24), condition=%wide.region_1.0_spmd, body=%wide.region_0.0_spmd.sunk | while | flops 4098 | bytes 114901 | solution.py:450
  75.2 1.2 %collective-permute-done = f32[8,128]{1,0:T(8,128)S(1)} collective-permute-done((f32[8,128]{1,0:T(8,128)S(1)}, f32[8,128]{1,0:T(8,128)S(1)}, u32[]{:S(2)}, u32[]{:S(2)}) %collective-permute-start) | collective-permute-done | bytes 4128 | tf_op jit(solution)/shard_map/while/body/ppermute | solution.py:396
  76.3 0.1 collective-permute-start.1
  76.5 3.5 %collective-permute-done.1 = f32[8,128]{1,0:T(8,128)S(1)} collective-permute-done((f32[8,128]{1,0:T(8,128)S(1)}, f32[8,128]{1,0:T(8,128)S(1)}, u32[]{:S(2)}, u32[]{:S(2)}) %collective-permute-start.1) | collective-permute-done | bytes 4128 | tf_op jit(solution)/shard_map/while/body/ppermute | solution.py:396
  80.0 3.6 %collective-permute-done.2 = f32[8,128]{1,0:T(8,128)S(1)} collective-permute-done((f32[8,128]{1,0:T(8,128)S(1)}, f32[8,128]{1,0:T(8,128)S(1)}, u32[]{:S(2)}, u32[]{:S(2)}) %collective-permute-start.2) | collective-permute-done | bytes 4128 | tf_op jit(solution)/shard_map/while/body/ppermute | solution.py:396
  83.6 5.1 %collective-permute-done.3 = f32[8,128]{1,0:T(8,128)S(1)} collective-permute-done((f32[8,128]{1,0:T(8,128)S(1)}, f32[8,128]{1,0:T(8,128)S(1)}, u32[]{:S(2)}, u32[]{:S(2)}) %collective-permute-start.3) | collective-permute-done | bytes 4128 | tf_op jit(solution)/shard_map/while/body/ppermute | solution.py:396
  88.7 0.6 fusion
  89.3 2.8 %text_end.1 = (f32[256,1152]{1,0:T(8,128)}, f32[8,128]{1,0:T(8,128)S(1)}) custom-call(f32[2]{0:T(128)S(1)} %pad_maximum_fusion.scalars, f32[256,1152]{1,0:T(8,128)S(1)} %copy-done, f32[256,1152]{1,0:T(8,128)S(1)} %get-tuple-element.80.own, bf16[256,1152]{1,0:T(8,128)(2,1)} %collective-permute-done.22.one, bf16[256,1152]{1,0:T(8,128)(2,1)} %collective-permute-done.23.two, ...), custom_call_target="tpu_custom_call" | custom-call | flops 2359296 | bytes 294912 | tf_op jit(solution)/shard_map/text_end/pallas_call | solution.py:370
  92.1 3.0 %image_end.1 = (f32[256,1152]{1,0:T(8,128)}, f32[8,128]{1,0:T(8,128)}) custom-call(f32[2]{0:T(128)S(1)} %pad_maximum_fusion.scalars, f32[256,1152]{1,0:T(8,128)S(1)} %copy-done.2, f32[256,1152]{1,0:T(8,128)S(1)} %get-tuple-element.77.own, bf16[128,1152]{1,0:T(8,128)(2,1)} %collective-permute-done.20.top, bf16[128,1152]{1,0:T(8,128)(2,1)} %collective-permute-done.21.bot, ...), custom_call_target="tpu_custom_call" | custom-call | flops 2359296 | bytes 294912 | tf_op jit(solution)/shard_map/image_end/pallas_call | solution.py:370
  (36 shorter events, 0.1 us)
Async XLA Ops:
  0.6 1.6 %copy-start = (f32[256,1152]{1,0:T(8,128)S(1)}, f32[256,1152]{1,0:T(8,128)}, u32[]{:S(2)}) copy-start(f32[256,1152]{1,0:T(8,128)} %emb.2) | copy-start | bytes 3538948
  0.6 1.4 %copy-start.1 = (f32[256,1152]{1,0:T(8,128)S(1)}, f32[256,1152]{1,0:T(8,128)}, u32[]{:S(2)}) copy-start(f32[256,1152]{1,0:T(8,128)} %emb.3) | copy-start | bytes 3538948
  3.0 15.2 %collective-permute-start.7 = (bf16[256,1152]{1,0:T(8,128)(2,1)S(1)}, bf16[256,1152]{1,0:T(8,128)(2,1)}, u32[]{:S(2)}, u32[]{:S(2)}) collective-permute-start(bf16[256,1152]{1,0:T(8,128)(2,1)S(1)} %get-tuple-element.56.own_t), channel_id=1, source_target_pairs={{0,32},{16,48},{32,0},{48,16},{64,96},{80,112},{96,64},{112,80},{1... | collective-permute-start | bytes 1769480 | tf_op jit(solution)/shard_map/ppermute | solution.py:396
  4.5 16.0 %collective-permute-start.4 = (bf16[256,1152]{1,0:T(8,128)(2,1)S(1)}, bf16[256,1152]{1,0:T(8,128)(2,1)S(1)}, u32[]{:S(2)}, u32[]{:S(2)}) collective-permute-start(bf16[256,1152]{1,0:T(8,128)(2,1)S(1)} %get-tuple-element.54.own_i), channel_id=1, source_target_pairs={{0,64},{16,80},{32,96},{48,112},{64,128},{80,144},{96,160},{112,17... | collective-permute-start | bytes 1769480 | tf_op jit(solution)/shard_map/ppermute | solution.py:396
  6.0 15.1 %collective-permute-start.5 = (bf16[256,1152]{1,0:T(8,128)(2,1)S(1)}, bf16[256,1152]{1,0:T(8,128)(2,1)S(1)}, u32[]{:S(2)}, u32[]{:S(2)}) collective-permute-start(bf16[256,1152]{1,0:T(8,128)(2,1)S(1)} %get-tuple-element.54.own_i), channel_id=1, source_target_pairs={{0,192},{16,208},{32,224},{48,240},{64,0},{80,16},{96,32},{112,48}... | collective-permute-start | bytes 1769480 | tf_op jit(solution)/shard_map/ppermute | solution.py:396
  7.8 16.2 %collective-permute-start.6 = (bf16[256,1152]{1,0:T(8,128)(2,1)S(1)}, bf16[256,1152]{1,0:T(8,128)(2,1)}, u32[]{:S(2)}, u32[]{:S(2)}) collective-permute-start(bf16[256,1152]{1,0:T(8,128)(2,1)S(1)} %get-tuple-element.56.own_t), channel_id=1, source_target_pairs={{0,16},{16,0},{32,48},{48,32},{64,80},{80,64},{96,112},{112,96},{1... | collective-permute-start | bytes 1769480 | tf_op jit(solution)/shard_map/ppermute | solution.py:396
  18.1 5.9 %collective-permute-start.8 = (bf16[256,1152]{1,0:T(8,128)(2,1)}, bf16[256,1152]{1,0:T(8,128)(2,1)}, u32[]{:S(2)}, u32[]{:S(2)}) collective-permute-start(bf16[256,1152]{1,0:T(8,128)(2,1)} %collective-permute-done.7.y_t), channel_id=1, source_target_pairs={{0,16},{16,0},{32,48},{48,32},{64,80},{80,64},{96,112},{112,96},{1... | collective-permute-start | bytes 1769480 | tf_op jit(solution)/shard_map/ppermute | solution.py:396
  20.6 12.9 %collective-permute-start.9 = (bf16[128,1152]{1,0:T(8,128)(2,1)S(1)}, bf16[128,1152]{1,0:T(8,128)(2,1)S(1)}, u32[]{:S(2)}, u32[]{:S(2)}) collective-permute-start(bf16[128,1152]{1,0:T(8,128)(2,1)S(1)} %cut.2), channel_id=1, source_target_pairs={{0,64},{16,80},{32,96},{48,112},{64,128},{80,144},{96,160},{112,17... | collective-permute-start | bytes 884744 | tf_op jit(solution)/shard_map/ppermute | solution.py:396
  21.2 12.3 %collective-permute-start.10 = (bf16[128,1152]{1,0:T(8,128)(2,1)S(1)}, bf16[128,1152]{1,0:T(8,128)(2,1)S(1)}, u32[]{:S(2)}, u32[]{:S(2)}) collective-permute-start(bf16[128,1152]{1,0:T(8,128)(2,1)S(1)} %cut.3), channel_id=1, source_target_pairs={{0,192},{16,208},{32,224},{48,240},{64,0},{80,16},{96,32},{112,48}... | collective-permute-start | bytes 884744 | tf_op jit(solution)/shard_map/ppermute | solution.py:396
  31.4 4.2 %copy-start.3 = (f32[128,1152]{1,0:T(8,128)}, f32[128,1152]{1,0:T(8,128)S(1)}, u32[]{:S(2)}) copy-start(f32[128,1152]{1,0:T(8,128)S(1)} %get-tuple-element.65.bot) | copy-start | bytes 1769476
  31.4 4.2 %copy-start.5 = (f32[128,1152]{1,0:T(8,128)}, f32[128,1152]{1,0:T(8,128)S(1)}, u32[]{:S(2)}) copy-start(f32[128,1152]{1,0:T(8,128)S(1)} %get-tuple-element.57.top) | copy-start | bytes 1769476
  31.4 12.0 %collective-permute-start.14 = (bf16[128,1152]{1,0:T(8,128)(2,1)S(1)}, bf16[128,1152]{1,0:T(8,128)(2,1)S(1)}, u32[]{:S(2)}, u32[]{:S(2)}) collective-permute-start(bf16[128,1152]{1,0:T(8,128)(2,1)S(1)} %get-tuple-element.70), channel_id=1, source_target_pairs={{0,192},{16,208},{32,224},{48,240},{64,0},{80,16},{96,32},{112,48}... | collective-permute-start | bytes 884744 | tf_op jit(solution)/shard_map/ppermute | solution.py:396
  32.0 14.7 %collective-permute-start.15 = (bf16[128,1152]{1,0:T(8,128)(2,1)S(1)}, bf16[128,1152]{1,0:T(8,128)(2,1)S(1)}, u32[]{:S(2)}, u32[]{:S(2)}) collective-permute-start(bf16[128,1152]{1,0:T(8,128)(2,1)S(1)} %get-tuple-element.71), channel_id=1, source_target_pairs={{0,64},{16,80},{32,96},{48,112},{64,128},{80,144},{96,160},{112,17... | collective-permute-start | bytes 884744 | tf_op jit(solution)/shard_map/ppermute | solution.py:396
  37.8 10.6 %collective-permute-start.13 = (bf16[256,1152]{1,0:T(8,128)(2,1)S(1)}, bf16[256,1152]{1,0:T(8,128)(2,1)S(1)}, u32[]{:S(2)}, u32[]{:S(2)}) collective-permute-start(bf16[256,1152]{1,0:T(8,128)(2,1)S(1)} %get-tuple-element.68), channel_id=1, source_target_pairs={{0,16},{16,0},{32,48},{48,32},{64,80},{80,64},{96,112},{112,96},{1... | collective-permute-start | bytes 1769480 | tf_op jit(solution)/shard_map/ppermute | solution.py:396
  37.9 3.7 %collective-permute-start.16 = (f32[8,128]{1,0:T(8,128)S(1)}, f32[8,128]{1,0:T(8,128)S(1)}, u32[]{:S(2)}, u32[]{:S(2)}) collective-permute-start(f32[8,128]{1,0:T(8,128)S(1)} %get-tuple-element.73), channel_id=1, source_target_pairs={{0,1},{1,0},{2,3},{3,2},{4,5},{5,4},{6,7},{7,6},{8,9},{9,8},{10,11... | collective-permute-start | bytes 12296 | tf_op jit(solution)/shard_map/ppermute | solution.py:420
  38.1 23.3 %collective-permute-start.11 = (bf16[128,1152]{1,0:T(8,128)(2,1)}, bf16[128,1152]{1,0:T(8,128)(2,1)}, u32[]{:S(2)}, u32[]{:S(2)}) collective-permute-start(bf16[128,1152]{1,0:T(8,128)(2,1)} %get-tuple-element.64), channel_id=1, source_target_pairs={{0,64},{16,80},{32,96},{48,112},{64,128},{80,144},{96,160},{112,17... | collective-permute-start | bytes 884744 | tf_op jit(solution)/shard_map/ppermute | solution.py:396
  41.6 19.8 %collective-permute-start.12 = (bf16[128,1152]{1,0:T(8,128)(2,1)}, bf16[128,1152]{1,0:T(8,128)(2,1)}, u32[]{:S(2)}, u32[]{:S(2)}) collective-permute-start(bf16[128,1152]{1,0:T(8,128)(2,1)} %get-tuple-element.66), channel_id=1, source_target_pairs={{0,192},{16,208},{32,224},{48,240},{64,0},{80,16},{96,32},{112,48}... | collective-permute-start | bytes 884744 | tf_op jit(solution)/shard_map/ppermute | solution.py:396
  43.4 5.1 %collective-permute-start.17 = (f32[8,128]{1,0:T(8,128)S(1)}, f32[8,128]{1,0:T(8,128)S(1)}, u32[]{:S(2)}, u32[]{:S(2)}) collective-permute-start(f32[8,128]{1,0:T(8,128)S(1)} %add.21.sums), channel_id=1, source_target_pairs={{0,2},{1,3},{2,0},{3,1},{4,6},{5,7},{6,4},{7,5},{8,10},{9,11},{10,... | collective-permute-start | bytes 12296 | tf_op jit(solution)/shard_map/ppermute | solution.py:420
  48.5 40.8 %collective-permute-start.22 = (bf16[256,1152]{1,0:T(8,128)(2,1)}, bf16[256,1152]{1,0:T(8,128)(2,1)}, u32[]{:S(2)}, u32[]{:S(2)}) collective-permute-start(bf16[256,1152]{1,0:T(8,128)(2,1)} %get-tuple-element.81), channel_id=1, source_target_pairs={{0,16},{16,0},{32,48},{48,32},{64,80},{80,64},{96,112},{112,96},{1... | collective-permute-start | bytes 1769480 | tf_op jit(solution)/shard_map/ppermute | solution.py:396
  49.4 39.9 %collective-permute-start.23 = (bf16[256,1152]{1,0:T(8,128)(2,1)}, bf16[256,1152]{1,0:T(8,128)(2,1)}, u32[]{:S(2)}, u32[]{:S(2)}) collective-permute-start(bf16[256,1152]{1,0:T(8,128)(2,1)} %get-tuple-element.82), channel_id=1, source_target_pairs={{0,32},{16,48},{32,0},{48,16},{64,96},{80,112},{96,64},{112,80},{1... | collective-permute-start | bytes 1769480 | tf_op jit(solution)/shard_map/ppermute | solution.py:396
  51.0 7.5 %collective-permute-start.18 = (f32[8,128]{1,0:T(8,128)S(1)}, f32[8,128]{1,0:T(8,128)S(1)}, u32[]{:S(2)}, u32[]{:S(2)}) collective-permute-start(f32[8,128]{1,0:T(8,128)S(1)} %get-tuple-element.74), channel_id=1, source_target_pairs={{0,4},{1,5},{2,6},{3,7},{4,0},{5,1},{6,2},{7,3},{8,12},{9,13},{10,... | collective-permute-start | bytes 12296 | tf_op jit(solution)/shard_map/ppermute | solution.py:420
  58.5 9.4 %collective-permute-start.19 = (f32[8,128]{1,0:T(8,128)S(1)}, f32[8,128]{1,0:T(8,128)S(1)}, u32[]{:S(2)}, u32[]{:S(2)}) collective-permute-start(f32[8,128]{1,0:T(8,128)S(1)} %add.22.sums), channel_id=1, source_target_pairs={{0,8},{1,9},{2,10},{3,11},{4,12},{5,13},{6,14},{7,15},{8,0},{9,1},... | collective-permute-start | bytes 12296 | tf_op jit(solution)/shard_map/ppermute | solution.py:420
  67.9 1.1 %copy-start.4 = (f32[128,1152]{1,0:T(8,128)S(1)}, f32[128,1152]{1,0:T(8,128)}, u32[]{:S(2)}) copy-start(f32[128,1152]{1,0:T(8,128)} %copy-done.3) | copy-start | bytes 1769476
  69.0 1.1 %copy-start.6 = (f32[128,1152]{1,0:T(8,128)S(1)}, f32[128,1152]{1,0:T(8,128)}, u32[]{:S(2)}) copy-start(f32[128,1152]{1,0:T(8,128)} %copy-done.5) | copy-start | bytes 1769476
  71.9 20.1 %collective-permute-start.20 = (bf16[128,1152]{1,0:T(8,128)(2,1)}, bf16[128,1152]{1,0:T(8,128)(2,1)}, u32[]{:S(2)}, u32[]{:S(2)}) collective-permute-start(bf16[128,1152]{1,0:T(8,128)(2,1)} %get-tuple-element.78), channel_id=1, source_target_pairs={{0,64},{16,80},{32,96},{48,112},{64,128},{80,144},{96,160},{112,17... | collective-permute-start | bytes 884744 | tf_op jit(solution)/shard_map/ppermute | solution.py:396
  71.9 20.2 %collective-permute-start.21 = (bf16[128,1152]{1,0:T(8,128)(2,1)}, bf16[128,1152]{1,0:T(8,128)(2,1)}, u32[]{:S(2)}, u32[]{:S(2)}) collective-permute-start(bf16[128,1152]{1,0:T(8,128)(2,1)} %get-tuple-element.79), channel_id=1, source_target_pairs={{0,192},{16,208},{32,224},{48,240},{64,0},{80,16},{96,32},{112,48}... | collective-permute-start | bytes 884744 | tf_op jit(solution)/shard_map/ppermute | solution.py:396
  75.2 1.2 %collective-permute-start = (f32[8,128]{1,0:T(8,128)S(1)}, f32[8,128]{1,0:T(8,128)S(1)}, u32[]{:S(2)}, u32[]{:S(2)}) collective-permute-start(f32[8,128]{1,0:T(8,128)S(1)} %get-tuple-element.120), channel_id=1, source_target_pairs={{0,16},{16,0},{32,48},{48,32},{64,80},{80,64},{96,112},{112,96},{1... | collective-permute-start | bytes 12296 | tf_op jit(solution)/shard_map/while/body/ppermute | solution.py:396
  76.3 3.6 %collective-permute-start.1 = (f32[8,128]{1,0:T(8,128)S(1)}, f32[8,128]{1,0:T(8,128)S(1)}, u32[]{:S(2)}, u32[]{:S(2)}) collective-permute-start(f32[8,128]{1,0:T(8,128)S(1)} %add.29), channel_id=1, source_target_pairs={{0,32},{16,48},{32,0},{48,16},{64,96},{80,112},{96,64},{112,80},{1... | collective-permute-start | bytes 12296 | tf_op jit(solution)/shard_map/while/body/ppermute | solution.py:396
  80.0 3.6 %collective-permute-start.2 = (f32[8,128]{1,0:T(8,128)S(1)}, f32[8,128]{1,0:T(8,128)S(1)}, u32[]{:S(2)}, u32[]{:S(2)}) collective-permute-start(f32[8,128]{1,0:T(8,128)S(1)} %add.30), channel_id=1, source_target_pairs={{0,64},{16,80},{32,96},{48,112},{64,0},{80,16},{96,32},{112,48},{1... | collective-permute-start | bytes 12296 | tf_op jit(solution)/shard_map/while/body/ppermute | solution.py:396
  83.6 5.1 %collective-permute-start.3 = (f32[8,128]{1,0:T(8,128)S(1)}, f32[8,128]{1,0:T(8,128)S(1)}, u32[]{:S(2)}, u32[]{:S(2)}) collective-permute-start(f32[8,128]{1,0:T(8,128)S(1)} %add.31), channel_id=1, source_target_pairs={{0,128},{16,144},{32,160},{48,176},{64,192},{80,208},{96,224},{112... | collective-permute-start | bytes 12296 | tf_op jit(solution)/shard_map/while/body/ppermute | solution.py:396
  89.3 2.8 %copy-start.2 = (f32[256,1152]{1,0:T(8,128)S(1)}, f32[256,1152]{1,0:T(8,128)}, u32[]{:S(2)}) copy-start(f32[256,1152]{1,0:T(8,128)} %emb.3) | copy-start | bytes 3538948

commit v4 on v3

--- a/solution.py
+++ b/solution.py
@@ -6,6 +6,7 @@
 from jax.sharding import PartitionSpec as P
 
 F32 = jnp.float32
+STEPS = (("blk", 4), ("blk", 8), ("group", 1), ("group", 2), ("group", 4), ("group", 8))
 BF16 = jnp.bfloat16
 HBM = pl.BlockSpec(memory_space=pltpu.HBM)
 VMEM = pl.BlockSpec(memory_space=pltpu.VMEM)
@@ -105,11 +106,9 @@
 
 def near_kernel(
     scalars, own_i, left_i, right_i, own_t, core_t, y_t, yc_t,
-    own_out, left_top_out, left_bot_out, right_top_out, right_bot_out,
-    images, texts, grads, sums_ref,
+    own_out, left_out, right_out, images, texts, grads, sums_ref,
 ):
     rows = own_i.shape[0]
-    half = rows // 2
     scale, bias = scalars[0], scalars[1]
     for i, src in enumerate((own_i, left_i, right_i)):
         images[pl.ds(i * rows, rows), :] = src[...]
@@ -133,14 +132,8 @@
             partial = jnp.dot(
                 grads[pl.ds(b * rows, rows), :], texts[...], preferred_element_type=F32
             )
-            if b == 0:
-                own_out[...] = partial
-            elif b == 1:
-                left_top_out[...] = partial[:half].astype(BF16)
-                left_bot_out[...] = partial[half:]
-            else:
-                right_top_out[...] = partial[:half]
-                right_bot_out[...] = partial[half:].astype(BF16)
+            out = (own_out, left_out, right_out)[b]
+            out[...] = partial.astype(out.dtype)
     write_sums(sums_ref, loss, scaled, grad)
 
 
@@ -174,52 +167,41 @@
     sums_ref[...] += near_sums[...]
 
 
-def far_grad_kernel(far_images, far_grads, near_images, texts, near_grads, far_top, far_bot, y_out, yc_out):
+def far_grad_kernel(
+    far_images, far_grads, near_images, texts, near_grads, far_out, y_out, mate_out
+):
     rows = far_images.shape[0]
-    half = rows // 2
-    partial = jnp.dot(far_grads[...], texts[...], preferred_element_type=F32)
-    far_top[...] = partial[:half].astype(BF16)
-    far_bot[...] = partial[half:].astype(BF16)
-    for t, out in ((3, yc_out), (2, y_out)):
+    far_out[...] = jnp.dot(
+        far_grads[...], texts[...], preferred_element_type=F32
+    ).astype(BF16)
+    for t, out in ((3, mate_out.at[pl.ds(0, rows)]), (1, mate_out.at[pl.ds(rows, rows)]), (2, y_out)):
         out[...] = text_grad(
             near_grads, near_images, far_grads, far_images, pl.ds(t * rows, rows)
         ).astype(out.dtype)
 
 
-def text_kernel(
-    near_grads, far_grads, near_images, far_images, own_p, top_p, bot_p,
-    own_out, core_out, own_sum, token,
-):
+def text_kernel(near_grads, far_grads, near_images, far_images, sums, own_out, sums_out):
     rows = far_images.shape[0]
-    for t, out in ((1, core_out), (0, own_out)):
-        out[...] = text_grad(
-            near_grads, near_images, far_grads, far_images, pl.ds(t * rows, rows)
-        ).astype(out.dtype)
-    half = rows // 2
-    own_sum[:half, :] = own_p[:half, :] + top_p[...].astype(F32)
-    own_sum[half:, :] = own_p[half:, :] + bot_p[...].astype(F32)
-    token[...] = jnp.zeros(token.shape, F32)
+    own_out[...] = text_grad(near_grads, near_images, far_grads, far_images, pl.ds(0, rows))
+    sums_out[...] = sums[...]
 
 
 def near_part(scalars, images, texts):
     rows, width = texts[0].shape
-    half = rows // 2
     shape = jax.ShapeDtypeStruct
     return pl.pallas_call(
         near_kernel,
         out_shape=(
             shape((rows, width), F32),
-            shape((half, width), BF16),
-            shape((half, width), F32),
-            shape((half, width), F32),
-            shape((half, width), BF16),
+            shape((rows, width), BF16),
+            shape((rows, width), BF16),
             shape((3 * rows, width), BF16),
             shape((4 * rows, width), BF16),
             shape((3 * rows, 4 * rows), BF16),
             shape((8, 128), F32),
         ),
         in_specs=[SMEM] + [VMEM] * 7,
-        out_specs=(VMEM,) * 9,
+        out_specs=(VMEM,) * 7,
         compiler_params=params(16),
         cost_estimate=pl.CostEstimate(
             flops=8 * 2 * 2 * 12 * rows * rows * width,
@@ -254,10 +236,11 @@
     shape = jax.ShapeDtypeStruct
     return pl.pallas_call(
         far_grad_kernel,
-        out_shape=(shape((rows // 2, width), BF16),) * 2
-        + (shape((rows, width), F32), shape((rows, width), BF16)),
+        out_shape=(
+            shape((rows, width), BF16), shape((rows, width), F32), shape((2 * rows, width), BF16)
+        ),
         in_specs=[VMEM] * 5,
-        out_specs=(VMEM,) * 4,
+        out_specs=(VMEM,) * 3,
         compiler_params=params(16),
         cost_estimate=pl.CostEstimate(
             flops=rows * rows * width, bytes_accessed=2 * rows * width, transcendentals=0
@@ -266,63 +249,40 @@
     )(far_images, far_grads, near_images, texts, near_grads)
 
 
-def text_part(near_grads, far_grads, near_images, far_images, own_p, top_p, bot_p):
+def text_part(near_grads, far_grads, near_images, far_images, sums):
     rows, width = far_images.shape
     shape = jax.ShapeDtypeStruct
     return pl.pallas_call(
         text_kernel,
-        out_shape=(
-            shape((rows, width), F32), shape((rows, width), BF16), shape((rows, width), F32),
-            shape((8, 128), F32),
-        ),
-        in_specs=[VMEM] * 7,
-        out_specs=(VMEM,) * 4,
-        compiler_params=params(16),
-        cost_estimate=pl.CostEstimate(
-            flops=64 * rows * rows * width, bytes_accessed=rows * width, transcendentals=0
-        ),
-        name="text",
-    )(near_grads, far_grads, near_images, far_images, own_p, top_p, bot_p)
-
-
-def relay_y_kernel(own, passing, after, sums, arrived, out, sums_out):
-    out[...] = (own[...] + passing[...].astype(F32)).astype(BF16)
-    sums_out[...] = sums[...] + arrived[...]
-
-
-def relay_y(own, passing, after, sums, arrived):
-    return pl.pallas_call(
-        relay_y_kernel,
-        out_shape=(
-            jax.ShapeDtypeStruct(passing.shape, BF16), jax.ShapeDtypeStruct(after.shape, F32)
-        ),
+        out_shape=(shape((rows, width), F32), shape(sums.shape, F32)),
         in_specs=[VMEM] * 5,
         out_specs=(VMEM,) * 2,
         compiler_params=params(16),
-        cost_estimate=pl.CostEstimate(flops=passing.size, bytes_accessed=passing.size, transcendentals=0),
+        cost_estimate=pl.CostEstimate(
+            flops=64 * rows * rows * width, bytes_accessed=rows * width, transcendentals=0
+        ),
+        name="text",
+    )(near_grads, far_grads, near_images, far_images, sums)
+
+
+def relay_y_kernel(own, passing, sums, arrived, out, sums_out):
+    rows = own.shape[0]
+    out[...] = (own[...] + passing[:rows, :].astype(F32)).astype(BF16)
+    sums_out[...] = sums[...] + arrived[...]
+
+
+def relay_y(own, passing, sums, arrived):
+    return pl.pallas_call(
+        relay_y_kernel,
+        out_shape=(
+            jax.ShapeDtypeStruct(own.shape, BF16), jax.ShapeDtypeStruct(sums.shape, F32)
+        ),
+        in_specs=[VMEM] * 4,
+        out_specs=(VMEM,) * 2,
+        compiler_params=params(16),
+        cost_estimate=pl.CostEstimate(flops=own.size, bytes_accessed=own.size, transcendentals=0),
         name="relay_y",
-    )(own, passing, after, sums, arrived)
-
-
-def relay_kernel(
-    top, top_passing, bot, bot_passing, sums, arrived, top_out, bot_out, sums_out
-):
-    top_out[...] = (top[...] + top_passing[...].astype(F32)).astype(BF16)
-    bot_out[...] = (bot[...] + bot_passing[...].astype(F32)).astype(BF16)
-    sums_out[...] = sums[...] + arrived[...]
-
-
-def relay(top, top_passing, bot, bot_passing, sums, arrived):
-    shape = jax.ShapeDtypeStruct
-    return pl.pallas_call(
-        relay_kernel,
-        out_shape=(shape(top.shape, BF16), shape(bot.shape, BF16), shape(sums.shape, F32)),
-        in_specs=[VMEM] * 6,
-        out_specs=(VMEM,) * 3,
-        compiler_params=params(16),
-        cost_estimate=pl.CostEstimate(flops=top.size, bytes_accessed=top.size, transcendentals=0),
-        name="relay",
-    )(top, top_passing, bot, bot_passing, sums, arrived)
+    )(own, passing, sums, arrived)
 
 
 def backnorm(emb, upstream, scale):
@@ -340,44 +300,36 @@
     return copy
 
 
-def text_end_kernel(scalars, emb, own, one, two, after, out, token, slots, sems):
+def end_kernel(scalars, emb, *refs):
+    *parts, sums, out, sums_out, slots, sems = refs
     step = emb.shape[0] // 4
     copies = []
     for i in range(4):
         at = pl.ds(i * step, step)
-        upstream = own[at, :] + one[at, :].astype(F32) + two[at, :].astype(F32)
+        upstream = parts[0][at, :]
+        for part in parts[1:]:
+            skip = part.shape[0] - 4 * step
+            upstream += part[pl.ds(skip + i * step, step), :].astype(F32)
         copies.append(write_rows(out, backnorm(emb[at, :], upstream, scalars[0]), slots, sems, i))
-    token[...] = after[...]
+    sums_out[...] = sums[...]
     for copy in copies:
         copy.wait()
 
 
-def image_end_kernel(scalars, emb, own, top, bot, after, out, token, slots, sems):
-    step = emb.shape[0] // 4
-    copies = []
-    for i in range(4):
-        at = pl.ds(i * step, step)
-        part = (top, bot)[i // 2][pl.ds(i % 2 * step, step), :]
-        values = backnorm(emb[at, :], own[at, :] + part.astype(F32), scalars[0])
-        copies.append(write_rows(out, values, slots, sems, i))
-    token[...] = after[...]
-    for copy in copies:
-        copy.wait()
-
-
-def end_part(kernel, name, cost, scalars, emb, *parts):
+def end_part(name, scalars, emb, *parts):
     rows, width = emb.shape
-    return pl.pallas_call(
-        kernel,
-        out_shape=(
-            jax.ShapeDtypeStruct((rows, width), F32), jax.ShapeDtypeStruct((8, 128), F32)
+    sums = parts[-1]
+    return pl.pallas_call(
+        end_kernel,
+        out_shape=(
+            jax.ShapeDtypeStruct((rows, width), F32), jax.ShapeDtypeStruct(sums.shape, F32)
         ),
         in_specs=[SMEM] + [VMEM] * (1 + len(parts)),
         out_specs=(HBM, VMEM),
         scratch_shapes=[pltpu.VMEM((rows, width), F32), pltpu.SemaphoreType.DMA((4,))],
         compiler_params=params(24),
         cost_estimate=pl.CostEstimate(
-            flops=cost * rows * width, bytes_accessed=rows * width, transcendentals=rows
+            flops=8 * rows * width, bytes_accessed=rows * width, transcendentals=rows
         ),
         name=name,
     )(scalars, emb, *parts)
@@ -407,54 +359,35 @@
     top_i = send(cut(left_i, 0), ahead)
     bot_i = send(cut(right_i, rows // 2), back)
 
-    (
-        own_p, left_top_p, left_bot_p, right_top_p, right_bot_p,
-        near_images, texts, near_grads, near_sums,
-    ) = near_part(scalars, (own_i, left_i, right_i), (own_t, core_t, y_t, yc_t))
-    from_left_bot = send(right_bot_p, ahead)
-    from_right_top = send(left_top_p, back)
-
+    own_p, left_p, right_p, near_images, texts, near_grads, near_sums = near_part(
+        scalars, (own_i, left_i, right_i), (own_t, core_t, y_t, yc_t)
+    )
+    from_left = send(right_p, ahead)
+    from_right = send(left_p, back)
     far_images, far_grads, sums = far_part(scalars, (top_i, bot_i), texts, near_sums)
 
-    def pair_group(value, k):
-        return lax.ppermute(value, "group", [(i, i ^ k) for i in range(groups)])
-
-    def pair_blk(value, k):
-        return send(value, [(i, i ^ k) for i in range(blocks)])
-
-    sums_1 = sums + pair_group(sums, 1)
-    far_top, far_bot, y_q, yc_q = far_grad_part(
-        far_images, far_grads, near_images, texts, near_grads
-    )
-    relay_top = send(far_top, ahead)
-    relay_bot = send(far_bot, back)
-    mate_y = send(yc_q, across_core)
-    own_q, core_q, own_p, token = text_part(
-        near_grads, far_grads, near_images, far_images, own_p, from_right_top, from_left_bot
-    )
-    y_sum, sums_2 = relay_y(y_q, mate_y, token, sums_1, pair_group(sums_1, 2))
+    def pair(value, axis, k):
+        return lax.ppermute(value, axis, [(i, i ^ k) for i in range(lax.axis_size(axis))])
+
+    sums_1 = sums + pair(sums, "blk", 1)
+    far_p, y_q, to_mate = far_grad_part(far_images, far_grads, near_images, texts, near_grads)
+    from_far = send(far_p, [(i, (i + 8) % blocks) for i in range(blocks)])
+    from_core = send(to_mate, across_core)
+    y_sum, sums_2 = relay_y(y_q, from_core, sums_1, pair(sums_1, "blk", 2))
     from_y = send(y_sum, across_y)
-    from_core = send(core_q, across_core)
-    sums_3 = sums_2 + pair_group(sums_2, 4)
-    top_sum, bot_sum, sums_4 = relay(
-        right_top_p, relay_top, left_bot_p, relay_bot, sums_3, pair_group(sums_3, 8)
-    )
-    from_left_top = send(top_sum, ahead)
-    from_right_bot = send(bot_sum, back)
-
-    def over_blk(_, value):
-        for k in (1, 2, 4, 8):
-            value = value + pair_blk(value, k)
+    own_q, sums_2 = text_part(near_grads, far_grads, near_images, far_images, sums_2)
+
+    def steps(_, value):
+        for axis, k in STEPS:
+            value = value + pair(value, axis, k)
         return value
 
-    sums_8 = lax.fori_loop(0, (scale > 0.0).astype(jnp.int32), over_blk, sums_4)
-
-    grad_text, token = end_part(
-        text_end_kernel, "text_end", 8, scalars, text_emb, own_q, from_core, from_y, sums_8
-    )
-    grad_image, _ = end_part(
-        image_end_kernel, "image_end", 8, scalars, image_emb,
-        own_p, from_left_top, from_right_bot, token,
+    sums_8 = lax.fori_loop(0, (scale > 0.0).astype(jnp.int32), steps, sums_2)
+    grad_text, sums_8 = end_part(
+        "text_end", scalars, text_emb, own_q, from_core, from_y, sums_8
+    )
+    grad_image, sums_8 = end_part(
+        "image_end", scalars, image_emb, own_p, from_left, from_right, from_far, sums_8
     )
     totals = sums_8[0] / (rows * blocks * groups)
     return (totals[0], grad_image, grad_text, totals[1], totals[2])

time: 95.6 us -> 111 us (1.16)
  local copies, waits for them, and re-layouts: 4.18 us -> 12.6 us
  waiting for transfers between devices: 36.4 us -> 44.2 us
  Pallas kernels: 23 us -> 21.6 us
    ppermute x4 -> x8, waiting for transfers between devices: 11.7 us -> 32.8 us  [pair(): lax.ppermute(value, axis, [(i, i ^ k) for i in range(lax.axis_size(axis))])]
    ppermute x20 -> x12, waiting for transfers between devices: 24.7 us -> 11.4 us  [send(): return lax.ppermute(value, 'blk', perm)]
    unnamed x14 -> x34, local copies, waits for them, and re-layouts: 3.58 us -> 12 us
    ppermute x4 -> x8, starting transfers between devices: 12.1 us -> 15.3 us  [pair(): lax.ppermute(value, axis, [(i, i ^ k) for i in range(lax.axis_size(axis))])]
    ppermute x20 -> x12, starting transfers between devices: 17.2 us -> 14 us  [send(): return lax.ppermute(value, 'blk', perm)]
    pallas_call x6 -> x5, Pallas kernels: 12.6 us -> 10.4 us  [the longest x2 5.55 us: end_part(): pl.pallas_call(end_kernel, out_shape=(jax.ShapeDtypeStruct((rows, width),...]
  transfers between devices with their start and end apart: 24 -> 20, of which waited for: 9 -> 10; matrix products, arithmetic and copies ran while one was open for 1% -> 0% of each run, Pallas kernels for 20% -> 11%
where the time goes in v4:
time: 111 us; the launch traced here: 110 us
  waiting for transfers between devices  44.2 us (40%)
  starting transfers between devices  29.3 us (26%)
  Pallas kernels  21.6 us (19%)
  local copies, waits for them, and re-layouts  12.6 us (11%)
  between operations  2.16 us (2%)
    ppermute x8, waiting for transfers between devices, pair(): lax.ppermute(value, axis, [(i, i ^ k) for i in range(lax.axis_size(axis))])  32.8 us
    ppermute x8, starting transfers between devices, pair(): lax.ppermute(value, axis, [(i, i ^ k) for i in range(lax.axis_size(axis))])  15.3 us
    ppermute x12, starting transfers between devices, send(): return lax.ppermute(value, 'blk', perm)  14 us
    unnamed x34, local copies, waits for them, and re-layouts  12 us
    ppermute x12, waiting for transfers between devices, send(): return lax.ppermute(value, 'blk', perm)  11.4 us
    pallas_call x1, Pallas kernels, near_part(): pl.pallas_call(near_kernel, out_shape=(shape((rows, width), F32), shape((...  8.18 us
    pallas_call x2, Pallas kernels, end_part(): pl.pallas_call(end_kernel, out_shape=(jax.ShapeDtypeStruct((rows, width),...  5.55 us
    pallas_call x1, Pallas kernels, far_grad_part(): pl.pallas_call(far_grad_kernel, out_shape=(shape((rows, width), BF16), sh...  3.11 us
  transfers between devices with their start and end apart: 20, of which 10 were waited for; matrix products, arithmetic and copies ran while one was open for 0% of the time, Pallas kernels for 11%

profile of v4, /device:TPU:32, one launch (start us, length us, event | category | flops | bytes accessed | tf_op | source)
XLA Modules:
  0.0 110.0 jit_solution(9819616088415507849)
XLA Ops:
  0.7 1.4 %copy-done.1 = f32[256,1152]{1,0:T(8,128)S(1)} copy-done((f32[256,1152]{1,0:T(8,128)S(1)}, f32[256,1152]{1,0:T(8,128)}, u32[]{:S(2)}) %copy-start.1) | copy-done | bytes 1179672
  2.0 0.2 normalize.2
  2.3 0.7 normalize.3
  3.0 1.6 %collective-permute-start.9 = (bf16[256,1152]{1,0:T(8,128)(2,1)S(1)}, bf16[256,1152]{1,0:T(8,128)(2,1)}, u32[]{:S(2)}, u32[]{:S(2)}) collective-permute-start(bf16[256,1152]{1,0:T(8,128)(2,1)S(1)} %get-tuple-element.49.own_t), channel_id=1, source_target_pairs={{0,32},{16,48},{32,0},{48,16},{64,96},{80,112},{96,64},{112,80},{1... | collective-permute-start | bytes 1769480 | tf_op jit(solution)/shard_map/ppermute | solution.py:348
  4.5 1.5 %collective-permute-start.6 = (bf16[256,1152]{1,0:T(8,128)(2,1)S(1)}, bf16[256,1152]{1,0:T(8,128)(2,1)S(1)}, u32[]{:S(2)}, u32[]{:S(2)}) collective-permute-start(bf16[256,1152]{1,0:T(8,128)(2,1)S(1)} %get-tuple-element.47.own_i), channel_id=1, source_target_pairs={{0,64},{16,80},{32,96},{48,112},{64,128},{80,144},{96,160},{112,17... | collective-permute-start | bytes 1769480 | tf_op jit(solution)/shard_map/ppermute | solution.py:348
  6.0 1.7 %collective-permute-start.7 = (bf16[256,1152]{1,0:T(8,128)(2,1)S(1)}, bf16[256,1152]{1,0:T(8,128)(2,1)S(1)}, u32[]{:S(2)}, u32[]{:S(2)}) collective-permute-start(bf16[256,1152]{1,0:T(8,128)(2,1)S(1)} %get-tuple-element.47.own_i), channel_id=1, source_target_pairs={{0,192},{16,208},{32,224},{48,240},{64,0},{80,16},{96,32},{112,48}... | collective-permute-start | bytes 1769480 | tf_op jit(solution)/shard_map/ppermute | solution.py:348
  7.8 10.4 %collective-permute-done.9.y_t = bf16[256,1152]{1,0:T(8,128)(2,1)} collective-permute-done((bf16[256,1152]{1,0:T(8,128)(2,1)S(1)}, bf16[256,1152]{1,0:T(8,128)(2,1)}, u32[]{:S(2)}, u32[]{:S(2)}) %collective-permute-start.9) | collective-permute-done | bytes 589856 | tf_op jit(solution)/shard_map/ppermute | solution.py:348
  19.5 0.1 pad_maximum_fusion.scalars
  19.6 1.0 collective-permute-done.6.left_i.block_ref
  20.6 0.6 collective-permute-start.13
  21.2 3.0 %collective-permute-start.14 = (bf16[128,1152]{1,0:T(8,128)(2,1)S(1)}, bf16[128,1152]{1,0:T(8,128)(2,1)S(1)}, u32[]{:S(2)}, u32[]{:S(2)}) collective-permute-start(bf16[128,1152]{1,0:T(8,128)(2,1)S(1)} %cut.3), channel_id=1, source_target_pairs={{0,192},{16,208},{32,224},{48,240},{64,0},{80,16},{96,32},{112,48}... | collective-permute-start | bytes 884744 | tf_op jit(solution)/shard_map/ppermute | solution.py:348
  24.2 1.1 copy-done.14
  25.3 1.1 copy-done.16
  26.3 8.2 %near.1 = (f32[256,1152]{1,0:T(8,128)S(1)}, bf16[256,1152]{1,0:T(8,128)(2,1)}, bf16[256,1152]{1,0:T(8,128)(2,1)}, bf16[768,1152]{1,0:T(8,128)(2,1)S(1)}, bf16[10...) custom-call(f32[2]{0:T(128)S(1)} %pad_maximum_fusion.scalars, ...), custom_call_target="tpu_custom_call" | custom-call | flops 28991029248 | bytes 7077888 | tf_op jit(solution)/shard_map/near/pallas_call | solution.py:192
  34.5 2.1 %far.1 = (bf16[256,1152]{1,0:T(8,128)(2,1)S(1)}, bf16[256,1024]{1,0:T(8,128)(2,1)S(1)}, f32[8,128]{1,0:T(8,128)S(1)}) custom-call(f32[2]{0:T(128)S(1)} %pad_maximum_fusion.scalars, bf16[128,1152]{1,0:T(8,128)(2,1)S(1)} %collective-permute-done.13.top_i, bf16[128,1152]{1,0:T(8,128)(2,1)S(1)} %collective-permute-done.14.bot_i, ...), custom_call_target="tpu_custom_call" | custom-call | flops 75497472 | bytes 589824 | tf_op jit(solution)/shard_map/far/pallas_call | solution.py:219
  36.6 3.1 %far_grad.1 = (bf16[256,1152]{1,0:T(8,128)(2,1)}, f32[256,1152]{1,0:T(8,128)S(1)}, bf16[512,1152]{1,0:T(8,128)(2,1)S(1)}) custom-call(bf16[256,1152]{1,0:T(8,128)(2,1)S(1)} %get-tuple-element.55.far_images, bf16[256,1024]{1,0:T(8,128)(2,1)S(1)} %get-tuple-element.56.far_grads, bf16[768,1152]{1,0:T(8,128)(2,1)S(1)} %get-tuple-element.57.near_images, ...), custom_call_target="tpu_custom_call" | custom-call | flops 75497472 | bytes 589824 | tf_op jit(solution)/shard_map/far_grad/pallas_call | solution.py:237
  39.8 1.1 %copy-done.5 = bf16[768,1024]{1,0:T(8,128)(2,1)} copy-done((bf16[768,1024]{1,0:T(8,128)(2,1)}, bf16[768,1024]{1,0:T(8,128)(2,1)S(1)}, u32[]{:S(2)}) %copy-start.5) | copy-done | bytes 1572888
  40.9 0.5 collective-permute-start.17
  41.4 2.3 %collective-permute-done.17 = f32[8,128]{1,0:T(8,128)S(1)} collective-permute-done((f32[8,128]{1,0:T(8,128)S(1)}, f32[8,128]{1,0:T(8,128)S(1)}, u32[]{:S(2)}, u32[]{:S(2)}) %collective-permute-start.17) | collective-permute-done | bytes 4128 | tf_op jit(solution)/shard_map/ppermute | solution.py:370
  43.8 0.6 collective-permute-start.18
  44.3 3.0 %collective-permute-done.18.arrived = f32[8,128]{1,0:T(8,128)S(1)} collective-permute-done((f32[8,128]{1,0:T(8,128)S(1)}, f32[8,128]{1,0:T(8,128)S(1)}, u32[]{:S(2)}, u32[]{:S(2)}) %collective-permute-start.18) | collective-permute-done | bytes 4128 | tf_op jit(solution)/shard_map/ppermute | solution.py:370
  47.4 0.9 relay_y.1
  48.3 0.6 collective-permute-start.19
  48.9 1.8 %collective-permute-start.15 = (bf16[256,1152]{1,0:T(8,128)(2,1)}, bf16[256,1152]{1,0:T(8,128)(2,1)}, u32[]{:S(2)}, u32[]{:S(2)}) collective-permute-start(bf16[256,1152]{1,0:T(8,128)(2,1)} %get-tuple-element.59), channel_id=1, source_target_pairs={{0,128},{16,144},{32,160},{48,176},{64,192},{80,208},{96,224},{112... | collective-permute-start | bytes 1769480 | tf_op jit(solution)/shard_map/ppermute | solution.py:348
  50.7 0.6 collective-permute-start.11
  51.3 2.6 %collective-permute-start.12 = (bf16[256,1152]{1,0:T(8,128)(2,1)}, bf16[256,1152]{1,0:T(8,128)(2,1)}, u32[]{:S(2)}, u32[]{:S(2)}) collective-permute-start(bf16[256,1152]{1,0:T(8,128)(2,1)} %get-tuple-element.52), channel_id=1, source_target_pairs={{0,192},{16,208},{32,224},{48,240},{64,0},{80,16},{96,32},{112,48}... | collective-permute-start | bytes 1769480 | tf_op jit(solution)/shard_map/ppermute | solution.py:348
  53.9 1.5 %copy-done.4 = bf16[768,1152]{1,0:T(8,128)(2,1)S(1)} copy-done((bf16[768,1152]{1,0:T(8,128)(2,1)S(1)}, bf16[768,1152]{1,0:T(8,128)(2,1)}, u32[]{:S(2)}) %copy-start.4) | copy-done | bytes 1769496
  55.4 1.4 %copy-done.6 = bf16[768,1024]{1,0:T(8,128)(2,1)S(1)} copy-done((bf16[768,1024]{1,0:T(8,128)(2,1)S(1)}, bf16[768,1024]{1,0:T(8,128)(2,1)}, u32[]{:S(2)}) %copy-start.6) | copy-done | bytes 1572888
  56.8 1.1 copy-done.10
  57.9 1.0 copy-done.12
  58.9 0.9 text.1
  59.8 1.0 copy-done.7
  60.8 41.7 %while.10 = (s32[]{:T(128)}, f32[8,128]{1,0:T(8,128)S(1)}, s32[]{:T(128)}, s32[]{:T(128)}) while((s32[]{:T(128)}, f32[8,128]{1,0:T(8,128)S(1)}, s32[]{:T(128)}, s32[]{:T(128)}) %tuple.24), condition=%wide.region_1.0_spmd, body=%wide.region_0.0_spmd.sunk | while | flops 6146 | bytes 172325 | solution.py:385
  60.8 15.4 %collective-permute-done = f32[8,128]{1,0:T(8,128)S(1)} collective-permute-done((f32[8,128]{1,0:T(8,128)S(1)}, f32[8,128]{1,0:T(8,128)S(1)}, u32[]{:S(2)}, u32[]{:S(2)}) %collective-permute-start) | collective-permute-done | bytes 4128 | tf_op jit(solution)/shard_map/while/body/ppermute | solution.py:370
  76.2 2.0 %collective-permute-start.1 = (f32[8,128]{1,0:T(8,128)S(1)}, f32[8,128]{1,0:T(8,128)S(1)}, u32[]{:S(2)}, u32[]{:S(2)}) collective-permute-start(f32[8,128]{1,0:T(8,128)S(1)} %add.33), channel_id=1, source_target_pairs={{0,128},{16,144},{32,160},{48,176},{64,192},{80,208},{96,224},{112... | collective-permute-start | bytes 12296 | tf_op jit(solution)/shard_map/while/body/ppermute | solution.py:370
  78.3 3.1 %collective-permute-done.1 = f32[8,128]{1,0:T(8,128)S(1)} collective-permute-done((f32[8,128]{1,0:T(8,128)S(1)}, f32[8,128]{1,0:T(8,128)S(1)}, u32[]{:S(2)}, u32[]{:S(2)}) %collective-permute-start.1) | collective-permute-done | bytes 4128 | tf_op jit(solution)/shard_map/while/body/ppermute | solution.py:370
  81.4 0.1 collective-permute-start.2
  81.5 3.5 %collective-permute-done.2 = f32[8,128]{1,0:T(8,128)S(1)} collective-permute-done((f32[8,128]{1,0:T(8,128)S(1)}, f32[8,128]{1,0:T(8,128)S(1)}, u32[]{:S(2)}, u32[]{:S(2)}) %collective-permute-start.2) | collective-permute-done | bytes 4128 | tf_op jit(solution)/shard_map/while/body/ppermute | solution.py:370
  85.0 3.2 %collective-permute-start.3 = (f32[8,128]{1,0:T(8,128)S(1)}, f32[8,128]{1,0:T(8,128)S(1)}, u32[]{:S(2)}, u32[]{:S(2)}) collective-permute-start(f32[8,128]{1,0:T(8,128)S(1)} %add.35), channel_id=1, source_target_pairs={{0,2},{1,3},{2,0},{3,1},{4,6},{5,7},{6,4},{7,5},{8,10},{9,11},{10,... | collective-permute-start | bytes 12296 | tf_op jit(solution)/shard_map/while/body/ppermute | solution.py:370
  88.2 1.6 %collective-permute-done.3 = f32[8,128]{1,0:T(8,128)S(1)} collective-permute-done((f32[8,128]{1,0:T(8,128)S(1)}, f32[8,128]{1,0:T(8,128)S(1)}, u32[]{:S(2)}, u32[]{:S(2)}) %collective-permute-start.3) | collective-permute-done | bytes 4128 | tf_op jit(solution)/shard_map/while/body/ppermute | solution.py:370
  89.8 5.9 %collective-permute-start.4 = (f32[8,128]{1,0:T(8,128)S(1)}, f32[8,128]{1,0:T(8,128)S(1)}, u32[]{:S(2)}, u32[]{:S(2)}) collective-permute-start(f32[8,128]{1,0:T(8,128)S(1)} %add.36), channel_id=1, source_target_pairs={{0,4},{1,5},{2,6},{3,7},{4,0},{5,1},{6,2},{7,3},{8,12},{9,13},{10,... | collective-permute-start | bytes 12296 | tf_op jit(solution)/shard_map/while/body/ppermute | solution.py:370
  95.8 1.6 %collective-permute-done.4 = f32[8,128]{1,0:T(8,128)S(1)} collective-permute-done((f32[8,128]{1,0:T(8,128)S(1)}, f32[8,128]{1,0:T(8,128)S(1)}, u32[]{:S(2)}, u32[]{:S(2)}) %collective-permute-start.4) | collective-permute-done | bytes 4128 | tf_op jit(solution)/shard_map/while/body/ppermute | solution.py:370
  97.4 2.9 %collective-permute-start.5 = (f32[8,128]{1,0:T(8,128)S(1)}, f32[8,128]{1,0:T(8,128)S(1)}, u32[]{:S(2)}, u32[]{:S(2)}) collective-permute-start(f32[8,128]{1,0:T(8,128)S(1)} %add.37), channel_id=1, source_target_pairs={{0,8},{1,9},{2,10},{3,11},{4,12},{5,13},{6,14},{7,15},{8,0},{9,1},... | collective-permute-start | bytes 12296 | tf_op jit(solution)/shard_map/while/body/ppermute | solution.py:370
  100.3 2.2 %collective-permute-done.5 = f32[8,128]{1,0:T(8,128)S(1)} collective-permute-done((f32[8,128]{1,0:T(8,128)S(1)}, f32[8,128]{1,0:T(8,128)S(1)}, u32[]{:S(2)}, u32[]{:S(2)}) %collective-permute-start.5) | collective-permute-done | bytes 4128 | tf_op jit(solution)/shard_map/while/body/ppermute | solution.py:370
  102.5 1.3 %copy-done.8 = f32[256,1152]{1,0:T(8,128)S(1)} copy-done((f32[256,1152]{1,0:T(8,128)S(1)}, f32[256,1152]{1,0:T(8,128)}, u32[]{:S(2)}) %copy-start.8) | copy-done | bytes 1179672
  103.8 2.6 %text_end.1 = (f32[256,1152]{1,0:T(8,128)}, f32[8,128]{1,0:T(8,128)S(1)}) custom-call(f32[2]{0:T(128)S(1)} %pad_maximum_fusion.scalars, f32[256,1152]{1,0:T(8,128)S(1)} %copy-done, f32[256,1152]{1,0:T(8,128)S(1)} %copy-done.8, bf16[512,1152]{1,0:T(8,128)(2,1)S(1)} %collective-permute-done.16.passing.refs_1_, ...), custom_call_target="tpu_custom_call" | custom-call | flops 2359296 | bytes 294912 | tf_op jit(solution)/shard_map/text_end/pallas_call | solution.py:322
  106.4 2.9 %image_end.1 = (f32[256,1152]{1,0:T(8,128)}, f32[8,128]{1,0:T(8,128)S(1)}) custom-call(f32[2]{0:T(128)S(1)} %pad_maximum_fusion.scalars, f32[256,1152]{1,0:T(8,128)S(1)} %copy-done.2, f32[256,1152]{1,0:T(8,128)S(1)} %get-tuple-element.50.refs_0_, bf16[256,1152]{1,0:T(8,128)(2,1)} %collective-permute-done.11.refs_1_, ...), custom_call_target="tpu_custom_call" | custom-call | flops 2359296 | bytes 294912 | tf_op jit(solution)/shard_map/image_end/pallas_call | solution.py:322
  109.4 0.6 fusion
  (48 shorter events, 0.2 us)
Async XLA Ops:
  0.6 1.6 %copy-start = (f32[256,1152]{1,0:T(8,128)S(1)}, f32[256,1152]{1,0:T(8,128)}, u32[]{:S(2)}) copy-start(f32[256,1152]{1,0:T(8,128)} %emb.2) | copy-start | bytes 3538948
  0.6 1.4 %copy-start.1 = (f32[256,1152]{1,0:T(8,128)S(1)}, f32[256,1152]{1,0:T(8,128)}, u32[]{:S(2)}) copy-start(f32[256,1152]{1,0:T(8,128)} %emb.3) | copy-start | bytes 3538948
  2.2 19.0 %copy-start.13 = (bf16[256,1152]{1,0:T(8,128)(2,1)}, bf16[256,1152]{1,0:T(8,128)(2,1)S(1)}, u32[]{:S(2)}) copy-start(bf16[256,1152]{1,0:T(8,128)(2,1)S(1)} %get-tuple-element.47.own_i) | copy-start | bytes 1769476
  3.0 21.2 %copy-start.15 = (bf16[256,1152]{1,0:T(8,128)(2,1)}, bf16[256,1152]{1,0:T(8,128)(2,1)S(1)}, u32[]{:S(2)}) copy-start(bf16[256,1152]{1,0:T(8,128)(2,1)S(1)} %get-tuple-element.49.own_t) | copy-start | bytes 1769476
  3.0 15.2 %collective-permute-start.9 = (bf16[256,1152]{1,0:T(8,128)(2,1)S(1)}, bf16[256,1152]{1,0:T(8,128)(2,1)}, u32[]{:S(2)}, u32[]{:S(2)}) collective-permute-start(bf16[256,1152]{1,0:T(8,128)(2,1)S(1)} %get-tuple-element.49.own_t), channel_id=1, source_target_pairs={{0,32},{16,48},{32,0},{48,16},{64,96},{80,112},{96,64},{112,80},{1... | collective-permute-start | bytes 1769480 | tf_op jit(solution)/shard_map/ppermute | solution.py:348
  4.5 16.0 %collective-permute-start.6 = (bf16[256,1152]{1,0:T(8,128)(2,1)S(1)}, bf16[256,1152]{1,0:T(8,128)(2,1)S(1)}, u32[]{:S(2)}, u32[]{:S(2)}) collective-permute-start(bf16[256,1152]{1,0:T(8,128)(2,1)S(1)} %get-tuple-element.47.own_i), channel_id=1, source_target_pairs={{0,64},{16,80},{32,96},{48,112},{64,128},{80,144},{96,160},{112,17... | collective-permute-start | bytes 1769480 | tf_op jit(solution)/shard_map/ppermute | solution.py:348
  6.0 15.1 %collective-permute-start.7 = (bf16[256,1152]{1,0:T(8,128)(2,1)S(1)}, bf16[256,1152]{1,0:T(8,128)(2,1)S(1)}, u32[]{:S(2)}, u32[]{:S(2)}) collective-permute-start(bf16[256,1152]{1,0:T(8,128)(2,1)S(1)} %get-tuple-element.47.own_i), channel_id=1, source_target_pairs={{0,192},{16,208},{32,224},{48,240},{64,0},{80,16},{96,32},{112,48}... | collective-permute-start | bytes 1769480 | tf_op jit(solution)/shard_map/ppermute | solution.py:348
  7.8 16.4 %collective-permute-start.8 = (bf16[256,1152]{1,0:T(8,128)(2,1)S(1)}, bf16[256,1152]{1,0:T(8,128)(2,1)}, u32[]{:S(2)}, u32[]{:S(2)}) collective-permute-start(bf16[256,1152]{1,0:T(8,128)(2,1)S(1)} %get-tuple-element.49.own_t), channel_id=1, source_target_pairs={{0,16},{16,0},{32,48},{48,32},{64,80},{80,64},{96,112},{112,96},{1... | collective-permute-start | bytes 1769480 | tf_op jit(solution)/shard_map/ppermute | solution.py:348
  18.1 6.0 %collective-permute-start.10 = (bf16[256,1152]{1,0:T(8,128)(2,1)}, bf16[256,1152]{1,0:T(8,128)(2,1)}, u32[]{:S(2)}, u32[]{:S(2)}) collective-permute-start(bf16[256,1152]{1,0:T(8,128)(2,1)} %collective-permute-done.9.y_t), channel_id=1, source_target_pairs={{0,16},{16,0},{32,48},{48,32},{64,80},{80,64},{96,112},{112,96},{1... | collective-permute-start | bytes 1769480 | tf_op jit(solution)/shard_map/ppermute | solution.py:348
  20.6 13.9 %collective-permute-start.13 = (bf16[128,1152]{1,0:T(8,128)(2,1)S(1)}, bf16[128,1152]{1,0:T(8,128)(2,1)S(1)}, u32[]{:S(2)}, u32[]{:S(2)}) collective-permute-start(bf16[128,1152]{1,0:T(8,128)(2,1)S(1)} %cut.2), channel_id=1, source_target_pairs={{0,64},{16,80},{32,96},{48,112},{64,128},{80,144},{96,160},{112,17... | collective-permute-start | bytes 884744 | tf_op jit(solution)/shard_map/ppermute | solution.py:348
  21.2 13.3 %collective-permute-start.14 = (bf16[128,1152]{1,0:T(8,128)(2,1)S(1)}, bf16[128,1152]{1,0:T(8,128)(2,1)S(1)}, u32[]{:S(2)}, u32[]{:S(2)}) collective-permute-start(bf16[128,1152]{1,0:T(8,128)(2,1)S(1)} %cut.3), channel_id=1, source_target_pairs={{0,192},{16,208},{32,224},{48,240},{64,0},{80,16},{96,32},{112,48}... | collective-permute-start | bytes 884744 | tf_op jit(solution)/shard_map/ppermute | solution.py:348
  24.2 1.1 copy-start.14
  25.3 1.1 copy-start.16
  34.5 2.1 %copy-start.3 = (bf16[768,1152]{1,0:T(8,128)(2,1)}, bf16[768,1152]{1,0:T(8,128)(2,1)S(1)}, u32[]{:S(2)}) copy-start(bf16[768,1152]{1,0:T(8,128)(2,1)S(1)} %get-tuple-element.57.near_images) | copy-start | bytes 5308420
  36.6 3.1 %copy-start.9 = (bf16[256,1152]{1,0:T(8,128)(2,1)}, bf16[256,1152]{1,0:T(8,128)(2,1)S(1)}, u32[]{:S(2)}) copy-start(bf16[256,1152]{1,0:T(8,128)(2,1)S(1)} %get-tuple-element.55.far_images) | copy-start | bytes 1769476
  36.6 3.1 %copy-start.11 = (bf16[256,1024]{1,0:T(8,128)(2,1)}, bf16[256,1024]{1,0:T(8,128)(2,1)S(1)}, u32[]{:S(2)}) copy-start(bf16[256,1024]{1,0:T(8,128)(2,1)S(1)} %get-tuple-element.56.far_grads) | copy-start | bytes 1572868
  39.8 1.1 %copy-start.5 = (bf16[768,1024]{1,0:T(8,128)(2,1)}, bf16[768,1024]{1,0:T(8,128)(2,1)S(1)}, u32[]{:S(2)}) copy-start(bf16[768,1024]{1,0:T(8,128)(2,1)S(1)} %get-tuple-element.58.near_grads) | copy-start | bytes 4718596
  40.9 6.5 %collective-permute-start.16 = (bf16[512,1152]{1,0:T(8,128)(2,1)S(1)}, bf16[512,1152]{1,0:T(8,128)(2,1)S(1)}, u32[]{:S(2)}, u32[]{:S(2)}) collective-permute-start(bf16[512,1152]{1,0:T(8,128)(2,1)S(1)} %get-tuple-element.61), channel_id=1, source_target_pairs={{0,16},{16,0},{32,48},{48,32},{64,80},{80,64},{96,112},{112,96},{1... | collective-permute-start | bytes 3538952 | tf_op jit(solution)/shard_map/ppermute | solution.py:348
  40.9 2.9 %collective-permute-start.17 = (f32[8,128]{1,0:T(8,128)S(1)}, f32[8,128]{1,0:T(8,128)S(1)}, u32[]{:S(2)}, u32[]{:S(2)}) collective-permute-start(f32[8,128]{1,0:T(8,128)S(1)} %get-tuple-element.62), channel_id=1, source_target_pairs={{0,16},{16,0},{32,48},{48,32},{64,80},{80,64},{96,112},{112,96},{1... | collective-permute-start | bytes 12296 | tf_op jit(solution)/shard_map/ppermute | solution.py:370
  43.8 3.6 %collective-permute-start.18 = (f32[8,128]{1,0:T(8,128)S(1)}, f32[8,128]{1,0:T(8,128)S(1)}, u32[]{:S(2)}, u32[]{:S(2)}) collective-permute-start(f32[8,128]{1,0:T(8,128)S(1)} %add.24.sums), channel_id=1, source_target_pairs={{0,32},{16,48},{32,0},{48,16},{64,96},{80,112},{96,64},{112,80},{1... | collective-permute-start | bytes 12296 | tf_op jit(solution)/shard_map/ppermute | solution.py:370
  48.3 54.2 %collective-permute-start.19 = (bf16[256,1152]{1,0:T(8,128)(2,1)}, bf16[256,1152]{1,0:T(8,128)(2,1)}, u32[]{:S(2)}, u32[]{:S(2)}) collective-permute-start(bf16[256,1152]{1,0:T(8,128)(2,1)} %get-tuple-element.65), channel_id=1, source_target_pairs={{0,32},{16,48},{32,0},{48,16},{64,96},{80,112},{96,64},{112,80},{1... | collective-permute-start | bytes 1769480 | tf_op jit(solution)/shard_map/ppermute | solution.py:348
  48.9 57.5 %collective-permute-start.15 = (bf16[256,1152]{1,0:T(8,128)(2,1)}, bf16[256,1152]{1,0:T(8,128)(2,1)}, u32[]{:S(2)}, u32[]{:S(2)}) collective-permute-start(bf16[256,1152]{1,0:T(8,128)(2,1)} %get-tuple-element.59), channel_id=1, source_target_pairs={{0,128},{16,144},{32,160},{48,176},{64,192},{80,208},{96,224},{112... | collective-permute-start | bytes 1769480 | tf_op jit(solution)/shard_map/ppermute | solution.py:348
  50.7 55.7 %collective-permute-start.11 = (bf16[256,1152]{1,0:T(8,128)(2,1)}, bf16[256,1152]{1,0:T(8,128)(2,1)}, u32[]{:S(2)}, u32[]{:S(2)}) collective-permute-start(bf16[256,1152]{1,0:T(8,128)(2,1)} %get-tuple-element.51), channel_id=1, source_target_pairs={{0,64},{16,80},{32,96},{48,112},{64,128},{80,144},{96,160},{112,17... | collective-permute-start | bytes 1769480 | tf_op jit(solution)/shard_map/ppermute | solution.py:348
  51.3 55.1 %collective-permute-start.12 = (bf16[256,1152]{1,0:T(8,128)(2,1)}, bf16[256,1152]{1,0:T(8,128)(2,1)}, u32[]{:S(2)}, u32[]{:S(2)}) collective-permute-start(bf16[256,1152]{1,0:T(8,128)(2,1)} %get-tuple-element.52), channel_id=1, source_target_pairs={{0,192},{16,208},{32,224},{48,240},{64,0},{80,16},{96,32},{112,48}... | collective-permute-start | bytes 1769480 | tf_op jit(solution)/shard_map/ppermute | solution.py:348
  53.9 1.5 %copy-start.4 = (bf16[768,1152]{1,0:T(8,128)(2,1)S(1)}, bf16[768,1152]{1,0:T(8,128)(2,1)}, u32[]{:S(2)}) copy-start(bf16[768,1152]{1,0:T(8,128)(2,1)} %copy-done.3) | copy-start | bytes 5308420
  55.4 1.4 %copy-start.6 = (bf16[768,1024]{1,0:T(8,128)(2,1)S(1)}, bf16[768,1024]{1,0:T(8,128)(2,1)}, u32[]{:S(2)}) copy-start(bf16[768,1024]{1,0:T(8,128)(2,1)} %copy-done.5) | copy-start | bytes 4718596
  56.8 1.1 copy-start.10
  57.9 1.0 copy-start.12
  59.8 1.0 copy-start.7
  60.8 15.4 %collective-permute-start = (f32[8,128]{1,0:T(8,128)S(1)}, f32[8,128]{1,0:T(8,128)S(1)}, u32[]{:S(2)}, u32[]{:S(2)}) collective-permute-start(f32[8,128]{1,0:T(8,128)S(1)} %get-tuple-element.106), channel_id=1, source_target_pairs={{0,64},{16,80},{32,96},{48,112},{64,0},{80,16},{96,32},{112,48},{1... | collective-permute-start | bytes 12296 | tf_op jit(solution)/shard_map/while/body/ppermute | solution.py:370
  76.2 5.1 %collective-permute-start.1 = (f32[8,128]{1,0:T(8,128)S(1)}, f32[8,128]{1,0:T(8,128)S(1)}, u32[]{:S(2)}, u32[]{:S(2)}) collective-permute-start(f32[8,128]{1,0:T(8,128)S(1)} %add.33), channel_id=1, source_target_pairs={{0,128},{16,144},{32,160},{48,176},{64,192},{80,208},{96,224},{112... | collective-permute-start | bytes 12296 | tf_op jit(solution)/shard_map/while/body/ppermute | solution.py:370
  81.4 3.6 %collective-permute-start.2 = (f32[8,128]{1,0:T(8,128)S(1)}, f32[8,128]{1,0:T(8,128)S(1)}, u32[]{:S(2)}, u32[]{:S(2)}) collective-permute-start(f32[8,128]{1,0:T(8,128)S(1)} %add.34), channel_id=1, source_target_pairs={{0,1},{1,0},{2,3},{3,2},{4,5},{5,4},{6,7},{7,6},{8,9},{9,8},{10,11... | collective-permute-start | bytes 12296 | tf_op jit(solution)/shard_map/while/body/ppermute | solution.py:370
  85.0 4.8 %collective-permute-start.3 = (f32[8,128]{1,0:T(8,128)S(1)}, f32[8,128]{1,0:T(8,128)S(1)}, u32[]{:S(2)}, u32[]{:S(2)}) collective-permute-start(f32[8,128]{1,0:T(8,128)S(1)} %add.35), channel_id=1, source_target_pairs={{0,2},{1,3},{2,0},{3,1},{4,6},{5,7},{6,4},{7,5},{8,10},{9,11},{10,... | collective-permute-start | bytes 12296 | tf_op jit(solution)/shard_map/while/body/ppermute | solution.py:370
  89.8 7.5 %collective-permute-start.4 = (f32[8,128]{1,0:T(8,128)S(1)}, f32[8,128]{1,0:T(8,128)S(1)}, u32[]{:S(2)}, u32[]{:S(2)}) collective-permute-start(f32[8,128]{1,0:T(8,128)S(1)} %add.36), channel_id=1, source_target_pairs={{0,4},{1,5},{2,6},{3,7},{4,0},{5,1},{6,2},{7,3},{8,12},{9,13},{10,... | collective-permute-start | bytes 12296 | tf_op jit(solution)/shard_map/while/body/ppermute | solution.py:370
  97.4 5.1 %collective-permute-start.5 = (f32[8,128]{1,0:T(8,128)S(1)}, f32[8,128]{1,0:T(8,128)S(1)}, u32[]{:S(2)}, u32[]{:S(2)}) collective-permute-start(f32[8,128]{1,0:T(8,128)S(1)} %add.37), channel_id=1, source_target_pairs={{0,8},{1,9},{2,10},{3,11},{4,12},{5,13},{6,14},{7,15},{8,0},{9,1},... | collective-permute-start | bytes 12296 | tf_op jit(solution)/shard_map/while/body/ppermute | solution.py:370
  102.5 1.3 %copy-start.8 = (f32[256,1152]{1,0:T(8,128)S(1)}, f32[256,1152]{1,0:T(8,128)}, u32[]{:S(2)}) copy-start(f32[256,1152]{1,0:T(8,128)} %copy-done.7) | copy-start | bytes 3538948
  103.8 2.7 %copy-start.2 = (f32[256,1152]{1,0:T(8,128)S(1)}, f32[256,1152]{1,0:T(8,128)}, u32[]{:S(2)}) copy-start(f32[256,1152]{1,0:T(8,128)} %emb.3) | copy-start | bytes 3538948

commit v5 on v4

--- a/solution.py
+++ b/solution.py
@@ -6,7 +6,10 @@
 from jax.sharding import PartitionSpec as P
 
 F32 = jnp.float32
-STEPS = (("blk", 4), ("blk", 8), ("group", 1), ("group", 2), ("group", 4), ("group", 8))
+BATCH = 65536
+IMAGE_COST = 512
+TEXT_COST = 16
+STEPS = (("group", 1), ("group", 2), ("group", 4), ("group", 8), ("blk", 4), ("blk", 8))
 BF16 = jnp.bfloat16
 HBM = pl.BlockSpec(memory_space=pltpu.HBM)
 VMEM = pl.BlockSpec(memory_space=pltpu.VMEM)
@@ -105,11 +108,11 @@
 
 
 def near_kernel(
-    scalars, own_i, left_i, right_i, own_t, core_t, y_t, yc_t,
-    own_out, left_out, right_out, images, texts, grads, sums_ref,
+    log_scale, bias, own_i, left_i, right_i, own_t, core_t, y_t, yc_t,
+    own_out, left_out, right_out, images, texts, grads, sums_ref, passes_ref,
 ):
     rows = own_i.shape[0]
-    scale, bias = scalars[0], scalars[1]
+    scale, bias = jnp.exp(jnp.full((1, rows), log_scale[0])), bias[0]
     for i, src in enumerate((own_i, left_i, right_i)):
         images[pl.ds(i * rows, rows), :] = src[...]
     for i, src in enumerate((own_t, core_t, y_t, yc_t)):
@@ -135,6 +138,7 @@
             out = (own_out, left_out, right_out)[b]
             out[...] = partial.astype(out.dtype)
     write_sums(sums_ref, loss, scaled, grad)
+    passes_ref[0] = 1
 
 
 def text_grad(grads, near_images, far_grads, far_images, at):
@@ -145,10 +149,10 @@
     )
 
 
-def far_kernel(scalars, top_i, bot_i, texts, near_sums, images, grads, sums_ref):
+def far_kernel(log_scale, bias, top_i, bot_i, texts, near_sums, images, grads, sums_ref):
     half = top_i.shape[0]
     rows = 2 * half
-    scale, bias = scalars[0], scalars[1]
+    scale, bias = jnp.exp(jnp.full((1, rows), log_scale[0])), bias[0]
     images[pl.ds(0, half), :] = top_i[...]
     images[pl.ds(half, half), :] = bot_i[...]
     loss = scaled = grad = jnp.zeros((8, rows), F32)
@@ -199,9 +203,10 @@
             shape((4 * rows, width), BF16),
             shape((3 * rows, 4 * rows), BF16),
             shape((8, 128), F32),
-        ),
-        in_specs=[SMEM] + [VMEM] * 7,
-        out_specs=(VMEM,) * 7,
+            shape((1,), jnp.int32),
+        ),
+        in_specs=[SMEM] * 2 + [VMEM] * 7,
+        out_specs=(VMEM,) * 7 + (SMEM,),
         compiler_params=params(16),
         cost_estimate=pl.CostEstimate(
             flops=8 * 2 * 2 * 12 * rows * rows * width,
@@ -209,7 +214,7 @@
             transcendentals=3 * 12 * rows * rows,
         ),
         name="near",
-    )(scalars, *images, *texts)
+    )(*scalars, *images, *texts)
 
 
 def far_part(scalars, far_images, texts, near_sums):
@@ -221,14 +226,14 @@
         out_shape=(
             shape((rows, width), BF16), shape((rows, 4 * rows), BF16), shape((8, 128), F32)
         ),
-        in_specs=[SMEM] + [VMEM] * 4,
+        in_specs=[SMEM] * 2 + [VMEM] * 4,
         out_specs=(VMEM,) * 3,
         compiler_params=params(16),
         cost_estimate=pl.CostEstimate(
             flops=rows * rows * width, bytes_accessed=2 * rows * width, transcendentals=rows * rows
         ),
         name="far",
-    )(scalars, *far_images, texts, near_sums)
+    )(*scalars, *far_images, texts, near_sums)
 
 
 def far_grad_part(far_images, far_grads, near_images, texts, near_grads):
@@ -259,10 +264,28 @@
         out_specs=(VMEM,) * 2,
         compiler_params=params(16),
         cost_estimate=pl.CostEstimate(
-            flops=64 * rows * rows * width, bytes_accessed=rows * width, transcendentals=0
+            flops=TEXT_COST * rows * rows * width, bytes_accessed=rows * width, transcendentals=0
         ),
         name="text",
     )(near_grads, far_grads, near_images, far_images, sums)
+
+
+def add_kernel(*refs):
+    *parts, out = refs
+    out[...] = sum((part[...] for part in parts[1:]), parts[0][...])
+
+
+def add(*parts):
+    one = parts[0]
+    return pl.pallas_call(
+        add_kernel,
+        out_shape=jax.ShapeDtypeStruct(one.shape, F32),
+        in_specs=[VMEM] * len(parts),
+        out_specs=VMEM,
+        compiler_params=params(16),
+        cost_estimate=pl.CostEstimate(flops=one.size, bytes_accessed=one.size, transcendentals=0),
+        name="add",
+    )(*parts)
 
 
 def relay_y_kernel(own, passing, sums, arrived, out, sums_out):
@@ -300,8 +323,9 @@
     return copy
 
 
-def end_kernel(scalars, emb, *refs):
+def end_kernel(log_scale, emb, *refs):
     *parts, sums, out, sums_out, slots, sems = refs
+    scale = jnp.exp(jnp.full((1, 1), log_scale[0]))
     step = emb.shape[0] // 4
     copies = []
     for i in range(4):
@@ -310,35 +334,37 @@
         for part in parts[1:]:
             skip = part.shape[0] - 4 * step
             upstream += part[pl.ds(skip + i * step, step), :].astype(F32)
-        copies.append(write_rows(out, backnorm(emb[at, :], upstream, scalars[0]), slots, sems, i))
-    sums_out[...] = sums[...]
+        copies.append(write_rows(out, backnorm(emb[at, :], upstream, scale), slots, sems, i))
+    if sums_out.shape == sums.shape:
+        sums_out[...] = sums[...]
+    else:
+        for i in range(3):
+            sums_out[i] = jnp.sum(sums[0:1, i : i + 1]) * (1.0 / BATCH)
     for copy in copies:
         copy.wait()
 
 
-def end_part(name, scalars, emb, *parts):
+def end_part(name, cost, sums_shape, log_scale, emb, *parts):
     rows, width = emb.shape
-    sums = parts[-1]
     return pl.pallas_call(
         end_kernel,
         out_shape=(
-            jax.ShapeDtypeStruct((rows, width), F32), jax.ShapeDtypeStruct(sums.shape, F32)
+            jax.ShapeDtypeStruct((rows, width), F32), jax.ShapeDtypeStruct(sums_shape, F32)
         ),
         in_specs=[SMEM] + [VMEM] * (1 + len(parts)),
-        out_specs=(HBM, VMEM),
+        out_specs=(HBM, VMEM if len(sums_shape) == 2 else SMEM),
         scratch_shapes=[pltpu.VMEM((rows, width), F32), pltpu.SemaphoreType.DMA((4,))],
         compiler_params=params(24),
         cost_estimate=pl.CostEstimate(
-            flops=8 * rows * width, bytes_accessed=rows * width, transcendentals=rows
+            flops=cost * rows * width, bytes_accessed=rows * width, transcendentals=rows
         ),
         name=name,
-    )(scalars, emb, *parts)
+    )(log_scale, emb, *parts)
 
 
 def shards(image_emb, text_emb, log_scale, bias):
     rows = image_emb.shape[0]
     blocks = lax.axis_size("blk")
-    groups = lax.axis_size("group")
     ahead = [(i, (i + 4) % blocks) for i in range(blocks)]
     back = [(i, (i - 4) % blocks) for i in range(blocks)]
     across_y = [(i, i ^ 2) for i in range(blocks)]
@@ -347,8 +373,7 @@
     def send(value, perm):
         return lax.ppermute(value, "blk", perm)
 
-    scale = jnp.exp(log_scale)
-    scalars = jnp.stack([scale, bias])
+    scalars = log_scale.reshape(1), bias.reshape(1)
     own_i, token = normalize(image_emb)
     own_t, _ = normalize(text_emb, token)
     left_i = send(own_i, ahead)
@@ -359,7 +384,7 @@
     top_i = send(cut(left_i, 0), ahead)
     bot_i = send(cut(right_i, rows // 2), back)
 
-    own_p, left_p, right_p, near_images, texts, near_grads, near_sums = near_part(
+    own_p, left_p, right_p, near_images, texts, near_grads, near_sums, passes = near_part(
         scalars, (own_i, left_i, right_i), (own_t, core_t, y_t, yc_t)
     )
     from_left = send(right_p, ahead)
@@ -369,7 +394,7 @@
     def pair(value, axis, k):
         return lax.ppermute(value, axis, [(i, i ^ k) for i in range(lax.axis_size(axis))])
 
-    sums_1 = sums + pair(sums, "blk", 1)
+    sums_1 = add(sums, pair(sums, "blk", 1))
     far_p, y_q, to_mate = far_grad_part(far_images, far_grads, near_images, texts, near_grads)
     from_far = send(far_p, [(i, (i + 8) % blocks) for i in range(blocks)])
     from_core = send(to_mate, across_core)
@@ -377,19 +402,20 @@
     from_y = send(y_sum, across_y)
     own_q, sums_2 = text_part(near_grads, far_grads, near_images, far_images, sums_2)
 
-    def steps(_, value):
+    def steps(carry):
+        left, value = carry
         for axis, k in STEPS:
             value = value + pair(value, axis, k)
-        return value
-
-    sums_8 = lax.fori_loop(0, (scale > 0.0).astype(jnp.int32), steps, sums_2)
-    grad_text, sums_8 = end_part(
-        "text_end", scalars, text_emb, own_q, from_core, from_y, sums_8
-    )
+        return left - 1, value
+
+    _, sums_8 = lax.while_loop(lambda carry: carry[0] > 0, steps, (passes[0], sums_2))
     grad_image, sums_8 = end_part(
-        "image_end", scalars, image_emb, own_p, from_left, from_right, from_far, sums_8
-    )
-    totals = sums_8[0] / (rows * blocks * groups)
+        "image_end", IMAGE_COST, (8, 128), scalars[0], image_emb,
+        own_p, from_left, from_right, from_far, add(sums_8),
+    )
+    grad_text, totals = end_part(
+        "text_end", 8, (3,), scalars[0], text_emb, own_q, from_core, from_y, sums_8
+    )
     return (totals[0], grad_image, grad_text, totals[1], totals[2])
 
 

time: 111 us -> 92.1 us (0.83)
  waiting for transfers between devices: 44.2 us -> 31.2 us
  local copies, waits for them, and re-layouts: 12.6 us -> 5.24 us
  loops' own time: 0.01 us -> 2.48 us
    ppermute x8, waiting for transfers between devices: 32.8 us -> 19.7 us  [pair(): lax.ppermute(value, axis, [(i, i ^ k) for i in range(lax.axis_size(axis))])]
    unnamed x34 -> x14, local copies, waits for them, and re-layouts: 12 us -> 4.65 us
    another operation x1, loops' own time: 0.01 us -> 2.48 us  [shards(): lax.while_loop(lambda carry: carry[0] > 0, steps, (passes[0], sums_2))]
  transfers between devices with their start and end apart: 20 -> 20, of which waited for: 10 -> 10; matrix products, arithmetic and copies ran while one was open for 0% -> 0% of each run, Pallas kernels for 11% -> 14%
where the time goes in v5:
time: 92.1 us; the launch traced here: 91.1 us
  waiting for transfers between devices  31.2 us (34%)
  starting transfers between devices  28.4 us (31%)
  Pallas kernels  21.7 us (24%)
  local copies, waits for them, and re-layouts  5.24 us (6%)
  loops' own time  2.48 us (3%)
  between operations  2.11 us (2%)
    ppermute x8, waiting for transfers between devices, pair(): lax.ppermute(value, axis, [(i, i ^ k) for i in range(lax.axis_size(axis))])  19.7 us
    ppermute x8, starting transfers between devices, pair(): lax.ppermute(value, axis, [(i, i ^ k) for i in range(lax.axis_size(axis))])  14.3 us
    ppermute x12, starting transfers between devices, send(): return lax.ppermute(value, 'blk', perm)  14.1 us
    ppermute x12, waiting for transfers between devices, send(): return lax.ppermute(value, 'blk', perm)  11.5 us
    pallas_call x1, Pallas kernels, near_part(): pl.pallas_call(near_kernel, out_shape=(shape((rows, width), F32), shape((...  8.16 us
    pallas_call x2, Pallas kernels, end_part(): pl.pallas_call(end_kernel, out_shape=(jax.ShapeDtypeStruct((rows, width),...  6.11 us
    unnamed x14, local copies, waits for them, and re-layouts  4.65 us
    pallas_call x1, Pallas kernels, far_grad_part(): pl.pallas_call(far_grad_kernel, out_shape=(shape((rows, width), BF16), sh...  3.09 us
  transfers between devices with their start and end apart: 20, of which 10 were waited for; matrix products, arithmetic and copies ran while one was open for 0% of the time, Pallas kernels for 14%

profile of v5, /device:TPU:32, one launch (start us, length us, event | category | flops | bytes accessed | tf_op | source)
XLA Modules:
  0.0 91.1 jit_solution(8962659717688075265)
XLA Ops:
  0.6 0.0 copy-start
  0.6 1.3 %copy-done = f32[256,1152]{1,0:T(8,128)S(1)} copy-done((f32[256,1152]{1,0:T(8,128)S(1)}, f32[256,1152]{1,0:T(8,128)}, u32[]{:S(2)}) %copy-start) | copy-done | bytes 1179672
  1.9 0.2 normalize.2
  2.1 1.1 %copy-done.2 = f32[256,1152]{1,0:T(8,128)S(1)} copy-done((f32[256,1152]{1,0:T(8,128)S(1)}, f32[256,1152]{1,0:T(8,128)}, u32[]{:S(2)}) %copy-start.2) | copy-done | bytes 1179672
  3.2 0.7 normalize.3
  3.9 1.6 %collective-permute-start.9 = (bf16[256,1152]{1,0:T(8,128)(2,1)S(1)}, bf16[256,1152]{1,0:T(8,128)(2,1)}, u32[]{:S(2)}, u32[]{:S(2)}) collective-permute-start(bf16[256,1152]{1,0:T(8,128)(2,1)S(1)} %get-tuple-element.44.own_t), channel_id=1, source_target_pairs={{0,32},{16,48},{32,0},{48,16},{64,96},{80,112},{96,64},{112,80},{1... | collective-permute-start | bytes 1769480 | tf_op jit(solution)/shard_map/ppermute | solution.py:374
  5.5 1.5 %collective-permute-start.6 = (bf16[256,1152]{1,0:T(8,128)(2,1)S(1)}, bf16[256,1152]{1,0:T(8,128)(2,1)S(1)}, u32[]{:S(2)}, u32[]{:S(2)}) collective-permute-start(bf16[256,1152]{1,0:T(8,128)(2,1)S(1)} %get-tuple-element.42.own_i), channel_id=1, source_target_pairs={{0,64},{16,80},{32,96},{48,112},{64,128},{80,144},{96,160},{112,17... | collective-permute-start | bytes 1769480 | tf_op jit(solution)/shard_map/ppermute | solution.py:374
  6.9 1.7 %collective-permute-start.7 = (bf16[256,1152]{1,0:T(8,128)(2,1)S(1)}, bf16[256,1152]{1,0:T(8,128)(2,1)S(1)}, u32[]{:S(2)}, u32[]{:S(2)}) collective-permute-start(bf16[256,1152]{1,0:T(8,128)(2,1)S(1)} %get-tuple-element.42.own_i), channel_id=1, source_target_pairs={{0,192},{16,208},{32,224},{48,240},{64,0},{80,16},{96,32},{112,48}... | collective-permute-start | bytes 1769480 | tf_op jit(solution)/shard_map/ppermute | solution.py:374
  8.7 0.0 collective-permute-start.8
  8.7 10.4 %collective-permute-done.9.y_t = bf16[256,1152]{1,0:T(8,128)(2,1)} collective-permute-done((bf16[256,1152]{1,0:T(8,128)(2,1)S(1)}, bf16[256,1152]{1,0:T(8,128)(2,1)}, u32[]{:S(2)}, u32[]{:S(2)}) %collective-permute-start.9) | collective-permute-done | bytes 589856 | tf_op jit(solution)/shard_map/ppermute | solution.py:374
  19.1 0.0 collective-permute-start.10
  20.4 1.1 %collective-permute-done.6.left_i.block_ref = bf16[256,1152]{1,0:T(8,128)(2,1)S(1)} collective-permute-done((bf16[256,1152]{1,0:T(8,128)(2,1)S(1)}, bf16[256,1152]{1,0:T(8,128)(2,1)S(1)}, u32[]{:S(2)}, u32[]{:S(2)}) %collective-permute-start.6) | collective-permute-done | bytes 589856 | tf_op jit(solution)/shard_map/ppermute | solution.py:374
  21.5 0.5 collective-permute-start.11
  22.0 0.0 collective-permute-done.7.right_i.block_ref
  22.0 3.1 %collective-permute-start.12 = (bf16[128,1152]{1,0:T(8,128)(2,1)S(1)}, bf16[128,1152]{1,0:T(8,128)(2,1)S(1)}, u32[]{:S(2)}, u32[]{:S(2)}) collective-permute-start(bf16[128,1152]{1,0:T(8,128)(2,1)S(1)} %cut.3), channel_id=1, source_target_pairs={{0,192},{16,208},{32,224},{48,240},{64,0},{80,16},{96,32},{112,48}... | collective-permute-start | bytes 884744 | tf_op jit(solution)/shard_map/ppermute | solution.py:374
  25.1 0.0 collective-permute-done.8.core_t
  25.1 8.2 %near.1 = (f32[256,1152]{1,0:T(8,128)S(1)}, bf16[256,1152]{1,0:T(8,128)(2,1)}, bf16[256,1152]{1,0:T(8,128)(2,1)}, bf16[768,1152]{1,0:T(8,128)(2,1)S(1)}, bf16[10...) custom-call(f32[1]{0:T(128)} %bitcast.6.log_scale, f32[1]{0:T(128)} %bitcast.10.bias, ...), custom_call_target="tpu_custom_call" | custom-call | flops 28991029248 | bytes 7077888 | tf_op jit(solution)/shard_map/near/pallas_call | solution.py:196
  33.3 0.0 copy-start.3
  33.3 1.5 %far.1 = (bf16[256,1152]{1,0:T(8,128)(2,1)S(1)}, bf16[256,1024]{1,0:T(8,128)(2,1)S(1)}, f32[8,128]{1,0:T(8,128)S(1)}) custom-call(f32[1]{0:T(128)} %bitcast.7.log_scale, f32[1]{0:T(128)} %bitcast.11.bias, bf16[128,1152]{1,0:T(8,128)(2,1)S(1)} %collective-permute-done.11.top_i, bf16[128,1152]{1,0:T(8,128)(2,1)S(1)} %collective-permute-done.12.bot_i, ...), custom_call_target="tpu_custom_call" | custom-call | flops 75497472 | bytes 589824 | tf_op jit(solution)/shard_map/far/pallas_call | solution.py:224
  34.9 3.1 %far_grad.1 = (bf16[256,1152]{1,0:T(8,128)(2,1)}, f32[256,1152]{1,0:T(8,128)S(1)}, bf16[512,1152]{1,0:T(8,128)(2,1)S(1)}) custom-call(bf16[256,1152]{1,0:T(8,128)(2,1)S(1)} %get-tuple-element.50.far_images, bf16[256,1024]{1,0:T(8,128)(2,1)S(1)} %get-tuple-element.48.far_grads, bf16[768,1152]{1,0:T(8,128)(2,1)S(1)} %get-tuple-element.49.near_images, ...), custom_call_target="tpu_custom_call" | custom-call | flops 75497472 | bytes 589824 | tf_op jit(solution)/shard_map/far_grad/pallas_call | solution.py:242
  37.9 0.9 collective-permute-start.19
  38.8 1.1 %collective-permute-start.17 = (bf16[256,1152]{1,0:T(8,128)(2,1)}, bf16[256,1152]{1,0:T(8,128)(2,1)}, u32[]{:S(2)}, u32[]{:S(2)}) collective-permute-start(bf16[256,1152]{1,0:T(8,128)(2,1)} %get-tuple-element.58), channel_id=1, source_target_pairs={{0,64},{16,80},{32,96},{48,112},{64,128},{80,144},{96,160},{112,17... | collective-permute-start | bytes 1769480 | tf_op jit(solution)/shard_map/ppermute | solution.py:374
  39.9 2.2 %collective-permute-start.18 = (bf16[256,1152]{1,0:T(8,128)(2,1)}, bf16[256,1152]{1,0:T(8,128)(2,1)}, u32[]{:S(2)}, u32[]{:S(2)}) collective-permute-start(bf16[256,1152]{1,0:T(8,128)(2,1)} %get-tuple-element.59), channel_id=1, source_target_pairs={{0,192},{16,208},{32,224},{48,240},{64,0},{80,16},{96,32},{112,48}... | collective-permute-start | bytes 1769480 | tf_op jit(solution)/shard_map/ppermute | solution.py:374
  42.1 1.2 %collective-permute-done.14.refs_1_ = f32[8,128]{1,0:T(8,128)S(1)} collective-permute-done((f32[8,128]{1,0:T(8,128)S(1)}, f32[8,128]{1,0:T(8,128)S(1)}, u32[]{:S(2)}, u32[]{:S(2)}) %collective-permute-start.14) | collective-permute-done | bytes 4128 | tf_op jit(solution)/shard_map/ppermute | solution.py:395
  43.2 1.6 %collective-permute-start.15 = (f32[8,128]{1,0:T(8,128)S(1)}, f32[8,128]{1,0:T(8,128)S(1)}, u32[]{:S(2)}, u32[]{:S(2)}) collective-permute-start(f32[8,128]{1,0:T(8,128)S(1)} %add.33.sums), channel_id=1, source_target_pairs={{0,32},{16,48},{32,0},{48,16},{64,96},{80,112},{96,64},{112,80},{1... | collective-permute-start | bytes 12296 | tf_op jit(solution)/shard_map/ppermute | solution.py:395
  44.8 2.0 %collective-permute-done.15.arrived = f32[8,128]{1,0:T(8,128)S(1)} collective-permute-done((f32[8,128]{1,0:T(8,128)S(1)}, f32[8,128]{1,0:T(8,128)S(1)}, u32[]{:S(2)}, u32[]{:S(2)}) %collective-permute-start.15) | collective-permute-done | bytes 4128 | tf_op jit(solution)/shard_map/ppermute | solution.py:395
  46.8 1.0 %relay_y.1 = (bf16[256,1152]{1,0:T(8,128)(2,1)}, f32[8,128]{1,0:T(8,128)S(1)}) custom-call(f32[256,1152]{1,0:T(8,128)S(1)} %get-tuple-element.51.own, bf16[512,1152]{1,0:T(8,128)(2,1)S(1)} %collective-permute-done.13.passing.refs_1_, f32[8,128]{1,0:T(8,128)S(1)} %add.33.sums, f32[8,128]{1,0:T(8,128)S(1)} %collective-permute-done.15.arrived), custom_call_target="tpu_custom_call" | custom-call | flops 294912 | bytes 294912 | tf_op jit(solution)/shard_map/relay_y/pallas_call | solution.py:298
  47.8 1.6 %collective-permute-start.16 = (bf16[256,1152]{1,0:T(8,128)(2,1)}, bf16[256,1152]{1,0:T(8,128)(2,1)}, u32[]{:S(2)}, u32[]{:S(2)}) collective-permute-start(bf16[256,1152]{1,0:T(8,128)(2,1)} %get-tuple-element.56), channel_id=1, source_target_pairs={{0,32},{16,48},{32,0},{48,16},{64,96},{80,112},{96,64},{112,80},{1... | collective-permute-start | bytes 1769480 | tf_op jit(solution)/shard_map/ppermute | solution.py:374
  49.4 0.9 text.1
  50.3 0.0 copy-start.5
  50.3 1.0 %copy-done.5 = f32[256,1152]{1,0:T(8,128)} copy-done((f32[256,1152]{1,0:T(8,128)}, f32[256,1152]{1,0:T(8,128)S(1)}, u32[]{:S(2)}) %copy-start.5) | copy-done | bytes 1179672
  51.3 31.7 %while.10 = (s32[]{:T(128)}, f32[8,128]{1,0:T(8,128)S(1)}, s32[]{:T(128)}) while((s32[]{:T(128)}, f32[8,128]{1,0:T(8,128)S(1)}, s32[]{:T(128)}) %tuple.24), condition=%wide.region_1.0_spmd, body=%wide.region_0.0_spmd.sunk | while | flops 6146 | bytes 172317 | solution.py:411
  51.9 0.2 collective-permute-start
  52.1 3.5 %collective-permute-done = f32[8,128]{1,0:T(8,128)S(1)} collective-permute-done((f32[8,128]{1,0:T(8,128)S(1)}, f32[8,128]{1,0:T(8,128)S(1)}, u32[]{:S(2)}, u32[]{:S(2)}) %collective-permute-start) | collective-permute-done | bytes 4128 | tf_op jit(solution)/shard_map/while/body/ppermute | solution.py:395
  55.6 3.3 %collective-permute-start.1 = (f32[8,128]{1,0:T(8,128)S(1)}, f32[8,128]{1,0:T(8,128)S(1)}, u32[]{:S(2)}, u32[]{:S(2)}) collective-permute-start(f32[8,128]{1,0:T(8,128)S(1)} %add.27), channel_id=1, source_target_pairs={{0,2},{1,3},{2,0},{3,1},{4,6},{5,7},{6,4},{7,5},{8,10},{9,11},{10,... | collective-permute-start | bytes 12296 | tf_op jit(solution)/shard_map/while/body/ppermute | solution.py:395
  58.9 1.6 %collective-permute-done.1 = f32[8,128]{1,0:T(8,128)S(1)} collective-permute-done((f32[8,128]{1,0:T(8,128)S(1)}, f32[8,128]{1,0:T(8,128)S(1)}, u32[]{:S(2)}, u32[]{:S(2)}) %collective-permute-start.1) | collective-permute-done | bytes 4128 | tf_op jit(solution)/shard_map/while/body/ppermute | solution.py:395
  60.5 5.9 %collective-permute-start.2 = (f32[8,128]{1,0:T(8,128)S(1)}, f32[8,128]{1,0:T(8,128)S(1)}, u32[]{:S(2)}, u32[]{:S(2)}) collective-permute-start(f32[8,128]{1,0:T(8,128)S(1)} %add.28), channel_id=1, source_target_pairs={{0,4},{1,5},{2,6},{3,7},{4,0},{5,1},{6,2},{7,3},{8,12},{9,13},{10,... | collective-permute-start | bytes 12296 | tf_op jit(solution)/shard_map/while/body/ppermute | solution.py:395
  66.4 1.6 %collective-permute-done.2 = f32[8,128]{1,0:T(8,128)S(1)} collective-permute-done((f32[8,128]{1,0:T(8,128)S(1)}, f32[8,128]{1,0:T(8,128)S(1)}, u32[]{:S(2)}, u32[]{:S(2)}) %collective-permute-start.2) | collective-permute-done | bytes 4128 | tf_op jit(solution)/shard_map/while/body/ppermute | solution.py:395
  68.0 2.9 %collective-permute-start.3 = (f32[8,128]{1,0:T(8,128)S(1)}, f32[8,128]{1,0:T(8,128)S(1)}, u32[]{:S(2)}, u32[]{:S(2)}) collective-permute-start(f32[8,128]{1,0:T(8,128)S(1)} %add.29), channel_id=1, source_target_pairs={{0,8},{1,9},{2,10},{3,11},{4,12},{5,13},{6,14},{7,15},{8,0},{9,1},... | collective-permute-start | bytes 12296 | tf_op jit(solution)/shard_map/while/body/ppermute | solution.py:395
  70.9 2.2 %collective-permute-done.3 = f32[8,128]{1,0:T(8,128)S(1)} collective-permute-done((f32[8,128]{1,0:T(8,128)S(1)}, f32[8,128]{1,0:T(8,128)S(1)}, u32[]{:S(2)}, u32[]{:S(2)}) %collective-permute-start.3) | collective-permute-done | bytes 4128 | tf_op jit(solution)/shard_map/while/body/ppermute | solution.py:395
  73.2 3.6 %collective-permute-done.4 = f32[8,128]{1,0:T(8,128)S(1)} collective-permute-done((f32[8,128]{1,0:T(8,128)S(1)}, f32[8,128]{1,0:T(8,128)S(1)}, u32[]{:S(2)}, u32[]{:S(2)}) %collective-permute-start.4) | collective-permute-done | bytes 4128 | tf_op jit(solution)/shard_map/while/body/ppermute | solution.py:395
  76.8 0.4 collective-permute-start.5
  77.8 4.0 %collective-permute-done.5 = f32[8,128]{1,0:T(8,128)S(1)} collective-permute-done((f32[8,128]{1,0:T(8,128)S(1)}, f32[8,128]{1,0:T(8,128)S(1)}, u32[]{:S(2)}, u32[]{:S(2)}) %collective-permute-start.5) | collective-permute-done | bytes 4128 | tf_op jit(solution)/shard_map/while/body/ppermute | solution.py:395
  83.1 0.0 copy-start.4
  83.1 1.3 %copy-done.4 = f32[256,1152]{1,0:T(8,128)S(1)} copy-done((f32[256,1152]{1,0:T(8,128)S(1)}, f32[256,1152]{1,0:T(8,128)}, u32[]{:S(2)}) %copy-start.4) | copy-done | bytes 1179672
  84.4 3.0 %image_end.1 = (f32[256,1152]{1,0:T(8,128)}, f32[8,128]{1,0:T(8,128)S(1)}) custom-call(f32[1]{0:T(128)} %bitcast.8.log_scale, f32[256,1152]{1,0:T(8,128)S(1)} %copy-done.1, f32[256,1152]{1,0:T(8,128)S(1)} %copy-done.4, bf16[256,1152]{1,0:T(8,128)(2,1)} %collective-permute-done.17.refs_1_, bf16[256,1152]{1,0:T(8,128)(2,1)} %collective-permute-done.18.refs_2_, ...), custom_call_target="tpu_custom_call" | custom-call | flops 150994944 | bytes 294912 | tf_op jit(solution)/shard_map/image_end/pallas_call | solution.py:349
  87.4 3.1 %text_end.1 = (f32[256,1152]{1,0:T(8,128)}, f32[3]{0:T(128)S(1)}) custom-call(f32[1]{0:T(128)} %bitcast.9.log_scale, f32[256,1152]{1,0:T(8,128)S(1)} %copy-done.2, f32[256,1152]{1,0:T(8,128)S(1)} %copy-done.6, bf16[512,1152]{1,0:T(8,128)(2,1)S(1)} %collective-permute-done.13.passing.refs_1_, bf16[256,1152]{1,0:T(8,128)(2,1)} %collective-permute-done.16.refs_2_, ...), custom_call_target="tpu_custom_call" | custom-call | flops 2359296 | bytes 294912 | tf_op jit(solution)/shard_map/text_end/pallas_call | solution.py:349
  90.5 0.6 fusion
  (27 shorter events, 0.1 us)
Async XLA Ops:
  0.6 1.3 %copy-start = (f32[256,1152]{1,0:T(8,128)S(1)}, f32[256,1152]{1,0:T(8,128)}, u32[]{:S(2)}) copy-start(f32[256,1152]{1,0:T(8,128)} %emb.2) | copy-start | bytes 3538948
  1.9 1.3 %copy-start.2 = (f32[256,1152]{1,0:T(8,128)S(1)}, f32[256,1152]{1,0:T(8,128)}, u32[]{:S(2)}) copy-start(f32[256,1152]{1,0:T(8,128)} %emb.3) | copy-start | bytes 3538948
  3.9 15.2 %collective-permute-start.9 = (bf16[256,1152]{1,0:T(8,128)(2,1)S(1)}, bf16[256,1152]{1,0:T(8,128)(2,1)}, u32[]{:S(2)}, u32[]{:S(2)}) collective-permute-start(bf16[256,1152]{1,0:T(8,128)(2,1)S(1)} %get-tuple-element.44.own_t), channel_id=1, source_target_pairs={{0,32},{16,48},{32,0},{48,16},{64,96},{80,112},{96,64},{112,80},{1... | collective-permute-start | bytes 1769480 | tf_op jit(solution)/shard_map/ppermute | solution.py:374
  5.5 16.0 %collective-permute-start.6 = (bf16[256,1152]{1,0:T(8,128)(2,1)S(1)}, bf16[256,1152]{1,0:T(8,128)(2,1)S(1)}, u32[]{:S(2)}, u32[]{:S(2)}) collective-permute-start(bf16[256,1152]{1,0:T(8,128)(2,1)S(1)} %get-tuple-element.42.own_i), channel_id=1, source_target_pairs={{0,64},{16,80},{32,96},{48,112},{64,128},{80,144},{96,160},{112,17... | collective-permute-start | bytes 1769480 | tf_op jit(solution)/shard_map/ppermute | solution.py:374
  6.9 15.0 %collective-permute-start.7 = (bf16[256,1152]{1,0:T(8,128)(2,1)S(1)}, bf16[256,1152]{1,0:T(8,128)(2,1)S(1)}, u32[]{:S(2)}, u32[]{:S(2)}) collective-permute-start(bf16[256,1152]{1,0:T(8,128)(2,1)S(1)} %get-tuple-element.42.own_i), channel_id=1, source_target_pairs={{0,192},{16,208},{32,224},{48,240},{64,0},{80,16},{96,32},{112,48}... | collective-permute-start | bytes 1769480 | tf_op jit(solution)/shard_map/ppermute | solution.py:374
  8.7 16.4 %collective-permute-start.8 = (bf16[256,1152]{1,0:T(8,128)(2,1)S(1)}, bf16[256,1152]{1,0:T(8,128)(2,1)}, u32[]{:S(2)}, u32[]{:S(2)}) collective-permute-start(bf16[256,1152]{1,0:T(8,128)(2,1)S(1)} %get-tuple-element.44.own_t), channel_id=1, source_target_pairs={{0,16},{16,0},{32,48},{48,32},{64,80},{80,64},{96,112},{112,96},{1... | collective-permute-start | bytes 1769480 | tf_op jit(solution)/shard_map/ppermute | solution.py:374
  19.1 6.0 %collective-permute-start.10 = (bf16[256,1152]{1,0:T(8,128)(2,1)}, bf16[256,1152]{1,0:T(8,128)(2,1)}, u32[]{:S(2)}, u32[]{:S(2)}) collective-permute-start(bf16[256,1152]{1,0:T(8,128)(2,1)} %collective-permute-done.9.y_t), channel_id=1, source_target_pairs={{0,16},{16,0},{32,48},{48,32},{64,80},{80,64},{96,112},{112,96},{1... | collective-permute-start | bytes 1769480 | tf_op jit(solution)/shard_map/ppermute | solution.py:374
  21.5 11.8 %collective-permute-start.11 = (bf16[128,1152]{1,0:T(8,128)(2,1)S(1)}, bf16[128,1152]{1,0:T(8,128)(2,1)S(1)}, u32[]{:S(2)}, u32[]{:S(2)}) collective-permute-start(bf16[128,1152]{1,0:T(8,128)(2,1)S(1)} %cut.2), channel_id=1, source_target_pairs={{0,64},{16,80},{32,96},{48,112},{64,128},{80,144},{96,160},{112,17... | collective-permute-start | bytes 884744 | tf_op jit(solution)/shard_map/ppermute | solution.py:374
  22.0 11.3 %collective-permute-start.12 = (bf16[128,1152]{1,0:T(8,128)(2,1)S(1)}, bf16[128,1152]{1,0:T(8,128)(2,1)S(1)}, u32[]{:S(2)}, u32[]{:S(2)}) collective-permute-start(bf16[128,1152]{1,0:T(8,128)(2,1)S(1)} %cut.3), channel_id=1, source_target_pairs={{0,192},{16,208},{32,224},{48,240},{64,0},{80,16},{96,32},{112,48}... | collective-permute-start | bytes 884744 | tf_op jit(solution)/shard_map/ppermute | solution.py:374
  33.3 1.6 %copy-start.3 = (f32[256,1152]{1,0:T(8,128)}, f32[256,1152]{1,0:T(8,128)S(1)}, u32[]{:S(2)}) copy-start(f32[256,1152]{1,0:T(8,128)S(1)} %get-tuple-element.57.refs_0_) | copy-start | bytes 3538948
  37.9 8.9 %collective-permute-start.13 = (bf16[512,1152]{1,0:T(8,128)(2,1)S(1)}, bf16[512,1152]{1,0:T(8,128)(2,1)S(1)}, u32[]{:S(2)}, u32[]{:S(2)}) collective-permute-start(bf16[512,1152]{1,0:T(8,128)(2,1)S(1)} %get-tuple-element.52), channel_id=1, source_target_pairs={{0,16},{16,0},{32,48},{48,32},{64,80},{80,64},{96,112},{112,96},{1... | collective-permute-start | bytes 3538952 | tf_op jit(solution)/shard_map/ppermute | solution.py:374
  37.9 45.1 %collective-permute-start.19 = (bf16[256,1152]{1,0:T(8,128)(2,1)}, bf16[256,1152]{1,0:T(8,128)(2,1)}, u32[]{:S(2)}, u32[]{:S(2)}) collective-permute-start(bf16[256,1152]{1,0:T(8,128)(2,1)} %get-tuple-element.60), channel_id=1, source_target_pairs={{0,128},{16,144},{32,160},{48,176},{64,192},{80,208},{96,224},{112... | collective-permute-start | bytes 1769480 | tf_op jit(solution)/shard_map/ppermute | solution.py:374
  38.8 44.2 %collective-permute-start.17 = (bf16[256,1152]{1,0:T(8,128)(2,1)}, bf16[256,1152]{1,0:T(8,128)(2,1)}, u32[]{:S(2)}, u32[]{:S(2)}) collective-permute-start(bf16[256,1152]{1,0:T(8,128)(2,1)} %get-tuple-element.58), channel_id=1, source_target_pairs={{0,64},{16,80},{32,96},{48,112},{64,128},{80,144},{96,160},{112,17... | collective-permute-start | bytes 1769480 | tf_op jit(solution)/shard_map/ppermute | solution.py:374
  39.9 43.2 %collective-permute-start.18 = (bf16[256,1152]{1,0:T(8,128)(2,1)}, bf16[256,1152]{1,0:T(8,128)(2,1)}, u32[]{:S(2)}, u32[]{:S(2)}) collective-permute-start(bf16[256,1152]{1,0:T(8,128)(2,1)} %get-tuple-element.59), channel_id=1, source_target_pairs={{0,192},{16,208},{32,224},{48,240},{64,0},{80,16},{96,32},{112,48}... | collective-permute-start | bytes 1769480 | tf_op jit(solution)/shard_map/ppermute | solution.py:374
  42.1 1.2 %collective-permute-start.14 = (f32[8,128]{1,0:T(8,128)S(1)}, f32[8,128]{1,0:T(8,128)S(1)}, u32[]{:S(2)}, u32[]{:S(2)}) collective-permute-start(f32[8,128]{1,0:T(8,128)S(1)} %get-tuple-element.53.refs_0_), channel_id=1, source_target_pairs={{0,16},{16,0},{32,48},{48,32},{64,80},{80,64},{96,112},{112,96},{1... | collective-permute-start | bytes 12296 | tf_op jit(solution)/shard_map/ppermute | solution.py:395
  43.2 3.6 %collective-permute-start.15 = (f32[8,128]{1,0:T(8,128)S(1)}, f32[8,128]{1,0:T(8,128)S(1)}, u32[]{:S(2)}, u32[]{:S(2)}) collective-permute-start(f32[8,128]{1,0:T(8,128)S(1)} %add.33.sums), channel_id=1, source_target_pairs={{0,32},{16,48},{32,0},{48,16},{64,96},{80,112},{96,64},{112,80},{1... | collective-permute-start | bytes 12296 | tf_op jit(solution)/shard_map/ppermute | solution.py:395
  47.8 39.6 %collective-permute-start.16 = (bf16[256,1152]{1,0:T(8,128)(2,1)}, bf16[256,1152]{1,0:T(8,128)(2,1)}, u32[]{:S(2)}, u32[]{:S(2)}) collective-permute-start(bf16[256,1152]{1,0:T(8,128)(2,1)} %get-tuple-element.56), channel_id=1, source_target_pairs={{0,32},{16,48},{32,0},{48,16},{64,96},{80,112},{96,64},{112,80},{1... | collective-permute-start | bytes 1769480 | tf_op jit(solution)/shard_map/ppermute | solution.py:374
  49.4 33.7 %copy-start.1 = (f32[256,1152]{1,0:T(8,128)S(1)}, f32[256,1152]{1,0:T(8,128)}, u32[]{:S(2)}) copy-start(f32[256,1152]{1,0:T(8,128)} %emb.2) | copy-start | bytes 3538948
  50.3 1.0 %copy-start.5 = (f32[256,1152]{1,0:T(8,128)}, f32[256,1152]{1,0:T(8,128)S(1)}, u32[]{:S(2)}) copy-start(f32[256,1152]{1,0:T(8,128)S(1)} %get-tuple-element.55.refs_0_) | copy-start | bytes 3538948
  51.9 3.7 %collective-permute-start = (f32[8,128]{1,0:T(8,128)S(1)}, f32[8,128]{1,0:T(8,128)S(1)}, u32[]{:S(2)}, u32[]{:S(2)}) collective-permute-start(f32[8,128]{1,0:T(8,128)S(1)} %get-tuple-element.92), channel_id=1, source_target_pairs={{0,1},{1,0},{2,3},{3,2},{4,5},{5,4},{6,7},{7,6},{8,9},{9,8},{10,11... | collective-permute-start | bytes 12296 | tf_op jit(solution)/shard_map/while/body/ppermute | solution.py:395
  55.6 4.8 %collective-permute-start.1 = (f32[8,128]{1,0:T(8,128)S(1)}, f32[8,128]{1,0:T(8,128)S(1)}, u32[]{:S(2)}, u32[]{:S(2)}) collective-permute-start(f32[8,128]{1,0:T(8,128)S(1)} %add.27), channel_id=1, source_target_pairs={{0,2},{1,3},{2,0},{3,1},{4,6},{5,7},{6,4},{7,5},{8,10},{9,11},{10,... | collective-permute-start | bytes 12296 | tf_op jit(solution)/shard_map/while/body/ppermute | solution.py:395
  60.5 7.5 %collective-permute-start.2 = (f32[8,128]{1,0:T(8,128)S(1)}, f32[8,128]{1,0:T(8,128)S(1)}, u32[]{:S(2)}, u32[]{:S(2)}) collective-permute-start(f32[8,128]{1,0:T(8,128)S(1)} %add.28), channel_id=1, source_target_pairs={{0,4},{1,5},{2,6},{3,7},{4,0},{5,1},{6,2},{7,3},{8,12},{9,13},{10,... | collective-permute-start | bytes 12296 | tf_op jit(solution)/shard_map/while/body/ppermute | solution.py:395
  68.0 5.1 %collective-permute-start.3 = (f32[8,128]{1,0:T(8,128)S(1)}, f32[8,128]{1,0:T(8,128)S(1)}, u32[]{:S(2)}, u32[]{:S(2)}) collective-permute-start(f32[8,128]{1,0:T(8,128)S(1)} %add.29), channel_id=1, source_target_pairs={{0,8},{1,9},{2,10},{3,11},{4,12},{5,13},{6,14},{7,15},{8,0},{9,1},... | collective-permute-start | bytes 12296 | tf_op jit(solution)/shard_map/while/body/ppermute | solution.py:395
  73.1 3.6 %collective-permute-start.4 = (f32[8,128]{1,0:T(8,128)S(1)}, f32[8,128]{1,0:T(8,128)S(1)}, u32[]{:S(2)}, u32[]{:S(2)}) collective-permute-start(f32[8,128]{1,0:T(8,128)S(1)} %add.30), channel_id=1, source_target_pairs={{0,64},{16,80},{32,96},{48,112},{64,0},{80,16},{96,32},{112,48},{1... | collective-permute-start | bytes 12296 | tf_op jit(solution)/shard_map/while/body/ppermute | solution.py:395
  76.8 5.1 %collective-permute-start.5 = (f32[8,128]{1,0:T(8,128)S(1)}, f32[8,128]{1,0:T(8,128)S(1)}, u32[]{:S(2)}, u32[]{:S(2)}) collective-permute-start(f32[8,128]{1,0:T(8,128)S(1)} %add.31), channel_id=1, source_target_pairs={{0,128},{16,144},{32,160},{48,176},{64,192},{80,208},{96,224},{112... | collective-permute-start | bytes 12296 | tf_op jit(solution)/shard_map/while/body/ppermute | solution.py:395
  83.1 1.3 %copy-start.4 = (f32[256,1152]{1,0:T(8,128)S(1)}, f32[256,1152]{1,0:T(8,128)}, u32[]{:S(2)}) copy-start(f32[256,1152]{1,0:T(8,128)} %copy-done.3) | copy-start | bytes 3538948
  84.4 3.0 %copy-start.6 = (f32[256,1152]{1,0:T(8,128)S(1)}, f32[256,1152]{1,0:T(8,128)}, u32[]{:S(2)}) copy-start(f32[256,1152]{1,0:T(8,128)} %copy-done.5) | copy-start | bytes 3538948

commit v6 on v5

--- a/solution.py
+++ b/solution.py
@@ -7,9 +7,8 @@
 
 F32 = jnp.float32
 BATCH = 65536
-IMAGE_COST = 512
 TEXT_COST = 16
-STEPS = (("group", 1), ("group", 2), ("group", 4), ("group", 8), ("blk", 4), ("blk", 8))
+STEPS = (("group", 1), ("group", 2), ("group", 4), ("group", 8))
 BF16 = jnp.bfloat16
 HBM = pl.BlockSpec(memory_space=pltpu.HBM)
 VMEM = pl.BlockSpec(memory_space=pltpu.VMEM)
@@ -172,7 +171,7 @@
 
 
 def far_grad_kernel(
-    far_images, far_grads, near_images, texts, near_grads, far_out, y_out, mate_out
+    far_images, far_grads, near_images, texts, near_grads, sums, far_out, y_out, mate_out, sums_out
 ):
     rows = far_images.shape[0]
     far_out[...] = jnp.dot(
@@ -182,6 +181,7 @@
         out[...] = text_grad(
             near_grads, near_images, far_grads, far_images, pl.ds(t * rows, rows)
         ).astype(out.dtype)
+    sums_out[...] = sums[...]
 
 
 def text_kernel(near_grads, far_grads, near_images, far_images, sums, own_out, sums_out):
@@ -236,22 +236,23 @@
     )(*scalars, *far_images, texts, near_sums)
 
 
-def far_grad_part(far_images, far_grads, near_images, texts, near_grads):
+def far_grad_part(far_images, far_grads, near_images, texts, near_grads, sums):
     rows, width = far_images.shape
     shape = jax.ShapeDtypeStruct
     return pl.pallas_call(
         far_grad_kernel,
         out_shape=(
-            shape((rows, width), BF16), shape((rows, width), F32), shape((2 * rows, width), BF16)
-        ),
-        in_specs=[VMEM] * 5,
-        out_specs=(VMEM,) * 3,
+            shape((rows, width), BF16), shape((rows, width), F32), shape((2 * rows, width), BF16),
+            shape(sums.shape, F32),
+        ),
+        in_specs=[VMEM] * 6,
+        out_specs=(VMEM,) * 4,
         compiler_params=params(16),
         cost_estimate=pl.CostEstimate(
             flops=rows * rows * width, bytes_accessed=2 * rows * width, transcendentals=0
         ),
         name="far_grad",
-    )(far_images, far_grads, near_images, texts, near_grads)
+    )(far_images, far_grads, near_images, texts, near_grads, sums)
 
 
 def text_part(near_grads, far_grads, near_images, far_images, sums):
@@ -314,52 +315,71 @@
     return (scale * inverse) * (upstream - hat * along)
 
 
-def write_rows(out, values, slots, sems, i):
-    rows = values.shape[0]
-    at = pl.ds(i * rows, rows)
-    slots[at, :] = values
-    copy = pltpu.make_async_copy(slots.at[at], out.at[at], sems.at[i])
-    copy.start()
-    return copy
-
-
-def end_kernel(log_scale, emb, *refs):
-    *parts, sums, out, sums_out, slots, sems = refs
+def end_kernel(
+    log_scale, text_emb, own_q, from_core, from_y, image_emb, own_p, from_left, from_right, from_far,
+    sums, text_out, image_out, sums_out, text_slots, image_slots, sems,
+):
     scale = jnp.exp(jnp.full((1, 1), log_scale[0]))
-    step = emb.shape[0] // 4
+    step = text_emb.shape[0] // 4
+    sets = (
+        (text_emb, (own_q, from_core, from_y), text_out, text_slots),
+        (image_emb, (own_p, from_left, from_right, from_far), image_out, image_slots),
+    )
     copies = []
-    for i in range(4):
-        at = pl.ds(i * step, step)
-        upstream = parts[0][at, :]
-        for part in parts[1:]:
-            skip = part.shape[0] - 4 * step
-            upstream += part[pl.ds(skip + i * step, step), :].astype(F32)
-        copies.append(write_rows(out, backnorm(emb[at, :], upstream, scale), slots, sems, i))
-    if sums_out.shape == sums.shape:
-        sums_out[...] = sums[...]
-    else:
-        for i in range(3):
-            sums_out[i] = jnp.sum(sums[0:1, i : i + 1]) * (1.0 / BATCH)
+    for emb, parts, out, slots in sets:
+        for i in range(4):
+            at = pl.ds(i * step, step)
+            upstream = parts[0][at, :]
+            for part in parts[1:]:
+                skip = part.shape[0] - 4 * step
+                upstream += part[pl.ds(skip + i * step, step), :].astype(F32)
+            slots[at, :] = backnorm(emb[at, :], upstream, scale)
+            copy = pltpu.make_async_copy(slots.at[at], out.at[at], sems.at[len(copies)])
+            copy.start()
+            copies.append(copy)
+    sums_out[...] = sums[...]
     for copy in copies:
         copy.wait()
 
 
-def end_part(name, cost, sums_shape, log_scale, emb, *parts):
-    rows, width = emb.shape
+def end_part(log_scale, text_parts, image_parts, sums):
+    rows, width = text_parts[0].shape
+    shape = jax.ShapeDtypeStruct
     return pl.pallas_call(
         end_kernel,
-        out_shape=(
-            jax.ShapeDtypeStruct((rows, width), F32), jax.ShapeDtypeStruct(sums_shape, F32)
-        ),
-        in_specs=[SMEM] + [VMEM] * (1 + len(parts)),
-        out_specs=(HBM, VMEM if len(sums_shape) == 2 else SMEM),
-        scratch_shapes=[pltpu.VMEM((rows, width), F32), pltpu.SemaphoreType.DMA((4,))],
+        out_shape=(shape((rows, width), F32),) * 2 + (shape(sums.shape, F32),),
+        in_specs=[SMEM] + [VMEM] * 10,
+        out_specs=(HBM, HBM, VMEM),
+        scratch_shapes=[
+            pltpu.VMEM((rows, width), F32),
+            pltpu.VMEM((rows, width), F32),
+            pltpu.SemaphoreType.DMA((8,)),
+        ],
         compiler_params=params(24),
         cost_estimate=pl.CostEstimate(
-            flops=cost * rows * width, bytes_accessed=rows * width, transcendentals=rows
-        ),
-        name=name,
-    )(log_scale, emb, *parts)
+            flops=16 * rows * width, bytes_accessed=2 * rows * width, transcendentals=2 * rows
+        ),
+        name="end",
+    )(log_scale, *text_parts, *image_parts, sums)
+
+
+def totals_kernel(*refs):
+    *parts, out = refs
+    total = sum((part[...] for part in parts[1:]), parts[0][...])
+    for i in range(3):
+        out[i] = jnp.sum(total[0:1, i : i + 1]) * (1.0 / BATCH)
+
+
+def totals_part(*parts):
+    return pl.pallas_call(
+        totals_kernel,
+        out_shape=jax.ShapeDtypeStruct((3,), F32),
+        in_specs=[VMEM] * len(parts),
+        out_specs=SMEM,
+        compiler_params=params(16),
+        cost_estimate=pl.CostEstimate(flops=4096, bytes_accessed=4096, transcendentals=0),
+        name="totals",
+    )(*parts)
 
 
 def shards(image_emb, text_emb, log_scale, bias):
@@ -394,8 +414,11 @@
     def pair(value, axis, k):
         return lax.ppermute(value, axis, [(i, i ^ k) for i in range(lax.axis_size(axis))])
 
-    sums_1 = add(sums, pair(sums, "blk", 1))
-    far_p, y_q, to_mate = far_grad_part(far_images, far_grads, near_images, texts, near_grads)
+    over_core = pair(sums, "blk", 1)
+    far_p, y_q, to_mate, sums = far_grad_part(
+        far_images, far_grads, near_images, texts, near_grads, sums
+    )
+    sums_1 = add(sums, over_core)
     from_far = send(far_p, [(i, (i + 8) % blocks) for i in range(blocks)])
     from_core = send(to_mate, across_core)
     y_sum, sums_2 = relay_y(y_q, from_core, sums_1, pair(sums_1, "blk", 2))
@@ -408,14 +431,15 @@
             value = value + pair(value, axis, k)
         return left - 1, value
 
-    _, sums_8 = lax.while_loop(lambda carry: carry[0] > 0, steps, (passes[0], sums_2))
-    grad_image, sums_8 = end_part(
-        "image_end", IMAGE_COST, (8, 128), scalars[0], image_emb,
-        own_p, from_left, from_right, from_far, add(sums_8),
-    )
-    grad_text, totals = end_part(
-        "text_end", 8, (3,), scalars[0], text_emb, own_q, from_core, from_y, sums_8
-    )
+    _, sums_6 = lax.while_loop(lambda carry: carry[0] > 0, steps, (passes[0], sums_2))
+    over_x = [pair(sums_6, "blk", k) for k in (4, 8, 12)]
+    grad_text, grad_image, sums_6 = end_part(
+        scalars[0],
+        (text_emb, own_q, from_core, from_y),
+        (image_emb, own_p, from_left, from_right, from_far),
+        sums_6,
+    )
+    totals = totals_part(sums_6, *over_x)
     return (totals[0], grad_image, grad_text, totals[1], totals[2])
 
 

time: 92.1 us -> 85.6 us (0.929)
  waiting for transfers between devices: 31.2 us -> 22.6 us
  starting transfers between devices: 28.4 us -> 31.7 us
  Pallas kernels: 21.7 us -> 20.2 us
    ppermute x8 -> x9, waiting for transfers between devices: 19.7 us -> 10.6 us  [pair(): lax.ppermute(value, axis, [(i, i ^ k) for i in range(lax.axis_size(axis))])]
    ppermute x8 -> x9, starting transfers between devices: 14.3 us -> 19.2 us  [pair(): lax.ppermute(value, axis, [(i, i ^ k) for i in range(lax.axis_size(axis))])]
    ppermute x12, starting transfers between devices: 14.1 us -> 12.5 us  [send(): return lax.ppermute(value, 'blk', perm)]
    pallas_call x2, Pallas kernels: 6.11 us -> 4.58 us  [the longest x1 3.88 us: end_part(): pl.pallas_call(end_kernel, out_shape=(shape((rows, width), F32),) * 2 + (...]
  transfers between devices with their start and end apart: 20 -> 21, of which waited for: 10 -> 8; matrix products, arithmetic and copies ran while one was open for 0% -> 0% of each run, Pallas kernels for 14% -> 16%
where the time goes in v6:
time: 85.6 us; the launch traced here: 84.7 us
  starting transfers between devices  31.7 us (37%)
  waiting for transfers between devices  22.6 us (26%)
  Pallas kernels  20.2 us (24%)
  local copies, waits for them, and re-layouts  5.58 us (7%)
  loops' own time  2.47 us (3%)
  between operations  2.11 us (2%)
    ppermute x9, starting transfers between devices, pair(): lax.ppermute(value, axis, [(i, i ^ k) for i in range(lax.axis_size(axis))])  19.2 us
    ppermute x12, starting transfers between devices, send(): return lax.ppermute(value, 'blk', perm)  12.5 us
    ppermute x12, waiting for transfers between devices, send(): return lax.ppermute(value, 'blk', perm)  12 us
    ppermute x9, waiting for transfers between devices, pair(): lax.ppermute(value, axis, [(i, i ^ k) for i in range(lax.axis_size(axis))])  10.6 us
    pallas_call x1, Pallas kernels, near_part(): pl.pallas_call(near_kernel, out_shape=(shape((rows, width), F32), shape((...  8.18 us
    unnamed x14, local copies, waits for them, and re-layouts  4.99 us
    pallas_call x1, Pallas kernels, end_part(): pl.pallas_call(end_kernel, out_shape=(shape((rows, width), F32),) * 2 + (...  3.88 us
    pallas_call x1, Pallas kernels, far_grad_part(): pl.pallas_call(far_grad_kernel, out_shape=(shape((rows, width), BF16), sh...  3.14 us
  transfers between devices with their start and end apart: 21, of which 8 were waited for; matrix products, arithmetic and copies ran while one was open for 0% of the time, Pallas kernels for 16%

profile of v6, /device:TPU:32, one launch (start us, length us, event | category | flops | bytes accessed | tf_op | source)
XLA Modules:
  0.0 84.7 jit_solution(5547868150677477975)
XLA Ops:
  0.6 0.0 copy-start.1
  0.7 1.4 %copy-done.1 = f32[256,1152]{1,0:T(8,128)S(1)} copy-done((f32[256,1152]{1,0:T(8,128)S(1)}, f32[256,1152]{1,0:T(8,128)}, u32[]{:S(2)}) %copy-start.1) | copy-done | bytes 1179672
  2.0 0.2 normalize.2
  2.2 0.1 copy-done
  2.3 0.7 normalize.3
  3.0 1.6 %collective-permute-start.7 = (bf16[256,1152]{1,0:T(8,128)(2,1)S(1)}, bf16[256,1152]{1,0:T(8,128)(2,1)}, u32[]{:S(2)}, u32[]{:S(2)}) collective-permute-start(bf16[256,1152]{1,0:T(8,128)(2,1)S(1)} %get-tuple-element.44.own_t), channel_id=1, source_target_pairs={{0,32},{16,48},{32,0},{48,16},{64,96},{80,112},{96,64},{112,80},{1... | collective-permute-start | bytes 1769480 | tf_op jit(solution)/shard_map/ppermute | solution.py:394
  4.5 2.8 %collective-permute-start.5 = (bf16[256,1152]{1,0:T(8,128)(2,1)S(1)}, bf16[256,1152]{1,0:T(8,128)(2,1)S(1)}, u32[]{:S(2)}, u32[]{:S(2)}) collective-permute-start(bf16[256,1152]{1,0:T(8,128)(2,1)S(1)} %get-tuple-element.42.own_i), channel_id=1, source_target_pairs={{0,192},{16,208},{32,224},{48,240},{64,0},{80,16},{96,32},{112,48}... | collective-permute-start | bytes 1769480 | tf_op jit(solution)/shard_map/ppermute | solution.py:394
  7.3 0.0 collective-permute-start.4
  7.3 0.0 collective-permute-start.6
  7.3 10.8 %collective-permute-done.7.y_t = bf16[256,1152]{1,0:T(8,128)(2,1)} collective-permute-done((bf16[256,1152]{1,0:T(8,128)(2,1)S(1)}, bf16[256,1152]{1,0:T(8,128)(2,1)}, u32[]{:S(2)}, u32[]{:S(2)}) %collective-permute-start.7) | collective-permute-done | bytes 589856 | tf_op jit(solution)/shard_map/ppermute | solution.py:394
  19.4 0.2 collective-permute-done.5.right_i.block_ref
  19.6 3.8 %collective-permute-start.10 = (bf16[128,1152]{1,0:T(8,128)(2,1)S(1)}, bf16[128,1152]{1,0:T(8,128)(2,1)S(1)}, u32[]{:S(2)}, u32[]{:S(2)}) collective-permute-start(bf16[128,1152]{1,0:T(8,128)(2,1)S(1)} %cut.3), channel_id=1, source_target_pairs={{0,192},{16,208},{32,224},{48,240},{64,0},{80,16},{96,32},{112,48}... | collective-permute-start | bytes 884744 | tf_op jit(solution)/shard_map/ppermute | solution.py:394
  23.4 0.0 collective-permute-done.4.left_i.block_ref
  23.4 0.3 collective-permute-start.9
  23.7 8.2 %near.1 = (f32[256,1152]{1,0:T(8,128)S(1)}, bf16[256,1152]{1,0:T(8,128)(2,1)}, bf16[256,1152]{1,0:T(8,128)(2,1)}, bf16[768,1152]{1,0:T(8,128)(2,1)S(1)}, bf16[10...) custom-call(f32[1]{0:T(128)} %bitcast.6.log_scale, f32[1]{0:T(128)} %bitcast.9.bias, ...), custom_call_target="tpu_custom_call" | custom-call | flops 28991029248 | bytes 7077888 | tf_op jit(solution)/shard_map/near/pallas_call | solution.py:196
  31.9 0.0 copy-start.3
  31.9 1.0 %collective-permute-done.9.top_i = bf16[128,1152]{1,0:T(8,128)(2,1)S(1)} collective-permute-done((bf16[128,1152]{1,0:T(8,128)(2,1)S(1)}, bf16[128,1152]{1,0:T(8,128)(2,1)S(1)}, u32[]{:S(2)}, u32[]{:S(2)}) %collective-permute-start.9) | collective-permute-done | bytes 294944 | tf_op jit(solution)/shard_map/ppermute | solution.py:394
  33.0 1.5 %far.1 = (bf16[256,1152]{1,0:T(8,128)(2,1)S(1)}, bf16[256,1024]{1,0:T(8,128)(2,1)S(1)}, f32[8,128]{1,0:T(8,128)S(1)}) custom-call(f32[1]{0:T(128)} %bitcast.7.log_scale, f32[1]{0:T(128)} %bitcast.10.bias, bf16[128,1152]{1,0:T(8,128)(2,1)S(1)} %collective-permute-done.9.top_i, bf16[128,1152]{1,0:T(8,128)(2,1)S(1)} %collective-permute-done.10.bot_i, ...), custom_call_target="tpu_custom_call" | custom-call | flops 75497472 | bytes 589824 | tf_op jit(solution)/shard_map/far/pallas_call | solution.py:224
  34.5 3.1 %far_grad.1 = (bf16[256,1152]{1,0:T(8,128)(2,1)}, f32[256,1152]{1,0:T(8,128)S(1)}, bf16[512,1152]{1,0:T(8,128)(2,1)S(1)}, f32[8,128]{1,0:T(8,128)S(1)}) custom-call(bf16[256,1152]{1,0:T(8,128)(2,1)S(1)} %get-tuple-element.50.far_images, bf16[256,1024]{1,0:T(8,128)(2,1)S(1)} %get-tuple-element.48.far_grads, ...), custom_call_target="tpu_custom_call" | custom-call | flops 75497472 | bytes 589824 | tf_op jit(solution)/shard_map/far_grad/pallas_call | solution.py:242
  37.7 0.5 collective-permute-start.12
  38.2 2.3 %collective-permute-done.12.refs_1_ = f32[8,128]{1,0:T(8,128)S(1)} collective-permute-done((f32[8,128]{1,0:T(8,128)S(1)}, f32[8,128]{1,0:T(8,128)S(1)}, u32[]{:S(2)}, u32[]{:S(2)}) %collective-permute-start.12) | collective-permute-done | bytes 4128 | tf_op jit(solution)/shard_map/ppermute | solution.py:415
  40.5 1.6 %collective-permute-start.13 = (f32[8,128]{1,0:T(8,128)S(1)}, f32[8,128]{1,0:T(8,128)S(1)}, u32[]{:S(2)}, u32[]{:S(2)}) collective-permute-start(f32[8,128]{1,0:T(8,128)S(1)} %add.22.sums), channel_id=1, source_target_pairs={{0,32},{16,48},{32,0},{48,16},{64,96},{80,112},{96,64},{112,80},{1... | collective-permute-start | bytes 12296 | tf_op jit(solution)/shard_map/ppermute | solution.py:415
  42.1 0.2 collective-permute-start.17
  42.2 1.8 %collective-permute-start.15 = (bf16[256,1152]{1,0:T(8,128)(2,1)}, bf16[256,1152]{1,0:T(8,128)(2,1)}, u32[]{:S(2)}, u32[]{:S(2)}) collective-permute-start(bf16[256,1152]{1,0:T(8,128)(2,1)} %get-tuple-element.59), channel_id=1, source_target_pairs={{0,64},{16,80},{32,96},{48,112},{64,128},{80,144},{96,160},{112,17... | collective-permute-start | bytes 1769480 | tf_op jit(solution)/shard_map/ppermute | solution.py:394
  44.0 1.4 %collective-permute-start.16 = (bf16[256,1152]{1,0:T(8,128)(2,1)}, bf16[256,1152]{1,0:T(8,128)(2,1)}, u32[]{:S(2)}, u32[]{:S(2)}) collective-permute-start(bf16[256,1152]{1,0:T(8,128)(2,1)} %get-tuple-element.60), channel_id=1, source_target_pairs={{0,192},{16,208},{32,224},{48,240},{64,0},{80,16},{96,32},{112,48}... | collective-permute-start | bytes 1769480 | tf_op jit(solution)/shard_map/ppermute | solution.py:394
  45.5 1.0 %relay_y.1 = (bf16[256,1152]{1,0:T(8,128)(2,1)}, f32[8,128]{1,0:T(8,128)S(1)}) custom-call(f32[256,1152]{1,0:T(8,128)S(1)} %get-tuple-element.52.own, bf16[512,1152]{1,0:T(8,128)(2,1)S(1)} %collective-permute-done.11.passing.from_core, f32[8,128]{1,0:T(8,128)S(1)} %add.22.sums, f32[8,128]{1,0:T(8,128)S(1)} %collective-permute-done.13.arrived), custom_call_target="tpu_custom_call" | custom-call | flops 294912 | bytes 294912 | tf_op jit(solution)/shard_map/relay_y/pallas_call | solution.py:299
  46.5 0.7 collective-permute-start.14
  47.2 0.9 %text.1 = (f32[256,1152]{1,0:T(8,128)S(1)}, f32[8,128]{1,0:T(8,128)S(1)}) custom-call(bf16[768,1024]{1,0:T(8,128)(2,1)S(1)} %get-tuple-element.45.near_grads, bf16[256,1024]{1,0:T(8,128)(2,1)S(1)} %get-tuple-element.48.far_grads, bf16[768,1152]{1,0:T(8,128)(2,1)S(1)} %get-tuple-element.49.near_images, bf16[256,1152]{1,0:T(8,128)(2,1)S(1)} %get-tuple-element.50.far_images, ...), custom_call_target="tpu_custom_call" | custom-call | flops 1207959552 | bytes 294912 | tf_op jit(solution)/shard_map/text/pallas_call | solution.py:261
  48.1 0.0 copy-start.5
  48.1 1.0 %copy-done.5 = f32[256,1152]{1,0:T(8,128)} copy-done((f32[256,1152]{1,0:T(8,128)}, f32[256,1152]{1,0:T(8,128)S(1)}, u32[]{:S(2)}) %copy-start.5) | copy-done | bytes 1179672
  49.1 23.0 %while.10 = (s32[]{:T(128)}, f32[8,128]{1,0:T(8,128)S(1)}, s32[]{:T(128)}) while((s32[]{:T(128)}, f32[8,128]{1,0:T(8,128)S(1)}, s32[]{:T(128)}) %tuple.24), condition=%wide.region_1.0_spmd, body=%wide.region_0.0_spmd.sunk | while | flops 4098 | bytes 114893 | solution.py:434
  49.7 0.2 collective-permute-start
  49.9 3.5 %collective-permute-done = f32[8,128]{1,0:T(8,128)S(1)} collective-permute-done((f32[8,128]{1,0:T(8,128)S(1)}, f32[8,128]{1,0:T(8,128)S(1)}, u32[]{:S(2)}, u32[]{:S(2)}) %collective-permute-start) | collective-permute-done | bytes 4128 | tf_op jit(solution)/shard_map/while/body/ppermute | solution.py:415
  53.4 3.3 %collective-permute-start.1 = (f32[8,128]{1,0:T(8,128)S(1)}, f32[8,128]{1,0:T(8,128)S(1)}, u32[]{:S(2)}, u32[]{:S(2)}) collective-permute-start(f32[8,128]{1,0:T(8,128)S(1)} %add.18), channel_id=1, source_target_pairs={{0,2},{1,3},{2,0},{3,1},{4,6},{5,7},{6,4},{7,5},{8,10},{9,11},{10,... | collective-permute-start | bytes 12296 | tf_op jit(solution)/shard_map/while/body/ppermute | solution.py:415
  56.7 1.6 %collective-permute-done.1 = f32[8,128]{1,0:T(8,128)S(1)} collective-permute-done((f32[8,128]{1,0:T(8,128)S(1)}, f32[8,128]{1,0:T(8,128)S(1)}, u32[]{:S(2)}, u32[]{:S(2)}) %collective-permute-start.1) | collective-permute-done | bytes 4128 | tf_op jit(solution)/shard_map/while/body/ppermute | solution.py:415
  58.3 5.9 %collective-permute-start.2 = (f32[8,128]{1,0:T(8,128)S(1)}, f32[8,128]{1,0:T(8,128)S(1)}, u32[]{:S(2)}, u32[]{:S(2)}) collective-permute-start(f32[8,128]{1,0:T(8,128)S(1)} %add.19), channel_id=1, source_target_pairs={{0,4},{1,5},{2,6},{3,7},{4,0},{5,1},{6,2},{7,3},{8,12},{9,13},{10,... | collective-permute-start | bytes 12296 | tf_op jit(solution)/shard_map/while/body/ppermute | solution.py:415
  64.2 1.6 %collective-permute-done.2 = f32[8,128]{1,0:T(8,128)S(1)} collective-permute-done((f32[8,128]{1,0:T(8,128)S(1)}, f32[8,128]{1,0:T(8,128)S(1)}, u32[]{:S(2)}, u32[]{:S(2)}) %collective-permute-start.2) | collective-permute-done | bytes 4128 | tf_op jit(solution)/shard_map/while/body/ppermute | solution.py:415
  65.8 2.9 %collective-permute-start.3 = (f32[8,128]{1,0:T(8,128)S(1)}, f32[8,128]{1,0:T(8,128)S(1)}, u32[]{:S(2)}, u32[]{:S(2)}) collective-permute-start(f32[8,128]{1,0:T(8,128)S(1)} %add.20), channel_id=1, source_target_pairs={{0,8},{1,9},{2,10},{3,11},{4,12},{5,13},{6,14},{7,15},{8,0},{9,1},... | collective-permute-start | bytes 12296 | tf_op jit(solution)/shard_map/while/body/ppermute | solution.py:415
  69.4 1.5 %collective-permute-done.3 = f32[8,128]{1,0:T(8,128)S(1)} collective-permute-done((f32[8,128]{1,0:T(8,128)S(1)}, f32[8,128]{1,0:T(8,128)S(1)}, u32[]{:S(2)}, u32[]{:S(2)}) %collective-permute-start.3) | collective-permute-done | bytes 4128 | tf_op jit(solution)/shard_map/while/body/ppermute | solution.py:415
  72.1 1.5 %collective-permute-start.18 = (f32[8,128]{1,0:T(8,128)S(1)}, f32[8,128]{1,0:T(8,128)S(1)}, u32[]{:S(2)}, u32[]{:S(2)}) collective-permute-start(f32[8,128]{1,0:T(8,128)S(1)} %get-tuple-element.64.sums), channel_id=1, source_target_pairs={{0,64},{16,80},{32,96},{48,112},{64,0},{80,16},{96,32},{112,48},{1... | collective-permute-start | bytes 12296 | tf_op jit(solution)/shard_map/ppermute | solution.py:415
  73.6 0.6 collective-permute-start.19
  74.2 2.7 %collective-permute-start.20 = (f32[8,128]{1,0:T(8,128)S(1)}, f32[8,128]{1,0:T(8,128)S(1)}, u32[]{:S(2)}, u32[]{:S(2)}) collective-permute-start(f32[8,128]{1,0:T(8,128)S(1)} %get-tuple-element.64.sums), channel_id=1, source_target_pairs={{0,192},{16,208},{32,224},{48,240},{64,128},{80,144},{96,160},{112... | collective-permute-start | bytes 12296 | tf_op jit(solution)/shard_map/ppermute | solution.py:415
  76.9 0.0 copy-start.4
  76.9 1.3 %copy-done.4 = f32[256,1152]{1,0:T(8,128)S(1)} copy-done((f32[256,1152]{1,0:T(8,128)S(1)}, f32[256,1152]{1,0:T(8,128)}, u32[]{:S(2)}) %copy-start.4) | copy-done | bytes 1179672
  78.2 1.3 %copy-done.6 = f32[256,1152]{1,0:T(8,128)S(1)} copy-done((f32[256,1152]{1,0:T(8,128)S(1)}, f32[256,1152]{1,0:T(8,128)}, u32[]{:S(2)}) %copy-start.6) | copy-done | bytes 1179672
  79.5 3.9 %end.1 = (f32[256,1152]{1,0:T(8,128)}, f32[256,1152]{1,0:T(8,128)}, f32[8,128]{1,0:T(8,128)S(1)}) custom-call(f32[1]{0:T(128)} %bitcast.8.log_scale, f32[256,1152]{1,0:T(8,128)S(1)} %copy-done, f32[256,1152]{1,0:T(8,128)S(1)} %copy-done.6, bf16[512,1152]{1,0:T(8,128)(2,1)S(1)} %collective-permute-done.11.passing.from_core, ...), custom_call_target="tpu_custom_call" | custom-call | flops 4718592 | bytes 589824 | tf_op jit(solution)/shard_map/end/pallas_call | solution.py:348
  83.4 0.7 totals.1
  84.1 0.6 fusion
  (26 shorter events, 0.1 us)
Async XLA Ops:
  0.6 1.6 %copy-start = (f32[256,1152]{1,0:T(8,128)S(1)}, f32[256,1152]{1,0:T(8,128)}, u32[]{:S(2)}) copy-start(f32[256,1152]{1,0:T(8,128)} %text_emb.1) | copy-start | bytes 3538948
  0.6 1.4 %copy-start.1 = (f32[256,1152]{1,0:T(8,128)S(1)}, f32[256,1152]{1,0:T(8,128)}, u32[]{:S(2)}) copy-start(f32[256,1152]{1,0:T(8,128)} %image_emb.1) | copy-start | bytes 3538948
  3.0 15.2 %collective-permute-start.7 = (bf16[256,1152]{1,0:T(8,128)(2,1)S(1)}, bf16[256,1152]{1,0:T(8,128)(2,1)}, u32[]{:S(2)}, u32[]{:S(2)}) collective-permute-start(bf16[256,1152]{1,0:T(8,128)(2,1)S(1)} %get-tuple-element.44.own_t), channel_id=1, source_target_pairs={{0,32},{16,48},{32,0},{48,16},{64,96},{80,112},{96,64},{112,80},{1... | collective-permute-start | bytes 1769480 | tf_op jit(solution)/shard_map/ppermute | solution.py:394
  4.5 15.1 %collective-permute-start.5 = (bf16[256,1152]{1,0:T(8,128)(2,1)S(1)}, bf16[256,1152]{1,0:T(8,128)(2,1)S(1)}, u32[]{:S(2)}, u32[]{:S(2)}) collective-permute-start(bf16[256,1152]{1,0:T(8,128)(2,1)S(1)} %get-tuple-element.42.own_i), channel_id=1, source_target_pairs={{0,192},{16,208},{32,224},{48,240},{64,0},{80,16},{96,32},{112,48}... | collective-permute-start | bytes 1769480 | tf_op jit(solution)/shard_map/ppermute | solution.py:394
  7.3 16.1 %collective-permute-start.4 = (bf16[256,1152]{1,0:T(8,128)(2,1)S(1)}, bf16[256,1152]{1,0:T(8,128)(2,1)S(1)}, u32[]{:S(2)}, u32[]{:S(2)}) collective-permute-start(bf16[256,1152]{1,0:T(8,128)(2,1)S(1)} %get-tuple-element.42.own_i), channel_id=1, source_target_pairs={{0,64},{16,80},{32,96},{48,112},{64,128},{80,144},{96,160},{112,17... | collective-permute-start | bytes 1769480 | tf_op jit(solution)/shard_map/ppermute | solution.py:394
  7.3 16.4 %collective-permute-start.6 = (bf16[256,1152]{1,0:T(8,128)(2,1)S(1)}, bf16[256,1152]{1,0:T(8,128)(2,1)}, u32[]{:S(2)}, u32[]{:S(2)}) collective-permute-start(bf16[256,1152]{1,0:T(8,128)(2,1)S(1)} %get-tuple-element.44.own_t), channel_id=1, source_target_pairs={{0,16},{16,0},{32,48},{48,32},{64,80},{80,64},{96,112},{112,96},{1... | collective-permute-start | bytes 1769480 | tf_op jit(solution)/shard_map/ppermute | solution.py:394
  18.1 5.6 %collective-permute-start.8 = (bf16[256,1152]{1,0:T(8,128)(2,1)}, bf16[256,1152]{1,0:T(8,128)(2,1)}, u32[]{:S(2)}, u32[]{:S(2)}) collective-permute-start(bf16[256,1152]{1,0:T(8,128)(2,1)} %collective-permute-done.7.y_t), channel_id=1, source_target_pairs={{0,16},{16,0},{32,48},{48,32},{64,80},{80,64},{96,112},{112,96},{1... | collective-permute-start | bytes 1769480 | tf_op jit(solution)/shard_map/ppermute | solution.py:394
  19.6 12.3 %collective-permute-start.10 = (bf16[128,1152]{1,0:T(8,128)(2,1)S(1)}, bf16[128,1152]{1,0:T(8,128)(2,1)S(1)}, u32[]{:S(2)}, u32[]{:S(2)}) collective-permute-start(bf16[128,1152]{1,0:T(8,128)(2,1)S(1)} %cut.3), channel_id=1, source_target_pairs={{0,192},{16,208},{32,224},{48,240},{64,0},{80,16},{96,32},{112,48}... | collective-permute-start | bytes 884744 | tf_op jit(solution)/shard_map/ppermute | solution.py:394
  23.4 9.5 %collective-permute-start.9 = (bf16[128,1152]{1,0:T(8,128)(2,1)S(1)}, bf16[128,1152]{1,0:T(8,128)(2,1)S(1)}, u32[]{:S(2)}, u32[]{:S(2)}) collective-permute-start(bf16[128,1152]{1,0:T(8,128)(2,1)S(1)} %cut.2), channel_id=1, source_target_pairs={{0,64},{16,80},{32,96},{48,112},{64,128},{80,144},{96,160},{112,17... | collective-permute-start | bytes 884744 | tf_op jit(solution)/shard_map/ppermute | solution.py:394
  31.9 2.6 %copy-start.3 = (f32[256,1152]{1,0:T(8,128)}, f32[256,1152]{1,0:T(8,128)S(1)}, u32[]{:S(2)}) copy-start(f32[256,1152]{1,0:T(8,128)S(1)} %get-tuple-element.58.own_p) | copy-start | bytes 3538948
  37.7 7.8 %collective-permute-start.11 = (bf16[512,1152]{1,0:T(8,128)(2,1)S(1)}, bf16[512,1152]{1,0:T(8,128)(2,1)S(1)}, u32[]{:S(2)}, u32[]{:S(2)}) collective-permute-start(bf16[512,1152]{1,0:T(8,128)(2,1)S(1)} %get-tuple-element.53), channel_id=1, source_target_pairs={{0,16},{16,0},{32,48},{48,32},{64,80},{80,64},{96,112},{112,96},{1... | collective-permute-start | bytes 3538952 | tf_op jit(solution)/shard_map/ppermute | solution.py:394
  37.7 2.9 %collective-permute-start.12 = (f32[8,128]{1,0:T(8,128)S(1)}, f32[8,128]{1,0:T(8,128)S(1)}, u32[]{:S(2)}, u32[]{:S(2)}) collective-permute-start(f32[8,128]{1,0:T(8,128)S(1)} %get-tuple-element.51.sums), channel_id=1, source_target_pairs={{0,16},{16,0},{32,48},{48,32},{64,80},{80,64},{96,112},{112,96},{1... | collective-permute-start | bytes 12296 | tf_op jit(solution)/shard_map/ppermute | solution.py:415
  40.5 5.0 %collective-permute-start.13 = (f32[8,128]{1,0:T(8,128)S(1)}, f32[8,128]{1,0:T(8,128)S(1)}, u32[]{:S(2)}, u32[]{:S(2)}) collective-permute-start(f32[8,128]{1,0:T(8,128)S(1)} %add.22.sums), channel_id=1, source_target_pairs={{0,32},{16,48},{32,0},{48,16},{64,96},{80,112},{96,64},{112,80},{1... | collective-permute-start | bytes 12296 | tf_op jit(solution)/shard_map/ppermute | solution.py:415
  42.1 31.5 %collective-permute-start.17 = (bf16[256,1152]{1,0:T(8,128)(2,1)}, bf16[256,1152]{1,0:T(8,128)(2,1)}, u32[]{:S(2)}, u32[]{:S(2)}) collective-permute-start(bf16[256,1152]{1,0:T(8,128)(2,1)} %get-tuple-element.61), channel_id=1, source_target_pairs={{0,128},{16,144},{32,160},{48,176},{64,192},{80,208},{96,224},{112... | collective-permute-start | bytes 1769480 | tf_op jit(solution)/shard_map/ppermute | solution.py:394
  42.2 32.0 %collective-permute-start.15 = (bf16[256,1152]{1,0:T(8,128)(2,1)}, bf16[256,1152]{1,0:T(8,128)(2,1)}, u32[]{:S(2)}, u32[]{:S(2)}) collective-permute-start(bf16[256,1152]{1,0:T(8,128)(2,1)} %get-tuple-element.59), channel_id=1, source_target_pairs={{0,64},{16,80},{32,96},{48,112},{64,128},{80,144},{96,160},{112,17... | collective-permute-start | bytes 1769480 | tf_op jit(solution)/shard_map/ppermute | solution.py:394
  44.0 32.9 %collective-permute-start.16 = (bf16[256,1152]{1,0:T(8,128)(2,1)}, bf16[256,1152]{1,0:T(8,128)(2,1)}, u32[]{:S(2)}, u32[]{:S(2)}) collective-permute-start(bf16[256,1152]{1,0:T(8,128)(2,1)} %get-tuple-element.60), channel_id=1, source_target_pairs={{0,192},{16,208},{32,224},{48,240},{64,0},{80,16},{96,32},{112,48}... | collective-permute-start | bytes 1769480 | tf_op jit(solution)/shard_map/ppermute | solution.py:394
  46.5 30.5 %collective-permute-start.14 = (bf16[256,1152]{1,0:T(8,128)(2,1)}, bf16[256,1152]{1,0:T(8,128)(2,1)}, u32[]{:S(2)}, u32[]{:S(2)}) collective-permute-start(bf16[256,1152]{1,0:T(8,128)(2,1)} %get-tuple-element.57), channel_id=1, source_target_pairs={{0,32},{16,48},{32,0},{48,16},{64,96},{80,112},{96,64},{112,80},{1... | collective-permute-start | bytes 1769480 | tf_op jit(solution)/shard_map/ppermute | solution.py:394
  47.2 29.7 %copy-start.2 = (f32[256,1152]{1,0:T(8,128)S(1)}, f32[256,1152]{1,0:T(8,128)}, u32[]{:S(2)}) copy-start(f32[256,1152]{1,0:T(8,128)} %image_emb.1) | copy-start | bytes 3538948
  48.1 1.0 %copy-start.5 = (f32[256,1152]{1,0:T(8,128)}, f32[256,1152]{1,0:T(8,128)S(1)}, u32[]{:S(2)}) copy-start(f32[256,1152]{1,0:T(8,128)S(1)} %get-tuple-element.56.own_q) | copy-start | bytes 3538948
  49.7 3.7 %collective-permute-start = (f32[8,128]{1,0:T(8,128)S(1)}, f32[8,128]{1,0:T(8,128)S(1)}, u32[]{:S(2)}, u32[]{:S(2)}) collective-permute-start(f32[8,128]{1,0:T(8,128)S(1)} %get-tuple-element.92), channel_id=1, source_target_pairs={{0,1},{1,0},{2,3},{3,2},{4,5},{5,4},{6,7},{7,6},{8,9},{9,8},{10,11... | collective-permute-start | bytes 12296 | tf_op jit(solution)/shard_map/while/body/ppermute | solution.py:415
  53.4 4.8 %collective-permute-start.1 = (f32[8,128]{1,0:T(8,128)S(1)}, f32[8,128]{1,0:T(8,128)S(1)}, u32[]{:S(2)}, u32[]{:S(2)}) collective-permute-start(f32[8,128]{1,0:T(8,128)S(1)} %add.18), channel_id=1, source_target_pairs={{0,2},{1,3},{2,0},{3,1},{4,6},{5,7},{6,4},{7,5},{8,10},{9,11},{10,... | collective-permute-start | bytes 12296 | tf_op jit(solution)/shard_map/while/body/ppermute | solution.py:415
  58.3 7.5 %collective-permute-start.2 = (f32[8,128]{1,0:T(8,128)S(1)}, f32[8,128]{1,0:T(8,128)S(1)}, u32[]{:S(2)}, u32[]{:S(2)}) collective-permute-start(f32[8,128]{1,0:T(8,128)S(1)} %add.19), channel_id=1, source_target_pairs={{0,4},{1,5},{2,6},{3,7},{4,0},{5,1},{6,2},{7,3},{8,12},{9,13},{10,... | collective-permute-start | bytes 12296 | tf_op jit(solution)/shard_map/while/body/ppermute | solution.py:415
  65.8 5.1 %collective-permute-start.3 = (f32[8,128]{1,0:T(8,128)S(1)}, f32[8,128]{1,0:T(8,128)S(1)}, u32[]{:S(2)}, u32[]{:S(2)}) collective-permute-start(f32[8,128]{1,0:T(8,128)S(1)} %add.20), channel_id=1, source_target_pairs={{0,8},{1,9},{2,10},{3,11},{4,12},{5,13},{6,14},{7,15},{8,0},{9,1},... | collective-permute-start | bytes 12296 | tf_op jit(solution)/shard_map/while/body/ppermute | solution.py:415
  72.1 11.2 %collective-permute-start.18 = (f32[8,128]{1,0:T(8,128)S(1)}, f32[8,128]{1,0:T(8,128)S(1)}, u32[]{:S(2)}, u32[]{:S(2)}) collective-permute-start(f32[8,128]{1,0:T(8,128)S(1)} %get-tuple-element.64.sums), channel_id=1, source_target_pairs={{0,64},{16,80},{32,96},{48,112},{64,0},{80,16},{96,32},{112,48},{1... | collective-permute-start | bytes 12296 | tf_op jit(solution)/shard_map/ppermute | solution.py:415
  73.6 9.8 %collective-permute-start.19 = (f32[8,128]{1,0:T(8,128)S(1)}, f32[8,128]{1,0:T(8,128)S(1)}, u32[]{:S(2)}, u32[]{:S(2)}) collective-permute-start(f32[8,128]{1,0:T(8,128)S(1)} %get-tuple-element.64.sums), channel_id=1, source_target_pairs={{0,128},{16,144},{32,160},{48,176},{64,192},{80,208},{96,224},{112... | collective-permute-start | bytes 12296 | tf_op jit(solution)/shard_map/ppermute | solution.py:415
  74.2 9.1 %collective-permute-start.20 = (f32[8,128]{1,0:T(8,128)S(1)}, f32[8,128]{1,0:T(8,128)S(1)}, u32[]{:S(2)}, u32[]{:S(2)}) collective-permute-start(f32[8,128]{1,0:T(8,128)S(1)} %get-tuple-element.64.sums), channel_id=1, source_target_pairs={{0,192},{16,208},{32,224},{48,240},{64,128},{80,144},{96,160},{112... | collective-permute-start | bytes 12296 | tf_op jit(solution)/shard_map/ppermute | solution.py:415
  76.9 1.3 %copy-start.4 = (f32[256,1152]{1,0:T(8,128)S(1)}, f32[256,1152]{1,0:T(8,128)}, u32[]{:S(2)}) copy-start(f32[256,1152]{1,0:T(8,128)} %copy-done.3) | copy-start | bytes 3538948
  78.2 1.3 %copy-start.6 = (f32[256,1152]{1,0:T(8,128)S(1)}, f32[256,1152]{1,0:T(8,128)}, u32[]{:S(2)}) copy-start(f32[256,1152]{1,0:T(8,128)} %copy-done.5) | copy-start | bytes 3538948

commit v7 on v6

--- a/solution.py
+++ b/solution.py
@@ -6,8 +6,9 @@
 from jax.sharding import PartitionSpec as P
 
 F32 = jnp.float32
+LOG2E = 1.4426950408889634
 BATCH = 65536
-TEXT_COST = 16
+GATE_COST = 1
 STEPS = (("group", 1), ("group", 2), ("group", 4), ("group", 8))
 BF16 = jnp.bfloat16
 HBM = pl.BlockSpec(memory_space=pltpu.HBM)
@@ -71,22 +72,20 @@
 
 
 def pair_tile(sim, scale, bias, diagonal):
-    scaled = scale * sim
-    logits = scaled + bias
+    logits = sim * scale + bias
     rows, columns = sim.shape
     if diagonal:
         positive = lax.broadcasted_iota(jnp.int32, (rows, columns), 0) == (
             lax.broadcasted_iota(jnp.int32, (rows, columns), 1)
         )
         logits = jnp.where(positive, -logits, logits)
-    odds = jnp.exp(logits)
+    odds = jnp.exp2(logits)
     total = 1.0 + odds
     inverse = pl.reciprocal(total, approx=True)
     inverse = inverse * (2.0 - total * inverse)
     grad = odds * inverse
     if diagonal:
         grad = jnp.where(positive, -grad, grad)
-    lost = (odds - (total - 1.0)) * inverse
     part = rows // 8
     product = total[:part]
     for i in range(1, 8):
@@ -95,8 +94,12 @@
     def fold(values):
         return jnp.sum(values.reshape(values.shape[0] // 8, 8, columns), axis=0)
 
-    loss = fold(jnp.log(product)) + fold(lost)
-    return grad.astype(BF16), loss, fold(grad * scaled), fold(grad)
+    return grad.astype(BF16), fold(jnp.log(product)), fold(grad * sim), fold(grad)
+
+
+def logit_factors(log_scale, bias, columns):
+    scale = jnp.exp(jnp.full((1, columns), log_scale[0]))
+    return scale, scale * LOG2E, bias[0] * LOG2E
 
 
 def write_sums(sums_ref, loss, scaled, grad):
@@ -111,7 +114,7 @@
     own_out, left_out, right_out, images, texts, grads, sums_ref, passes_ref,
 ):
     rows = own_i.shape[0]
-    scale, bias = jnp.exp(jnp.full((1, rows), log_scale[0])), bias[0]
+    factor, scale, bias = logit_factors(log_scale, bias, rows)
     for i, src in enumerate((own_i, left_i, right_i)):
         images[pl.ds(i * rows, rows), :] = src[...]
     for i, src in enumerate((own_t, core_t, y_t, yc_t)):
@@ -136,7 +139,7 @@
             )
             out = (own_out, left_out, right_out)[b]
             out[...] = partial.astype(out.dtype)
-    write_sums(sums_ref, loss, scaled, grad)
+    write_sums(sums_ref, loss, scaled * factor, grad)
     passes_ref[0] = 1
 
 
@@ -151,7 +154,7 @@
 def far_kernel(log_scale, bias, top_i, bot_i, texts, near_sums, images, grads, sums_ref):
     half = top_i.shape[0]
     rows = 2 * half
-    scale, bias = jnp.exp(jnp.full((1, rows), log_scale[0])), bias[0]
+    factor, scale, bias = logit_factors(log_scale, bias, rows)
     images[pl.ds(0, half), :] = top_i[...]
     images[pl.ds(half, half), :] = bot_i[...]
     loss = scaled = grad = jnp.zeros((8, rows), F32)
@@ -166,37 +169,37 @@
         grads[:, pl.ds(t * rows, rows)] = grad_q
         loss, scaled, grad = loss + loss_now, scaled + scaled_now, grad + grad_now
         sim = sim_next
-    write_sums(sums_ref, loss, scaled, grad)
+    write_sums(sums_ref, loss, scaled * factor, grad)
     sums_ref[...] += near_sums[...]
 
 
 def far_grad_kernel(
-    far_images, far_grads, near_images, texts, near_grads, sums, far_out, y_out, mate_out, sums_out
+    far_images, far_grads, near_images, texts, near_grads, sums,
+    far_out, y_out, mate_out, own_out, sums_out,
 ):
     rows = far_images.shape[0]
     far_out[...] = jnp.dot(
         far_grads[...], texts[...], preferred_element_type=F32
     ).astype(BF16)
-    for t, out in ((3, mate_out.at[pl.ds(0, rows)]), (1, mate_out.at[pl.ds(rows, rows)]), (2, y_out)):
+    for t, out in (
+        (3, mate_out.at[pl.ds(0, rows)]),
+        (1, mate_out.at[pl.ds(rows, rows)]),
+        (2, y_out),
+        (0, own_out),
+    ):
         out[...] = text_grad(
             near_grads, near_images, far_grads, far_images, pl.ds(t * rows, rows)
         ).astype(out.dtype)
     sums_out[...] = sums[...]
 
 
-def text_kernel(near_grads, far_grads, near_images, far_images, sums, own_out, sums_out):
-    rows = far_images.shape[0]
-    own_out[...] = text_grad(near_grads, near_images, far_grads, far_images, pl.ds(0, rows))
-    sums_out[...] = sums[...]
-
-
 def near_part(scalars, images, texts):
     rows, width = texts[0].shape
     shape = jax.ShapeDtypeStruct
     return pl.pallas_call(
         near_kernel,
         out_shape=(
-            shape((rows, width), F32),
+            shape((rows, width), BF16),
             shape((rows, width), BF16),
             shape((rows, width), BF16),
             shape((3 * rows, width), BF16),
@@ -243,32 +246,16 @@
         far_grad_kernel,
         out_shape=(
             shape((rows, width), BF16), shape((rows, width), F32), shape((2 * rows, width), BF16),
-            shape(sums.shape, F32),
+            shape((rows, width), BF16), shape(sums.shape, F32),
         ),
         in_specs=[VMEM] * 6,
-        out_specs=(VMEM,) * 4,
+        out_specs=(VMEM,) * 5,
         compiler_params=params(16),
         cost_estimate=pl.CostEstimate(
             flops=rows * rows * width, bytes_accessed=2 * rows * width, transcendentals=0
         ),
         name="far_grad",
     )(far_images, far_grads, near_images, texts, near_grads, sums)
-
-
-def text_part(near_grads, far_grads, near_images, far_images, sums):
-    rows, width = far_images.shape
-    shape = jax.ShapeDtypeStruct
-    return pl.pallas_call(
-        text_kernel,
-        out_shape=(shape((rows, width), F32), shape(sums.shape, F32)),
-        in_specs=[VMEM] * 5,
-        out_specs=(VMEM,) * 2,
-        compiler_params=params(16),
-        cost_estimate=pl.CostEstimate(
-            flops=TEXT_COST * rows * rows * width, bytes_accessed=rows * width, transcendentals=0
-        ),
-        name="text",
-    )(near_grads, far_grads, near_images, far_images, sums)
 
 
 def add_kernel(*refs):
@@ -284,7 +271,9 @@
         in_specs=[VMEM] * len(parts),
         out_specs=VMEM,
         compiler_params=params(16),
-        cost_estimate=pl.CostEstimate(flops=one.size, bytes_accessed=one.size, transcendentals=0),
+        cost_estimate=pl.CostEstimate(
+            flops=GATE_COST * one.size, bytes_accessed=one.size, transcendentals=0
+        ),
         name="add",
     )(*parts)
 
@@ -329,8 +318,8 @@
     for emb, parts, out, slots in sets:
         for i in range(4):
             at = pl.ds(i * step, step)
-            upstream = parts[0][at, :]
-            for part in parts[1:]:
+            upstream = jnp.zeros((step, emb.shape[1]), F32)
+            for part in parts:
                 skip = part.shape[0] - 4 * step
                 upstream += part[pl.ds(skip + i * step, step), :].astype(F32)
             slots[at, :] = backnorm(emb[at, :], upstream, scale)
@@ -364,18 +353,18 @@
 
 
 def totals_kernel(*refs):
-    *parts, out = refs
+    parts, outs = refs[:-3], refs[-3:]
     total = sum((part[...] for part in parts[1:]), parts[0][...])
-    for i in range(3):
-        out[i] = jnp.sum(total[0:1, i : i + 1]) * (1.0 / BATCH)
+    for i, out in enumerate(outs):
+        out[0] = jnp.sum(total[0:1, i : i + 1]) * (1.0 / BATCH)
 
 
 def totals_part(*parts):
     return pl.pallas_call(
         totals_kernel,
-        out_shape=jax.ShapeDtypeStruct((3,), F32),
+        out_shape=(jax.ShapeDtypeStruct((1,), F32),) * 3,
         in_specs=[VMEM] * len(parts),
-        out_specs=SMEM,
+        out_specs=(SMEM,) * 3,
         compiler_params=params(16),
         cost_estimate=pl.CostEstimate(flops=4096, bytes_accessed=4096, transcendentals=0),
         name="totals",
@@ -414,16 +403,16 @@
     def pair(value, axis, k):
         return lax.ppermute(value, axis, [(i, i ^ k) for i in range(lax.axis_size(axis))])
 
-    over_core = pair(sums, "blk", 1)
-    far_p, y_q, to_mate, sums = far_grad_part(
+    over_y = pair(sums, "blk", 2)
+    far_p, y_q, to_mate, own_q, sums = far_grad_part(
         far_images, far_grads, near_images, texts, near_grads, sums
     )
-    sums_1 = add(sums, over_core)
+    sums_1 = add(sums, over_y)
     from_far = send(far_p, [(i, (i + 8) % blocks) for i in range(blocks)])
     from_core = send(to_mate, across_core)
-    y_sum, sums_2 = relay_y(y_q, from_core, sums_1, pair(sums_1, "blk", 2))
+    y_sum, sums_2 = relay_y(y_q, from_core, sums_1, pair(sums_1, "blk", 1))
     from_y = send(y_sum, across_y)
-    own_q, sums_2 = text_part(near_grads, far_grads, near_images, far_images, sums_2)
+    sums_2 = add(sums_2)
 
     def steps(carry):
         left, value = carry
@@ -439,8 +428,8 @@
         (image_emb, own_p, from_left, from_right, from_far),
         sums_6,
     )
-    totals = totals_part(sums_6, *over_x)
-    return (totals[0], grad_image, grad_text, totals[1], totals[2])
+    loss, grad_scale, grad_bias = (total.reshape(()) for total in totals_part(sums_6, *over_x))
+    return (loss, grad_image, grad_text, grad_scale, grad_bias)
 
 
 def solution(mesh):

time: 85.6 us -> 83.9 us (0.980)
  local copies, waits for them, and re-layouts: 5.58 us -> 3.57 us
    ppermute x12, starting transfers between devices: 12.5 us -> 14.6 us  [send(): return lax.ppermute(value, 'blk', perm)]
    ppermute x9, starting transfers between devices: 19.2 us -> 17.6 us  [pair(): lax.ppermute(value, axis, [(i, i ^ k) for i in range(lax.axis_size(axis))])]
    pallas_call x3 -> x2, Pallas kernels: 9.77 us -> 8.26 us  [the longest x1 7.63 us: near_part(): pl.pallas_call(near_kernel, out_shape=(shape((rows, width), BF16), shape(...]
    unnamed x14, local copies, waits for them, and re-layouts: 4.99 us -> 3.57 us
    pallas_call x1, Pallas kernels: 3.14 us -> 4.2 us  [far_grad_part(): pl.pallas_call(far_grad_kernel, out_shape=(shape((rows, width), BF16), sh...]
  transfers between devices with their start and end apart: 21 -> 21, of which waited for: 8 -> 7; matrix products, arithmetic and copies ran while one was open for 0% -> 0% of each run, Pallas kernels for 16% -> 15%
where the time goes in v7:
time: 83.9 us; the launch traced here: 83 us
  starting transfers between devices  32.1 us (38%)
  waiting for transfers between devices  22.8 us (27%)
  Pallas kernels  19.7 us (23%)
  local copies, waits for them, and re-layouts  3.57 us (4%)
  loops' own time  2.47 us (3%)
  between operations  2.28 us (3%)
    ppermute x9, starting transfers between devices, pair(): lax.ppermute(value, axis, [(i, i ^ k) for i in range(lax.axis_size(axis))])  17.6 us
    ppermute x12, starting transfers between devices, send(): return lax.ppermute(value, 'blk', perm)  14.6 us
    ppermute x12, waiting for transfers between devices, send(): return lax.ppermute(value, 'blk', perm)  11.5 us
    ppermute x9, waiting for transfers between devices, pair(): lax.ppermute(value, axis, [(i, i ^ k) for i in range(lax.axis_size(axis))])  11.4 us
    pallas_call x1, Pallas kernels, near_part(): pl.pallas_call(near_kernel, out_shape=(shape((rows, width), BF16), shape(...  7.63 us
    pallas_call x1, Pallas kernels, far_grad_part(): pl.pallas_call(far_grad_kernel, out_shape=(shape((rows, width), BF16), sh...  4.2 us
    pallas_call x1, Pallas kernels, end_part(): pl.pallas_call(end_kernel, out_shape=(shape((rows, width), F32),) * 2 + (...  3.94 us
    unnamed x14, local copies, waits for them, and re-layouts  3.57 us
  transfers between devices with their start and end apart: 21, of which 7 were waited for; matrix products, arithmetic and copies ran while one was open for 0% of the time, Pallas kernels for 15%

profile of v7, /device:TPU:32, one launch (start us, length us, event | category | flops | bytes accessed | tf_op | source)
XLA Modules:
  0.0 83.0 jit_solution(11531738950317562460)
XLA Ops:
  0.6 0.0 copy-start.1
  0.7 1.4 %copy-done.1 = f32[256,1152]{1,0:T(8,128)S(1)} copy-done((f32[256,1152]{1,0:T(8,128)S(1)}, f32[256,1152]{1,0:T(8,128)}, u32[]{:S(2)}) %copy-start.1) | copy-done | bytes 1179672
  2.0 0.2 normalize.2
  2.2 0.1 copy-done
  2.3 0.7 normalize.3
  3.0 1.6 %collective-permute-start.9 = (bf16[256,1152]{1,0:T(8,128)(2,1)S(1)}, bf16[256,1152]{1,0:T(8,128)(2,1)}, u32[]{:S(2)}, u32[]{:S(2)}) collective-permute-start(bf16[256,1152]{1,0:T(8,128)(2,1)S(1)} %get-tuple-element.46.own_t), channel_id=1, source_target_pairs={{0,32},{16,48},{32,0},{48,16},{64,96},{80,112},{96,64},{112,80},{1... | collective-permute-start | bytes 1769480 | tf_op jit(solution)/shard_map/ppermute | solution.py:383
  4.5 1.5 %collective-permute-start.4 = (bf16[256,1152]{1,0:T(8,128)(2,1)S(1)}, bf16[256,1152]{1,0:T(8,128)(2,1)S(1)}, u32[]{:S(2)}, u32[]{:S(2)}) collective-permute-start(bf16[256,1152]{1,0:T(8,128)(2,1)S(1)} %get-tuple-element.44.own_i), channel_id=1, source_target_pairs={{0,64},{16,80},{32,96},{48,112},{64,128},{80,144},{96,160},{112,17... | collective-permute-start | bytes 1769480 | tf_op jit(solution)/shard_map/ppermute | solution.py:383
  6.0 1.7 %collective-permute-start.6 = (bf16[256,1152]{1,0:T(8,128)(2,1)S(1)}, bf16[256,1152]{1,0:T(8,128)(2,1)S(1)}, u32[]{:S(2)}, u32[]{:S(2)}) collective-permute-start(bf16[256,1152]{1,0:T(8,128)(2,1)S(1)} %get-tuple-element.44.own_i), channel_id=1, source_target_pairs={{0,192},{16,208},{32,224},{48,240},{64,0},{80,16},{96,32},{112,48}... | collective-permute-start | bytes 1769480 | tf_op jit(solution)/shard_map/ppermute | solution.py:383
  7.8 0.0 collective-permute-start.8
  7.8 10.4 %collective-permute-done.9.y_t = bf16[256,1152]{1,0:T(8,128)(2,1)} collective-permute-done((bf16[256,1152]{1,0:T(8,128)(2,1)S(1)}, bf16[256,1152]{1,0:T(8,128)(2,1)}, u32[]{:S(2)}, u32[]{:S(2)}) %collective-permute-start.9) | collective-permute-done | bytes 589856 | tf_op jit(solution)/shard_map/ppermute | solution.py:383
  19.4 1.1 %collective-permute-done.4.block_ref.left_i = bf16[256,1152]{1,0:T(8,128)(2,1)S(1)} collective-permute-done((bf16[256,1152]{1,0:T(8,128)(2,1)S(1)}, bf16[256,1152]{1,0:T(8,128)(2,1)S(1)}, u32[]{:S(2)}, u32[]{:S(2)}) %collective-permute-start.4) | collective-permute-done | bytes 589856 | tf_op jit(solution)/shard_map/ppermute | solution.py:383
  20.6 0.5 collective-permute-start.5
  21.1 0.0 collective-permute-done.6.block_ref.right_i
  21.1 3.1 %collective-permute-start.7 = (bf16[128,1152]{1,0:T(8,128)(2,1)S(1)}, bf16[128,1152]{1,0:T(8,128)(2,1)S(1)}, u32[]{:S(2)}, u32[]{:S(2)}) collective-permute-start(bf16[128,1152]{1,0:T(8,128)(2,1)S(1)} %cut.3), channel_id=1, source_target_pairs={{0,192},{16,208},{32,224},{48,240},{64,0},{80,16},{96,32},{112,48}... | collective-permute-start | bytes 884744 | tf_op jit(solution)/shard_map/ppermute | solution.py:383
  24.2 7.6 %near.1 = (bf16[256,1152]{1,0:T(8,128)(2,1)S(1)}, bf16[256,1152]{1,0:T(8,128)(2,1)}, bf16[256,1152]{1,0:T(8,128)(2,1)}, bf16[768,1152]{1,0:T(8,128)(2,1)S(1)}, b...) custom-call(f32[1]{0:T(128)} %bitcast.6.log_scale, ...), custom_call_target="tpu_custom_call" | custom-call | flops 28991029248 | bytes 7077888 | tf_op jit(solution)/shard_map/near/pallas_call | solution.py:199
  31.8 0.0 collective-permute-done.5.top_i
  31.8 0.0 collective-permute-done.7.bot_i
  31.8 1.4 %far.1 = (bf16[256,1152]{1,0:T(8,128)(2,1)S(1)}, bf16[256,1024]{1,0:T(8,128)(2,1)S(1)}, f32[8,128]{1,0:T(8,128)S(1)}) custom-call(f32[1]{0:T(128)} %bitcast.7.log_scale, f32[1]{0:T(128)} %bitcast.10.bias, bf16[128,1152]{1,0:T(8,128)(2,1)S(1)} %collective-permute-done.5.top_i, bf16[128,1152]{1,0:T(8,128)(2,1)S(1)} %collective-permute-done.7.bot_i, ...), custom_call_target="tpu_custom_call" | custom-call | flops 75497472 | bytes 589824 | tf_op jit(solution)/shard_map/far/pallas_call | solution.py:227
  33.2 4.2 %far_grad.1 = (bf16[256,1152]{1,0:T(8,128)(2,1)}, f32[256,1152]{1,0:T(8,128)S(1)}, bf16[512,1152]{1,0:T(8,128)(2,1)S(1)}, bf16[256,1152]{1,0:T(8,128)(2,1)S(1)}, f32[8,128]{1,0:T(8,128)S(1)}) custom-call(bf16[256,1152]{1,0:T(8,128)(2,1)S(1)} %get-tuple-element.49.far_images, bf16[256,1024]{1,0:T(8,128)(2,1)S(1)} %get-tuple-element.50.far_grads, ...), custom_call_target="tpu_custom_call" | custom-call | flops 75497472 | bytes 589824 | tf_op jit(solution)/shard_map/far_grad/pallas_call | solution.py:245
  37.4 0.0 collective-permute-start.11
  37.4 0.5 collective-permute-start.12
  37.9 3.1 %collective-permute-done.12.refs_1_ = f32[8,128]{1,0:T(8,128)S(1)} collective-permute-done((f32[8,128]{1,0:T(8,128)S(1)}, f32[8,128]{1,0:T(8,128)S(1)}, u32[]{:S(2)}, u32[]{:S(2)}) %collective-permute-start.12) | collective-permute-done | bytes 4128 | tf_op jit(solution)/shard_map/ppermute | solution.py:404
  41.1 0.0 collective-permute-start.13
  41.1 1.4 %collective-permute-start.17 = (bf16[256,1152]{1,0:T(8,128)(2,1)}, bf16[256,1152]{1,0:T(8,128)(2,1)}, u32[]{:S(2)}, u32[]{:S(2)}) collective-permute-start(bf16[256,1152]{1,0:T(8,128)(2,1)} %get-tuple-element.62), channel_id=1, source_target_pairs={{0,128},{16,144},{32,160},{48,176},{64,192},{80,208},{96,224},{112... | collective-permute-start | bytes 1769480 | tf_op jit(solution)/shard_map/ppermute | solution.py:383
  42.4 1.1 %collective-permute-start.15 = (bf16[256,1152]{1,0:T(8,128)(2,1)}, bf16[256,1152]{1,0:T(8,128)(2,1)}, u32[]{:S(2)}, u32[]{:S(2)}) collective-permute-start(bf16[256,1152]{1,0:T(8,128)(2,1)} %get-tuple-element.60), channel_id=1, source_target_pairs={{0,64},{16,80},{32,96},{48,112},{64,128},{80,144},{96,160},{112,17... | collective-permute-start | bytes 1769480 | tf_op jit(solution)/shard_map/ppermute | solution.py:383
  43.5 2.2 %collective-permute-start.16 = (bf16[256,1152]{1,0:T(8,128)(2,1)}, bf16[256,1152]{1,0:T(8,128)(2,1)}, u32[]{:S(2)}, u32[]{:S(2)}) collective-permute-start(bf16[256,1152]{1,0:T(8,128)(2,1)} %get-tuple-element.61), channel_id=1, source_target_pairs={{0,192},{16,208},{32,224},{48,240},{64,0},{80,16},{96,32},{112,48}... | collective-permute-start | bytes 1769480 | tf_op jit(solution)/shard_map/ppermute | solution.py:383
  45.7 1.0 %relay_y.1 = (bf16[256,1152]{1,0:T(8,128)(2,1)}, f32[8,128]{1,0:T(8,128)S(1)}) custom-call(f32[256,1152]{1,0:T(8,128)S(1)} %get-tuple-element.56.own, bf16[512,1152]{1,0:T(8,128)(2,1)S(1)} %collective-permute-done.11.passing.from_core, f32[8,128]{1,0:T(8,128)S(1)} %add.23.sums, f32[8,128]{1,0:T(8,128)S(1)} %collective-permute-done.13.arrived), custom_call_target="tpu_custom_call" | custom-call | flops 294912 | bytes 294912 | tf_op jit(solution)/shard_map/relay_y/pallas_call | solution.py:288
  46.6 1.6 %collective-permute-start.14 = (bf16[256,1152]{1,0:T(8,128)(2,1)}, bf16[256,1152]{1,0:T(8,128)(2,1)}, u32[]{:S(2)}, u32[]{:S(2)}) collective-permute-start(bf16[256,1152]{1,0:T(8,128)(2,1)} %get-tuple-element.58), channel_id=1, source_target_pairs={{0,32},{16,48},{32,0},{48,16},{64,96},{80,112},{96,64},{112,80},{1... | collective-permute-start | bytes 1769480 | tf_op jit(solution)/shard_map/ppermute | solution.py:383
  48.2 23.0 %while.10 = (s32[]{:T(128)}, f32[8,128]{1,0:T(8,128)S(1)}, s32[]{:T(128)}) while((s32[]{:T(128)}, f32[8,128]{1,0:T(8,128)S(1)}, s32[]{:T(128)}) %tuple.22), condition=%wide.region_1.0_spmd, body=%wide.region_0.0_spmd.sunk | while | flops 4098 | bytes 114893 | solution.py:423
  48.9 0.2 collective-permute-start
  49.1 3.5 %collective-permute-done = f32[8,128]{1,0:T(8,128)S(1)} collective-permute-done((f32[8,128]{1,0:T(8,128)S(1)}, f32[8,128]{1,0:T(8,128)S(1)}, u32[]{:S(2)}, u32[]{:S(2)}) %collective-permute-start) | collective-permute-done | bytes 4128 | tf_op jit(solution)/shard_map/while/body/ppermute | solution.py:404
  52.6 3.3 %collective-permute-start.1 = (f32[8,128]{1,0:T(8,128)S(1)}, f32[8,128]{1,0:T(8,128)S(1)}, u32[]{:S(2)}, u32[]{:S(2)}) collective-permute-start(f32[8,128]{1,0:T(8,128)S(1)} %add.19), channel_id=1, source_target_pairs={{0,2},{1,3},{2,0},{3,1},{4,6},{5,7},{6,4},{7,5},{8,10},{9,11},{10,... | collective-permute-start | bytes 12296 | tf_op jit(solution)/shard_map/while/body/ppermute | solution.py:404
  55.8 1.6 %collective-permute-done.1 = f32[8,128]{1,0:T(8,128)S(1)} collective-permute-done((f32[8,128]{1,0:T(8,128)S(1)}, f32[8,128]{1,0:T(8,128)S(1)}, u32[]{:S(2)}, u32[]{:S(2)}) %collective-permute-start.1) | collective-permute-done | bytes 4128 | tf_op jit(solution)/shard_map/while/body/ppermute | solution.py:404
  57.4 5.9 %collective-permute-start.2 = (f32[8,128]{1,0:T(8,128)S(1)}, f32[8,128]{1,0:T(8,128)S(1)}, u32[]{:S(2)}, u32[]{:S(2)}) collective-permute-start(f32[8,128]{1,0:T(8,128)S(1)} %add.20), channel_id=1, source_target_pairs={{0,4},{1,5},{2,6},{3,7},{4,0},{5,1},{6,2},{7,3},{8,12},{9,13},{10,... | collective-permute-start | bytes 12296 | tf_op jit(solution)/shard_map/while/body/ppermute | solution.py:404
  63.4 1.6 %collective-permute-done.2 = f32[8,128]{1,0:T(8,128)S(1)} collective-permute-done((f32[8,128]{1,0:T(8,128)S(1)}, f32[8,128]{1,0:T(8,128)S(1)}, u32[]{:S(2)}, u32[]{:S(2)}) %collective-permute-start.2) | collective-permute-done | bytes 4128 | tf_op jit(solution)/shard_map/while/body/ppermute | solution.py:404
  65.0 2.9 %collective-permute-start.3 = (f32[8,128]{1,0:T(8,128)S(1)}, f32[8,128]{1,0:T(8,128)S(1)}, u32[]{:S(2)}, u32[]{:S(2)}) collective-permute-start(f32[8,128]{1,0:T(8,128)S(1)} %add.21), channel_id=1, source_target_pairs={{0,8},{1,9},{2,10},{3,11},{4,12},{5,13},{6,14},{7,15},{8,0},{9,1},... | collective-permute-start | bytes 12296 | tf_op jit(solution)/shard_map/while/body/ppermute | solution.py:404
  68.5 1.6 %collective-permute-done.3 = f32[8,128]{1,0:T(8,128)S(1)} collective-permute-done((f32[8,128]{1,0:T(8,128)S(1)}, f32[8,128]{1,0:T(8,128)S(1)}, u32[]{:S(2)}, u32[]{:S(2)}) %collective-permute-start.3) | collective-permute-done | bytes 4128 | tf_op jit(solution)/shard_map/while/body/ppermute | solution.py:404
  71.2 0.1 collective-permute-start.18
  71.3 0.0 collective-permute-done.17.from_far
  71.4 1.7 %collective-permute-start.19 = (f32[8,128]{1,0:T(8,128)S(1)}, f32[8,128]{1,0:T(8,128)S(1)}, u32[]{:S(2)}, u32[]{:S(2)}) collective-permute-start(f32[8,128]{1,0:T(8,128)S(1)} %get-tuple-element.65.sums), channel_id=1, source_target_pairs={{0,128},{16,144},{32,160},{48,176},{64,192},{80,208},{96,224},{112... | collective-permute-start | bytes 12296 | tf_op jit(solution)/shard_map/ppermute | solution.py:404
  73.0 0.0 collective-permute-done.15.from_left
  73.0 3.0 %collective-permute-start.20 = (f32[8,128]{1,0:T(8,128)S(1)}, f32[8,128]{1,0:T(8,128)S(1)}, u32[]{:S(2)}, u32[]{:S(2)}) collective-permute-start(f32[8,128]{1,0:T(8,128)S(1)} %get-tuple-element.65.sums), channel_id=1, source_target_pairs={{0,192},{16,208},{32,224},{48,240},{64,128},{80,144},{96,160},{112... | collective-permute-start | bytes 12296 | tf_op jit(solution)/shard_map/ppermute | solution.py:404
  76.0 0.0 collective-permute-done.16.from_right
  76.0 0.0 collective-permute-done.14.from_y
  76.1 1.1 %copy-done.4 = bf16[256,1152]{1,0:T(8,128)(2,1)S(1)} copy-done((bf16[256,1152]{1,0:T(8,128)(2,1)S(1)}, bf16[256,1152]{1,0:T(8,128)(2,1)}, u32[]{:S(2)}) %copy-start.4) | copy-done | bytes 589848
  77.1 1.1 %copy-done.6 = bf16[256,1152]{1,0:T(8,128)(2,1)S(1)} copy-done((bf16[256,1152]{1,0:T(8,128)(2,1)S(1)}, bf16[256,1152]{1,0:T(8,128)(2,1)}, u32[]{:S(2)}) %copy-start.6) | copy-done | bytes 589848
  78.2 3.9 %end.1 = (f32[256,1152]{1,0:T(8,128)}, f32[256,1152]{1,0:T(8,128)}, f32[8,128]{1,0:T(8,128)S(1)}) custom-call(f32[1]{0:T(128)} %bitcast.8.log_scale, f32[256,1152]{1,0:T(8,128)S(1)} %copy-done, bf16[256,1152]{1,0:T(8,128)(2,1)S(1)} %copy-done.6, bf16[512,1152]{1,0:T(8,128)(2,1)S(1)} %collective-permute-done.11.passing.from_core, ...), custom_call_target="tpu_custom_call" | custom-call | flops 4718592 | bytes 589824 | tf_op jit(solution)/shard_map/end/pallas_call | solution.py:337
  82.2 0.6 totals.1
  (25 shorter events, 0.1 us)
Async XLA Ops:
  0.6 1.6 %copy-start = (f32[256,1152]{1,0:T(8,128)S(1)}, f32[256,1152]{1,0:T(8,128)}, u32[]{:S(2)}) copy-start(f32[256,1152]{1,0:T(8,128)} %text_emb.1) | copy-start | bytes 3538948
  0.6 1.4 %copy-start.1 = (f32[256,1152]{1,0:T(8,128)S(1)}, f32[256,1152]{1,0:T(8,128)}, u32[]{:S(2)}) copy-start(f32[256,1152]{1,0:T(8,128)} %image_emb.1) | copy-start | bytes 3538948
  3.0 15.2 %collective-permute-start.9 = (bf16[256,1152]{1,0:T(8,128)(2,1)S(1)}, bf16[256,1152]{1,0:T(8,128)(2,1)}, u32[]{:S(2)}, u32[]{:S(2)}) collective-permute-start(bf16[256,1152]{1,0:T(8,128)(2,1)S(1)} %get-tuple-element.46.own_t), channel_id=1, source_target_pairs={{0,32},{16,48},{32,0},{48,16},{64,96},{80,112},{96,64},{112,80},{1... | collective-permute-start | bytes 1769480 | tf_op jit(solution)/shard_map/ppermute | solution.py:383
  4.5 16.0 %collective-permute-start.4 = (bf16[256,1152]{1,0:T(8,128)(2,1)S(1)}, bf16[256,1152]{1,0:T(8,128)(2,1)S(1)}, u32[]{:S(2)}, u32[]{:S(2)}) collective-permute-start(bf16[256,1152]{1,0:T(8,128)(2,1)S(1)} %get-tuple-element.44.own_i), channel_id=1, source_target_pairs={{0,64},{16,80},{32,96},{48,112},{64,128},{80,144},{96,160},{112,17... | collective-permute-start | bytes 1769480 | tf_op jit(solution)/shard_map/ppermute | solution.py:383
  6.0 15.0 %collective-permute-start.6 = (bf16[256,1152]{1,0:T(8,128)(2,1)S(1)}, bf16[256,1152]{1,0:T(8,128)(2,1)S(1)}, u32[]{:S(2)}, u32[]{:S(2)}) collective-permute-start(bf16[256,1152]{1,0:T(8,128)(2,1)S(1)} %get-tuple-element.44.own_i), channel_id=1, source_target_pairs={{0,192},{16,208},{32,224},{48,240},{64,0},{80,16},{96,32},{112,48}... | collective-permute-start | bytes 1769480 | tf_op jit(solution)/shard_map/ppermute | solution.py:383
  7.8 16.4 %collective-permute-start.8 = (bf16[256,1152]{1,0:T(8,128)(2,1)S(1)}, bf16[256,1152]{1,0:T(8,128)(2,1)}, u32[]{:S(2)}, u32[]{:S(2)}) collective-permute-start(bf16[256,1152]{1,0:T(8,128)(2,1)S(1)} %get-tuple-element.46.own_t), channel_id=1, source_target_pairs={{0,16},{16,0},{32,48},{48,32},{64,80},{80,64},{96,112},{112,96},{1... | collective-permute-start | bytes 1769480 | tf_op jit(solution)/shard_map/ppermute | solution.py:383
  18.1 6.0 %collective-permute-start.10 = (bf16[256,1152]{1,0:T(8,128)(2,1)}, bf16[256,1152]{1,0:T(8,128)(2,1)}, u32[]{:S(2)}, u32[]{:S(2)}) collective-permute-start(bf16[256,1152]{1,0:T(8,128)(2,1)} %collective-permute-done.9.y_t), channel_id=1, source_target_pairs={{0,16},{16,0},{32,48},{48,32},{64,80},{80,64},{96,112},{112,96},{1... | collective-permute-start | bytes 1769480 | tf_op jit(solution)/shard_map/ppermute | solution.py:383
  20.6 11.3 %collective-permute-start.5 = (bf16[128,1152]{1,0:T(8,128)(2,1)S(1)}, bf16[128,1152]{1,0:T(8,128)(2,1)S(1)}, u32[]{:S(2)}, u32[]{:S(2)}) collective-permute-start(bf16[128,1152]{1,0:T(8,128)(2,1)S(1)} %cut.2), channel_id=1, source_target_pairs={{0,64},{16,80},{32,96},{48,112},{64,128},{80,144},{96,160},{112,17... | collective-permute-start | bytes 884744 | tf_op jit(solution)/shard_map/ppermute | solution.py:383
  21.1 10.8 %collective-permute-start.7 = (bf16[128,1152]{1,0:T(8,128)(2,1)S(1)}, bf16[128,1152]{1,0:T(8,128)(2,1)S(1)}, u32[]{:S(2)}, u32[]{:S(2)}) collective-permute-start(bf16[128,1152]{1,0:T(8,128)(2,1)S(1)} %cut.3), channel_id=1, source_target_pairs={{0,192},{16,208},{32,224},{48,240},{64,0},{80,16},{96,32},{112,48}... | collective-permute-start | bytes 884744 | tf_op jit(solution)/shard_map/ppermute | solution.py:383
  31.8 1.4 %copy-start.3 = (bf16[256,1152]{1,0:T(8,128)(2,1)}, bf16[256,1152]{1,0:T(8,128)(2,1)S(1)}, u32[]{:S(2)}) copy-start(bf16[256,1152]{1,0:T(8,128)(2,1)S(1)} %get-tuple-element.59.own_p) | copy-start | bytes 1769476
  37.4 9.2 %copy-start.5 = (bf16[256,1152]{1,0:T(8,128)(2,1)}, bf16[256,1152]{1,0:T(8,128)(2,1)S(1)}, u32[]{:S(2)}) copy-start(bf16[256,1152]{1,0:T(8,128)(2,1)S(1)} %get-tuple-element.54.own_q) | copy-start | bytes 1769476
  37.4 8.2 %collective-permute-start.11 = (bf16[512,1152]{1,0:T(8,128)(2,1)S(1)}, bf16[512,1152]{1,0:T(8,128)(2,1)S(1)}, u32[]{:S(2)}, u32[]{:S(2)}) collective-permute-start(bf16[512,1152]{1,0:T(8,128)(2,1)S(1)} %get-tuple-element.55), channel_id=1, source_target_pairs={{0,16},{16,0},{32,48},{48,32},{64,80},{80,64},{96,112},{112,96},{1... | collective-permute-start | bytes 3538952 | tf_op jit(solution)/shard_map/ppermute | solution.py:383
  37.4 3.6 %collective-permute-start.12 = (f32[8,128]{1,0:T(8,128)S(1)}, f32[8,128]{1,0:T(8,128)S(1)}, u32[]{:S(2)}, u32[]{:S(2)}) collective-permute-start(f32[8,128]{1,0:T(8,128)S(1)} %get-tuple-element.53.sums), channel_id=1, source_target_pairs={{0,32},{16,48},{32,0},{48,16},{64,96},{80,112},{96,64},{112,80},{1... | collective-permute-start | bytes 12296 | tf_op jit(solution)/shard_map/ppermute | solution.py:404
  41.1 4.6 %collective-permute-start.13 = (f32[8,128]{1,0:T(8,128)S(1)}, f32[8,128]{1,0:T(8,128)S(1)}, u32[]{:S(2)}, u32[]{:S(2)}) collective-permute-start(f32[8,128]{1,0:T(8,128)S(1)} %add.23.sums), channel_id=1, source_target_pairs={{0,16},{16,0},{32,48},{48,32},{64,80},{80,64},{96,112},{112,96},{1... | collective-permute-start | bytes 12296 | tf_op jit(solution)/shard_map/ppermute | solution.py:404
  41.1 30.3 %collective-permute-start.17 = (bf16[256,1152]{1,0:T(8,128)(2,1)}, bf16[256,1152]{1,0:T(8,128)(2,1)}, u32[]{:S(2)}, u32[]{:S(2)}) collective-permute-start(bf16[256,1152]{1,0:T(8,128)(2,1)} %get-tuple-element.62), channel_id=1, source_target_pairs={{0,128},{16,144},{32,160},{48,176},{64,192},{80,208},{96,224},{112... | collective-permute-start | bytes 1769480 | tf_op jit(solution)/shard_map/ppermute | solution.py:383
  42.4 30.6 %collective-permute-start.15 = (bf16[256,1152]{1,0:T(8,128)(2,1)}, bf16[256,1152]{1,0:T(8,128)(2,1)}, u32[]{:S(2)}, u32[]{:S(2)}) collective-permute-start(bf16[256,1152]{1,0:T(8,128)(2,1)} %get-tuple-element.60), channel_id=1, source_target_pairs={{0,64},{16,80},{32,96},{48,112},{64,128},{80,144},{96,160},{112,17... | collective-permute-start | bytes 1769480 | tf_op jit(solution)/shard_map/ppermute | solution.py:383
  43.5 32.5 %collective-permute-start.16 = (bf16[256,1152]{1,0:T(8,128)(2,1)}, bf16[256,1152]{1,0:T(8,128)(2,1)}, u32[]{:S(2)}, u32[]{:S(2)}) collective-permute-start(bf16[256,1152]{1,0:T(8,128)(2,1)} %get-tuple-element.61), channel_id=1, source_target_pairs={{0,192},{16,208},{32,224},{48,240},{64,0},{80,16},{96,32},{112,48}... | collective-permute-start | bytes 1769480 | tf_op jit(solution)/shard_map/ppermute | solution.py:383
  45.7 30.4 %copy-start.2 = (f32[256,1152]{1,0:T(8,128)S(1)}, f32[256,1152]{1,0:T(8,128)}, u32[]{:S(2)}) copy-start(f32[256,1152]{1,0:T(8,128)} %image_emb.1) | copy-start | bytes 3538948
  46.6 29.4 %collective-permute-start.14 = (bf16[256,1152]{1,0:T(8,128)(2,1)}, bf16[256,1152]{1,0:T(8,128)(2,1)}, u32[]{:S(2)}, u32[]{:S(2)}) collective-permute-start(bf16[256,1152]{1,0:T(8,128)(2,1)} %get-tuple-element.58), channel_id=1, source_target_pairs={{0,32},{16,48},{32,0},{48,16},{64,96},{80,112},{96,64},{112,80},{1... | collective-permute-start | bytes 1769480 | tf_op jit(solution)/shard_map/ppermute | solution.py:383
  48.9 3.7 %collective-permute-start = (f32[8,128]{1,0:T(8,128)S(1)}, f32[8,128]{1,0:T(8,128)S(1)}, u32[]{:S(2)}, u32[]{:S(2)}) collective-permute-start(f32[8,128]{1,0:T(8,128)S(1)} %get-tuple-element.93), channel_id=1, source_target_pairs={{0,1},{1,0},{2,3},{3,2},{4,5},{5,4},{6,7},{7,6},{8,9},{9,8},{10,11... | collective-permute-start | bytes 12296 | tf_op jit(solution)/shard_map/while/body/ppermute | solution.py:404
  52.6 4.9 %collective-permute-start.1 = (f32[8,128]{1,0:T(8,128)S(1)}, f32[8,128]{1,0:T(8,128)S(1)}, u32[]{:S(2)}, u32[]{:S(2)}) collective-permute-start(f32[8,128]{1,0:T(8,128)S(1)} %add.19), channel_id=1, source_target_pairs={{0,2},{1,3},{2,0},{3,1},{4,6},{5,7},{6,4},{7,5},{8,10},{9,11},{10,... | collective-permute-start | bytes 12296 | tf_op jit(solution)/shard_map/while/body/ppermute | solution.py:404
  57.4 7.5 %collective-permute-start.2 = (f32[8,128]{1,0:T(8,128)S(1)}, f32[8,128]{1,0:T(8,128)S(1)}, u32[]{:S(2)}, u32[]{:S(2)}) collective-permute-start(f32[8,128]{1,0:T(8,128)S(1)} %add.20), channel_id=1, source_target_pairs={{0,4},{1,5},{2,6},{3,7},{4,0},{5,1},{6,2},{7,3},{8,12},{9,13},{10,... | collective-permute-start | bytes 12296 | tf_op jit(solution)/shard_map/while/body/ppermute | solution.py:404
  65.0 5.1 %collective-permute-start.3 = (f32[8,128]{1,0:T(8,128)S(1)}, f32[8,128]{1,0:T(8,128)S(1)}, u32[]{:S(2)}, u32[]{:S(2)}) collective-permute-start(f32[8,128]{1,0:T(8,128)S(1)} %add.21), channel_id=1, source_target_pairs={{0,8},{1,9},{2,10},{3,11},{4,12},{5,13},{6,14},{7,15},{8,0},{9,1},... | collective-permute-start | bytes 12296 | tf_op jit(solution)/shard_map/while/body/ppermute | solution.py:404
  71.2 10.9 %collective-permute-start.18 = (f32[8,128]{1,0:T(8,128)S(1)}, f32[8,128]{1,0:T(8,128)S(1)}, u32[]{:S(2)}, u32[]{:S(2)}) collective-permute-start(f32[8,128]{1,0:T(8,128)S(1)} %get-tuple-element.65.sums), channel_id=1, source_target_pairs={{0,64},{16,80},{32,96},{48,112},{64,0},{80,16},{96,32},{112,48},{1... | collective-permute-start | bytes 12296 | tf_op jit(solution)/shard_map/ppermute | solution.py:404
  71.4 10.8 %collective-permute-start.19 = (f32[8,128]{1,0:T(8,128)S(1)}, f32[8,128]{1,0:T(8,128)S(1)}, u32[]{:S(2)}, u32[]{:S(2)}) collective-permute-start(f32[8,128]{1,0:T(8,128)S(1)} %get-tuple-element.65.sums), channel_id=1, source_target_pairs={{0,128},{16,144},{32,160},{48,176},{64,192},{80,208},{96,224},{112... | collective-permute-start | bytes 12296 | tf_op jit(solution)/shard_map/ppermute | solution.py:404
  73.0 9.1 %collective-permute-start.20 = (f32[8,128]{1,0:T(8,128)S(1)}, f32[8,128]{1,0:T(8,128)S(1)}, u32[]{:S(2)}, u32[]{:S(2)}) collective-permute-start(f32[8,128]{1,0:T(8,128)S(1)} %get-tuple-element.65.sums), channel_id=1, source_target_pairs={{0,192},{16,208},{32,224},{48,240},{64,128},{80,144},{96,160},{112... | collective-permute-start | bytes 12296 | tf_op jit(solution)/shard_map/ppermute | solution.py:404
  76.1 1.1 %copy-start.4 = (bf16[256,1152]{1,0:T(8,128)(2,1)S(1)}, bf16[256,1152]{1,0:T(8,128)(2,1)}, u32[]{:S(2)}) copy-start(bf16[256,1152]{1,0:T(8,128)(2,1)} %copy-done.3) | copy-start | bytes 1769476
  77.1 1.1 %copy-start.6 = (bf16[256,1152]{1,0:T(8,128)(2,1)S(1)}, bf16[256,1152]{1,0:T(8,128)(2,1)}, u32[]{:S(2)}) copy-start(bf16[256,1152]{1,0:T(8,128)(2,1)} %copy-done.5) | copy-start | bytes 1769476

commit v8 on v7

--- a/solution.py
+++ b/solution.py
@@ -9,8 +9,10 @@
 LOG2E = 1.4426950408889634
 BATCH = 65536
 GATE_COST = 1
-STEPS = (("group", 1), ("group", 2), ("group", 4), ("group", 8))
+CUT_COST = 1024 * 32
+STEPS = (("group", 1), ("group", 2), ("group", 7), (("blk", "group"), 2 * 16 + 8))
 BF16 = jnp.bfloat16
+ANY = pl.BlockSpec(memory_space=pl.ANY)
 HBM = pl.BlockSpec(memory_space=pltpu.HBM)
 VMEM = pl.BlockSpec(memory_space=pltpu.VMEM)
 SMEM = pl.BlockSpec(memory_space=pltpu.SMEM)
@@ -60,7 +62,9 @@
         in_specs=[VMEM],
         out_specs=VMEM,
         compiler_params=params(16),
-        cost_estimate=pl.CostEstimate(flops=0, bytes_accessed=rows * width, transcendentals=0),
+        cost_estimate=pl.CostEstimate(
+            flops=CUT_COST * rows * width, bytes_accessed=rows * width, transcendentals=0
+        ),
         name="cut",
     )(block)
 
@@ -111,14 +115,21 @@
 
 def near_kernel(
     log_scale, bias, own_i, left_i, right_i, own_t, core_t, y_t, yc_t,
-    own_out, left_out, right_out, images, texts, grads, sums_ref, passes_ref,
+    own_out, left_out, right_out, images, texts, grads, sums_ref, passes_ref, sems,
 ):
     rows = own_i.shape[0]
     factor, scale, bias = logit_factors(log_scale, bias, rows)
-    for i, src in enumerate((own_i, left_i, right_i)):
-        images[pl.ds(i * rows, rows), :] = src[...]
-    for i, src in enumerate((own_t, core_t, y_t, yc_t)):
-        texts[pl.ds(i * rows, rows), :] = src[...]
+    blocks = [(own_i, images, 0), (own_t, texts, 0)]
+    blocks += [(src, texts, i) for i, src in enumerate((core_t, y_t, yc_t), 1)]
+    blocks += [(src, images, i) for i, src in enumerate((left_i, right_i), 1)]
+    copies = [
+        pltpu.make_async_copy(src, dst.at[pl.ds(i * rows, rows)], sems.at[k])
+        for k, (src, dst, i) in enumerate(blocks)
+    ]
+    for copy in copies:
+        copy.start()
+    copies[0].wait()
+    copies[1].wait()
     loss = scaled = grad = jnp.zeros((8, rows), F32)
     tiles = [(b, t) for b in range(3) for t in range(4)]
 
@@ -128,6 +139,10 @@
 
     sim = sim_of(0)
     for k, (b, t) in enumerate(tiles):
+        if k < 3:
+            copies[k + 2].wait()
+        elif k in (3, 7):
+            copies[5 + k // 7].wait()
         sim_next = sim_of(k + 1) if k + 1 < len(tiles) else None
         grad_q, loss_now, scaled_now, grad_now = pair_tile(sim, scale, bias, k == 0)
         grads[pl.ds(b * rows, rows), pl.ds(t * rows, rows)] = grad_q
@@ -208,8 +223,9 @@
             shape((8, 128), F32),
             shape((1,), jnp.int32),
         ),
-        in_specs=[SMEM] * 2 + [VMEM] * 7,
+        in_specs=[SMEM] * 2 + [ANY] * 7,
         out_specs=(VMEM,) * 7 + (SMEM,),
+        scratch_shapes=[pltpu.SemaphoreType.DMA((7,))],
         compiler_params=params(16),
         cost_estimate=pl.CostEstimate(
             flops=8 * 2 * 2 * 12 * rows * rows * width,
@@ -278,24 +294,24 @@
     )(*parts)
 
 
-def relay_y_kernel(own, passing, sums, arrived, out, sums_out):
+def relay_y_kernel(own, passing, sums, sums_a, sums_b, sums_c, out, sums_out):
     rows = own.shape[0]
     out[...] = (own[...] + passing[:rows, :].astype(F32)).astype(BF16)
-    sums_out[...] = sums[...] + arrived[...]
-
-
-def relay_y(own, passing, sums, arrived):
+    sums_out[...] = sums[...] + sums_a[...] + sums_b[...] + sums_c[...]
+
+
+def relay_y(own, passing, sums, *arrived):
     return pl.pallas_call(
         relay_y_kernel,
         out_shape=(
             jax.ShapeDtypeStruct(own.shape, BF16), jax.ShapeDtypeStruct(sums.shape, F32)
         ),
-        in_specs=[VMEM] * 4,
+        in_specs=[VMEM] * 6,
         out_specs=(VMEM,) * 2,
         compiler_params=params(16),
         cost_estimate=pl.CostEstimate(flops=own.size, bytes_accessed=own.size, transcendentals=0),
         name="relay_y",
-    )(own, passing, sums, arrived)
+    )(own, passing, sums, *arrived)
 
 
 def backnorm(emb, upstream, scale):
@@ -403,14 +419,13 @@
     def pair(value, axis, k):
         return lax.ppermute(value, axis, [(i, i ^ k) for i in range(lax.axis_size(axis))])
 
-    over_y = pair(sums, "blk", 2)
+    over_y_core = [pair(sums, "blk", k) for k in (3, 2, 1)]
     far_p, y_q, to_mate, own_q, sums = far_grad_part(
         far_images, far_grads, near_images, texts, near_grads, sums
     )
-    sums_1 = add(sums, over_y)
     from_far = send(far_p, [(i, (i + 8) % blocks) for i in range(blocks)])
     from_core = send(to_mate, across_core)
-    y_sum, sums_2 = relay_y(y_q, from_core, sums_1, pair(sums_1, "blk", 1))
+    y_sum, sums_2 = relay_y(y_q, from_core, sums, *over_y_core)
     from_y = send(y_sum, across_y)
     sums_2 = add(sums_2)
 

time: 83.9 us -> 81.1 us (0.967)
  waiting for transfers between devices: 22.8 us -> 20.8 us
    ppermute x9 -> x10, waiting for transfers between devices: 11.4 us -> 9.06 us  [pair(): lax.ppermute(value, axis, [(i, i ^ k) for i in range(lax.axis_size(axis))])]
    ppermute x12, starting transfers between devices: 14.6 us -> 13.4 us  [send(): return lax.ppermute(value, 'blk', perm)]
    ppermute x9 -> x10, starting transfers between devices: 17.6 us -> 17.9 us  [pair(): lax.ppermute(value, axis, [(i, i ^ k) for i in range(lax.axis_size(axis))])]
  transfers between devices with their start and end apart: 21 -> 22, of which waited for: 7 -> 8; matrix products, arithmetic and copies ran while one was open for 0% -> 0% of each run, Pallas kernels for 15% -> 17%
where the time goes in v8:
time: 81.1 us; the launch traced here: 80.8 us
  starting transfers between devices  31.4 us (39%)
  waiting for transfers between devices  20.8 us (26%)
  Pallas kernels  20.3 us (25%)
  local copies, waits for them, and re-layouts  3.5 us (4%)
  loops' own time  2.47 us (3%)
  between operations  2.28 us (3%)
    ppermute x10, starting transfers between devices, pair(): lax.ppermute(value, axis, [(i, i ^ k) for i in range(lax.axis_size(axis))])  17.9 us
    ppermute x12, starting transfers between devices, send(): return lax.ppermute(value, 'blk', perm)  13.4 us
    ppermute x12, waiting for transfers between devices, send(): return lax.ppermute(value, 'blk', perm)  11.7 us
    ppermute x10, waiting for transfers between devices, pair(): lax.ppermute(value, axis, [(i, i ^ k) for i in range(lax.axis_size(axis))])  9.06 us
    pallas_call x1, Pallas kernels, near_part(): pl.pallas_call(near_kernel, out_shape=(shape((rows, width), BF16), shape(...  8.32 us
    pallas_call x1, Pallas kernels, far_grad_part(): pl.pallas_call(far_grad_kernel, out_shape=(shape((rows, width), BF16), sh...  4.21 us
    pallas_call x1, Pallas kernels, end_part(): pl.pallas_call(end_kernel, out_shape=(shape((rows, width), F32),) * 2 + (...  3.94 us
    unnamed x14, local copies, waits for them, and re-layouts  3.5 us
  transfers between devices with their start and end apart: 22, of which 8 were waited for; matrix products, arithmetic and copies ran while one was open for 0% of the time, Pallas kernels for 17%

profile of v8, /device:TPU:32, one launch (start us, length us, event | category | flops | bytes accessed | tf_op | source)
XLA Modules:
  0.0 80.8 jit_solution(13785382696814782821)
XLA Ops:
  0.6 0.0 copy-start.1
  0.7 1.4 %copy-done.1 = f32[256,1152]{1,0:T(8,128)S(1)} copy-done((f32[256,1152]{1,0:T(8,128)S(1)}, f32[256,1152]{1,0:T(8,128)}, u32[]{:S(2)}) %copy-start.1) | copy-done | bytes 1179672
  2.0 0.2 normalize.2
  2.2 1.6 %collective-permute-start.4 = (bf16[256,1152]{1,0:T(8,128)(2,1)S(1)}, bf16[256,1152]{1,0:T(8,128)(2,1)S(1)}, u32[]{:S(2)}, u32[]{:S(2)}) collective-permute-start(bf16[256,1152]{1,0:T(8,128)(2,1)S(1)} %get-tuple-element.44.own_i), channel_id=1, source_target_pairs={{0,64},{16,80},{32,96},{48,112},{64,128},{80,144},{96,160},{112,17... | collective-permute-start | bytes 1769480 | tf_op jit(solution)/shard_map/ppermute | solution.py:399
  3.8 1.7 %collective-permute-start.6 = (bf16[256,1152]{1,0:T(8,128)(2,1)S(1)}, bf16[256,1152]{1,0:T(8,128)(2,1)S(1)}, u32[]{:S(2)}, u32[]{:S(2)}) collective-permute-start(bf16[256,1152]{1,0:T(8,128)(2,1)S(1)} %get-tuple-element.44.own_i), channel_id=1, source_target_pairs={{0,192},{16,208},{32,224},{48,240},{64,0},{80,16},{96,32},{112,48}... | collective-permute-start | bytes 1769480 | tf_op jit(solution)/shard_map/ppermute | solution.py:399
  5.5 0.7 normalize.3
  6.2 1.6 %collective-permute-start.9 = (bf16[256,1152]{1,0:T(8,128)(2,1)S(1)}, bf16[256,1152]{1,0:T(8,128)(2,1)}, u32[]{:S(2)}, u32[]{:S(2)}) collective-permute-start(bf16[256,1152]{1,0:T(8,128)(2,1)S(1)} %get-tuple-element.46.own_t), channel_id=1, source_target_pairs={{0,32},{16,48},{32,0},{48,16},{64,96},{80,112},{96,64},{112,80},{1... | collective-permute-start | bytes 1769480 | tf_op jit(solution)/shard_map/ppermute | solution.py:399
  9.1 9.5 %collective-permute-done.4.block_ref.left_i = bf16[256,1152]{1,0:T(8,128)(2,1)S(1)} collective-permute-done((bf16[256,1152]{1,0:T(8,128)(2,1)S(1)}, bf16[256,1152]{1,0:T(8,128)(2,1)S(1)}, u32[]{:S(2)}, u32[]{:S(2)}) %collective-permute-start.4) | collective-permute-done | bytes 589856 | tf_op jit(solution)/shard_map/ppermute | solution.py:399
  18.6 0.4 collective-permute-start.5
  18.9 1.9 %collective-permute-done.9.y_t = bf16[256,1152]{1,0:T(8,128)(2,1)} collective-permute-done((bf16[256,1152]{1,0:T(8,128)(2,1)S(1)}, bf16[256,1152]{1,0:T(8,128)(2,1)}, u32[]{:S(2)}, u32[]{:S(2)}) %collective-permute-start.9) | collective-permute-done | bytes 589856 | tf_op jit(solution)/shard_map/ppermute | solution.py:399
  20.8 0.0 collective-permute-start.10
  20.9 1.8 %collective-permute-start.7 = (bf16[128,1152]{1,0:T(8,128)(2,1)S(1)}, bf16[128,1152]{1,0:T(8,128)(2,1)S(1)}, u32[]{:S(2)}, u32[]{:S(2)}) collective-permute-start(bf16[128,1152]{1,0:T(8,128)(2,1)S(1)} %cut.3), channel_id=1, source_target_pairs={{0,192},{16,208},{32,224},{48,240},{64,0},{80,16},{96,32},{112,48}... | collective-permute-start | bytes 884744 | tf_op jit(solution)/shard_map/ppermute | solution.py:399
  22.7 0.0 collective-permute-done.8.core_t
  22.7 0.4 collective-permute-done.10.yc_t
  23.0 8.3 %near.1 = (bf16[256,1152]{1,0:T(8,128)(2,1)S(1)}, bf16[256,1152]{1,0:T(8,128)(2,1)}, bf16[256,1152]{1,0:T(8,128)(2,1)}, bf16[768,1152]{1,0:T(8,128)(2,1)S(1)}, b...) custom-call(f32[1]{0:T(128)} %bitcast.6.log_scale, ...), custom_call_target="tpu_custom_call" | custom-call | flops 28991029248 | bytes 7077888 | tf_op jit(solution)/shard_map/near/pallas_call | solution.py:214
  31.4 1.4 %far.1 = (bf16[256,1152]{1,0:T(8,128)(2,1)S(1)}, bf16[256,1024]{1,0:T(8,128)(2,1)S(1)}, f32[8,128]{1,0:T(8,128)S(1)}) custom-call(f32[1]{0:T(128)} %bitcast.7.log_scale, f32[1]{0:T(128)} %bitcast.10.bias, bf16[128,1152]{1,0:T(8,128)(2,1)S(1)} %collective-permute-done.5.top_i, bf16[128,1152]{1,0:T(8,128)(2,1)S(1)} %collective-permute-done.7.bot_i, ...), custom_call_target="tpu_custom_call" | custom-call | flops 75497472 | bytes 589824 | tf_op jit(solution)/shard_map/far/pallas_call | solution.py:243
  32.8 4.2 %far_grad.1 = (bf16[256,1152]{1,0:T(8,128)(2,1)}, f32[256,1152]{1,0:T(8,128)S(1)}, bf16[512,1152]{1,0:T(8,128)(2,1)S(1)}, bf16[256,1152]{1,0:T(8,128)(2,1)S(1)}, f32[8,128]{1,0:T(8,128)S(1)}) custom-call(bf16[256,1152]{1,0:T(8,128)(2,1)S(1)} %get-tuple-element.49.far_images, bf16[256,1024]{1,0:T(8,128)(2,1)S(1)} %get-tuple-element.50.far_grads, ...), custom_call_target="tpu_custom_call" | custom-call | flops 75497472 | bytes 589824 | tf_op jit(solution)/shard_map/far_grad/pallas_call | solution.py:261
  37.0 0.1 collective-permute-start.11
  37.1 1.6 %collective-permute-start.12 = (f32[8,128]{1,0:T(8,128)S(1)}, f32[8,128]{1,0:T(8,128)S(1)}, u32[]{:S(2)}, u32[]{:S(2)}) collective-permute-start(f32[8,128]{1,0:T(8,128)S(1)} %get-tuple-element.53.sums), channel_id=1, source_target_pairs={{0,48},{16,32},{32,16},{48,0},{64,112},{80,96},{96,80},{112,64},{1... | collective-permute-start | bytes 12296 | tf_op jit(solution)/shard_map/ppermute | solution.py:420
  38.7 0.5 collective-permute-start.13
  39.1 1.8 %collective-permute-start.18 = (bf16[256,1152]{1,0:T(8,128)(2,1)}, bf16[256,1152]{1,0:T(8,128)(2,1)}, u32[]{:S(2)}, u32[]{:S(2)}) collective-permute-start(bf16[256,1152]{1,0:T(8,128)(2,1)} %get-tuple-element.62), channel_id=1, source_target_pairs={{0,128},{16,144},{32,160},{48,176},{64,192},{80,208},{96,224},{112... | collective-permute-start | bytes 1769480 | tf_op jit(solution)/shard_map/ppermute | solution.py:399
  41.0 0.9 %collective-permute-start.16 = (bf16[256,1152]{1,0:T(8,128)(2,1)}, bf16[256,1152]{1,0:T(8,128)(2,1)}, u32[]{:S(2)}, u32[]{:S(2)}) collective-permute-start(bf16[256,1152]{1,0:T(8,128)(2,1)} %get-tuple-element.60), channel_id=1, source_target_pairs={{0,64},{16,80},{32,96},{48,112},{64,128},{80,144},{96,160},{112,17... | collective-permute-start | bytes 1769480 | tf_op jit(solution)/shard_map/ppermute | solution.py:399
  41.9 0.4 collective-permute-done.13.sums_b
  42.3 1.9 %collective-permute-start.17 = (bf16[256,1152]{1,0:T(8,128)(2,1)}, bf16[256,1152]{1,0:T(8,128)(2,1)}, u32[]{:S(2)}, u32[]{:S(2)}) collective-permute-start(bf16[256,1152]{1,0:T(8,128)(2,1)} %get-tuple-element.61), channel_id=1, source_target_pairs={{0,192},{16,208},{32,224},{48,240},{64,0},{80,16},{96,32},{112,48}... | collective-permute-start | bytes 1769480 | tf_op jit(solution)/shard_map/ppermute | solution.py:399
  44.2 0.0 collective-permute-done.14.sums_c
  44.2 0.0 collective-permute-done.11.passing.from_core
  44.2 0.9 %relay_y.1 = (bf16[256,1152]{1,0:T(8,128)(2,1)}, f32[8,128]{1,0:T(8,128)S(1)}) custom-call(f32[256,1152]{1,0:T(8,128)S(1)} %get-tuple-element.56.own, bf16[512,1152]{1,0:T(8,128)(2,1)S(1)} %collective-permute-done.11.passing.from_core, f32[8,128]{1,0:T(8,128)S(1)} %get-tuple-element.57.sums, f32[8,128]{1,0:T(8,128)S(1)} %collective-permute-done.12.sums_a, ...), custom_call_target="tpu_custom_call" | custom-call | flops 294912 | bytes 294912 | tf_op jit(solution)/shard_map/relay_y/pallas_call | solution.py:304
  45.2 1.6 %collective-permute-start.15 = (bf16[256,1152]{1,0:T(8,128)(2,1)}, bf16[256,1152]{1,0:T(8,128)(2,1)}, u32[]{:S(2)}, u32[]{:S(2)}) collective-permute-start(bf16[256,1152]{1,0:T(8,128)(2,1)} %get-tuple-element.58), channel_id=1, source_target_pairs={{0,32},{16,48},{32,0},{48,16},{64,96},{80,112},{96,64},{112,80},{1... | collective-permute-start | bytes 1769480 | tf_op jit(solution)/shard_map/ppermute | solution.py:399
  46.7 22.3 %while.10 = (s32[]{:T(128)}, f32[8,128]{1,0:T(8,128)S(1)}, s32[]{:T(128)}) while((s32[]{:T(128)}, f32[8,128]{1,0:T(8,128)S(1)}, s32[]{:T(128)}) %tuple.22), condition=%wide.region_1.0_spmd, body=%wide.region_0.0_spmd.sunk | while | flops 4098 | bytes 114893 | solution.py:438
  47.4 0.2 collective-permute-start
  47.6 3.5 %collective-permute-done = f32[8,128]{1,0:T(8,128)S(1)} collective-permute-done((f32[8,128]{1,0:T(8,128)S(1)}, f32[8,128]{1,0:T(8,128)S(1)}, u32[]{:S(2)}, u32[]{:S(2)}) %collective-permute-start) | collective-permute-done | bytes 4128 | tf_op jit(solution)/shard_map/while/body/ppermute | solution.py:420
  51.1 3.3 %collective-permute-start.1 = (f32[8,128]{1,0:T(8,128)S(1)}, f32[8,128]{1,0:T(8,128)S(1)}, u32[]{:S(2)}, u32[]{:S(2)}) collective-permute-start(f32[8,128]{1,0:T(8,128)S(1)} %add.18), channel_id=1, source_target_pairs={{0,2},{1,3},{2,0},{3,1},{4,6},{5,7},{6,4},{7,5},{8,10},{9,11},{10,... | collective-permute-start | bytes 12296 | tf_op jit(solution)/shard_map/while/body/ppermute | solution.py:420
  54.4 1.6 %collective-permute-done.1 = f32[8,128]{1,0:T(8,128)S(1)} collective-permute-done((f32[8,128]{1,0:T(8,128)S(1)}, f32[8,128]{1,0:T(8,128)S(1)}, u32[]{:S(2)}, u32[]{:S(2)}) %collective-permute-start.1) | collective-permute-done | bytes 4128 | tf_op jit(solution)/shard_map/while/body/ppermute | solution.py:420
  55.9 5.5 %collective-permute-start.2 = (f32[8,128]{1,0:T(8,128)S(1)}, f32[8,128]{1,0:T(8,128)S(1)}, u32[]{:S(2)}, u32[]{:S(2)}) collective-permute-start(f32[8,128]{1,0:T(8,128)S(1)} %add.19), channel_id=1, source_target_pairs={{0,7},{1,6},{2,5},{3,4},{4,3},{5,2},{6,1},{7,0},{8,15},{9,14},{10,... | collective-permute-start | bytes 12296 | tf_op jit(solution)/shard_map/while/body/ppermute | solution.py:420
  61.4 1.6 %collective-permute-done.2 = f32[8,128]{1,0:T(8,128)S(1)} collective-permute-done((f32[8,128]{1,0:T(8,128)S(1)}, f32[8,128]{1,0:T(8,128)S(1)}, u32[]{:S(2)}, u32[]{:S(2)}) %collective-permute-start.2) | collective-permute-done | bytes 4128 | tf_op jit(solution)/shard_map/while/body/ppermute | solution.py:420
  63.0 2.2 %collective-permute-start.3 = (f32[8,128]{1,0:T(8,128)S(1)}, f32[8,128]{1,0:T(8,128)S(1)}, u32[]{:S(2)}, u32[]{:S(2)}) collective-permute-start(f32[8,128]{1,0:T(8,128)S(1)} %add.20), channel_id=1, source_target_pairs={{0,40},{1,41},{2,42},{3,43},{4,44},{5,45},{6,46},{7,47},{8,32},{9,... | collective-permute-start | bytes 12296 | tf_op jit(solution)/shard_map/while/body/ppermute | solution.py:420
  65.9 2.0 %collective-permute-done.3 = f32[8,128]{1,0:T(8,128)S(1)} collective-permute-done((f32[8,128]{1,0:T(8,128)S(1)}, f32[8,128]{1,0:T(8,128)S(1)}, u32[]{:S(2)}, u32[]{:S(2)}) %collective-permute-start.3) | collective-permute-done | bytes 4128 | tf_op jit(solution)/shard_map/while/body/ppermute | solution.py:420
  69.0 0.1 collective-permute-start.19
  69.1 0.0 collective-permute-done.18.from_far
  69.1 1.5 %collective-permute-start.20 = (f32[8,128]{1,0:T(8,128)S(1)}, f32[8,128]{1,0:T(8,128)S(1)}, u32[]{:S(2)}, u32[]{:S(2)}) collective-permute-start(f32[8,128]{1,0:T(8,128)S(1)} %get-tuple-element.65.sums), channel_id=1, source_target_pairs={{0,128},{16,144},{32,160},{48,176},{64,192},{80,208},{96,224},{112... | collective-permute-start | bytes 12296 | tf_op jit(solution)/shard_map/ppermute | solution.py:420
  70.6 0.0 collective-permute-done.16.from_left
  70.6 3.2 %collective-permute-start.21 = (f32[8,128]{1,0:T(8,128)S(1)}, f32[8,128]{1,0:T(8,128)S(1)}, u32[]{:S(2)}, u32[]{:S(2)}) collective-permute-start(f32[8,128]{1,0:T(8,128)S(1)} %get-tuple-element.65.sums), channel_id=1, source_target_pairs={{0,192},{16,208},{32,224},{48,240},{64,128},{80,144},{96,160},{112... | collective-permute-start | bytes 12296 | tf_op jit(solution)/shard_map/ppermute | solution.py:420
  73.8 0.0 collective-permute-done.15.from_y
  73.8 1.1 %copy-done.4 = bf16[256,1152]{1,0:T(8,128)(2,1)S(1)} copy-done((bf16[256,1152]{1,0:T(8,128)(2,1)S(1)}, bf16[256,1152]{1,0:T(8,128)(2,1)}, u32[]{:S(2)}) %copy-start.4) | copy-done | bytes 589848
  74.9 1.1 %copy-done.6 = bf16[256,1152]{1,0:T(8,128)(2,1)S(1)} copy-done((bf16[256,1152]{1,0:T(8,128)(2,1)S(1)}, bf16[256,1152]{1,0:T(8,128)(2,1)}, u32[]{:S(2)}) %copy-start.6) | copy-done | bytes 589848
  76.0 3.9 %end.1 = (f32[256,1152]{1,0:T(8,128)}, f32[256,1152]{1,0:T(8,128)}, f32[8,128]{1,0:T(8,128)S(1)}) custom-call(f32[1]{0:T(128)} %bitcast.8.log_scale, f32[256,1152]{1,0:T(8,128)S(1)} %copy-done, bf16[256,1152]{1,0:T(8,128)(2,1)S(1)} %copy-done.6, bf16[512,1152]{1,0:T(8,128)(2,1)S(1)} %collective-permute-done.11.passing.from_core, ...), custom_call_target="tpu_custom_call" | custom-call | flops 4718592 | bytes 589824 | tf_op jit(solution)/shard_map/end/pallas_call | solution.py:353
  79.9 0.0 collective-permute-done.20.refs_2_
  79.9 0.6 totals.1
  (26 shorter events, 0.1 us)
Async XLA Ops:
  0.6 4.9 %copy-start = (f32[256,1152]{1,0:T(8,128)S(1)}, f32[256,1152]{1,0:T(8,128)}, u32[]{:S(2)}) copy-start(f32[256,1152]{1,0:T(8,128)} %text_emb.1) | copy-start | bytes 3538948
  0.6 1.4 %copy-start.1 = (f32[256,1152]{1,0:T(8,128)S(1)}, f32[256,1152]{1,0:T(8,128)}, u32[]{:S(2)}) copy-start(f32[256,1152]{1,0:T(8,128)} %image_emb.1) | copy-start | bytes 3538948
  2.2 16.4 %collective-permute-start.4 = (bf16[256,1152]{1,0:T(8,128)(2,1)S(1)}, bf16[256,1152]{1,0:T(8,128)(2,1)S(1)}, u32[]{:S(2)}, u32[]{:S(2)}) collective-permute-start(bf16[256,1152]{1,0:T(8,128)(2,1)S(1)} %get-tuple-element.44.own_i), channel_id=1, source_target_pairs={{0,64},{16,80},{32,96},{48,112},{64,128},{80,144},{96,160},{112,17... | collective-permute-start | bytes 1769480 | tf_op jit(solution)/shard_map/ppermute | solution.py:399
  3.8 17.1 %collective-permute-start.6 = (bf16[256,1152]{1,0:T(8,128)(2,1)S(1)}, bf16[256,1152]{1,0:T(8,128)(2,1)S(1)}, u32[]{:S(2)}, u32[]{:S(2)}) collective-permute-start(bf16[256,1152]{1,0:T(8,128)(2,1)S(1)} %get-tuple-element.44.own_i), channel_id=1, source_target_pairs={{0,192},{16,208},{32,224},{48,240},{64,0},{80,16},{96,32},{112,48}... | collective-permute-start | bytes 1769480 | tf_op jit(solution)/shard_map/ppermute | solution.py:399
  6.2 14.6 %collective-permute-start.9 = (bf16[256,1152]{1,0:T(8,128)(2,1)S(1)}, bf16[256,1152]{1,0:T(8,128)(2,1)}, u32[]{:S(2)}, u32[]{:S(2)}) collective-permute-start(bf16[256,1152]{1,0:T(8,128)(2,1)S(1)} %get-tuple-element.46.own_t), channel_id=1, source_target_pairs={{0,32},{16,48},{32,0},{48,16},{64,96},{80,112},{96,64},{112,80},{1... | collective-permute-start | bytes 1769480 | tf_op jit(solution)/shard_map/ppermute | solution.py:399
  7.8 14.9 %collective-permute-start.8 = (bf16[256,1152]{1,0:T(8,128)(2,1)S(1)}, bf16[256,1152]{1,0:T(8,128)(2,1)}, u32[]{:S(2)}, u32[]{:S(2)}) collective-permute-start(bf16[256,1152]{1,0:T(8,128)(2,1)S(1)} %get-tuple-element.46.own_t), channel_id=1, source_target_pairs={{0,16},{16,0},{32,48},{48,32},{64,80},{80,64},{96,112},{112,96},{1... | collective-permute-start | bytes 1769480 | tf_op jit(solution)/shard_map/ppermute | solution.py:399
  18.6 12.8 %collective-permute-start.5 = (bf16[128,1152]{1,0:T(8,128)(2,1)S(1)}, bf16[128,1152]{1,0:T(8,128)(2,1)S(1)}, u32[]{:S(2)}, u32[]{:S(2)}) collective-permute-start(bf16[128,1152]{1,0:T(8,128)(2,1)S(1)} %cut.2), channel_id=1, source_target_pairs={{0,64},{16,80},{32,96},{48,112},{64,128},{80,144},{96,160},{112,17... | collective-permute-start | bytes 884744 | tf_op jit(solution)/shard_map/ppermute | solution.py:399
  20.8 2.2 %collective-permute-start.10 = (bf16[256,1152]{1,0:T(8,128)(2,1)}, bf16[256,1152]{1,0:T(8,128)(2,1)S(1)}, u32[]{:S(2)}, u32[]{:S(2)}) collective-permute-start(bf16[256,1152]{1,0:T(8,128)(2,1)} %collective-permute-done.9.y_t), channel_id=1, source_target_pairs={{0,16},{16,0},{32,48},{48,32},{64,80},{80,64},{96,112},{112,96},{1... | collective-permute-start | bytes 1769480 | tf_op jit(solution)/shard_map/ppermute | solution.py:399
  20.9 10.5 %collective-permute-start.7 = (bf16[128,1152]{1,0:T(8,128)(2,1)S(1)}, bf16[128,1152]{1,0:T(8,128)(2,1)S(1)}, u32[]{:S(2)}, u32[]{:S(2)}) collective-permute-start(bf16[128,1152]{1,0:T(8,128)(2,1)S(1)} %cut.3), channel_id=1, source_target_pairs={{0,192},{16,208},{32,224},{48,240},{64,0},{80,16},{96,32},{112,48}... | collective-permute-start | bytes 884744 | tf_op jit(solution)/shard_map/ppermute | solution.py:399
  31.4 1.4 %copy-start.3 = (bf16[256,1152]{1,0:T(8,128)(2,1)}, bf16[256,1152]{1,0:T(8,128)(2,1)S(1)}, u32[]{:S(2)}) copy-start(bf16[256,1152]{1,0:T(8,128)(2,1)S(1)} %get-tuple-element.59.own_p) | copy-start | bytes 1769476
  37.0 8.2 %copy-start.5 = (bf16[256,1152]{1,0:T(8,128)(2,1)}, bf16[256,1152]{1,0:T(8,128)(2,1)S(1)}, u32[]{:S(2)}) copy-start(bf16[256,1152]{1,0:T(8,128)(2,1)S(1)} %get-tuple-element.54.own_q) | copy-start | bytes 1769476
  37.0 7.2 %collective-permute-start.11 = (bf16[512,1152]{1,0:T(8,128)(2,1)S(1)}, bf16[512,1152]{1,0:T(8,128)(2,1)S(1)}, u32[]{:S(2)}, u32[]{:S(2)}) collective-permute-start(bf16[512,1152]{1,0:T(8,128)(2,1)S(1)} %get-tuple-element.55), channel_id=1, source_target_pairs={{0,16},{16,0},{32,48},{48,32},{64,80},{80,64},{96,112},{112,96},{1... | collective-permute-start | bytes 3538952 | tf_op jit(solution)/shard_map/ppermute | solution.py:399
  37.1 3.8 %collective-permute-start.12 = (f32[8,128]{1,0:T(8,128)S(1)}, f32[8,128]{1,0:T(8,128)S(1)}, u32[]{:S(2)}, u32[]{:S(2)}) collective-permute-start(f32[8,128]{1,0:T(8,128)S(1)} %get-tuple-element.53.sums), channel_id=1, source_target_pairs={{0,48},{16,32},{32,16},{48,0},{64,112},{80,96},{96,80},{112,64},{1... | collective-permute-start | bytes 12296 | tf_op jit(solution)/shard_map/ppermute | solution.py:420
  38.7 3.6 %collective-permute-start.13 = (f32[8,128]{1,0:T(8,128)S(1)}, f32[8,128]{1,0:T(8,128)S(1)}, u32[]{:S(2)}, u32[]{:S(2)}) collective-permute-start(f32[8,128]{1,0:T(8,128)S(1)} %get-tuple-element.53.sums), channel_id=1, source_target_pairs={{0,32},{16,48},{32,0},{48,16},{64,96},{80,112},{96,64},{112,80},{1... | collective-permute-start | bytes 12296 | tf_op jit(solution)/shard_map/ppermute | solution.py:420
  39.1 5.1 %collective-permute-start.14 = (f32[8,128]{1,0:T(8,128)S(1)}, f32[8,128]{1,0:T(8,128)S(1)}, u32[]{:S(2)}, u32[]{:S(2)}) collective-permute-start(f32[8,128]{1,0:T(8,128)S(1)} %get-tuple-element.53.sums), channel_id=1, source_target_pairs={{0,16},{16,0},{32,48},{48,32},{64,80},{80,64},{96,112},{112,96},{1... | collective-permute-start | bytes 12296 | tf_op jit(solution)/shard_map/ppermute | solution.py:420
  39.1 30.0 %collective-permute-start.18 = (bf16[256,1152]{1,0:T(8,128)(2,1)}, bf16[256,1152]{1,0:T(8,128)(2,1)}, u32[]{:S(2)}, u32[]{:S(2)}) collective-permute-start(bf16[256,1152]{1,0:T(8,128)(2,1)} %get-tuple-element.62), channel_id=1, source_target_pairs={{0,128},{16,144},{32,160},{48,176},{64,192},{80,208},{96,224},{112... | collective-permute-start | bytes 1769480 | tf_op jit(solution)/shard_map/ppermute | solution.py:399
  41.0 29.6 %collective-permute-start.16 = (bf16[256,1152]{1,0:T(8,128)(2,1)}, bf16[256,1152]{1,0:T(8,128)(2,1)}, u32[]{:S(2)}, u32[]{:S(2)}) collective-permute-start(bf16[256,1152]{1,0:T(8,128)(2,1)} %get-tuple-element.60), channel_id=1, source_target_pairs={{0,64},{16,80},{32,96},{48,112},{64,128},{80,144},{96,160},{112,17... | collective-permute-start | bytes 1769480 | tf_op jit(solution)/shard_map/ppermute | solution.py:399
  42.3 31.5 %collective-permute-start.17 = (bf16[256,1152]{1,0:T(8,128)(2,1)}, bf16[256,1152]{1,0:T(8,128)(2,1)}, u32[]{:S(2)}, u32[]{:S(2)}) collective-permute-start(bf16[256,1152]{1,0:T(8,128)(2,1)} %get-tuple-element.61), channel_id=1, source_target_pairs={{0,192},{16,208},{32,224},{48,240},{64,0},{80,16},{96,32},{112,48}... | collective-permute-start | bytes 1769480 | tf_op jit(solution)/shard_map/ppermute | solution.py:399
  44.2 29.6 %copy-start.2 = (f32[256,1152]{1,0:T(8,128)S(1)}, f32[256,1152]{1,0:T(8,128)}, u32[]{:S(2)}) copy-start(f32[256,1152]{1,0:T(8,128)} %image_emb.1) | copy-start | bytes 3538948
  45.2 28.7 %collective-permute-start.15 = (bf16[256,1152]{1,0:T(8,128)(2,1)}, bf16[256,1152]{1,0:T(8,128)(2,1)}, u32[]{:S(2)}, u32[]{:S(2)}) collective-permute-start(bf16[256,1152]{1,0:T(8,128)(2,1)} %get-tuple-element.58), channel_id=1, source_target_pairs={{0,32},{16,48},{32,0},{48,16},{64,96},{80,112},{96,64},{112,80},{1... | collective-permute-start | bytes 1769480 | tf_op jit(solution)/shard_map/ppermute | solution.py:399
  47.4 3.7 %collective-permute-start = (f32[8,128]{1,0:T(8,128)S(1)}, f32[8,128]{1,0:T(8,128)S(1)}, u32[]{:S(2)}, u32[]{:S(2)}) collective-permute-start(f32[8,128]{1,0:T(8,128)S(1)} %get-tuple-element.93), channel_id=1, source_target_pairs={{0,1},{1,0},{2,3},{3,2},{4,5},{5,4},{6,7},{7,6},{8,9},{9,8},{10,11... | collective-permute-start | bytes 12296 | tf_op jit(solution)/shard_map/while/body/ppermute | solution.py:420
  51.1 4.9 %collective-permute-start.1 = (f32[8,128]{1,0:T(8,128)S(1)}, f32[8,128]{1,0:T(8,128)S(1)}, u32[]{:S(2)}, u32[]{:S(2)}) collective-permute-start(f32[8,128]{1,0:T(8,128)S(1)} %add.18), channel_id=1, source_target_pairs={{0,2},{1,3},{2,0},{3,1},{4,6},{5,7},{6,4},{7,5},{8,10},{9,11},{10,... | collective-permute-start | bytes 12296 | tf_op jit(solution)/shard_map/while/body/ppermute | solution.py:420
  55.9 7.1 %collective-permute-start.2 = (f32[8,128]{1,0:T(8,128)S(1)}, f32[8,128]{1,0:T(8,128)S(1)}, u32[]{:S(2)}, u32[]{:S(2)}) collective-permute-start(f32[8,128]{1,0:T(8,128)S(1)} %add.19), channel_id=1, source_target_pairs={{0,7},{1,6},{2,5},{3,4},{4,3},{5,2},{6,1},{7,0},{8,15},{9,14},{10,... | collective-permute-start | bytes 12296 | tf_op jit(solution)/shard_map/while/body/ppermute | solution.py:420
  63.0 4.8 %collective-permute-start.3 = (f32[8,128]{1,0:T(8,128)S(1)}, f32[8,128]{1,0:T(8,128)S(1)}, u32[]{:S(2)}, u32[]{:S(2)}) collective-permute-start(f32[8,128]{1,0:T(8,128)S(1)} %add.20), channel_id=1, source_target_pairs={{0,40},{1,41},{2,42},{3,43},{4,44},{5,45},{6,46},{7,47},{8,32},{9,... | collective-permute-start | bytes 12296 | tf_op jit(solution)/shard_map/while/body/ppermute | solution.py:420
  69.0 10.9 %collective-permute-start.19 = (f32[8,128]{1,0:T(8,128)S(1)}, f32[8,128]{1,0:T(8,128)S(1)}, u32[]{:S(2)}, u32[]{:S(2)}) collective-permute-start(f32[8,128]{1,0:T(8,128)S(1)} %get-tuple-element.65.sums), channel_id=1, source_target_pairs={{0,64},{16,80},{32,96},{48,112},{64,0},{80,16},{96,32},{112,48},{1... | collective-permute-start | bytes 12296 | tf_op jit(solution)/shard_map/ppermute | solution.py:420
  69.1 10.8 %collective-permute-start.20 = (f32[8,128]{1,0:T(8,128)S(1)}, f32[8,128]{1,0:T(8,128)S(1)}, u32[]{:S(2)}, u32[]{:S(2)}) collective-permute-start(f32[8,128]{1,0:T(8,128)S(1)} %get-tuple-element.65.sums), channel_id=1, source_target_pairs={{0,128},{16,144},{32,160},{48,176},{64,192},{80,208},{96,224},{112... | collective-permute-start | bytes 12296 | tf_op jit(solution)/shard_map/ppermute | solution.py:420
  70.6 9.3 %collective-permute-start.21 = (f32[8,128]{1,0:T(8,128)S(1)}, f32[8,128]{1,0:T(8,128)S(1)}, u32[]{:S(2)}, u32[]{:S(2)}) collective-permute-start(f32[8,128]{1,0:T(8,128)S(1)} %get-tuple-element.65.sums), channel_id=1, source_target_pairs={{0,192},{16,208},{32,224},{48,240},{64,128},{80,144},{96,160},{112... | collective-permute-start | bytes 12296 | tf_op jit(solution)/shard_map/ppermute | solution.py:420
  73.8 1.1 %copy-start.4 = (bf16[256,1152]{1,0:T(8,128)(2,1)S(1)}, bf16[256,1152]{1,0:T(8,128)(2,1)}, u32[]{:S(2)}) copy-start(bf16[256,1152]{1,0:T(8,128)(2,1)} %copy-done.3) | copy-start | bytes 1769476
  74.9 1.1 %copy-start.6 = (bf16[256,1152]{1,0:T(8,128)(2,1)S(1)}, bf16[256,1152]{1,0:T(8,128)(2,1)}, u32[]{:S(2)}) copy-start(bf16[256,1152]{1,0:T(8,128)(2,1)} %copy-done.5) | copy-start | bytes 1769476

commit v9 on v8

--- a/solution.py
+++ b/solution.py
@@ -119,9 +119,8 @@
 ):
     rows = own_i.shape[0]
     factor, scale, bias = logit_factors(log_scale, bias, rows)
-    blocks = [(own_i, images, 0), (own_t, texts, 0)]
+    blocks = [(own_i, images, 0), (own_t, texts, 0), (left_i, images, 1), (right_i, images, 2)]
     blocks += [(src, texts, i) for i, src in enumerate((core_t, y_t, yc_t), 1)]
-    blocks += [(src, images, i) for i, src in enumerate((left_i, right_i), 1)]
     copies = [
         pltpu.make_async_copy(src, dst.at[pl.ds(i * rows, rows)], sems.at[k])
         for k, (src, dst, i) in enumerate(blocks)
@@ -131,7 +130,7 @@
     copies[0].wait()
     copies[1].wait()
     loss = scaled = grad = jnp.zeros((8, rows), F32)
-    tiles = [(b, t) for b in range(3) for t in range(4)]
+    tiles = [(b, t) for t in range(4) for b in range(3)]
 
     def sim_of(k):
         b, t = tiles[k]
@@ -139,10 +138,10 @@
 
     sim = sim_of(0)
     for k, (b, t) in enumerate(tiles):
-        if k < 3:
+        if k < 2:
             copies[k + 2].wait()
-        elif k in (3, 7):
-            copies[5 + k // 7].wait()
+        elif k in (2, 5, 8):
+            copies[k // 3 + 4].wait()
         sim_next = sim_of(k + 1) if k + 1 < len(tiles) else None
         grad_q, loss_now, scaled_now, grad_now = pair_tile(sim, scale, bias, k == 0)
         grads[pl.ds(b * rows, rows), pl.ds(t * rows, rows)] = grad_q
@@ -190,22 +189,29 @@
 
 def far_grad_kernel(
     far_images, far_grads, near_images, texts, near_grads, sums,
-    far_out, y_out, mate_out, own_out, sums_out,
+    far_out, mate_out, own_out, y_out, sums_out, blocks, sems,
 ):
     rows = far_images.shape[0]
-    far_out[...] = jnp.dot(
-        far_grads[...], texts[...], preferred_element_type=F32
-    ).astype(BF16)
-    for t, out in (
-        (3, mate_out.at[pl.ds(0, rows)]),
-        (1, mate_out.at[pl.ds(rows, rows)]),
-        (2, y_out),
-        (0, own_out),
-    ):
-        out[...] = text_grad(
-            near_grads, near_images, far_grads, far_images, pl.ds(t * rows, rows)
-        ).astype(out.dtype)
+    copies = []
+
+    def leave(values, out):
+        i = len(copies)
+        blocks[i] = values.astype(BF16)
+        copy = pltpu.make_async_copy(blocks.at[i], out, sems.at[i])
+        copy.start()
+        copies.append(copy)
+
+    def text_block(t):
+        return text_grad(near_grads, near_images, far_grads, far_images, pl.ds(t * rows, rows))
+
+    leave(jnp.dot(far_grads[...], texts[...], preferred_element_type=F32), far_out)
+    leave(text_block(3), mate_out.at[pl.ds(0, rows)])
+    leave(text_block(1), mate_out.at[pl.ds(rows, rows)])
+    leave(text_block(0), own_out)
+    y_out[...] = text_block(2)
     sums_out[...] = sums[...]
+    for copy in copies:
+        copy.wait()
 
 
 def near_part(scalars, images, texts):
@@ -261,11 +267,12 @@
     return pl.pallas_call(
         far_grad_kernel,
         out_shape=(
-            shape((rows, width), BF16), shape((rows, width), F32), shape((2 * rows, width), BF16),
-            shape((rows, width), BF16), shape(sums.shape, F32),
+            shape((rows, width), BF16), shape((2 * rows, width), BF16), shape((rows, width), BF16),
+            shape((rows, width), F32), shape(sums.shape, F32),
         ),
         in_specs=[VMEM] * 6,
-        out_specs=(VMEM,) * 5,
+        out_specs=(ANY,) * 3 + (VMEM,) * 2,
+        scratch_shapes=[pltpu.VMEM((4, rows, width), BF16), pltpu.SemaphoreType.DMA((4,))],
         compiler_params=params(16),
         cost_estimate=pl.CostEstimate(
             flops=rows * rows * width, bytes_accessed=2 * rows * width, transcendentals=0
@@ -322,24 +329,28 @@
 
 def end_kernel(
     log_scale, text_emb, own_q, from_core, from_y, image_emb, own_p, from_left, from_right, from_far,
-    sums, text_out, image_out, sums_out, text_slots, image_slots, sems,
+    sums, text_out, image_out, sums_out, embs, blocks, in_sems, out_sems,
 ):
     scale = jnp.exp(jnp.full((1, 1), log_scale[0]))
-    step = text_emb.shape[0] // 4
-    sets = (
-        (text_emb, (own_q, from_core, from_y), text_out, text_slots),
-        (image_emb, (own_p, from_left, from_right, from_far), image_out, image_slots),
-    )
+    rows = embs.shape[1]
+    step = rows // 4
+    sources = (own_q, from_core.at[pl.ds(rows, rows)], from_y, own_p, from_left, from_right, from_far)
+    pairs = [(text_emb, embs.at[0])] + [(sources[i], blocks.at[i]) for i in range(3)]
+    pairs += [(image_emb, embs.at[1])] + [(sources[i], blocks.at[i]) for i in range(3, 7)]
+    loads = [pltpu.make_async_copy(src, dst, in_sems.at[k]) for k, (src, dst) in enumerate(pairs)]
+    for load in loads:
+        load.start()
     copies = []
-    for emb, parts, out, slots in sets:
+    for k, (parts, out) in enumerate(((range(3), text_out), (range(3, 7), image_out))):
+        for load in loads[5 * k - k : 4 + 5 * k]:
+            load.wait()
         for i in range(4):
             at = pl.ds(i * step, step)
-            upstream = jnp.zeros((step, emb.shape[1]), F32)
+            upstream = jnp.zeros((step, embs.shape[2]), F32)
             for part in parts:
-                skip = part.shape[0] - 4 * step
-                upstream += part[pl.ds(skip + i * step, step), :].astype(F32)
-            slots[at, :] = backnorm(emb[at, :], upstream, scale)
-            copy = pltpu.make_async_copy(slots.at[at], out.at[at], sems.at[len(copies)])
+                upstream += blocks[part, at, :].astype(F32)
+            embs[k, at, :] = backnorm(embs[k, at, :], upstream, scale)
+            copy = pltpu.make_async_copy(embs.at[k, at], out.at[at], out_sems.at[len(copies)])
             copy.start()
             copies.append(copy)
     sums_out[...] = sums[...]
@@ -353,11 +364,12 @@
     return pl.pallas_call(
         end_kernel,
         out_shape=(shape((rows, width), F32),) * 2 + (shape(sums.shape, F32),),
-        in_specs=[SMEM] + [VMEM] * 10,
+        in_specs=[SMEM] + [ANY] * 9 + [VMEM],
         out_specs=(HBM, HBM, VMEM),
         scratch_shapes=[
-            pltpu.VMEM((rows, width), F32),
-            pltpu.VMEM((rows, width), F32),
+            pltpu.VMEM((2, rows, width), F32),
+            pltpu.VMEM((7, rows, width), BF16),
+            pltpu.SemaphoreType.DMA((9,)),
             pltpu.SemaphoreType.DMA((8,)),
         ],
         compiler_params=params(24),
@@ -420,7 +432,7 @@
         return lax.ppermute(value, axis, [(i, i ^ k) for i in range(lax.axis_size(axis))])
 
     over_y_core = [pair(sums, "blk", k) for k in (3, 2, 1)]
-    far_p, y_q, to_mate, own_q, sums = far_grad_part(
+    far_p, to_mate, own_q, y_q, sums = far_grad_part(
         far_images, far_grads, near_images, texts, near_grads, sums
     )
     from_far = send(far_p, [(i, (i + 8) % blocks) for i in range(blocks)])

time: 81.1 us -> 82.1 us (1.012)
  Pallas kernels: 20.3 us -> 21.3 us
  transfers between devices with their start and end apart: 22 -> 22, of which waited for: 8 -> 8; matrix products, arithmetic and copies ran while one was open for 0% -> 0% of each run, Pallas kernels for 17% -> 18%
where the time goes in v9:
time: 82.1 us; the launch traced here: 81.8 us
  starting transfers between devices  31 us (38%)
  Pallas kernels  21.3 us (26%)
  waiting for transfers between devices  21.3 us (26%)
  local copies, waits for them, and re-layouts  3.5 us (4%)
  loops' own time  2.47 us (3%)
  between operations  2.29 us (3%)
    ppermute x10, starting transfers between devices, pair(): lax.ppermute(value, axis, [(i, i ^ k) for i in range(lax.axis_size(axis))])  18 us
    ppermute x12, starting transfers between devices, send(): return lax.ppermute(value, 'blk', perm)  12.9 us
    ppermute x12, waiting for transfers between devices, send(): return lax.ppermute(value, 'blk', perm)  11.7 us
    ppermute x10, waiting for transfers between devices, pair(): lax.ppermute(value, axis, [(i, i ^ k) for i in range(lax.axis_size(axis))])  9.55 us
    pallas_call x1, Pallas kernels, near_part(): pl.pallas_call(near_kernel, out_shape=(shape((rows, width), BF16), shape(...  8.9 us
    pallas_call x1, Pallas kernels, far_grad_part(): pl.pallas_call(far_grad_kernel, out_shape=(shape((rows, width), BF16), sh...  4.58 us
    pallas_call x1, Pallas kernels, end_part(): pl.pallas_call(end_kernel, out_shape=(shape((rows, width), F32),) * 2 + (...  3.96 us
    unnamed x14, local copies, waits for them, and re-layouts  3.5 us
  transfers between devices with their start and end apart: 22, of which 8 were waited for; matrix products, arithmetic and copies ran while one was open for 0% of the time, Pallas kernels for 18%

profile of v9, /device:TPU:32, one launch (start us, length us, event | category | flops | bytes accessed | tf_op | source)
XLA Modules:
  0.0 81.8 jit_solution(18039556152133075766)
XLA Ops:
  0.6 0.0 copy-start.1
  0.7 1.4 %copy-done.1 = f32[256,1152]{1,0:T(8,128)S(1)} copy-done((f32[256,1152]{1,0:T(8,128)S(1)}, f32[256,1152]{1,0:T(8,128)}, u32[]{:S(2)}) %copy-start.1) | copy-done | bytes 1179672
  2.0 0.2 normalize.2
  2.2 1.6 %collective-permute-start.4 = (bf16[256,1152]{1,0:T(8,128)(2,1)S(1)}, bf16[256,1152]{1,0:T(8,128)(2,1)S(1)}, u32[]{:S(2)}, u32[]{:S(2)}) collective-permute-start(bf16[256,1152]{1,0:T(8,128)(2,1)S(1)} %get-tuple-element.44.own_i), channel_id=1, source_target_pairs={{0,64},{16,80},{32,96},{48,112},{64,128},{80,144},{96,160},{112,17... | collective-permute-start | bytes 1769480 | tf_op jit(solution)/shard_map/ppermute | solution.py:411
  3.8 1.7 %collective-permute-start.6 = (bf16[256,1152]{1,0:T(8,128)(2,1)S(1)}, bf16[256,1152]{1,0:T(8,128)(2,1)S(1)}, u32[]{:S(2)}, u32[]{:S(2)}) collective-permute-start(bf16[256,1152]{1,0:T(8,128)(2,1)S(1)} %get-tuple-element.44.own_i), channel_id=1, source_target_pairs={{0,192},{16,208},{32,224},{48,240},{64,0},{80,16},{96,32},{112,48}... | collective-permute-start | bytes 1769480 | tf_op jit(solution)/shard_map/ppermute | solution.py:411
  5.5 0.7 normalize.3
  6.2 1.6 %collective-permute-start.9 = (bf16[256,1152]{1,0:T(8,128)(2,1)S(1)}, bf16[256,1152]{1,0:T(8,128)(2,1)}, u32[]{:S(2)}, u32[]{:S(2)}) collective-permute-start(bf16[256,1152]{1,0:T(8,128)(2,1)S(1)} %get-tuple-element.46.own_t), channel_id=1, source_target_pairs={{0,32},{16,48},{32,0},{48,16},{64,96},{80,112},{96,64},{112,80},{1... | collective-permute-start | bytes 1769480 | tf_op jit(solution)/shard_map/ppermute | solution.py:411
  7.8 0.0 collective-permute-start.8
  9.1 9.5 %collective-permute-done.4.block_ref.left_i = bf16[256,1152]{1,0:T(8,128)(2,1)S(1)} collective-permute-done((bf16[256,1152]{1,0:T(8,128)(2,1)S(1)}, bf16[256,1152]{1,0:T(8,128)(2,1)S(1)}, u32[]{:S(2)}, u32[]{:S(2)}) %collective-permute-start.4) | collective-permute-done | bytes 589856 | tf_op jit(solution)/shard_map/ppermute | solution.py:411
  18.6 0.4 collective-permute-start.5
  18.9 1.9 %collective-permute-done.9.y_t = bf16[256,1152]{1,0:T(8,128)(2,1)} collective-permute-done((bf16[256,1152]{1,0:T(8,128)(2,1)S(1)}, bf16[256,1152]{1,0:T(8,128)(2,1)}, u32[]{:S(2)}, u32[]{:S(2)}) %collective-permute-start.9) | collective-permute-done | bytes 589856 | tf_op jit(solution)/shard_map/ppermute | solution.py:411
  20.8 0.0 collective-permute-start.10
  20.8 0.0 collective-permute-done.6.block_ref.right_i
  20.9 1.8 %collective-permute-start.7 = (bf16[128,1152]{1,0:T(8,128)(2,1)S(1)}, bf16[128,1152]{1,0:T(8,128)(2,1)S(1)}, u32[]{:S(2)}, u32[]{:S(2)}) collective-permute-start(bf16[128,1152]{1,0:T(8,128)(2,1)S(1)} %cut.3), channel_id=1, source_target_pairs={{0,192},{16,208},{32,224},{48,240},{64,0},{80,16},{96,32},{112,48}... | collective-permute-start | bytes 884744 | tf_op jit(solution)/shard_map/ppermute | solution.py:411
  22.7 0.0 collective-permute-done.8.core_t
  22.7 0.4 collective-permute-done.10.yc_t
  23.0 8.9 %near.1 = (bf16[256,1152]{1,0:T(8,128)(2,1)S(1)}, bf16[256,1152]{1,0:T(8,128)(2,1)}, bf16[256,1152]{1,0:T(8,128)(2,1)}, bf16[768,1152]{1,0:T(8,128)(2,1)S(1)}, b...) custom-call(f32[1]{0:T(128)} %bitcast.6.log_scale, ...), custom_call_target="tpu_custom_call" | custom-call | flops 28991029248 | bytes 7077888 | tf_op jit(solution)/shard_map/near/pallas_call | solution.py:220
  32.0 0.0 collective-permute-done.5.top_i
  32.0 0.0 collective-permute-done.7.bot_i
  32.0 1.4 %far.1 = (bf16[256,1152]{1,0:T(8,128)(2,1)S(1)}, bf16[256,1024]{1,0:T(8,128)(2,1)S(1)}, f32[8,128]{1,0:T(8,128)S(1)}) custom-call(f32[1]{0:T(128)} %bitcast.7.log_scale, f32[1]{0:T(128)} %bitcast.10.bias, bf16[128,1152]{1,0:T(8,128)(2,1)S(1)} %collective-permute-done.5.top_i, bf16[128,1152]{1,0:T(8,128)(2,1)S(1)} %collective-permute-done.7.bot_i, ...), custom_call_target="tpu_custom_call" | custom-call | flops 75497472 | bytes 589824 | tf_op jit(solution)/shard_map/far/pallas_call | solution.py:249
  33.4 4.6 %far_grad.1 = (bf16[256,1152]{1,0:T(8,128)(2,1)}, bf16[512,1152]{1,0:T(8,128)(2,1)S(1)}, bf16[256,1152]{1,0:T(8,128)(2,1)S(1)}, f32[256,1152]{1,0:T(8,128)S(1)}, f32[8,128]{1,0:T(8,128)S(1)}) custom-call(bf16[256,1152]{1,0:T(8,128)(2,1)S(1)} %get-tuple-element.49.far_images, bf16[256,1024]{1,0:T(8,128)(2,1)S(1)} %get-tuple-element.50.far_grads, ...), custom_call_target="tpu_custom_call" | custom-call | flops 75497472 | bytes 589824 | tf_op jit(solution)/shard_map/far_grad/pallas_call | solution.py:267
  38.0 0.2 collective-permute-start.11
  38.1 1.6 %collective-permute-start.12 = (f32[8,128]{1,0:T(8,128)S(1)}, f32[8,128]{1,0:T(8,128)S(1)}, u32[]{:S(2)}, u32[]{:S(2)}) collective-permute-start(f32[8,128]{1,0:T(8,128)S(1)} %get-tuple-element.53.sums), channel_id=1, source_target_pairs={{0,48},{16,32},{32,16},{48,0},{64,112},{80,96},{96,80},{112,64},{1... | collective-permute-start | bytes 12296 | tf_op jit(solution)/shard_map/ppermute | solution.py:432
  39.7 0.5 collective-permute-start.13
  40.2 0.0 collective-permute-start.14
  40.2 1.7 %collective-permute-start.18 = (bf16[256,1152]{1,0:T(8,128)(2,1)}, bf16[256,1152]{1,0:T(8,128)(2,1)}, u32[]{:S(2)}, u32[]{:S(2)}) collective-permute-start(bf16[256,1152]{1,0:T(8,128)(2,1)} %get-tuple-element.62), channel_id=1, source_target_pairs={{0,128},{16,144},{32,160},{48,176},{64,192},{80,208},{96,224},{112... | collective-permute-start | bytes 1769480 | tf_op jit(solution)/shard_map/ppermute | solution.py:411
  41.9 0.0 collective-permute-done.12.sums_a
  41.9 0.6 collective-permute-start.16
  42.5 0.8 collective-permute-done.13.sums_b
  43.4 1.8 %collective-permute-start.17 = (bf16[256,1152]{1,0:T(8,128)(2,1)}, bf16[256,1152]{1,0:T(8,128)(2,1)}, u32[]{:S(2)}, u32[]{:S(2)}) collective-permute-start(bf16[256,1152]{1,0:T(8,128)(2,1)} %get-tuple-element.61), channel_id=1, source_target_pairs={{0,192},{16,208},{32,224},{48,240},{64,0},{80,16},{96,32},{112,48}... | collective-permute-start | bytes 1769480 | tf_op jit(solution)/shard_map/ppermute | solution.py:411
  45.2 0.9 %relay_y.1 = (bf16[256,1152]{1,0:T(8,128)(2,1)}, f32[8,128]{1,0:T(8,128)S(1)}) custom-call(f32[256,1152]{1,0:T(8,128)S(1)} %get-tuple-element.56.own, bf16[512,1152]{1,0:T(8,128)(2,1)S(1)} %collective-permute-done.11.passing.from_core, f32[8,128]{1,0:T(8,128)S(1)} %get-tuple-element.57.sums, f32[8,128]{1,0:T(8,128)S(1)} %collective-permute-done.12.sums_a, ...), custom_call_target="tpu_custom_call" | custom-call | flops 294912 | bytes 294912 | tf_op jit(solution)/shard_map/relay_y/pallas_call | solution.py:311
  46.1 1.6 %collective-permute-start.15 = (bf16[256,1152]{1,0:T(8,128)(2,1)}, bf16[256,1152]{1,0:T(8,128)(2,1)}, u32[]{:S(2)}, u32[]{:S(2)}) collective-permute-start(bf16[256,1152]{1,0:T(8,128)(2,1)} %get-tuple-element.58), channel_id=1, source_target_pairs={{0,32},{16,48},{32,0},{48,16},{64,96},{80,112},{96,64},{112,80},{1... | collective-permute-start | bytes 1769480 | tf_op jit(solution)/shard_map/ppermute | solution.py:411
  47.7 22.4 %while.10 = (s32[]{:T(128)}, f32[8,128]{1,0:T(8,128)S(1)}, s32[]{:T(128)}) while((s32[]{:T(128)}, f32[8,128]{1,0:T(8,128)S(1)}, s32[]{:T(128)}) %tuple.22), condition=%wide.region_1.0_spmd, body=%wide.region_0.0_spmd.sunk | while | flops 4098 | bytes 114893 | solution.py:450
  48.4 0.2 collective-permute-start
  48.6 3.5 %collective-permute-done = f32[8,128]{1,0:T(8,128)S(1)} collective-permute-done((f32[8,128]{1,0:T(8,128)S(1)}, f32[8,128]{1,0:T(8,128)S(1)}, u32[]{:S(2)}, u32[]{:S(2)}) %collective-permute-start) | collective-permute-done | bytes 4128 | tf_op jit(solution)/shard_map/while/body/ppermute | solution.py:432
  52.1 3.3 %collective-permute-start.1 = (f32[8,128]{1,0:T(8,128)S(1)}, f32[8,128]{1,0:T(8,128)S(1)}, u32[]{:S(2)}, u32[]{:S(2)}) collective-permute-start(f32[8,128]{1,0:T(8,128)S(1)} %add.18), channel_id=1, source_target_pairs={{0,2},{1,3},{2,0},{3,1},{4,6},{5,7},{6,4},{7,5},{8,10},{9,11},{10,... | collective-permute-start | bytes 12296 | tf_op jit(solution)/shard_map/while/body/ppermute | solution.py:432
  55.3 1.6 %collective-permute-done.1 = f32[8,128]{1,0:T(8,128)S(1)} collective-permute-done((f32[8,128]{1,0:T(8,128)S(1)}, f32[8,128]{1,0:T(8,128)S(1)}, u32[]{:S(2)}, u32[]{:S(2)}) %collective-permute-start.1) | collective-permute-done | bytes 4128 | tf_op jit(solution)/shard_map/while/body/ppermute | solution.py:432
  56.9 5.6 %collective-permute-start.2 = (f32[8,128]{1,0:T(8,128)S(1)}, f32[8,128]{1,0:T(8,128)S(1)}, u32[]{:S(2)}, u32[]{:S(2)}) collective-permute-start(f32[8,128]{1,0:T(8,128)S(1)} %add.19), channel_id=1, source_target_pairs={{0,7},{1,6},{2,5},{3,4},{4,3},{5,2},{6,1},{7,0},{8,15},{9,14},{10,... | collective-permute-start | bytes 12296 | tf_op jit(solution)/shard_map/while/body/ppermute | solution.py:432
  62.5 1.6 %collective-permute-done.2 = f32[8,128]{1,0:T(8,128)S(1)} collective-permute-done((f32[8,128]{1,0:T(8,128)S(1)}, f32[8,128]{1,0:T(8,128)S(1)}, u32[]{:S(2)}, u32[]{:S(2)}) %collective-permute-start.2) | collective-permute-done | bytes 4128 | tf_op jit(solution)/shard_map/while/body/ppermute | solution.py:432
  64.1 2.1 %collective-permute-start.3 = (f32[8,128]{1,0:T(8,128)S(1)}, f32[8,128]{1,0:T(8,128)S(1)}, u32[]{:S(2)}, u32[]{:S(2)}) collective-permute-start(f32[8,128]{1,0:T(8,128)S(1)} %add.20), channel_id=1, source_target_pairs={{0,40},{1,41},{2,42},{3,43},{4,44},{5,45},{6,46},{7,47},{8,32},{9,... | collective-permute-start | bytes 12296 | tf_op jit(solution)/shard_map/while/body/ppermute | solution.py:432
  66.8 2.1 %collective-permute-done.3 = f32[8,128]{1,0:T(8,128)S(1)} collective-permute-done((f32[8,128]{1,0:T(8,128)S(1)}, f32[8,128]{1,0:T(8,128)S(1)}, u32[]{:S(2)}, u32[]{:S(2)}) %collective-permute-start.3) | collective-permute-done | bytes 4128 | tf_op jit(solution)/shard_map/while/body/ppermute | solution.py:432
  70.1 0.1 collective-permute-start.19
  70.2 1.5 %collective-permute-start.20 = (f32[8,128]{1,0:T(8,128)S(1)}, f32[8,128]{1,0:T(8,128)S(1)}, u32[]{:S(2)}, u32[]{:S(2)}) collective-permute-start(f32[8,128]{1,0:T(8,128)S(1)} %get-tuple-element.65.sums), channel_id=1, source_target_pairs={{0,128},{16,144},{32,160},{48,176},{64,192},{80,208},{96,224},{112... | collective-permute-start | bytes 12296 | tf_op jit(solution)/shard_map/ppermute | solution.py:432
  71.6 3.2 %collective-permute-start.21 = (f32[8,128]{1,0:T(8,128)S(1)}, f32[8,128]{1,0:T(8,128)S(1)}, u32[]{:S(2)}, u32[]{:S(2)}) collective-permute-start(f32[8,128]{1,0:T(8,128)S(1)} %get-tuple-element.65.sums), channel_id=1, source_target_pairs={{0,192},{16,208},{32,224},{48,240},{64,128},{80,144},{96,160},{112... | collective-permute-start | bytes 12296 | tf_op jit(solution)/shard_map/ppermute | solution.py:432
  74.9 1.1 %copy-done.4 = bf16[256,1152]{1,0:T(8,128)(2,1)S(1)} copy-done((bf16[256,1152]{1,0:T(8,128)(2,1)S(1)}, bf16[256,1152]{1,0:T(8,128)(2,1)}, u32[]{:S(2)}) %copy-start.4) | copy-done | bytes 589848
  75.9 1.1 %copy-done.6 = bf16[256,1152]{1,0:T(8,128)(2,1)S(1)} copy-done((bf16[256,1152]{1,0:T(8,128)(2,1)S(1)}, bf16[256,1152]{1,0:T(8,128)(2,1)}, u32[]{:S(2)}) %copy-start.6) | copy-done | bytes 589848
  77.0 4.0 %end.1 = (f32[256,1152]{1,0:T(8,128)}, f32[256,1152]{1,0:T(8,128)}, f32[8,128]{1,0:T(8,128)S(1)}) custom-call(f32[1]{0:T(128)} %bitcast.8.log_scale, f32[256,1152]{1,0:T(8,128)S(1)} %copy-done, bf16[256,1152]{1,0:T(8,128)(2,1)S(1)} %copy-done.6, bf16[512,1152]{1,0:T(8,128)(2,1)S(1)} %collective-permute-done.11.passing.from_core, ...), custom_call_target="tpu_custom_call" | custom-call | flops 4718592 | bytes 589824 | tf_op jit(solution)/shard_map/end/pallas_call | solution.py:364
  81.0 0.6 totals.1
  (26 shorter events, 0.1 us)
Async XLA Ops:
  0.6 4.9 %copy-start = (f32[256,1152]{1,0:T(8,128)S(1)}, f32[256,1152]{1,0:T(8,128)}, u32[]{:S(2)}) copy-start(f32[256,1152]{1,0:T(8,128)} %text_emb.1) | copy-start | bytes 3538948
  0.6 1.4 %copy-start.1 = (f32[256,1152]{1,0:T(8,128)S(1)}, f32[256,1152]{1,0:T(8,128)}, u32[]{:S(2)}) copy-start(f32[256,1152]{1,0:T(8,128)} %image_emb.1) | copy-start | bytes 3538948
  2.2 16.4 %collective-permute-start.4 = (bf16[256,1152]{1,0:T(8,128)(2,1)S(1)}, bf16[256,1152]{1,0:T(8,128)(2,1)S(1)}, u32[]{:S(2)}, u32[]{:S(2)}) collective-permute-start(bf16[256,1152]{1,0:T(8,128)(2,1)S(1)} %get-tuple-element.44.own_i), channel_id=1, source_target_pairs={{0,64},{16,80},{32,96},{48,112},{64,128},{80,144},{96,160},{112,17... | collective-permute-start | bytes 1769480 | tf_op jit(solution)/shard_map/ppermute | solution.py:411
  3.8 17.1 %collective-permute-start.6 = (bf16[256,1152]{1,0:T(8,128)(2,1)S(1)}, bf16[256,1152]{1,0:T(8,128)(2,1)S(1)}, u32[]{:S(2)}, u32[]{:S(2)}) collective-permute-start(bf16[256,1152]{1,0:T(8,128)(2,1)S(1)} %get-tuple-element.44.own_i), channel_id=1, source_target_pairs={{0,192},{16,208},{32,224},{48,240},{64,0},{80,16},{96,32},{112,48}... | collective-permute-start | bytes 1769480 | tf_op jit(solution)/shard_map/ppermute | solution.py:411
  6.2 14.6 %collective-permute-start.9 = (bf16[256,1152]{1,0:T(8,128)(2,1)S(1)}, bf16[256,1152]{1,0:T(8,128)(2,1)}, u32[]{:S(2)}, u32[]{:S(2)}) collective-permute-start(bf16[256,1152]{1,0:T(8,128)(2,1)S(1)} %get-tuple-element.46.own_t), channel_id=1, source_target_pairs={{0,32},{16,48},{32,0},{48,16},{64,96},{80,112},{96,64},{112,80},{1... | collective-permute-start | bytes 1769480 | tf_op jit(solution)/shard_map/ppermute | solution.py:411
  7.8 14.9 %collective-permute-start.8 = (bf16[256,1152]{1,0:T(8,128)(2,1)S(1)}, bf16[256,1152]{1,0:T(8,128)(2,1)}, u32[]{:S(2)}, u32[]{:S(2)}) collective-permute-start(bf16[256,1152]{1,0:T(8,128)(2,1)S(1)} %get-tuple-element.46.own_t), channel_id=1, source_target_pairs={{0,16},{16,0},{32,48},{48,32},{64,80},{80,64},{96,112},{112,96},{1... | collective-permute-start | bytes 1769480 | tf_op jit(solution)/shard_map/ppermute | solution.py:411
  18.6 13.4 %collective-permute-start.5 = (bf16[128,1152]{1,0:T(8,128)(2,1)S(1)}, bf16[128,1152]{1,0:T(8,128)(2,1)S(1)}, u32[]{:S(2)}, u32[]{:S(2)}) collective-permute-start(bf16[128,1152]{1,0:T(8,128)(2,1)S(1)} %cut.2), channel_id=1, source_target_pairs={{0,64},{16,80},{32,96},{48,112},{64,128},{80,144},{96,160},{112,17... | collective-permute-start | bytes 884744 | tf_op jit(solution)/shard_map/ppermute | solution.py:411
  20.8 2.2 %collective-permute-start.10 = (bf16[256,1152]{1,0:T(8,128)(2,1)}, bf16[256,1152]{1,0:T(8,128)(2,1)S(1)}, u32[]{:S(2)}, u32[]{:S(2)}) collective-permute-start(bf16[256,1152]{1,0:T(8,128)(2,1)} %collective-permute-done.9.y_t), channel_id=1, source_target_pairs={{0,16},{16,0},{32,48},{48,32},{64,80},{80,64},{96,112},{112,96},{1... | collective-permute-start | bytes 1769480 | tf_op jit(solution)/shard_map/ppermute | solution.py:411
  20.9 11.1 %collective-permute-start.7 = (bf16[128,1152]{1,0:T(8,128)(2,1)S(1)}, bf16[128,1152]{1,0:T(8,128)(2,1)S(1)}, u32[]{:S(2)}, u32[]{:S(2)}) collective-permute-start(bf16[128,1152]{1,0:T(8,128)(2,1)S(1)} %cut.3), channel_id=1, source_target_pairs={{0,192},{16,208},{32,224},{48,240},{64,0},{80,16},{96,32},{112,48}... | collective-permute-start | bytes 884744 | tf_op jit(solution)/shard_map/ppermute | solution.py:411
  31.9 1.4 %copy-start.3 = (bf16[256,1152]{1,0:T(8,128)(2,1)}, bf16[256,1152]{1,0:T(8,128)(2,1)S(1)}, u32[]{:S(2)}) copy-start(bf16[256,1152]{1,0:T(8,128)(2,1)S(1)} %get-tuple-element.59.own_p) | copy-start | bytes 1769476
  38.0 8.2 %copy-start.5 = (bf16[256,1152]{1,0:T(8,128)(2,1)}, bf16[256,1152]{1,0:T(8,128)(2,1)S(1)}, u32[]{:S(2)}) copy-start(bf16[256,1152]{1,0:T(8,128)(2,1)S(1)} %get-tuple-element.54.own_q) | copy-start | bytes 1769476
  38.0 7.2 %collective-permute-start.11 = (bf16[512,1152]{1,0:T(8,128)(2,1)S(1)}, bf16[512,1152]{1,0:T(8,128)(2,1)S(1)}, u32[]{:S(2)}, u32[]{:S(2)}) collective-permute-start(bf16[512,1152]{1,0:T(8,128)(2,1)S(1)} %get-tuple-element.55), channel_id=1, source_target_pairs={{0,16},{16,0},{32,48},{48,32},{64,80},{80,64},{96,112},{112,96},{1... | collective-permute-start | bytes 3538952 | tf_op jit(solution)/shard_map/ppermute | solution.py:411
  38.1 3.8 %collective-permute-start.12 = (f32[8,128]{1,0:T(8,128)S(1)}, f32[8,128]{1,0:T(8,128)S(1)}, u32[]{:S(2)}, u32[]{:S(2)}) collective-permute-start(f32[8,128]{1,0:T(8,128)S(1)} %get-tuple-element.53.sums), channel_id=1, source_target_pairs={{0,48},{16,32},{32,16},{48,0},{64,112},{80,96},{96,80},{112,64},{1... | collective-permute-start | bytes 12296 | tf_op jit(solution)/shard_map/ppermute | solution.py:432
  39.7 3.6 %collective-permute-start.13 = (f32[8,128]{1,0:T(8,128)S(1)}, f32[8,128]{1,0:T(8,128)S(1)}, u32[]{:S(2)}, u32[]{:S(2)}) collective-permute-start(f32[8,128]{1,0:T(8,128)S(1)} %get-tuple-element.53.sums), channel_id=1, source_target_pairs={{0,32},{16,48},{32,0},{48,16},{64,96},{80,112},{96,64},{112,80},{1... | collective-permute-start | bytes 12296 | tf_op jit(solution)/shard_map/ppermute | solution.py:432
  40.2 5.0 %collective-permute-start.14 = (f32[8,128]{1,0:T(8,128)S(1)}, f32[8,128]{1,0:T(8,128)S(1)}, u32[]{:S(2)}, u32[]{:S(2)}) collective-permute-start(f32[8,128]{1,0:T(8,128)S(1)} %get-tuple-element.53.sums), channel_id=1, source_target_pairs={{0,16},{16,0},{32,48},{48,32},{64,80},{80,64},{96,112},{112,96},{1... | collective-permute-start | bytes 12296 | tf_op jit(solution)/shard_map/ppermute | solution.py:432
  40.2 30.0 %collective-permute-start.18 = (bf16[256,1152]{1,0:T(8,128)(2,1)}, bf16[256,1152]{1,0:T(8,128)(2,1)}, u32[]{:S(2)}, u32[]{:S(2)}) collective-permute-start(bf16[256,1152]{1,0:T(8,128)(2,1)} %get-tuple-element.62), channel_id=1, source_target_pairs={{0,128},{16,144},{32,160},{48,176},{64,192},{80,208},{96,224},{112... | collective-permute-start | bytes 1769480 | tf_op jit(solution)/shard_map/ppermute | solution.py:411
  41.9 29.7 %collective-permute-start.16 = (bf16[256,1152]{1,0:T(8,128)(2,1)}, bf16[256,1152]{1,0:T(8,128)(2,1)}, u32[]{:S(2)}, u32[]{:S(2)}) collective-permute-start(bf16[256,1152]{1,0:T(8,128)(2,1)} %get-tuple-element.60), channel_id=1, source_target_pairs={{0,64},{16,80},{32,96},{48,112},{64,128},{80,144},{96,160},{112,17... | collective-permute-start | bytes 1769480 | tf_op jit(solution)/shard_map/ppermute | solution.py:411
  43.4 31.5 %collective-permute-start.17 = (bf16[256,1152]{1,0:T(8,128)(2,1)}, bf16[256,1152]{1,0:T(8,128)(2,1)}, u32[]{:S(2)}, u32[]{:S(2)}) collective-permute-start(bf16[256,1152]{1,0:T(8,128)(2,1)} %get-tuple-element.61), channel_id=1, source_target_pairs={{0,192},{16,208},{32,224},{48,240},{64,0},{80,16},{96,32},{112,48}... | collective-permute-start | bytes 1769480 | tf_op jit(solution)/shard_map/ppermute | solution.py:411
  45.2 29.7 %copy-start.2 = (f32[256,1152]{1,0:T(8,128)S(1)}, f32[256,1152]{1,0:T(8,128)}, u32[]{:S(2)}) copy-start(f32[256,1152]{1,0:T(8,128)} %image_emb.1) | copy-start | bytes 3538948
  46.1 28.7 %collective-permute-start.15 = (bf16[256,1152]{1,0:T(8,128)(2,1)}, bf16[256,1152]{1,0:T(8,128)(2,1)}, u32[]{:S(2)}, u32[]{:S(2)}) collective-permute-start(bf16[256,1152]{1,0:T(8,128)(2,1)} %get-tuple-element.58), channel_id=1, source_target_pairs={{0,32},{16,48},{32,0},{48,16},{64,96},{80,112},{96,64},{112,80},{1... | collective-permute-start | bytes 1769480 | tf_op jit(solution)/shard_map/ppermute | solution.py:411
  48.4 3.7 %collective-permute-start = (f32[8,128]{1,0:T(8,128)S(1)}, f32[8,128]{1,0:T(8,128)S(1)}, u32[]{:S(2)}, u32[]{:S(2)}) collective-permute-start(f32[8,128]{1,0:T(8,128)S(1)} %get-tuple-element.93), channel_id=1, source_target_pairs={{0,1},{1,0},{2,3},{3,2},{4,5},{5,4},{6,7},{7,6},{8,9},{9,8},{10,11... | collective-permute-start | bytes 12296 | tf_op jit(solution)/shard_map/while/body/ppermute | solution.py:432
  52.1 4.9 %collective-permute-start.1 = (f32[8,128]{1,0:T(8,128)S(1)}, f32[8,128]{1,0:T(8,128)S(1)}, u32[]{:S(2)}, u32[]{:S(2)}) collective-permute-start(f32[8,128]{1,0:T(8,128)S(1)} %add.18), channel_id=1, source_target_pairs={{0,2},{1,3},{2,0},{3,1},{4,6},{5,7},{6,4},{7,5},{8,10},{9,11},{10,... | collective-permute-start | bytes 12296 | tf_op jit(solution)/shard_map/while/body/ppermute | solution.py:432
  56.9 7.2 %collective-permute-start.2 = (f32[8,128]{1,0:T(8,128)S(1)}, f32[8,128]{1,0:T(8,128)S(1)}, u32[]{:S(2)}, u32[]{:S(2)}) collective-permute-start(f32[8,128]{1,0:T(8,128)S(1)} %add.19), channel_id=1, source_target_pairs={{0,7},{1,6},{2,5},{3,4},{4,3},{5,2},{6,1},{7,0},{8,15},{9,14},{10,... | collective-permute-start | bytes 12296 | tf_op jit(solution)/shard_map/while/body/ppermute | solution.py:432
  64.1 4.8 %collective-permute-start.3 = (f32[8,128]{1,0:T(8,128)S(1)}, f32[8,128]{1,0:T(8,128)S(1)}, u32[]{:S(2)}, u32[]{:S(2)}) collective-permute-start(f32[8,128]{1,0:T(8,128)S(1)} %add.20), channel_id=1, source_target_pairs={{0,40},{1,41},{2,42},{3,43},{4,44},{5,45},{6,46},{7,47},{8,32},{9,... | collective-permute-start | bytes 12296 | tf_op jit(solution)/shard_map/while/body/ppermute | solution.py:432
  70.1 10.9 %collective-permute-start.19 = (f32[8,128]{1,0:T(8,128)S(1)}, f32[8,128]{1,0:T(8,128)S(1)}, u32[]{:S(2)}, u32[]{:S(2)}) collective-permute-start(f32[8,128]{1,0:T(8,128)S(1)} %get-tuple-element.65.sums), channel_id=1, source_target_pairs={{0,64},{16,80},{32,96},{48,112},{64,0},{80,16},{96,32},{112,48},{1... | collective-permute-start | bytes 12296 | tf_op jit(solution)/shard_map/ppermute | solution.py:432
  70.2 10.8 %collective-permute-start.20 = (f32[8,128]{1,0:T(8,128)S(1)}, f32[8,128]{1,0:T(8,128)S(1)}, u32[]{:S(2)}, u32[]{:S(2)}) collective-permute-start(f32[8,128]{1,0:T(8,128)S(1)} %get-tuple-element.65.sums), channel_id=1, source_target_pairs={{0,128},{16,144},{32,160},{48,176},{64,192},{80,208},{96,224},{112... | collective-permute-start | bytes 12296 | tf_op jit(solution)/shard_map/ppermute | solution.py:432
  71.6 9.3 %collective-permute-start.21 = (f32[8,128]{1,0:T(8,128)S(1)}, f32[8,128]{1,0:T(8,128)S(1)}, u32[]{:S(2)}, u32[]{:S(2)}) collective-permute-start(f32[8,128]{1,0:T(8,128)S(1)} %get-tuple-element.65.sums), channel_id=1, source_target_pairs={{0,192},{16,208},{32,224},{48,240},{64,128},{80,144},{96,160},{112... | collective-permute-start | bytes 12296 | tf_op jit(solution)/shard_map/ppermute | solution.py:432
  74.9 1.1 %copy-start.4 = (bf16[256,1152]{1,0:T(8,128)(2,1)S(1)}, bf16[256,1152]{1,0:T(8,128)(2,1)}, u32[]{:S(2)}) copy-start(bf16[256,1152]{1,0:T(8,128)(2,1)} %copy-done.3) | copy-start | bytes 1769476
  75.9 1.1 %copy-start.6 = (bf16[256,1152]{1,0:T(8,128)(2,1)S(1)}, bf16[256,1152]{1,0:T(8,128)(2,1)}, u32[]{:S(2)}) copy-start(bf16[256,1152]{1,0:T(8,128)(2,1)} %copy-done.5) | copy-start | bytes 1769476

commit v10 on v7

--- a/solution.py
+++ b/solution.py
@@ -9,7 +9,8 @@
 LOG2E = 1.4426950408889634
 BATCH = 65536
 GATE_COST = 1
-STEPS = (("group", 1), ("group", 2), ("group", 4), ("group", 8))
+CUT_COST = 1024 * 32
+STEPS = (("group", 1), ("group", 2), ("group", 7), (("blk", "group"), 2 * 16 + 8))
 BF16 = jnp.bfloat16
 HBM = pl.BlockSpec(memory_space=pltpu.HBM)
 VMEM = pl.BlockSpec(memory_space=pltpu.VMEM)
@@ -60,7 +61,9 @@
         in_specs=[VMEM],
         out_specs=VMEM,
         compiler_params=params(16),
-        cost_estimate=pl.CostEstimate(flops=0, bytes_accessed=rows * width, transcendentals=0),
+        cost_estimate=pl.CostEstimate(
+            flops=CUT_COST * rows * width, bytes_accessed=rows * width, transcendentals=0
+        ),
         name="cut",
     )(block)
 
@@ -174,7 +177,7 @@
 
 
 def far_grad_kernel(
-    far_images, far_grads, near_images, texts, near_grads, sums,
+    far_images, far_grads, near_images, texts, near_grads, own_p, sums,
     far_out, y_out, mate_out, own_out, sums_out,
 ):
     rows = far_images.shape[0]
@@ -185,11 +188,12 @@
         (3, mate_out.at[pl.ds(0, rows)]),
         (1, mate_out.at[pl.ds(rows, rows)]),
         (2, y_out),
-        (0, own_out),
+        (0, own_out.at[pl.ds(0, rows)]),
     ):
         out[...] = text_grad(
             near_grads, near_images, far_grads, far_images, pl.ds(t * rows, rows)
         ).astype(out.dtype)
+    own_out[pl.ds(rows, rows), :] = own_p[...]
     sums_out[...] = sums[...]
 
 
@@ -239,23 +243,23 @@
     )(*scalars, *far_images, texts, near_sums)
 
 
-def far_grad_part(far_images, far_grads, near_images, texts, near_grads, sums):
+def far_grad_part(far_images, far_grads, near_images, texts, near_grads, own_p, sums):
     rows, width = far_images.shape
     shape = jax.ShapeDtypeStruct
     return pl.pallas_call(
         far_grad_kernel,
         out_shape=(
             shape((rows, width), BF16), shape((rows, width), F32), shape((2 * rows, width), BF16),
-            shape((rows, width), BF16), shape(sums.shape, F32),
-        ),
-        in_specs=[VMEM] * 6,
+            shape((2 * rows, width), BF16), shape(sums.shape, F32),
+        ),
+        in_specs=[VMEM] * 7,
         out_specs=(VMEM,) * 5,
         compiler_params=params(16),
         cost_estimate=pl.CostEstimate(
             flops=rows * rows * width, bytes_accessed=2 * rows * width, transcendentals=0
         ),
         name="far_grad",
-    )(far_images, far_grads, near_images, texts, near_grads, sums)
+    )(far_images, far_grads, near_images, texts, near_grads, own_p, sums)
 
 
 def add_kernel(*refs):
@@ -278,24 +282,24 @@
     )(*parts)
 
 
-def relay_y_kernel(own, passing, sums, arrived, out, sums_out):
+def relay_y_kernel(own, passing, sums, sums_a, sums_b, sums_c, out, sums_out):
     rows = own.shape[0]
     out[...] = (own[...] + passing[:rows, :].astype(F32)).astype(BF16)
-    sums_out[...] = sums[...] + arrived[...]
-
-
-def relay_y(own, passing, sums, arrived):
+    sums_out[...] = sums[...] + sums_a[...] + sums_b[...] + sums_c[...]
+
+
+def relay_y(own, passing, sums, *arrived):
     return pl.pallas_call(
         relay_y_kernel,
         out_shape=(
             jax.ShapeDtypeStruct(own.shape, BF16), jax.ShapeDtypeStruct(sums.shape, F32)
         ),
-        in_specs=[VMEM] * 4,
+        in_specs=[VMEM] * 6,
         out_specs=(VMEM,) * 2,
         compiler_params=params(16),
         cost_estimate=pl.CostEstimate(flops=own.size, bytes_accessed=own.size, transcendentals=0),
         name="relay_y",
-    )(own, passing, sums, arrived)
+    )(own, passing, sums, *arrived)
 
 
 def backnorm(emb, upstream, scale):
@@ -305,20 +309,20 @@
 
 
 def end_kernel(
-    log_scale, text_emb, own_q, from_core, from_y, image_emb, own_p, from_left, from_right, from_far,
-    sums, text_out, image_out, sums_out, text_slots, image_slots, sems,
+    log_scale, own, text_emb, from_core, from_y, image_emb, from_left, from_right, from_far, sums,
+    text_out, image_out, sums_out, text_slots, image_slots, sems,
 ):
     scale = jnp.exp(jnp.full((1, 1), log_scale[0]))
     step = text_emb.shape[0] // 4
     sets = (
-        (text_emb, (own_q, from_core, from_y), text_out, text_slots),
-        (image_emb, (own_p, from_left, from_right, from_far), image_out, image_slots),
+        (text_emb, (from_core, from_y), text_out, text_slots),
+        (image_emb, (from_left, from_right, from_far), image_out, image_slots),
     )
     copies = []
-    for emb, parts, out, slots in sets:
+    for k, (emb, parts, out, slots) in enumerate(sets):
         for i in range(4):
             at = pl.ds(i * step, step)
-            upstream = jnp.zeros((step, emb.shape[1]), F32)
+            upstream = own[pl.ds((4 * k + i) * step, step), :].astype(F32)
             for part in parts:
                 skip = part.shape[0] - 4 * step
                 upstream += part[pl.ds(skip + i * step, step), :].astype(F32)
@@ -331,13 +335,13 @@
         copy.wait()
 
 
-def end_part(log_scale, text_parts, image_parts, sums):
+def end_part(log_scale, own, text_parts, image_parts, sums):
     rows, width = text_parts[0].shape
     shape = jax.ShapeDtypeStruct
     return pl.pallas_call(
         end_kernel,
         out_shape=(shape((rows, width), F32),) * 2 + (shape(sums.shape, F32),),
-        in_specs=[SMEM] + [VMEM] * 10,
+        in_specs=[SMEM] + [VMEM] * 9,
         out_specs=(HBM, HBM, VMEM),
         scratch_shapes=[
             pltpu.VMEM((rows, width), F32),
@@ -349,7 +353,7 @@
             flops=16 * rows * width, bytes_accessed=2 * rows * width, transcendentals=2 * rows
         ),
         name="end",
-    )(log_scale, *text_parts, *image_parts, sums)
+    )(log_scale, own, *text_parts, *image_parts, sums)
 
 
 def totals_kernel(*refs):
@@ -403,29 +407,28 @@
     def pair(value, axis, k):
         return lax.ppermute(value, axis, [(i, i ^ k) for i in range(lax.axis_size(axis))])
 
-    over_y = pair(sums, "blk", 2)
-    far_p, y_q, to_mate, own_q, sums = far_grad_part(
-        far_images, far_grads, near_images, texts, near_grads, sums
-    )
-    sums_1 = add(sums, over_y)
+    over_y_core = [pair(sums, "blk", k) for k in (3, 2, 1)]
+    far_p, y_q, to_mate, own, sums = far_grad_part(
+        far_images, far_grads, near_images, texts, near_grads, own_p, sums
+    )
     from_far = send(far_p, [(i, (i + 8) % blocks) for i in range(blocks)])
     from_core = send(to_mate, across_core)
-    y_sum, sums_2 = relay_y(y_q, from_core, sums_1, pair(sums_1, "blk", 1))
+    y_sum, sums_2 = relay_y(y_q, from_core, sums, *over_y_core)
     from_y = send(y_sum, across_y)
     sums_2 = add(sums_2)
 
-    def steps(carry):
-        left, value = carry
+    def steps(value):
         for axis, k in STEPS:
             value = value + pair(value, axis, k)
-        return left - 1, value
-
-    _, sums_6 = lax.while_loop(lambda carry: carry[0] > 0, steps, (passes[0], sums_2))
+        return value
+
+    sums_6 = lax.cond(passes[0] > 0, steps, lambda value: value, sums_2)
     over_x = [pair(sums_6, "blk", k) for k in (4, 8, 12)]
     grad_text, grad_image, sums_6 = end_part(
         scalars[0],
-        (text_emb, own_q, from_core, from_y),
-        (image_emb, own_p, from_left, from_right, from_far),
+        own,
+        (text_emb, from_core, from_y),
+        (image_emb, from_left, from_right, from_far),
         sums_6,
     )
     loss, grad_scale, grad_bias = (total.reshape(()) for total in totals_part(sums_6, *over_x))

time: 83.9 us -> 80.4 us (0.958)
  starting transfers between devices: 32.1 us -> 28.2 us
  waiting for transfers between devices: 22.8 us -> 25.7 us
  loops' own time: 2.47 us -> 0.02 us
  local copies, waits for them, and re-layouts: 3.57 us -> 2.55 us
    ppermute x12, waiting for transfers between devices: 11.5 us -> 15.9 us  [send(): return lax.ppermute(value, 'blk', perm)]
    ppermute x12, starting transfers between devices: 14.6 us -> 11.8 us  [send(): return lax.ppermute(value, 'blk', perm)]
    another operation x1, loops' own time: 2.47 us -> 0.02 us  [shards(): sums_6 = lax.cond(passes[0] > 0, steps, lambda value: value, sums_2)]
    ppermute x9 -> x10, waiting for transfers between devices: 11.4 us -> 9.76 us  [pair(): lax.ppermute(value, axis, [(i, i ^ k) for i in range(lax.axis_size(axis))])]
    ppermute x9 -> x10, starting transfers between devices: 17.6 us -> 16.4 us  [pair(): lax.ppermute(value, axis, [(i, i ^ k) for i in range(lax.axis_size(axis))])]
    pallas_call x2, Pallas kernels: 0.04 us -> 1.11 us  [cut(): pl.pallas_call(kernel, out_shape=jax.ShapeDtypeStruct((rows // 2, width),...]
    unnamed x14 -> x10, local copies, waits for them, and re-layouts: 3.57 us -> 2.55 us
  transfers between devices with their start and end apart: 21 -> 22, of which waited for: 7 -> 10; matrix products, arithmetic and copies ran while one was open for 0% -> 0% of each run, Pallas kernels for 15% -> 18%
where the time goes in v10:
time: 80.4 us; the launch traced here: 79.5 us
  starting transfers between devices  28.2 us (35%)
  waiting for transfers between devices  25.7 us (32%)
  Pallas kernels  20.1 us (25%)
  between operations  2.92 us (4%)
  local copies, waits for them, and re-layouts  2.55 us (3%)
    ppermute x10, starting transfers between devices, pair(): lax.ppermute(value, axis, [(i, i ^ k) for i in range(lax.axis_size(axis))])  16.4 us
    ppermute x12, waiting for transfers between devices, send(): return lax.ppermute(value, 'blk', perm)  15.9 us
    ppermute x12, starting transfers between devices, send(): return lax.ppermute(value, 'blk', perm)  11.8 us
    ppermute x10, waiting for transfers between devices, pair(): lax.ppermute(value, axis, [(i, i ^ k) for i in range(lax.axis_size(axis))])  9.76 us
    pallas_call x1, Pallas kernels, near_part(): pl.pallas_call(near_kernel, out_shape=(shape((rows, width), BF16), shape(...  7.5 us
    pallas_call x1, Pallas kernels, end_part(): pl.pallas_call(end_kernel, out_shape=(shape((rows, width), F32),) * 2 + (...  3.94 us
    pallas_call x1, Pallas kernels, far_grad_part(): pl.pallas_call(far_grad_kernel, out_shape=(shape((rows, width), BF16), sh...  3.67 us
    unnamed x10, local copies, waits for them, and re-layouts  2.55 us
  transfers between devices with their start and end apart: 22, of which 10 were waited for; matrix products, arithmetic and copies ran while one was open for 0% of the time, Pallas kernels for 18%

profile of v10, /device:TPU:32, one launch (start us, length us, event | category | flops | bytes accessed | tf_op | source)
XLA Modules:
  0.0 79.5 jit_solution(4364832507367530173)
XLA Ops:
  0.6 0.0 copy-start
  0.6 1.3 %copy-done = f32[256,1152]{1,0:T(8,128)S(1)} copy-done((f32[256,1152]{1,0:T(8,128)S(1)}, f32[256,1152]{1,0:T(8,128)}, u32[]{:S(2)}) %copy-start) | copy-done | bytes 1179672
  1.9 0.2 normalize.2
  2.1 2.8 %collective-permute-start.6 = (bf16[256,1152]{1,0:T(8,128)(2,1)S(1)}, bf16[256,1152]{1,0:T(8,128)(2,1)S(1)}, u32[]{:S(2)}, u32[]{:S(2)}) collective-permute-start(bf16[256,1152]{1,0:T(8,128)(2,1)S(1)} %get-tuple-element.37.own_i), channel_id=1, source_target_pairs={{0,192},{16,208},{32,224},{48,240},{64,0},{80,16},{96,32},{112,48}... | collective-permute-start | bytes 1769480 | tf_op jit(solution)/shard_map/ppermute | solution.py:387
  4.9 0.7 normalize.3
  5.6 1.6 %collective-permute-start.9 = (bf16[256,1152]{1,0:T(8,128)(2,1)S(1)}, bf16[256,1152]{1,0:T(8,128)(2,1)S(1)}, u32[]{:S(2)}, u32[]{:S(2)}) collective-permute-start(bf16[256,1152]{1,0:T(8,128)(2,1)S(1)} %get-tuple-element.39.own_t), channel_id=1, source_target_pairs={{0,32},{16,48},{32,0},{48,16},{64,96},{80,112},{96,64},{112,80},{1... | collective-permute-start | bytes 1769480 | tf_op jit(solution)/shard_map/ppermute | solution.py:387
  8.5 9.0 %collective-permute-done.6.block_ref.right_i = bf16[256,1152]{1,0:T(8,128)(2,1)S(1)} collective-permute-done((bf16[256,1152]{1,0:T(8,128)(2,1)S(1)}, bf16[256,1152]{1,0:T(8,128)(2,1)S(1)}, u32[]{:S(2)}, u32[]{:S(2)}) %collective-permute-start.6) | collective-permute-done | bytes 589856 | tf_op jit(solution)/shard_map/ppermute | solution.py:387
  17.5 3.8 %collective-permute-start.7 = (bf16[128,1152]{1,0:T(8,128)(2,1)S(1)}, bf16[128,1152]{1,0:T(8,128)(2,1)S(1)}, u32[]{:S(2)}, u32[]{:S(2)}) collective-permute-start(bf16[128,1152]{1,0:T(8,128)(2,1)S(1)} %cut.3), channel_id=1, source_target_pairs={{0,192},{16,208},{32,224},{48,240},{64,0},{80,16},{96,32},{112,48}... | collective-permute-start | bytes 884744 | tf_op jit(solution)/shard_map/ppermute | solution.py:387
  21.3 3.0 %collective-permute-done.4.block_ref.left_i = bf16[256,1152]{1,0:T(8,128)(2,1)} collective-permute-done((bf16[256,1152]{1,0:T(8,128)(2,1)S(1)}, bf16[256,1152]{1,0:T(8,128)(2,1)}, u32[]{:S(2)}, u32[]{:S(2)}) %collective-permute-start.4) | collective-permute-done | bytes 589856 | tf_op jit(solution)/shard_map/ppermute | solution.py:387
  24.3 1.1 %cut.2 = bf16[128,1152]{1,0:T(8,128)(2,1)S(1)} custom-call(bf16[256,1152]{1,0:T(8,128)(2,1)} %collective-permute-done.4.block_ref.left_i), custom_call_target="tpu_custom_call" | custom-call | flops 9663676416 | bytes 294912 | tf_op jit(solution)/shard_map/cut/pallas_call | solution.py:58
  25.3 0.3 collective-permute-start.5
  25.6 0.0 collective-permute-done.8.core_t
  25.6 0.0 collective-permute-done.10.yc_t
  25.6 7.5 %near.1 = (bf16[256,1152]{1,0:T(8,128)(2,1)S(1)}, bf16[256,1152]{1,0:T(8,128)(2,1)}, bf16[256,1152]{1,0:T(8,128)(2,1)}, bf16[768,1152]{1,0:T(8,128)(2,1)S(1)}, b...) custom-call(f32[1]{0:T(128)} %bitcast.6.log_scale, ...), custom_call_target="tpu_custom_call" | custom-call | flops 28991029248 | bytes 7077888 | tf_op jit(solution)/shard_map/near/pallas_call | solution.py:203
  33.1 0.0 collective-permute-done.7.bot_i
  33.2 2.3 %collective-permute-done.5.top_i = bf16[128,1152]{1,0:T(8,128)(2,1)S(1)} collective-permute-done((bf16[128,1152]{1,0:T(8,128)(2,1)S(1)}, bf16[128,1152]{1,0:T(8,128)(2,1)S(1)}, u32[]{:S(2)}, u32[]{:S(2)}) %collective-permute-start.5) | collective-permute-done | bytes 294944 | tf_op jit(solution)/shard_map/ppermute | solution.py:387
  35.5 1.4 %far.1 = (bf16[256,1152]{1,0:T(8,128)(2,1)S(1)}, bf16[256,1024]{1,0:T(8,128)(2,1)S(1)}, f32[8,128]{1,0:T(8,128)S(1)}) custom-call(f32[1]{0:T(128)} %bitcast.7.log_scale, f32[1]{0:T(128)} %bitcast.10.bias, bf16[128,1152]{1,0:T(8,128)(2,1)S(1)} %collective-permute-done.5.top_i, bf16[128,1152]{1,0:T(8,128)(2,1)S(1)} %collective-permute-done.7.bot_i, ...), custom_call_target="tpu_custom_call" | custom-call | flops 75497472 | bytes 589824 | tf_op jit(solution)/shard_map/far/pallas_call | solution.py:231
  36.9 3.7 %far_grad.1 = (bf16[256,1152]{1,0:T(8,128)(2,1)}, f32[256,1152]{1,0:T(8,128)S(1)}, bf16[512,1152]{1,0:T(8,128)(2,1)S(1)}, bf16[512,1152]{1,0:T(8,128)(2,1)S(1)}, f32[8,128]{1,0:T(8,128)S(1)}) custom-call(bf16[256,1152]{1,0:T(8,128)(2,1)S(1)} %get-tuple-element.42.far_images, bf16[256,1024]{1,0:T(8,128)(2,1)S(1)} %get-tuple-element.43.far_grads, ...), custom_call_target="tpu_custom_call" | custom-call | flops 75497472 | bytes 589824 | tf_op jit(solution)/shard_map/far_grad/pallas_call | solution.py:249
  40.5 0.0 copy-start.3
  40.5 0.1 collective-permute-start.11
  40.6 0.5 collective-permute-start.14
  41.1 0.4 collective-permute-start.13
  41.6 1.0 %collective-permute-start.12 = (f32[8,128]{1,0:T(8,128)S(1)}, f32[8,128]{1,0:T(8,128)S(1)}, u32[]{:S(2)}, u32[]{:S(2)}) collective-permute-start(f32[8,128]{1,0:T(8,128)S(1)} %get-tuple-element.47.sums), channel_id=1, source_target_pairs={{0,48},{16,32},{32,16},{48,0},{64,112},{80,96},{96,80},{112,64},{1... | collective-permute-start | bytes 12296 | tf_op jit(solution)/shard_map/ppermute | solution.py:408
  42.6 0.0 collective-permute-start.18
  42.6 0.9 %collective-permute-done.14.sums_c = f32[8,128]{1,0:T(8,128)S(1)} collective-permute-done((f32[8,128]{1,0:T(8,128)S(1)}, f32[8,128]{1,0:T(8,128)S(1)}, u32[]{:S(2)}, u32[]{:S(2)}) %collective-permute-start.14) | collective-permute-done | bytes 4128 | tf_op jit(solution)/shard_map/ppermute | solution.py:408
  43.5 0.9 %collective-permute-start.16 = (bf16[256,1152]{1,0:T(8,128)(2,1)}, bf16[256,1152]{1,0:T(8,128)(2,1)}, u32[]{:S(2)}, u32[]{:S(2)}) collective-permute-start(bf16[256,1152]{1,0:T(8,128)(2,1)} %get-tuple-element.53), channel_id=1, source_target_pairs={{0,64},{16,80},{32,96},{48,112},{64,128},{80,144},{96,160},{112,17... | collective-permute-start | bytes 1769480 | tf_op jit(solution)/shard_map/ppermute | solution.py:387
  44.4 0.4 collective-permute-done.13.sums_b
  44.7 2.0 %collective-permute-start.17 = (bf16[256,1152]{1,0:T(8,128)(2,1)}, bf16[256,1152]{1,0:T(8,128)(2,1)}, u32[]{:S(2)}, u32[]{:S(2)}) collective-permute-start(bf16[256,1152]{1,0:T(8,128)(2,1)} %get-tuple-element.54), channel_id=1, source_target_pairs={{0,192},{16,208},{32,224},{48,240},{64,0},{80,16},{96,32},{112,48}... | collective-permute-start | bytes 1769480 | tf_op jit(solution)/shard_map/ppermute | solution.py:387
  46.7 1.0 %relay_y.1 = (bf16[256,1152]{1,0:T(8,128)(2,1)}, f32[8,128]{1,0:T(8,128)S(1)}) custom-call(f32[256,1152]{1,0:T(8,128)S(1)} %get-tuple-element.50.own, bf16[512,1152]{1,0:T(8,128)(2,1)S(1)} %collective-permute-done.11.passing.from_core, f32[8,128]{1,0:T(8,128)S(1)} %get-tuple-element.51.sums, f32[8,128]{1,0:T(8,128)S(1)} %collective-permute-done.12.sums_a, ...), custom_call_target="tpu_custom_call" | custom-call | flops 294912 | bytes 294912 | tf_op jit(solution)/shard_map/relay_y/pallas_call | solution.py:292
  47.7 0.4 collective-permute-start.15
  48.8 20.5 %conditional.1 = (f32[8,128]{1,0:T(8,128)S(1)}) conditional(s32[]{:T(128)} %bitcast.2, f32[8,128]{1,0:T(8,128)S(1)} %add.13, f32[8,128]{1,0:T(8,128)S(1)} %add.13), branch_computations={%region_0.0_spmd, %region_1.0_spmd} | conditional | flops 4096 | bytes 114856 | solution.py:425
  48.8 0.2 collective-permute-start
  49.0 3.5 %collective-permute-done = f32[8,128]{1,0:T(8,128)S(1)} collective-permute-done((f32[8,128]{1,0:T(8,128)S(1)}, f32[8,128]{1,0:T(8,128)S(1)}, u32[]{:S(2)}, u32[]{:S(2)}) %collective-permute-start) | collective-permute-done | bytes 4128 | tf_op jit(solution)/shard_map/cond/branch_1_fun/ppermute | solution.py:408
  52.5 3.3 %collective-permute-start.1 = (f32[8,128]{1,0:T(8,128)S(1)}, f32[8,128]{1,0:T(8,128)S(1)}, u32[]{:S(2)}, u32[]{:S(2)}) collective-permute-start(f32[8,128]{1,0:T(8,128)S(1)} %add.9), channel_id=1, source_target_pairs={{0,2},{1,3},{2,0},{3,1},{4,6},{5,7},{6,4},{7,5},{8,10},{9,11},{10,... | collective-permute-start | bytes 12296 | tf_op jit(solution)/shard_map/cond/branch_1_fun/ppermute | solution.py:408
  55.8 1.6 %collective-permute-done.1 = f32[8,128]{1,0:T(8,128)S(1)} collective-permute-done((f32[8,128]{1,0:T(8,128)S(1)}, f32[8,128]{1,0:T(8,128)S(1)}, u32[]{:S(2)}, u32[]{:S(2)}) %collective-permute-start.1) | collective-permute-done | bytes 4128 | tf_op jit(solution)/shard_map/cond/branch_1_fun/ppermute | solution.py:408
  57.4 5.5 %collective-permute-start.2 = (f32[8,128]{1,0:T(8,128)S(1)}, f32[8,128]{1,0:T(8,128)S(1)}, u32[]{:S(2)}, u32[]{:S(2)}) collective-permute-start(f32[8,128]{1,0:T(8,128)S(1)} %add.10), channel_id=1, source_target_pairs={{0,7},{1,6},{2,5},{3,4},{4,3},{5,2},{6,1},{7,0},{8,15},{9,14},{10,... | collective-permute-start | bytes 12296 | tf_op jit(solution)/shard_map/cond/branch_1_fun/ppermute | solution.py:408
  62.9 1.6 %collective-permute-done.2 = f32[8,128]{1,0:T(8,128)S(1)} collective-permute-done((f32[8,128]{1,0:T(8,128)S(1)}, f32[8,128]{1,0:T(8,128)S(1)}, u32[]{:S(2)}, u32[]{:S(2)}) %collective-permute-start.2) | collective-permute-done | bytes 4128 | tf_op jit(solution)/shard_map/cond/branch_1_fun/ppermute | solution.py:408
  64.5 3.0 %collective-permute-start.3 = (f32[8,128]{1,0:T(8,128)S(1)}, f32[8,128]{1,0:T(8,128)S(1)}, u32[]{:S(2)}, u32[]{:S(2)}) collective-permute-start(f32[8,128]{1,0:T(8,128)S(1)} %add.11), channel_id=1, source_target_pairs={{0,40},{1,41},{2,42},{3,43},{4,44},{5,45},{6,46},{7,47},{8,32},{9,... | collective-permute-start | bytes 12296 | tf_op jit(solution)/shard_map/cond/branch_1_fun/ppermute | solution.py:408
  67.5 1.8 %collective-permute-done.3 = f32[8,128]{1,0:T(8,128)S(1)} collective-permute-done((f32[8,128]{1,0:T(8,128)S(1)}, f32[8,128]{1,0:T(8,128)S(1)}, u32[]{:S(2)}, u32[]{:S(2)}) %collective-permute-start.3) | collective-permute-done | bytes 4128 | tf_op jit(solution)/shard_map/cond/branch_1_fun/ppermute | solution.py:408
  69.3 0.2 collective-permute-start.21
  69.5 1.9 %collective-permute-start.20 = (f32[8,128]{1,0:T(8,128)S(1)}, f32[8,128]{1,0:T(8,128)S(1)}, u32[]{:S(2)}, u32[]{:S(2)}) collective-permute-start(f32[8,128]{1,0:T(8,128)S(1)} %get-tuple-element.64.sums), channel_id=1, source_target_pairs={{0,128},{16,144},{32,160},{48,176},{64,192},{80,208},{96,224},{112... | collective-permute-start | bytes 12296 | tf_op jit(solution)/shard_map/ppermute | solution.py:408
  71.4 1.7 %collective-permute-done.16.from_left = bf16[256,1152]{1,0:T(8,128)(2,1)} collective-permute-done((bf16[256,1152]{1,0:T(8,128)(2,1)}, bf16[256,1152]{1,0:T(8,128)(2,1)}, u32[]{:S(2)}, u32[]{:S(2)}) %collective-permute-start.16) | collective-permute-done | bytes 589856 | tf_op jit(solution)/shard_map/ppermute | solution.py:387
  73.1 0.3 collective-permute-start.19
  73.4 0.0 copy-start.4
  73.4 1.3 %copy-done.4 = bf16[512,1152]{1,0:T(8,128)(2,1)S(1)} copy-done((bf16[512,1152]{1,0:T(8,128)(2,1)S(1)}, bf16[512,1152]{1,0:T(8,128)(2,1)}, u32[]{:S(2)}) %copy-start.4) | copy-done | bytes 1179672
  74.7 3.9 %end.1 = (f32[256,1152]{1,0:T(8,128)}, f32[256,1152]{1,0:T(8,128)}, f32[8,128]{1,0:T(8,128)S(1)}) custom-call(f32[1]{0:T(128)} %bitcast.8.log_scale, bf16[512,1152]{1,0:T(8,128)(2,1)S(1)} %copy-done.4, f32[256,1152]{1,0:T(8,128)S(1)} %copy-done.2, bf16[512,1152]{1,0:T(8,128)(2,1)S(1)} %collective-permute-done.11.passing.from_core, ...), custom_call_target="tpu_custom_call" | custom-call | flops 4718592 | bytes 589824 | tf_op jit(solution)/shard_map/end/pallas_call | solution.py:341
  78.6 0.0 collective-permute-done.21.refs_3_
  78.6 0.6 totals.1
  (22 shorter events, 0.1 us)
Async XLA Ops:
  0.6 1.3 %copy-start = (f32[256,1152]{1,0:T(8,128)S(1)}, f32[256,1152]{1,0:T(8,128)}, u32[]{:S(2)}) copy-start(f32[256,1152]{1,0:T(8,128)} %image_emb.1) | copy-start | bytes 3538948
  1.9 3.0 %copy-start.2 = (f32[256,1152]{1,0:T(8,128)S(1)}, f32[256,1152]{1,0:T(8,128)}, u32[]{:S(2)}) copy-start(f32[256,1152]{1,0:T(8,128)} %text_emb.1) | copy-start | bytes 3538948
  2.1 15.4 %collective-permute-start.6 = (bf16[256,1152]{1,0:T(8,128)(2,1)S(1)}, bf16[256,1152]{1,0:T(8,128)(2,1)S(1)}, u32[]{:S(2)}, u32[]{:S(2)}) collective-permute-start(bf16[256,1152]{1,0:T(8,128)(2,1)S(1)} %get-tuple-element.37.own_i), channel_id=1, source_target_pairs={{0,192},{16,208},{32,224},{48,240},{64,0},{80,16},{96,32},{112,48}... | collective-permute-start | bytes 1769480 | tf_op jit(solution)/shard_map/ppermute | solution.py:387
  5.6 15.7 %collective-permute-start.9 = (bf16[256,1152]{1,0:T(8,128)(2,1)S(1)}, bf16[256,1152]{1,0:T(8,128)(2,1)S(1)}, u32[]{:S(2)}, u32[]{:S(2)}) collective-permute-start(bf16[256,1152]{1,0:T(8,128)(2,1)S(1)} %get-tuple-element.39.own_t), channel_id=1, source_target_pairs={{0,32},{16,48},{32,0},{48,16},{64,96},{80,112},{96,64},{112,80},{1... | collective-permute-start | bytes 1769480 | tf_op jit(solution)/shard_map/ppermute | solution.py:387
  7.2 18.4 %collective-permute-start.8 = (bf16[256,1152]{1,0:T(8,128)(2,1)S(1)}, bf16[256,1152]{1,0:T(8,128)(2,1)}, u32[]{:S(2)}, u32[]{:S(2)}) collective-permute-start(bf16[256,1152]{1,0:T(8,128)(2,1)S(1)} %get-tuple-element.39.own_t), channel_id=1, source_target_pairs={{0,16},{16,0},{32,48},{48,32},{64,80},{80,64},{96,112},{112,96},{1... | collective-permute-start | bytes 1769480 | tf_op jit(solution)/shard_map/ppermute | solution.py:387
  7.2 17.1 %collective-permute-start.4 = (bf16[256,1152]{1,0:T(8,128)(2,1)S(1)}, bf16[256,1152]{1,0:T(8,128)(2,1)}, u32[]{:S(2)}, u32[]{:S(2)}) collective-permute-start(bf16[256,1152]{1,0:T(8,128)(2,1)S(1)} %get-tuple-element.37.own_i), channel_id=1, source_target_pairs={{0,64},{16,80},{32,96},{48,112},{64,128},{80,144},{96,160},{112,17... | collective-permute-start | bytes 1769480 | tf_op jit(solution)/shard_map/ppermute | solution.py:387
  17.5 15.6 %collective-permute-start.7 = (bf16[128,1152]{1,0:T(8,128)(2,1)S(1)}, bf16[128,1152]{1,0:T(8,128)(2,1)S(1)}, u32[]{:S(2)}, u32[]{:S(2)}) collective-permute-start(bf16[128,1152]{1,0:T(8,128)(2,1)S(1)} %cut.3), channel_id=1, source_target_pairs={{0,192},{16,208},{32,224},{48,240},{64,0},{80,16},{96,32},{112,48}... | collective-permute-start | bytes 884744 | tf_op jit(solution)/shard_map/ppermute | solution.py:387
  21.3 4.3 %collective-permute-start.10 = (bf16[256,1152]{1,0:T(8,128)(2,1)S(1)}, bf16[256,1152]{1,0:T(8,128)(2,1)S(1)}, u32[]{:S(2)}, u32[]{:S(2)}) collective-permute-start(bf16[256,1152]{1,0:T(8,128)(2,1)S(1)} %collective-permute-done.9.y_t), channel_id=1, source_target_pairs={{0,16},{16,0},{32,48},{48,32},{64,80},{80,64},{96,112},{112,96},{1... | collective-permute-start | bytes 1769480 | tf_op jit(solution)/shard_map/ppermute | solution.py:387
  25.3 10.1 %collective-permute-start.5 = (bf16[128,1152]{1,0:T(8,128)(2,1)S(1)}, bf16[128,1152]{1,0:T(8,128)(2,1)S(1)}, u32[]{:S(2)}, u32[]{:S(2)}) collective-permute-start(bf16[128,1152]{1,0:T(8,128)(2,1)S(1)} %cut.2), channel_id=1, source_target_pairs={{0,64},{16,80},{32,96},{48,112},{64,128},{80,144},{96,160},{112,17... | collective-permute-start | bytes 884744 | tf_op jit(solution)/shard_map/ppermute | solution.py:387
  40.5 7.2 %copy-start.3 = (bf16[512,1152]{1,0:T(8,128)(2,1)}, bf16[512,1152]{1,0:T(8,128)(2,1)S(1)}, u32[]{:S(2)}) copy-start(bf16[512,1152]{1,0:T(8,128)(2,1)S(1)} %get-tuple-element.48.own) | copy-start | bytes 3538948
  40.5 6.2 %collective-permute-start.11 = (bf16[512,1152]{1,0:T(8,128)(2,1)S(1)}, bf16[512,1152]{1,0:T(8,128)(2,1)S(1)}, u32[]{:S(2)}, u32[]{:S(2)}) collective-permute-start(bf16[512,1152]{1,0:T(8,128)(2,1)S(1)} %get-tuple-element.49), channel_id=1, source_target_pairs={{0,16},{16,0},{32,48},{48,32},{64,80},{80,64},{96,112},{112,96},{1... | collective-permute-start | bytes 3538952 | tf_op jit(solution)/shard_map/ppermute | solution.py:387
  40.6 2.8 %collective-permute-start.14 = (f32[8,128]{1,0:T(8,128)S(1)}, f32[8,128]{1,0:T(8,128)S(1)}, u32[]{:S(2)}, u32[]{:S(2)}) collective-permute-start(f32[8,128]{1,0:T(8,128)S(1)} %get-tuple-element.47.sums), channel_id=1, source_target_pairs={{0,16},{16,0},{32,48},{48,32},{64,80},{80,64},{96,112},{112,96},{1... | collective-permute-start | bytes 12296 | tf_op jit(solution)/shard_map/ppermute | solution.py:408
  41.1 3.6 %collective-permute-start.13 = (f32[8,128]{1,0:T(8,128)S(1)}, f32[8,128]{1,0:T(8,128)S(1)}, u32[]{:S(2)}, u32[]{:S(2)}) collective-permute-start(f32[8,128]{1,0:T(8,128)S(1)} %get-tuple-element.47.sums), channel_id=1, source_target_pairs={{0,32},{16,48},{32,0},{48,16},{64,96},{80,112},{96,64},{112,80},{1... | collective-permute-start | bytes 12296 | tf_op jit(solution)/shard_map/ppermute | solution.py:408
  41.6 5.1 %collective-permute-start.12 = (f32[8,128]{1,0:T(8,128)S(1)}, f32[8,128]{1,0:T(8,128)S(1)}, u32[]{:S(2)}, u32[]{:S(2)}) collective-permute-start(f32[8,128]{1,0:T(8,128)S(1)} %get-tuple-element.47.sums), channel_id=1, source_target_pairs={{0,48},{16,32},{32,16},{48,0},{64,112},{80,96},{96,80},{112,64},{1... | collective-permute-start | bytes 12296 | tf_op jit(solution)/shard_map/ppermute | solution.py:408
  42.6 26.9 %collective-permute-start.18 = (bf16[256,1152]{1,0:T(8,128)(2,1)}, bf16[256,1152]{1,0:T(8,128)(2,1)}, u32[]{:S(2)}, u32[]{:S(2)}) collective-permute-start(bf16[256,1152]{1,0:T(8,128)(2,1)} %get-tuple-element.55), channel_id=1, source_target_pairs={{0,128},{16,144},{32,160},{48,176},{64,192},{80,208},{96,224},{112... | collective-permute-start | bytes 1769480 | tf_op jit(solution)/shard_map/ppermute | solution.py:387
  43.5 29.6 %collective-permute-start.16 = (bf16[256,1152]{1,0:T(8,128)(2,1)}, bf16[256,1152]{1,0:T(8,128)(2,1)}, u32[]{:S(2)}, u32[]{:S(2)}) collective-permute-start(bf16[256,1152]{1,0:T(8,128)(2,1)} %get-tuple-element.53), channel_id=1, source_target_pairs={{0,64},{16,80},{32,96},{48,112},{64,128},{80,144},{96,160},{112,17... | collective-permute-start | bytes 1769480 | tf_op jit(solution)/shard_map/ppermute | solution.py:387
  44.7 28.6 %collective-permute-start.17 = (bf16[256,1152]{1,0:T(8,128)(2,1)}, bf16[256,1152]{1,0:T(8,128)(2,1)}, u32[]{:S(2)}, u32[]{:S(2)}) collective-permute-start(bf16[256,1152]{1,0:T(8,128)(2,1)} %get-tuple-element.54), channel_id=1, source_target_pairs={{0,192},{16,208},{32,224},{48,240},{64,0},{80,16},{96,32},{112,48}... | collective-permute-start | bytes 1769480 | tf_op jit(solution)/shard_map/ppermute | solution.py:387
  46.7 26.7 %copy-start.1 = (f32[256,1152]{1,0:T(8,128)S(1)}, f32[256,1152]{1,0:T(8,128)}, u32[]{:S(2)}) copy-start(f32[256,1152]{1,0:T(8,128)} %image_emb.1) | copy-start | bytes 3538948
  47.7 25.7 %collective-permute-start.15 = (bf16[256,1152]{1,0:T(8,128)(2,1)}, bf16[256,1152]{1,0:T(8,128)(2,1)}, u32[]{:S(2)}, u32[]{:S(2)}) collective-permute-start(bf16[256,1152]{1,0:T(8,128)(2,1)} %get-tuple-element.52), channel_id=1, source_target_pairs={{0,32},{16,48},{32,0},{48,16},{64,96},{80,112},{96,64},{112,80},{1... | collective-permute-start | bytes 1769480 | tf_op jit(solution)/shard_map/ppermute | solution.py:387
  48.8 3.7 %collective-permute-start = (f32[8,128]{1,0:T(8,128)S(1)}, f32[8,128]{1,0:T(8,128)S(1)}, u32[]{:S(2)}, u32[]{:S(2)}) collective-permute-start(f32[8,128]{1,0:T(8,128)S(1)} %param.1), channel_id=1, source_target_pairs={{0,1},{1,0},{2,3},{3,2},{4,5},{5,4},{6,7},{7,6},{8,9},{9,8},{10,11... | collective-permute-start | bytes 12296 | tf_op jit(solution)/shard_map/cond/branch_1_fun/ppermute | solution.py:408
  52.5 4.9 %collective-permute-start.1 = (f32[8,128]{1,0:T(8,128)S(1)}, f32[8,128]{1,0:T(8,128)S(1)}, u32[]{:S(2)}, u32[]{:S(2)}) collective-permute-start(f32[8,128]{1,0:T(8,128)S(1)} %add.9), channel_id=1, source_target_pairs={{0,2},{1,3},{2,0},{3,1},{4,6},{5,7},{6,4},{7,5},{8,10},{9,11},{10,... | collective-permute-start | bytes 12296 | tf_op jit(solution)/shard_map/cond/branch_1_fun/ppermute | solution.py:408
  57.4 7.1 %collective-permute-start.2 = (f32[8,128]{1,0:T(8,128)S(1)}, f32[8,128]{1,0:T(8,128)S(1)}, u32[]{:S(2)}, u32[]{:S(2)}) collective-permute-start(f32[8,128]{1,0:T(8,128)S(1)} %add.10), channel_id=1, source_target_pairs={{0,7},{1,6},{2,5},{3,4},{4,3},{5,2},{6,1},{7,0},{8,15},{9,14},{10,... | collective-permute-start | bytes 12296 | tf_op jit(solution)/shard_map/cond/branch_1_fun/ppermute | solution.py:408
  64.5 4.8 %collective-permute-start.3 = (f32[8,128]{1,0:T(8,128)S(1)}, f32[8,128]{1,0:T(8,128)S(1)}, u32[]{:S(2)}, u32[]{:S(2)}) collective-permute-start(f32[8,128]{1,0:T(8,128)S(1)} %add.11), channel_id=1, source_target_pairs={{0,40},{1,41},{2,42},{3,43},{4,44},{5,45},{6,46},{7,47},{8,32},{9,... | collective-permute-start | bytes 12296 | tf_op jit(solution)/shard_map/cond/branch_1_fun/ppermute | solution.py:408
  69.3 9.3 %collective-permute-start.21 = (f32[8,128]{1,0:T(8,128)S(1)}, f32[8,128]{1,0:T(8,128)S(1)}, u32[]{:S(2)}, u32[]{:S(2)}) collective-permute-start(f32[8,128]{1,0:T(8,128)S(1)} %get-tuple-element.64.sums), channel_id=1, source_target_pairs={{0,192},{16,208},{32,224},{48,240},{64,128},{80,144},{96,160},{112... | collective-permute-start | bytes 12296 | tf_op jit(solution)/shard_map/ppermute | solution.py:408
  69.5 9.2 %collective-permute-start.20 = (f32[8,128]{1,0:T(8,128)S(1)}, f32[8,128]{1,0:T(8,128)S(1)}, u32[]{:S(2)}, u32[]{:S(2)}) collective-permute-start(f32[8,128]{1,0:T(8,128)S(1)} %get-tuple-element.64.sums), channel_id=1, source_target_pairs={{0,128},{16,144},{32,160},{48,176},{64,192},{80,208},{96,224},{112... | collective-permute-start | bytes 12296 | tf_op jit(solution)/shard_map/ppermute | solution.py:408
  73.1 5.6 %collective-permute-start.19 = (f32[8,128]{1,0:T(8,128)S(1)}, f32[8,128]{1,0:T(8,128)S(1)}, u32[]{:S(2)}, u32[]{:S(2)}) collective-permute-start(f32[8,128]{1,0:T(8,128)S(1)} %get-tuple-element.64.sums), channel_id=1, source_target_pairs={{0,64},{16,80},{32,96},{48,112},{64,0},{80,16},{96,32},{112,48},{1... | collective-permute-start | bytes 12296 | tf_op jit(solution)/shard_map/ppermute | solution.py:408
  73.4 1.3 %copy-start.4 = (bf16[512,1152]{1,0:T(8,128)(2,1)S(1)}, bf16[512,1152]{1,0:T(8,128)(2,1)}, u32[]{:S(2)}) copy-start(bf16[512,1152]{1,0:T(8,128)(2,1)} %copy-done.3) | copy-start | bytes 3538948

commit v11 on v10

--- a/solution.py
+++ b/solution.py
@@ -9,7 +9,7 @@
 LOG2E = 1.4426950408889634
 BATCH = 65536
 GATE_COST = 1
-CUT_COST = 1024 * 32
+CUT_COST = 1
 STEPS = (("group", 1), ("group", 2), ("group", 7), (("blk", "group"), 2 * 16 + 8))
 BF16 = jnp.bfloat16
 HBM = pl.BlockSpec(memory_space=pltpu.HBM)
@@ -178,12 +178,13 @@
 
 def far_grad_kernel(
     far_images, far_grads, near_images, texts, near_grads, own_p, sums,
-    far_out, y_out, mate_out, own_out, sums_out,
+    far_top, far_bot, y_out, mate_out, own_out, sums_out,
 ):
     rows = far_images.shape[0]
-    far_out[...] = jnp.dot(
-        far_grads[...], texts[...], preferred_element_type=F32
-    ).astype(BF16)
+    half = rows // 2
+    partial = jnp.dot(far_grads[...], texts[...], preferred_element_type=F32)
+    far_top[...] = partial[:half].astype(BF16)
+    far_bot[...] = partial[half:].astype(BF16)
     for t, out in (
         (3, mate_out.at[pl.ds(0, rows)]),
         (1, mate_out.at[pl.ds(rows, rows)]),
@@ -204,7 +205,7 @@
         near_kernel,
         out_shape=(
             shape((rows, width), BF16),
-            shape((rows, width), BF16),
+            shape((rows, width), F32),
             shape((rows, width), BF16),
             shape((3 * rows, width), BF16),
             shape((4 * rows, width), BF16),
@@ -248,12 +249,13 @@
     shape = jax.ShapeDtypeStruct
     return pl.pallas_call(
         far_grad_kernel,
-        out_shape=(
-            shape((rows, width), BF16), shape((rows, width), F32), shape((2 * rows, width), BF16),
+        out_shape=(shape((rows // 2, width), BF16),) * 2
+        + (
+            shape((rows, width), F32), shape((2 * rows, width), BF16),
             shape((2 * rows, width), BF16), shape(sums.shape, F32),
         ),
         in_specs=[VMEM] * 7,
-        out_specs=(VMEM,) * 5,
+        out_specs=(VMEM,) * 6,
         compiler_params=params(16),
         cost_estimate=pl.CostEstimate(
             flops=rows * rows * width, bytes_accessed=2 * rows * width, transcendentals=0
@@ -282,24 +284,30 @@
     )(*parts)
 
 
-def relay_y_kernel(own, passing, sums, sums_a, sums_b, sums_c, out, sums_out):
-    rows = own.shape[0]
-    out[...] = (own[...] + passing[:rows, :].astype(F32)).astype(BF16)
+def relay_kernel(
+    y_own, y_passing, left, left_passing, sums, sums_a, sums_b, sums_c, y_out, left_out, sums_out
+):
+    rows = y_own.shape[0]
+    half = rows // 2
+    y_out[...] = (y_own[...] + y_passing[:rows, :].astype(F32)).astype(BF16)
+    left_out[:half, :] = left[:half, :].astype(BF16)
+    left_out[half:, :] = (left[half:, :] + left_passing[...].astype(F32)).astype(BF16)
     sums_out[...] = sums[...] + sums_a[...] + sums_b[...] + sums_c[...]
 
 
-def relay_y(own, passing, sums, *arrived):
-    return pl.pallas_call(
-        relay_y_kernel,
-        out_shape=(
-            jax.ShapeDtypeStruct(own.shape, BF16), jax.ShapeDtypeStruct(sums.shape, F32)
-        ),
-        in_specs=[VMEM] * 6,
-        out_specs=(VMEM,) * 2,
-        compiler_params=params(16),
-        cost_estimate=pl.CostEstimate(flops=own.size, bytes_accessed=own.size, transcendentals=0),
-        name="relay_y",
-    )(own, passing, sums, *arrived)
+def relay(y_own, y_passing, left, left_passing, sums, *arrived):
+    shape = jax.ShapeDtypeStruct
+    return pl.pallas_call(
+        relay_kernel,
+        out_shape=(shape(y_own.shape, BF16), shape(left.shape, BF16), shape(sums.shape, F32)),
+        in_specs=[VMEM] * 8,
+        out_specs=(VMEM,) * 3,
+        compiler_params=params(16),
+        cost_estimate=pl.CostEstimate(
+            flops=y_own.size, bytes_accessed=y_own.size, transcendentals=0
+        ),
+        name="relay",
+    )(y_own, y_passing, left, left_passing, sums, *arrived)
 
 
 def backnorm(emb, upstream, scale):
@@ -324,8 +332,9 @@
             at = pl.ds(i * step, step)
             upstream = own[pl.ds((4 * k + i) * step, step), :].astype(F32)
             for part in parts:
-                skip = part.shape[0] - 4 * step
-                upstream += part[pl.ds(skip + i * step, step), :].astype(F32)
+                start = max(part.shape[0] - 4 * step, 0) + i * step
+                if start < part.shape[0]:
+                    upstream += part[pl.ds(start, step), :].astype(F32)
             slots[at, :] = backnorm(emb[at, :], upstream, scale)
             copy = pltpu.make_async_copy(slots.at[at], out.at[at], sems.at[len(copies)])
             copy.start()
@@ -401,19 +410,20 @@
         scalars, (own_i, left_i, right_i), (own_t, core_t, y_t, yc_t)
     )
     from_left = send(right_p, ahead)
-    from_right = send(left_p, back)
     far_images, far_grads, sums = far_part(scalars, (top_i, bot_i), texts, near_sums)
 
     def pair(value, axis, k):
         return lax.ppermute(value, axis, [(i, i ^ k) for i in range(lax.axis_size(axis))])
 
     over_y_core = [pair(sums, "blk", k) for k in (3, 2, 1)]
-    far_p, y_q, to_mate, own, sums = far_grad_part(
+    far_top, far_bot, y_q, to_mate, own, sums = far_grad_part(
         far_images, far_grads, near_images, texts, near_grads, own_p, sums
     )
-    from_far = send(far_p, [(i, (i + 8) % blocks) for i in range(blocks)])
+    from_far = send(far_top, [(i, (i + 8) % blocks) for i in range(blocks)])
+    relay_bot = send(far_bot, back)
     from_core = send(to_mate, across_core)
-    y_sum, sums_2 = relay_y(y_q, from_core, sums, *over_y_core)
+    y_sum, left_sum, sums_2 = relay(y_q, from_core, left_p, relay_bot, sums, *over_y_core)
+    from_right = send(left_sum, back)
     from_y = send(y_sum, across_y)
     sums_2 = add(sums_2)
 

time: 80.4 us -> 85.1 us (1.058)
  starting transfers between devices: 28.2 us -> 31.8 us
  local copies, waits for them, and re-layouts: 2.55 us -> 3.64 us
    ppermute x12 -> x13, starting transfers between devices: 11.8 us -> 13.9 us  [send(): return lax.ppermute(value, 'blk', perm)]
    ppermute x10, starting transfers between devices: 16.4 us -> 17.9 us  [pair(): lax.ppermute(value, axis, [(i, i ^ k) for i in range(lax.axis_size(axis))])]
    unnamed x10, local copies, waits for them, and re-layouts: 2.55 us -> 3.64 us
    pallas_call x2, Pallas kernels: 1.11 us -> 0.04 us  [cut(): pl.pallas_call(kernel, out_shape=jax.ShapeDtypeStruct((rows // 2, width),...]
    ppermute x12 -> x13, waiting for transfers between devices: 15.9 us -> 16.5 us  [send(): return lax.ppermute(value, 'blk', perm)]
  transfers between devices with their start and end apart: 22 -> 23, of which waited for: 10 -> 9; matrix products, arithmetic and copies ran while one was open for 0% -> 0% of each run, Pallas kernels for 18% -> 15%
where the time goes in v11:
time: 85.1 us; the launch traced here: 84.3 us
  starting transfers between devices  31.8 us (37%)
  waiting for transfers between devices  26.5 us (31%)
  Pallas kernels  19.3 us (23%)
  local copies, waits for them, and re-layouts  3.64 us (4%)
  between operations  2.92 us (3%)
    ppermute x10, starting transfers between devices, pair(): lax.ppermute(value, axis, [(i, i ^ k) for i in range(lax.axis_size(axis))])  17.9 us
    ppermute x13, waiting for transfers between devices, send(): return lax.ppermute(value, 'blk', perm)  16.5 us
    ppermute x13, starting transfers between devices, send(): return lax.ppermute(value, 'blk', perm)  13.9 us
    ppermute x10, waiting for transfers between devices, pair(): lax.ppermute(value, axis, [(i, i ^ k) for i in range(lax.axis_size(axis))])  10.1 us
    pallas_call x1, Pallas kernels, near_part(): pl.pallas_call(near_kernel, out_shape=(shape((rows, width), BF16), shape(...  7.68 us
    pallas_call x1, Pallas kernels, end_part(): pl.pallas_call(end_kernel, out_shape=(shape((rows, width), F32),) * 2 + (...  3.8 us
    pallas_call x1, Pallas kernels, far_grad_part(): pl.pallas_call(far_grad_kernel, out_shape=(shape((rows // 2, width), BF16...  3.67 us
    unnamed x10, local copies, waits for them, and re-layouts  3.64 us
  transfers between devices with their start and end apart: 23, of which 9 were waited for; matrix products, arithmetic and copies ran while one was open for 0% of the time, Pallas kernels for 15%

profile of v11, /device:TPU:32, one launch (start us, length us, event | category | flops | bytes accessed | tf_op | source)
XLA Modules:
  0.0 84.3 jit_solution(13376829529998256813)
XLA Ops:
  0.6 0.0 copy-start
  0.6 1.3 %copy-done = f32[256,1152]{1,0:T(8,128)S(1)} copy-done((f32[256,1152]{1,0:T(8,128)S(1)}, f32[256,1152]{1,0:T(8,128)}, u32[]{:S(2)}) %copy-start) | copy-done | bytes 1179672
  1.9 0.2 normalize.2
  2.1 1.1 %copy-done.2 = f32[256,1152]{1,0:T(8,128)S(1)} copy-done((f32[256,1152]{1,0:T(8,128)S(1)}, f32[256,1152]{1,0:T(8,128)}, u32[]{:S(2)}) %copy-start.2) | copy-done | bytes 1179672
  3.2 0.7 normalize.3
  3.9 1.6 %collective-permute-start.9 = (bf16[256,1152]{1,0:T(8,128)(2,1)S(1)}, bf16[256,1152]{1,0:T(8,128)(2,1)}, u32[]{:S(2)}, u32[]{:S(2)}) collective-permute-start(bf16[256,1152]{1,0:T(8,128)(2,1)S(1)} %get-tuple-element.41.own_t), channel_id=1, source_target_pairs={{0,32},{16,48},{32,0},{48,16},{64,96},{80,112},{96,64},{112,80},{1... | collective-permute-start | bytes 1769480 | tf_op jit(solution)/shard_map/ppermute | solution.py:396
  5.5 2.8 %collective-permute-start.6 = (bf16[256,1152]{1,0:T(8,128)(2,1)S(1)}, bf16[256,1152]{1,0:T(8,128)(2,1)S(1)}, u32[]{:S(2)}, u32[]{:S(2)}) collective-permute-start(bf16[256,1152]{1,0:T(8,128)(2,1)S(1)} %get-tuple-element.39.own_i), channel_id=1, source_target_pairs={{0,192},{16,208},{32,224},{48,240},{64,0},{80,16},{96,32},{112,48}... | collective-permute-start | bytes 1769480 | tf_op jit(solution)/shard_map/ppermute | solution.py:396
  8.2 10.8 %collective-permute-done.9.y_t = bf16[256,1152]{1,0:T(8,128)(2,1)} collective-permute-done((bf16[256,1152]{1,0:T(8,128)(2,1)S(1)}, bf16[256,1152]{1,0:T(8,128)(2,1)}, u32[]{:S(2)}, u32[]{:S(2)}) %collective-permute-start.9) | collective-permute-done | bytes 589856 | tf_op jit(solution)/shard_map/ppermute | solution.py:396
  19.1 0.0 collective-permute-start.10
  20.4 0.2 collective-permute-done.6.block_ref.right_i
  20.5 3.8 %collective-permute-start.7 = (bf16[128,1152]{1,0:T(8,128)(2,1)S(1)}, bf16[128,1152]{1,0:T(8,128)(2,1)S(1)}, u32[]{:S(2)}, u32[]{:S(2)}) collective-permute-start(bf16[128,1152]{1,0:T(8,128)(2,1)S(1)} %cut.3), channel_id=1, source_target_pairs={{0,192},{16,208},{32,224},{48,240},{64,0},{80,16},{96,32},{112,48}... | collective-permute-start | bytes 884744 | tf_op jit(solution)/shard_map/ppermute | solution.py:396
  24.3 0.0 collective-permute-done.4.block_ref.left_i
  24.3 0.3 collective-permute-start.5
  24.6 7.7 %near.1 = (bf16[256,1152]{1,0:T(8,128)(2,1)S(1)}, f32[256,1152]{1,0:T(8,128)S(1)}, bf16[256,1152]{1,0:T(8,128)(2,1)}, bf16[768,1152]{1,0:T(8,128)(2,1)S(1)}, bf1...) custom-call(f32[1]{0:T(128)} %bitcast.6.log_scale, ...), custom_call_target="tpu_custom_call" | custom-call | flops 28991029248 | bytes 7077888 | tf_op jit(solution)/shard_map/near/pallas_call | solution.py:204
  32.3 0.0 collective-permute-done.7.bot_i
  32.3 1.5 %collective-permute-done.5.top_i = bf16[128,1152]{1,0:T(8,128)(2,1)S(1)} collective-permute-done((bf16[128,1152]{1,0:T(8,128)(2,1)S(1)}, bf16[128,1152]{1,0:T(8,128)(2,1)S(1)}, u32[]{:S(2)}, u32[]{:S(2)}) %collective-permute-start.5) | collective-permute-done | bytes 294944 | tf_op jit(solution)/shard_map/ppermute | solution.py:396
  33.9 1.4 %far.1 = (bf16[256,1152]{1,0:T(8,128)(2,1)S(1)}, bf16[256,1024]{1,0:T(8,128)(2,1)S(1)}, f32[8,128]{1,0:T(8,128)S(1)}) custom-call(f32[1]{0:T(128)} %bitcast.7.log_scale, f32[1]{0:T(128)} %bitcast.10.bias, bf16[128,1152]{1,0:T(8,128)(2,1)S(1)} %collective-permute-done.5.top_i, bf16[128,1152]{1,0:T(8,128)(2,1)S(1)} %collective-permute-done.7.bot_i, ...), custom_call_target="tpu_custom_call" | custom-call | flops 75497472 | bytes 589824 | tf_op jit(solution)/shard_map/far/pallas_call | solution.py:232
  35.3 3.7 %far_grad.1 = (bf16[128,1152]{1,0:T(8,128)(2,1)}, bf16[128,1152]{1,0:T(8,128)(2,1)S(1)}, f32[256,1152]{1,0:T(8,128)S(1)}, bf16[512,1152]{1,0:T(8,128)(2,1)S(1)},...) custom-call(bf16[256,1152]{1,0:T(8,128)(2,1)S(1)} %get-tuple-element.44.far_images, ...), custom_call_target="tpu_custom_call" | custom-call | flops 75497472 | bytes 589824 | tf_op jit(solution)/shard_map/far_grad/pallas_call | solution.py:250
  38.9 0.0 copy-start.3
  39.0 0.1 collective-permute-start.11
  39.1 1.7 %collective-permute-start.12 = (bf16[128,1152]{1,0:T(8,128)(2,1)S(1)}, bf16[128,1152]{1,0:T(8,128)(2,1)S(1)}, u32[]{:S(2)}, u32[]{:S(2)}) collective-permute-start(bf16[128,1152]{1,0:T(8,128)(2,1)S(1)} %get-tuple-element.54), channel_id=1, source_target_pairs={{0,192},{16,208},{32,224},{48,240},{64,0},{80,16},{96,32},{112,48}... | collective-permute-start | bytes 884744 | tf_op jit(solution)/shard_map/ppermute | solution.py:396
  40.8 0.2 collective-permute-start.15
  41.0 0.5 collective-permute-start.14
  41.4 1.2 %collective-permute-start.13 = (f32[8,128]{1,0:T(8,128)S(1)}, f32[8,128]{1,0:T(8,128)S(1)}, u32[]{:S(2)}, u32[]{:S(2)}) collective-permute-start(f32[8,128]{1,0:T(8,128)S(1)} %get-tuple-element.49.sums), channel_id=1, source_target_pairs={{0,48},{16,32},{32,16},{48,0},{64,112},{80,96},{96,80},{112,64},{1... | collective-permute-start | bytes 12296 | tf_op jit(solution)/shard_map/ppermute | solution.py:416
  42.7 0.0 collective-permute-done.15.sums_c
  42.7 0.4 collective-permute-start.17
  43.0 1.5 %collective-permute-done.14.sums_b = f32[8,128]{1,0:T(8,128)S(1)} collective-permute-done((f32[8,128]{1,0:T(8,128)S(1)}, f32[8,128]{1,0:T(8,128)S(1)}, u32[]{:S(2)}, u32[]{:S(2)}) %collective-permute-start.14) | collective-permute-done | bytes 4128 | tf_op jit(solution)/shard_map/ppermute | solution.py:416
  44.6 0.0 collective-permute-done.13.sums_a
  44.6 3.9 %collective-permute-done.12.left_passing = bf16[128,1152]{1,0:T(8,128)(2,1)S(1)} collective-permute-done((bf16[128,1152]{1,0:T(8,128)(2,1)S(1)}, bf16[128,1152]{1,0:T(8,128)(2,1)S(1)}, u32[]{:S(2)}, u32[]{:S(2)}) %collective-permute-start.12) | collective-permute-done | bytes 294944 | tf_op jit(solution)/shard_map/ppermute | solution.py:396
  48.5 1.2 %relay.1 = (bf16[256,1152]{1,0:T(8,128)(2,1)}, bf16[256,1152]{1,0:T(8,128)(2,1)}, f32[8,128]{1,0:T(8,128)S(1)}) custom-call(f32[256,1152]{1,0:T(8,128)S(1)} %get-tuple-element.52.y_own, bf16[512,1152]{1,0:T(8,128)(2,1)S(1)} %collective-permute-done.11.y_passing.from_core, f32[256,1152]{1,0:T(8,128)S(1)} %get-tuple-element.53.left, ...), custom_call_target="tpu_custom_call" | custom-call | flops 294912 | bytes 294912 | tf_op jit(solution)/shard_map/relay/pallas_call | solution.py:300
  49.7 1.6 %collective-permute-start.16 = (bf16[256,1152]{1,0:T(8,128)(2,1)}, bf16[256,1152]{1,0:T(8,128)(2,1)}, u32[]{:S(2)}, u32[]{:S(2)}) collective-permute-start(bf16[256,1152]{1,0:T(8,128)(2,1)} %get-tuple-element.56), channel_id=1, source_target_pairs={{0,32},{16,48},{32,0},{48,16},{64,96},{80,112},{96,64},{112,80},{1... | collective-permute-start | bytes 1769480 | tf_op jit(solution)/shard_map/ppermute | solution.py:396
  51.3 1.8 %collective-permute-start.18 = (bf16[256,1152]{1,0:T(8,128)(2,1)}, bf16[256,1152]{1,0:T(8,128)(2,1)}, u32[]{:S(2)}, u32[]{:S(2)}) collective-permute-start(bf16[256,1152]{1,0:T(8,128)(2,1)} %get-tuple-element.58), channel_id=1, source_target_pairs={{0,192},{16,208},{32,224},{48,240},{64,0},{80,16},{96,32},{112,48}... | collective-permute-start | bytes 1769480 | tf_op jit(solution)/shard_map/ppermute | solution.py:396
  53.7 20.5 %conditional.1 = (f32[8,128]{1,0:T(8,128)S(1)}) conditional(s32[]{:T(128)} %bitcast.2, f32[8,128]{1,0:T(8,128)S(1)} %add.13, f32[8,128]{1,0:T(8,128)S(1)} %add.13), branch_computations={%region_0.0_spmd, %region_1.0_spmd} | conditional | flops 4096 | bytes 114856 | solution.py:435
  53.8 0.2 collective-permute-start
  54.0 3.5 %collective-permute-done = f32[8,128]{1,0:T(8,128)S(1)} collective-permute-done((f32[8,128]{1,0:T(8,128)S(1)}, f32[8,128]{1,0:T(8,128)S(1)}, u32[]{:S(2)}, u32[]{:S(2)}) %collective-permute-start) | collective-permute-done | bytes 4128 | tf_op jit(solution)/shard_map/cond/branch_1_fun/ppermute | solution.py:416
  57.5 3.3 %collective-permute-start.1 = (f32[8,128]{1,0:T(8,128)S(1)}, f32[8,128]{1,0:T(8,128)S(1)}, u32[]{:S(2)}, u32[]{:S(2)}) collective-permute-start(f32[8,128]{1,0:T(8,128)S(1)} %add.9), channel_id=1, source_target_pairs={{0,2},{1,3},{2,0},{3,1},{4,6},{5,7},{6,4},{7,5},{8,10},{9,11},{10,... | collective-permute-start | bytes 12296 | tf_op jit(solution)/shard_map/cond/branch_1_fun/ppermute | solution.py:416
  60.7 1.6 %collective-permute-done.1 = f32[8,128]{1,0:T(8,128)S(1)} collective-permute-done((f32[8,128]{1,0:T(8,128)S(1)}, f32[8,128]{1,0:T(8,128)S(1)}, u32[]{:S(2)}, u32[]{:S(2)}) %collective-permute-start.1) | collective-permute-done | bytes 4128 | tf_op jit(solution)/shard_map/cond/branch_1_fun/ppermute | solution.py:416
  62.3 5.5 %collective-permute-start.2 = (f32[8,128]{1,0:T(8,128)S(1)}, f32[8,128]{1,0:T(8,128)S(1)}, u32[]{:S(2)}, u32[]{:S(2)}) collective-permute-start(f32[8,128]{1,0:T(8,128)S(1)} %add.10), channel_id=1, source_target_pairs={{0,7},{1,6},{2,5},{3,4},{4,3},{5,2},{6,1},{7,0},{8,15},{9,14},{10,... | collective-permute-start | bytes 12296 | tf_op jit(solution)/shard_map/cond/branch_1_fun/ppermute | solution.py:416
  67.8 1.6 %collective-permute-done.2 = f32[8,128]{1,0:T(8,128)S(1)} collective-permute-done((f32[8,128]{1,0:T(8,128)S(1)}, f32[8,128]{1,0:T(8,128)S(1)}, u32[]{:S(2)}, u32[]{:S(2)}) %collective-permute-start.2) | collective-permute-done | bytes 4128 | tf_op jit(solution)/shard_map/cond/branch_1_fun/ppermute | solution.py:416
  69.4 3.0 %collective-permute-start.3 = (f32[8,128]{1,0:T(8,128)S(1)}, f32[8,128]{1,0:T(8,128)S(1)}, u32[]{:S(2)}, u32[]{:S(2)}) collective-permute-start(f32[8,128]{1,0:T(8,128)S(1)} %add.11), channel_id=1, source_target_pairs={{0,40},{1,41},{2,42},{3,43},{4,44},{5,45},{6,46},{7,47},{8,32},{9,... | collective-permute-start | bytes 12296 | tf_op jit(solution)/shard_map/cond/branch_1_fun/ppermute | solution.py:416
  72.4 1.8 %collective-permute-done.3 = f32[8,128]{1,0:T(8,128)S(1)} collective-permute-done((f32[8,128]{1,0:T(8,128)S(1)}, f32[8,128]{1,0:T(8,128)S(1)}, u32[]{:S(2)}, u32[]{:S(2)}) %collective-permute-start.3) | collective-permute-done | bytes 4128 | tf_op jit(solution)/shard_map/cond/branch_1_fun/ppermute | solution.py:416
  74.2 2.9 %collective-permute-start.22 = (f32[8,128]{1,0:T(8,128)S(1)}, f32[8,128]{1,0:T(8,128)S(1)}, u32[]{:S(2)}, u32[]{:S(2)}) collective-permute-start(f32[8,128]{1,0:T(8,128)S(1)} %get-tuple-element.68.sums), channel_id=1, source_target_pairs={{0,192},{16,208},{32,224},{48,240},{64,128},{80,144},{96,160},{112... | collective-permute-start | bytes 12296 | tf_op jit(solution)/shard_map/ppermute | solution.py:416
  77.1 0.7 collective-permute-start.21
  77.9 0.5 collective-permute-start.20
  78.3 0.0 copy-start.4
  78.4 1.3 %copy-done.4 = bf16[512,1152]{1,0:T(8,128)(2,1)S(1)} copy-done((bf16[512,1152]{1,0:T(8,128)(2,1)S(1)}, bf16[512,1152]{1,0:T(8,128)(2,1)}, u32[]{:S(2)}) %copy-start.4) | copy-done | bytes 1179672
  79.6 3.8 %end.1 = (f32[256,1152]{1,0:T(8,128)}, f32[256,1152]{1,0:T(8,128)}, f32[8,128]{1,0:T(8,128)S(1)}) custom-call(f32[1]{0:T(128)} %bitcast.8.log_scale, bf16[512,1152]{1,0:T(8,128)(2,1)S(1)} %copy-done.4, f32[256,1152]{1,0:T(8,128)S(1)} %copy-done.2, bf16[512,1152]{1,0:T(8,128)(2,1)S(1)} %collective-permute-done.11.y_passing.from_core, ...), custom_call_target="tpu_custom_call" | custom-call | flops 4718592 | bytes 589824 | tf_op jit(solution)/shard_map/end/pallas_call | solution.py:350
  83.5 0.6 totals.1
  (24 shorter events, 0.1 us)
Async XLA Ops:
  0.6 1.3 %copy-start = (f32[256,1152]{1,0:T(8,128)S(1)}, f32[256,1152]{1,0:T(8,128)}, u32[]{:S(2)}) copy-start(f32[256,1152]{1,0:T(8,128)} %image_emb.1) | copy-start | bytes 3538948
  1.9 1.3 %copy-start.2 = (f32[256,1152]{1,0:T(8,128)S(1)}, f32[256,1152]{1,0:T(8,128)}, u32[]{:S(2)}) copy-start(f32[256,1152]{1,0:T(8,128)} %text_emb.1) | copy-start | bytes 3538948
  3.9 15.2 %collective-permute-start.9 = (bf16[256,1152]{1,0:T(8,128)(2,1)S(1)}, bf16[256,1152]{1,0:T(8,128)(2,1)}, u32[]{:S(2)}, u32[]{:S(2)}) collective-permute-start(bf16[256,1152]{1,0:T(8,128)(2,1)S(1)} %get-tuple-element.41.own_t), channel_id=1, source_target_pairs={{0,32},{16,48},{32,0},{48,16},{64,96},{80,112},{96,64},{112,80},{1... | collective-permute-start | bytes 1769480 | tf_op jit(solution)/shard_map/ppermute | solution.py:396
  5.5 15.1 %collective-permute-start.6 = (bf16[256,1152]{1,0:T(8,128)(2,1)S(1)}, bf16[256,1152]{1,0:T(8,128)(2,1)S(1)}, u32[]{:S(2)}, u32[]{:S(2)}) collective-permute-start(bf16[256,1152]{1,0:T(8,128)(2,1)S(1)} %get-tuple-element.39.own_i), channel_id=1, source_target_pairs={{0,192},{16,208},{32,224},{48,240},{64,0},{80,16},{96,32},{112,48}... | collective-permute-start | bytes 1769480 | tf_op jit(solution)/shard_map/ppermute | solution.py:396
  8.2 16.1 %collective-permute-start.4 = (bf16[256,1152]{1,0:T(8,128)(2,1)S(1)}, bf16[256,1152]{1,0:T(8,128)(2,1)S(1)}, u32[]{:S(2)}, u32[]{:S(2)}) collective-permute-start(bf16[256,1152]{1,0:T(8,128)(2,1)S(1)} %get-tuple-element.39.own_i), channel_id=1, source_target_pairs={{0,64},{16,80},{32,96},{48,112},{64,128},{80,144},{96,160},{112,17... | collective-permute-start | bytes 1769480 | tf_op jit(solution)/shard_map/ppermute | solution.py:396
  8.2 16.4 %collective-permute-start.8 = (bf16[256,1152]{1,0:T(8,128)(2,1)S(1)}, bf16[256,1152]{1,0:T(8,128)(2,1)}, u32[]{:S(2)}, u32[]{:S(2)}) collective-permute-start(bf16[256,1152]{1,0:T(8,128)(2,1)S(1)} %get-tuple-element.41.own_t), channel_id=1, source_target_pairs={{0,16},{16,0},{32,48},{48,32},{64,80},{80,64},{96,112},{112,96},{1... | collective-permute-start | bytes 1769480 | tf_op jit(solution)/shard_map/ppermute | solution.py:396
  19.1 5.6 %collective-permute-start.10 = (bf16[256,1152]{1,0:T(8,128)(2,1)}, bf16[256,1152]{1,0:T(8,128)(2,1)}, u32[]{:S(2)}, u32[]{:S(2)}) collective-permute-start(bf16[256,1152]{1,0:T(8,128)(2,1)} %collective-permute-done.9.y_t), channel_id=1, source_target_pairs={{0,16},{16,0},{32,48},{48,32},{64,80},{80,64},{96,112},{112,96},{1... | collective-permute-start | bytes 1769480 | tf_op jit(solution)/shard_map/ppermute | solution.py:396
  20.5 11.8 %collective-permute-start.7 = (bf16[128,1152]{1,0:T(8,128)(2,1)S(1)}, bf16[128,1152]{1,0:T(8,128)(2,1)S(1)}, u32[]{:S(2)}, u32[]{:S(2)}) collective-permute-start(bf16[128,1152]{1,0:T(8,128)(2,1)S(1)} %cut.3), channel_id=1, source_target_pairs={{0,192},{16,208},{32,224},{48,240},{64,0},{80,16},{96,32},{112,48}... | collective-permute-start | bytes 884744 | tf_op jit(solution)/shard_map/ppermute | solution.py:396
  24.3 9.5 %collective-permute-start.5 = (bf16[128,1152]{1,0:T(8,128)(2,1)S(1)}, bf16[128,1152]{1,0:T(8,128)(2,1)S(1)}, u32[]{:S(2)}, u32[]{:S(2)}) collective-permute-start(bf16[128,1152]{1,0:T(8,128)(2,1)S(1)} %cut.2), channel_id=1, source_target_pairs={{0,64},{16,80},{32,96},{48,112},{64,128},{80,144},{96,160},{112,17... | collective-permute-start | bytes 884744 | tf_op jit(solution)/shard_map/ppermute | solution.py:396
  38.9 10.8 %copy-start.3 = (bf16[512,1152]{1,0:T(8,128)(2,1)}, bf16[512,1152]{1,0:T(8,128)(2,1)S(1)}, u32[]{:S(2)}) copy-start(bf16[512,1152]{1,0:T(8,128)(2,1)S(1)} %get-tuple-element.50.own) | copy-start | bytes 3538948
  39.0 9.5 %collective-permute-start.11 = (bf16[512,1152]{1,0:T(8,128)(2,1)S(1)}, bf16[512,1152]{1,0:T(8,128)(2,1)S(1)}, u32[]{:S(2)}, u32[]{:S(2)}) collective-permute-start(bf16[512,1152]{1,0:T(8,128)(2,1)S(1)} %get-tuple-element.51), channel_id=1, source_target_pairs={{0,16},{16,0},{32,48},{48,32},{64,80},{80,64},{96,112},{112,96},{1... | collective-permute-start | bytes 3538952 | tf_op jit(solution)/shard_map/ppermute | solution.py:396
  39.1 9.4 %collective-permute-start.12 = (bf16[128,1152]{1,0:T(8,128)(2,1)S(1)}, bf16[128,1152]{1,0:T(8,128)(2,1)S(1)}, u32[]{:S(2)}, u32[]{:S(2)}) collective-permute-start(bf16[128,1152]{1,0:T(8,128)(2,1)S(1)} %get-tuple-element.54), channel_id=1, source_target_pairs={{0,192},{16,208},{32,224},{48,240},{64,0},{80,16},{96,32},{112,48}... | collective-permute-start | bytes 884744 | tf_op jit(solution)/shard_map/ppermute | solution.py:396
  40.8 1.9 %collective-permute-start.15 = (f32[8,128]{1,0:T(8,128)S(1)}, f32[8,128]{1,0:T(8,128)S(1)}, u32[]{:S(2)}, u32[]{:S(2)}) collective-permute-start(f32[8,128]{1,0:T(8,128)S(1)} %get-tuple-element.49.sums), channel_id=1, source_target_pairs={{0,16},{16,0},{32,48},{48,32},{64,80},{80,64},{96,112},{112,96},{1... | collective-permute-start | bytes 12296 | tf_op jit(solution)/shard_map/ppermute | solution.py:416
  41.0 3.6 %collective-permute-start.14 = (f32[8,128]{1,0:T(8,128)S(1)}, f32[8,128]{1,0:T(8,128)S(1)}, u32[]{:S(2)}, u32[]{:S(2)}) collective-permute-start(f32[8,128]{1,0:T(8,128)S(1)} %get-tuple-element.49.sums), channel_id=1, source_target_pairs={{0,32},{16,48},{32,0},{48,16},{64,96},{80,112},{96,64},{112,80},{1... | collective-permute-start | bytes 12296 | tf_op jit(solution)/shard_map/ppermute | solution.py:416
  41.4 3.1 %collective-permute-start.13 = (f32[8,128]{1,0:T(8,128)S(1)}, f32[8,128]{1,0:T(8,128)S(1)}, u32[]{:S(2)}, u32[]{:S(2)}) collective-permute-start(f32[8,128]{1,0:T(8,128)S(1)} %get-tuple-element.49.sums), channel_id=1, source_target_pairs={{0,48},{16,32},{32,16},{48,0},{64,112},{80,96},{96,80},{112,64},{1... | collective-permute-start | bytes 12296 | tf_op jit(solution)/shard_map/ppermute | solution.py:416
  42.7 35.2 %collective-permute-start.17 = (bf16[256,1152]{1,0:T(8,128)(2,1)}, bf16[256,1152]{1,0:T(8,128)(2,1)}, u32[]{:S(2)}, u32[]{:S(2)}) collective-permute-start(bf16[256,1152]{1,0:T(8,128)(2,1)} %get-tuple-element.57), channel_id=1, source_target_pairs={{0,64},{16,80},{32,96},{48,112},{64,128},{80,144},{96,160},{112,17... | collective-permute-start | bytes 1769480 | tf_op jit(solution)/shard_map/ppermute | solution.py:396
  48.5 29.9 %copy-start.1 = (f32[256,1152]{1,0:T(8,128)S(1)}, f32[256,1152]{1,0:T(8,128)}, u32[]{:S(2)}) copy-start(f32[256,1152]{1,0:T(8,128)} %image_emb.1) | copy-start | bytes 3538948
  49.7 28.6 %collective-permute-start.16 = (bf16[256,1152]{1,0:T(8,128)(2,1)}, bf16[256,1152]{1,0:T(8,128)(2,1)}, u32[]{:S(2)}, u32[]{:S(2)}) collective-permute-start(bf16[256,1152]{1,0:T(8,128)(2,1)} %get-tuple-element.56), channel_id=1, source_target_pairs={{0,32},{16,48},{32,0},{48,16},{64,96},{80,112},{96,64},{112,80},{1... | collective-permute-start | bytes 1769480 | tf_op jit(solution)/shard_map/ppermute | solution.py:396
  51.3 27.0 %collective-permute-start.18 = (bf16[256,1152]{1,0:T(8,128)(2,1)}, bf16[256,1152]{1,0:T(8,128)(2,1)}, u32[]{:S(2)}, u32[]{:S(2)}) collective-permute-start(bf16[256,1152]{1,0:T(8,128)(2,1)} %get-tuple-element.58), channel_id=1, source_target_pairs={{0,192},{16,208},{32,224},{48,240},{64,0},{80,16},{96,32},{112,48}... | collective-permute-start | bytes 1769480 | tf_op jit(solution)/shard_map/ppermute | solution.py:396
  53.1 24.1 %collective-permute-start.19 = (bf16[128,1152]{1,0:T(8,128)(2,1)}, bf16[128,1152]{1,0:T(8,128)(2,1)}, u32[]{:S(2)}, u32[]{:S(2)}) collective-permute-start(bf16[128,1152]{1,0:T(8,128)(2,1)} %get-tuple-element.59), channel_id=1, source_target_pairs={{0,128},{16,144},{32,160},{48,176},{64,192},{80,208},{96,224},{112... | collective-permute-start | bytes 884744 | tf_op jit(solution)/shard_map/ppermute | solution.py:396
  53.8 3.7 %collective-permute-start = (f32[8,128]{1,0:T(8,128)S(1)}, f32[8,128]{1,0:T(8,128)S(1)}, u32[]{:S(2)}, u32[]{:S(2)}) collective-permute-start(f32[8,128]{1,0:T(8,128)S(1)} %param.1), channel_id=1, source_target_pairs={{0,1},{1,0},{2,3},{3,2},{4,5},{5,4},{6,7},{7,6},{8,9},{9,8},{10,11... | collective-permute-start | bytes 12296 | tf_op jit(solution)/shard_map/cond/branch_1_fun/ppermute | solution.py:416
  57.5 4.9 %collective-permute-start.1 = (f32[8,128]{1,0:T(8,128)S(1)}, f32[8,128]{1,0:T(8,128)S(1)}, u32[]{:S(2)}, u32[]{:S(2)}) collective-permute-start(f32[8,128]{1,0:T(8,128)S(1)} %add.9), channel_id=1, source_target_pairs={{0,2},{1,3},{2,0},{3,1},{4,6},{5,7},{6,4},{7,5},{8,10},{9,11},{10,... | collective-permute-start | bytes 12296 | tf_op jit(solution)/shard_map/cond/branch_1_fun/ppermute | solution.py:416
  62.3 7.1 %collective-permute-start.2 = (f32[8,128]{1,0:T(8,128)S(1)}, f32[8,128]{1,0:T(8,128)S(1)}, u32[]{:S(2)}, u32[]{:S(2)}) collective-permute-start(f32[8,128]{1,0:T(8,128)S(1)} %add.10), channel_id=1, source_target_pairs={{0,7},{1,6},{2,5},{3,4},{4,3},{5,2},{6,1},{7,0},{8,15},{9,14},{10,... | collective-permute-start | bytes 12296 | tf_op jit(solution)/shard_map/cond/branch_1_fun/ppermute | solution.py:416
  69.4 4.8 %collective-permute-start.3 = (f32[8,128]{1,0:T(8,128)S(1)}, f32[8,128]{1,0:T(8,128)S(1)}, u32[]{:S(2)}, u32[]{:S(2)}) collective-permute-start(f32[8,128]{1,0:T(8,128)S(1)} %add.11), channel_id=1, source_target_pairs={{0,40},{1,41},{2,42},{3,43},{4,44},{5,45},{6,46},{7,47},{8,32},{9,... | collective-permute-start | bytes 12296 | tf_op jit(solution)/shard_map/cond/branch_1_fun/ppermute | solution.py:416
  74.2 9.2 %collective-permute-start.22 = (f32[8,128]{1,0:T(8,128)S(1)}, f32[8,128]{1,0:T(8,128)S(1)}, u32[]{:S(2)}, u32[]{:S(2)}) collective-permute-start(f32[8,128]{1,0:T(8,128)S(1)} %get-tuple-element.68.sums), channel_id=1, source_target_pairs={{0,192},{16,208},{32,224},{48,240},{64,128},{80,144},{96,160},{112... | collective-permute-start | bytes 12296 | tf_op jit(solution)/shard_map/ppermute | solution.py:416
  77.1 6.3 %collective-permute-start.21 = (f32[8,128]{1,0:T(8,128)S(1)}, f32[8,128]{1,0:T(8,128)S(1)}, u32[]{:S(2)}, u32[]{:S(2)}) collective-permute-start(f32[8,128]{1,0:T(8,128)S(1)} %get-tuple-element.68.sums), channel_id=1, source_target_pairs={{0,128},{16,144},{32,160},{48,176},{64,192},{80,208},{96,224},{112... | collective-permute-start | bytes 12296 | tf_op jit(solution)/shard_map/ppermute | solution.py:416
  77.9 5.6 %collective-permute-start.20 = (f32[8,128]{1,0:T(8,128)S(1)}, f32[8,128]{1,0:T(8,128)S(1)}, u32[]{:S(2)}, u32[]{:S(2)}) collective-permute-start(f32[8,128]{1,0:T(8,128)S(1)} %get-tuple-element.68.sums), channel_id=1, source_target_pairs={{0,64},{16,80},{32,96},{48,112},{64,0},{80,16},{96,32},{112,48},{1... | collective-permute-start | bytes 12296 | tf_op jit(solution)/shard_map/ppermute | solution.py:416
  78.3 1.3 %copy-start.4 = (bf16[512,1152]{1,0:T(8,128)(2,1)S(1)}, bf16[512,1152]{1,0:T(8,128)(2,1)}, u32[]{:S(2)}) copy-start(bf16[512,1152]{1,0:T(8,128)(2,1)} %copy-done.3) | copy-start | bytes 3538948

commit v12 on v10

--- a/solution.py
+++ b/solution.py
@@ -9,7 +9,7 @@
 LOG2E = 1.4426950408889634
 BATCH = 65536
 GATE_COST = 1
-CUT_COST = 1024 * 32
+CUT_COST = 1
 STEPS = (("group", 1), ("group", 2), ("group", 7), (("blk", "group"), 2 * 16 + 8))
 BF16 = jnp.bfloat16
 HBM = pl.BlockSpec(memory_space=pltpu.HBM)

time: 80.4 us -> 79.3 us (0.986)
  waiting for transfers between devices: 25.7 us -> 23.2 us
  starting transfers between devices: 28.2 us -> 30 us
  local copies, waits for them, and re-layouts: 2.55 us -> 3.64 us
  Pallas kernels: 20.1 us -> 19.2 us
    ppermute x12, waiting for transfers between devices: 15.9 us -> 13.1 us  [send(): return lax.ppermute(value, 'blk', perm)]
    ppermute x12, starting transfers between devices: 11.8 us -> 13.3 us  [send(): return lax.ppermute(value, 'blk', perm)]
    unnamed x10, local copies, waits for them, and re-layouts: 2.55 us -> 3.64 us
    pallas_call x2, Pallas kernels: 1.11 us -> 0.04 us  [cut(): pl.pallas_call(kernel, out_shape=jax.ShapeDtypeStruct((rows // 2, width),...]
  transfers between devices with their start and end apart: 22 -> 22, of which waited for: 10 -> 9; matrix products, arithmetic and copies ran while one was open for 0% -> 0% of each run, Pallas kernels for 18% -> 16%
where the time goes in v12:
time: 79.3 us; the launch traced here: 79 us
  starting transfers between devices  30 us (38%)
  waiting for transfers between devices  23.2 us (29%)
  Pallas kernels  19.2 us (24%)
  local copies, waits for them, and re-layouts  3.64 us (5%)
  between operations  2.92 us (4%)
    ppermute x10, starting transfers between devices, pair(): lax.ppermute(value, axis, [(i, i ^ k) for i in range(lax.axis_size(axis))])  16.8 us
    ppermute x12, starting transfers between devices, send(): return lax.ppermute(value, 'blk', perm)  13.3 us
    ppermute x12, waiting for transfers between devices, send(): return lax.ppermute(value, 'blk', perm)  13.1 us
    ppermute x10, waiting for transfers between devices, pair(): lax.ppermute(value, axis, [(i, i ^ k) for i in range(lax.axis_size(axis))])  10.1 us
    pallas_call x1, Pallas kernels, near_part(): pl.pallas_call(near_kernel, out_shape=(shape((rows, width), BF16), shape(...  7.67 us
    pallas_call x1, Pallas kernels, end_part(): pl.pallas_call(end_kernel, out_shape=(shape((rows, width), F32),) * 2 + (...  3.94 us
    pallas_call x1, Pallas kernels, far_grad_part(): pl.pallas_call(far_grad_kernel, out_shape=(shape((rows, width), BF16), sh...  3.67 us
    unnamed x10, local copies, waits for them, and re-layouts  3.64 us
  transfers between devices with their start and end apart: 22, of which 9 were waited for; matrix products, arithmetic and copies ran while one was open for 0% of the time, Pallas kernels for 16%

profile of v12, /device:TPU:32, one launch (start us, length us, event | category | flops | bytes accessed | tf_op | source)
XLA Modules:
  0.0 79.0 jit_solution(265918136433124526)
XLA Ops:
  0.6 0.0 copy-start
  0.6 1.3 %copy-done = f32[256,1152]{1,0:T(8,128)S(1)} copy-done((f32[256,1152]{1,0:T(8,128)S(1)}, f32[256,1152]{1,0:T(8,128)}, u32[]{:S(2)}) %copy-start) | copy-done | bytes 1179672
  1.9 0.2 normalize.2
  2.1 1.1 %copy-done.2 = f32[256,1152]{1,0:T(8,128)S(1)} copy-done((f32[256,1152]{1,0:T(8,128)S(1)}, f32[256,1152]{1,0:T(8,128)}, u32[]{:S(2)}) %copy-start.2) | copy-done | bytes 1179672
  3.2 0.7 normalize.3
  3.9 1.6 %collective-permute-start.9 = (bf16[256,1152]{1,0:T(8,128)(2,1)S(1)}, bf16[256,1152]{1,0:T(8,128)(2,1)}, u32[]{:S(2)}, u32[]{:S(2)}) collective-permute-start(bf16[256,1152]{1,0:T(8,128)(2,1)S(1)} %get-tuple-element.39.own_t), channel_id=1, source_target_pairs={{0,32},{16,48},{32,0},{48,16},{64,96},{80,112},{96,64},{112,80},{1... | collective-permute-start | bytes 1769480 | tf_op jit(solution)/shard_map/ppermute | solution.py:387
  5.5 2.8 %collective-permute-start.6 = (bf16[256,1152]{1,0:T(8,128)(2,1)S(1)}, bf16[256,1152]{1,0:T(8,128)(2,1)S(1)}, u32[]{:S(2)}, u32[]{:S(2)}) collective-permute-start(bf16[256,1152]{1,0:T(8,128)(2,1)S(1)} %get-tuple-element.37.own_i), channel_id=1, source_target_pairs={{0,192},{16,208},{32,224},{48,240},{64,0},{80,16},{96,32},{112,48}... | collective-permute-start | bytes 1769480 | tf_op jit(solution)/shard_map/ppermute | solution.py:387
  8.2 0.0 collective-permute-start.4
  8.2 10.8 %collective-permute-done.9.y_t = bf16[256,1152]{1,0:T(8,128)(2,1)} collective-permute-done((bf16[256,1152]{1,0:T(8,128)(2,1)S(1)}, bf16[256,1152]{1,0:T(8,128)(2,1)}, u32[]{:S(2)}, u32[]{:S(2)}) %collective-permute-start.9) | collective-permute-done | bytes 589856 | tf_op jit(solution)/shard_map/ppermute | solution.py:387
  20.4 0.2 collective-permute-done.6.block_ref.right_i
  20.5 3.8 %collective-permute-start.7 = (bf16[128,1152]{1,0:T(8,128)(2,1)S(1)}, bf16[128,1152]{1,0:T(8,128)(2,1)S(1)}, u32[]{:S(2)}, u32[]{:S(2)}) collective-permute-start(bf16[128,1152]{1,0:T(8,128)(2,1)S(1)} %cut.3), channel_id=1, source_target_pairs={{0,192},{16,208},{32,224},{48,240},{64,0},{80,16},{96,32},{112,48}... | collective-permute-start | bytes 884744 | tf_op jit(solution)/shard_map/ppermute | solution.py:387
  24.3 0.0 collective-permute-done.4.block_ref.left_i
  24.3 0.3 collective-permute-start.5
  24.6 0.0 collective-permute-done.10.yc_t
  24.6 7.7 %near.1 = (bf16[256,1152]{1,0:T(8,128)(2,1)S(1)}, bf16[256,1152]{1,0:T(8,128)(2,1)}, bf16[256,1152]{1,0:T(8,128)(2,1)}, bf16[768,1152]{1,0:T(8,128)(2,1)S(1)}, b...) custom-call(f32[1]{0:T(128)} %bitcast.6.log_scale, ...), custom_call_target="tpu_custom_call" | custom-call | flops 28991029248 | bytes 7077888 | tf_op jit(solution)/shard_map/near/pallas_call | solution.py:203
  32.3 1.5 %collective-permute-done.5.top_i = bf16[128,1152]{1,0:T(8,128)(2,1)S(1)} collective-permute-done((bf16[128,1152]{1,0:T(8,128)(2,1)S(1)}, bf16[128,1152]{1,0:T(8,128)(2,1)S(1)}, u32[]{:S(2)}, u32[]{:S(2)}) %collective-permute-start.5) | collective-permute-done | bytes 294944 | tf_op jit(solution)/shard_map/ppermute | solution.py:387
  33.9 1.4 %far.1 = (bf16[256,1152]{1,0:T(8,128)(2,1)S(1)}, bf16[256,1024]{1,0:T(8,128)(2,1)S(1)}, f32[8,128]{1,0:T(8,128)S(1)}) custom-call(f32[1]{0:T(128)} %bitcast.7.log_scale, f32[1]{0:T(128)} %bitcast.10.bias, bf16[128,1152]{1,0:T(8,128)(2,1)S(1)} %collective-permute-done.5.top_i, bf16[128,1152]{1,0:T(8,128)(2,1)S(1)} %collective-permute-done.7.bot_i, ...), custom_call_target="tpu_custom_call" | custom-call | flops 75497472 | bytes 589824 | tf_op jit(solution)/shard_map/far/pallas_call | solution.py:231
  35.3 3.7 %far_grad.1 = (bf16[256,1152]{1,0:T(8,128)(2,1)}, f32[256,1152]{1,0:T(8,128)S(1)}, bf16[512,1152]{1,0:T(8,128)(2,1)S(1)}, bf16[512,1152]{1,0:T(8,128)(2,1)S(1)}, f32[8,128]{1,0:T(8,128)S(1)}) custom-call(bf16[256,1152]{1,0:T(8,128)(2,1)S(1)} %get-tuple-element.42.far_images, bf16[256,1024]{1,0:T(8,128)(2,1)S(1)} %get-tuple-element.43.far_grads, ...), custom_call_target="tpu_custom_call" | custom-call | flops 75497472 | bytes 589824 | tf_op jit(solution)/shard_map/far_grad/pallas_call | solution.py:249
  38.9 0.0 copy-start.3
  39.0 0.1 collective-permute-start.11
  39.1 0.5 collective-permute-start.14
  39.6 1.6 %collective-permute-start.13 = (f32[8,128]{1,0:T(8,128)S(1)}, f32[8,128]{1,0:T(8,128)S(1)}, u32[]{:S(2)}, u32[]{:S(2)}) collective-permute-start(f32[8,128]{1,0:T(8,128)S(1)} %get-tuple-element.47.sums), channel_id=1, source_target_pairs={{0,32},{16,48},{32,0},{48,16},{64,96},{80,112},{96,64},{112,80},{1... | collective-permute-start | bytes 12296 | tf_op jit(solution)/shard_map/ppermute | solution.py:408
  41.1 0.0 collective-permute-start.18
  41.1 0.8 collective-permute-done.14.sums_c
  41.9 1.6 %collective-permute-start.16 = (bf16[256,1152]{1,0:T(8,128)(2,1)}, bf16[256,1152]{1,0:T(8,128)(2,1)}, u32[]{:S(2)}, u32[]{:S(2)}) collective-permute-start(bf16[256,1152]{1,0:T(8,128)(2,1)} %get-tuple-element.53), channel_id=1, source_target_pairs={{0,64},{16,80},{32,96},{48,112},{64,128},{80,144},{96,160},{112,17... | collective-permute-start | bytes 1769480 | tf_op jit(solution)/shard_map/ppermute | solution.py:387
  43.5 0.0 collective-permute-done.13.sums_b
  43.5 1.6 %collective-permute-start.17 = (bf16[256,1152]{1,0:T(8,128)(2,1)}, bf16[256,1152]{1,0:T(8,128)(2,1)}, u32[]{:S(2)}, u32[]{:S(2)}) collective-permute-start(bf16[256,1152]{1,0:T(8,128)(2,1)} %get-tuple-element.54), channel_id=1, source_target_pairs={{0,192},{16,208},{32,224},{48,240},{64,0},{80,16},{96,32},{112,48}... | collective-permute-start | bytes 1769480 | tf_op jit(solution)/shard_map/ppermute | solution.py:387
  45.1 0.0 collective-permute-done.12.sums_a
  45.1 0.0 collective-permute-done.11.passing.from_core
  45.2 1.0 %relay_y.1 = (bf16[256,1152]{1,0:T(8,128)(2,1)}, f32[8,128]{1,0:T(8,128)S(1)}) custom-call(f32[256,1152]{1,0:T(8,128)S(1)} %get-tuple-element.50.own, bf16[512,1152]{1,0:T(8,128)(2,1)S(1)} %collective-permute-done.11.passing.from_core, f32[8,128]{1,0:T(8,128)S(1)} %get-tuple-element.51.sums, f32[8,128]{1,0:T(8,128)S(1)} %collective-permute-done.12.sums_a, ...), custom_call_target="tpu_custom_call" | custom-call | flops 294912 | bytes 294912 | tf_op jit(solution)/shard_map/relay_y/pallas_call | solution.py:292
  46.1 1.6 %collective-permute-start.15 = (bf16[256,1152]{1,0:T(8,128)(2,1)}, bf16[256,1152]{1,0:T(8,128)(2,1)}, u32[]{:S(2)}, u32[]{:S(2)}) collective-permute-start(bf16[256,1152]{1,0:T(8,128)(2,1)} %get-tuple-element.52), channel_id=1, source_target_pairs={{0,32},{16,48},{32,0},{48,16},{64,96},{80,112},{96,64},{112,80},{1... | collective-permute-start | bytes 1769480 | tf_op jit(solution)/shard_map/ppermute | solution.py:387
  48.3 20.5 %conditional.1 = (f32[8,128]{1,0:T(8,128)S(1)}) conditional(s32[]{:T(128)} %bitcast.2, f32[8,128]{1,0:T(8,128)S(1)} %add.13, f32[8,128]{1,0:T(8,128)S(1)} %add.13), branch_computations={%region_0.0_spmd, %region_1.0_spmd} | conditional | flops 4096 | bytes 114856 | solution.py:425
  48.4 0.2 collective-permute-start
  48.5 3.5 %collective-permute-done = f32[8,128]{1,0:T(8,128)S(1)} collective-permute-done((f32[8,128]{1,0:T(8,128)S(1)}, f32[8,128]{1,0:T(8,128)S(1)}, u32[]{:S(2)}, u32[]{:S(2)}) %collective-permute-start) | collective-permute-done | bytes 4128 | tf_op jit(solution)/shard_map/cond/branch_1_fun/ppermute | solution.py:408
  52.1 3.3 %collective-permute-start.1 = (f32[8,128]{1,0:T(8,128)S(1)}, f32[8,128]{1,0:T(8,128)S(1)}, u32[]{:S(2)}, u32[]{:S(2)}) collective-permute-start(f32[8,128]{1,0:T(8,128)S(1)} %add.9), channel_id=1, source_target_pairs={{0,2},{1,3},{2,0},{3,1},{4,6},{5,7},{6,4},{7,5},{8,10},{9,11},{10,... | collective-permute-start | bytes 12296 | tf_op jit(solution)/shard_map/cond/branch_1_fun/ppermute | solution.py:408
  55.3 1.6 %collective-permute-done.1 = f32[8,128]{1,0:T(8,128)S(1)} collective-permute-done((f32[8,128]{1,0:T(8,128)S(1)}, f32[8,128]{1,0:T(8,128)S(1)}, u32[]{:S(2)}, u32[]{:S(2)}) %collective-permute-start.1) | collective-permute-done | bytes 4128 | tf_op jit(solution)/shard_map/cond/branch_1_fun/ppermute | solution.py:408
  56.9 5.5 %collective-permute-start.2 = (f32[8,128]{1,0:T(8,128)S(1)}, f32[8,128]{1,0:T(8,128)S(1)}, u32[]{:S(2)}, u32[]{:S(2)}) collective-permute-start(f32[8,128]{1,0:T(8,128)S(1)} %add.10), channel_id=1, source_target_pairs={{0,7},{1,6},{2,5},{3,4},{4,3},{5,2},{6,1},{7,0},{8,15},{9,14},{10,... | collective-permute-start | bytes 12296 | tf_op jit(solution)/shard_map/cond/branch_1_fun/ppermute | solution.py:408
  62.4 1.6 %collective-permute-done.2 = f32[8,128]{1,0:T(8,128)S(1)} collective-permute-done((f32[8,128]{1,0:T(8,128)S(1)}, f32[8,128]{1,0:T(8,128)S(1)}, u32[]{:S(2)}, u32[]{:S(2)}) %collective-permute-start.2) | collective-permute-done | bytes 4128 | tf_op jit(solution)/shard_map/cond/branch_1_fun/ppermute | solution.py:408
  64.0 2.2 %collective-permute-start.3 = (f32[8,128]{1,0:T(8,128)S(1)}, f32[8,128]{1,0:T(8,128)S(1)}, u32[]{:S(2)}, u32[]{:S(2)}) collective-permute-start(f32[8,128]{1,0:T(8,128)S(1)} %add.11), channel_id=1, source_target_pairs={{0,40},{1,41},{2,42},{3,43},{4,44},{5,45},{6,46},{7,47},{8,32},{9,... | collective-permute-start | bytes 12296 | tf_op jit(solution)/shard_map/cond/branch_1_fun/ppermute | solution.py:408
  66.2 2.6 %collective-permute-done.3 = f32[8,128]{1,0:T(8,128)S(1)} collective-permute-done((f32[8,128]{1,0:T(8,128)S(1)}, f32[8,128]{1,0:T(8,128)S(1)}, u32[]{:S(2)}, u32[]{:S(2)}) %collective-permute-start.3) | collective-permute-done | bytes 4128 | tf_op jit(solution)/shard_map/cond/branch_1_fun/ppermute | solution.py:408
  68.8 0.1 collective-permute-start.21
  68.9 2.1 %collective-permute-start.20 = (f32[8,128]{1,0:T(8,128)S(1)}, f32[8,128]{1,0:T(8,128)S(1)}, u32[]{:S(2)}, u32[]{:S(2)}) collective-permute-start(f32[8,128]{1,0:T(8,128)S(1)} %get-tuple-element.64.sums), channel_id=1, source_target_pairs={{0,128},{16,144},{32,160},{48,176},{64,192},{80,208},{96,224},{112... | collective-permute-start | bytes 12296 | tf_op jit(solution)/shard_map/ppermute | solution.py:408
  71.0 0.5 collective-permute-done.16.from_left
  71.5 1.4 %collective-permute-start.19 = (f32[8,128]{1,0:T(8,128)S(1)}, f32[8,128]{1,0:T(8,128)S(1)}, u32[]{:S(2)}, u32[]{:S(2)}) collective-permute-start(f32[8,128]{1,0:T(8,128)S(1)} %get-tuple-element.64.sums), channel_id=1, source_target_pairs={{0,64},{16,80},{32,96},{48,112},{64,0},{80,16},{96,32},{112,48},{1... | collective-permute-start | bytes 12296 | tf_op jit(solution)/shard_map/ppermute | solution.py:408
  72.9 0.0 copy-start.4
  73.0 1.3 %copy-done.4 = bf16[512,1152]{1,0:T(8,128)(2,1)S(1)} copy-done((bf16[512,1152]{1,0:T(8,128)(2,1)S(1)}, bf16[512,1152]{1,0:T(8,128)(2,1)}, u32[]{:S(2)}) %copy-start.4) | copy-done | bytes 1179672
  74.2 3.9 %end.1 = (f32[256,1152]{1,0:T(8,128)}, f32[256,1152]{1,0:T(8,128)}, f32[8,128]{1,0:T(8,128)S(1)}) custom-call(f32[1]{0:T(128)} %bitcast.8.log_scale, bf16[512,1152]{1,0:T(8,128)(2,1)S(1)} %copy-done.4, f32[256,1152]{1,0:T(8,128)S(1)} %copy-done.2, bf16[512,1152]{1,0:T(8,128)(2,1)S(1)} %collective-permute-done.11.passing.from_core, ...), custom_call_target="tpu_custom_call" | custom-call | flops 4718592 | bytes 589824 | tf_op jit(solution)/shard_map/end/pallas_call | solution.py:341
  78.2 0.6 totals.1
  (22 shorter events, 0.1 us)
Async XLA Ops:
  0.6 1.3 %copy-start = (f32[256,1152]{1,0:T(8,128)S(1)}, f32[256,1152]{1,0:T(8,128)}, u32[]{:S(2)}) copy-start(f32[256,1152]{1,0:T(8,128)} %image_emb.1) | copy-start | bytes 3538948
  1.9 1.3 %copy-start.2 = (f32[256,1152]{1,0:T(8,128)S(1)}, f32[256,1152]{1,0:T(8,128)}, u32[]{:S(2)}) copy-start(f32[256,1152]{1,0:T(8,128)} %text_emb.1) | copy-start | bytes 3538948
  3.9 15.2 %collective-permute-start.9 = (bf16[256,1152]{1,0:T(8,128)(2,1)S(1)}, bf16[256,1152]{1,0:T(8,128)(2,1)}, u32[]{:S(2)}, u32[]{:S(2)}) collective-permute-start(bf16[256,1152]{1,0:T(8,128)(2,1)S(1)} %get-tuple-element.39.own_t), channel_id=1, source_target_pairs={{0,32},{16,48},{32,0},{48,16},{64,96},{80,112},{96,64},{112,80},{1... | collective-permute-start | bytes 1769480 | tf_op jit(solution)/shard_map/ppermute | solution.py:387
  5.5 15.1 %collective-permute-start.6 = (bf16[256,1152]{1,0:T(8,128)(2,1)S(1)}, bf16[256,1152]{1,0:T(8,128)(2,1)S(1)}, u32[]{:S(2)}, u32[]{:S(2)}) collective-permute-start(bf16[256,1152]{1,0:T(8,128)(2,1)S(1)} %get-tuple-element.37.own_i), channel_id=1, source_target_pairs={{0,192},{16,208},{32,224},{48,240},{64,0},{80,16},{96,32},{112,48}... | collective-permute-start | bytes 1769480 | tf_op jit(solution)/shard_map/ppermute | solution.py:387
  8.2 16.1 %collective-permute-start.4 = (bf16[256,1152]{1,0:T(8,128)(2,1)S(1)}, bf16[256,1152]{1,0:T(8,128)(2,1)S(1)}, u32[]{:S(2)}, u32[]{:S(2)}) collective-permute-start(bf16[256,1152]{1,0:T(8,128)(2,1)S(1)} %get-tuple-element.37.own_i), channel_id=1, source_target_pairs={{0,64},{16,80},{32,96},{48,112},{64,128},{80,144},{96,160},{112,17... | collective-permute-start | bytes 1769480 | tf_op jit(solution)/shard_map/ppermute | solution.py:387
  8.2 16.4 %collective-permute-start.8 = (bf16[256,1152]{1,0:T(8,128)(2,1)S(1)}, bf16[256,1152]{1,0:T(8,128)(2,1)}, u32[]{:S(2)}, u32[]{:S(2)}) collective-permute-start(bf16[256,1152]{1,0:T(8,128)(2,1)S(1)} %get-tuple-element.39.own_t), channel_id=1, source_target_pairs={{0,16},{16,0},{32,48},{48,32},{64,80},{80,64},{96,112},{112,96},{1... | collective-permute-start | bytes 1769480 | tf_op jit(solution)/shard_map/ppermute | solution.py:387
  19.1 5.6 %collective-permute-start.10 = (bf16[256,1152]{1,0:T(8,128)(2,1)}, bf16[256,1152]{1,0:T(8,128)(2,1)}, u32[]{:S(2)}, u32[]{:S(2)}) collective-permute-start(bf16[256,1152]{1,0:T(8,128)(2,1)} %collective-permute-done.9.y_t), channel_id=1, source_target_pairs={{0,16},{16,0},{32,48},{48,32},{64,80},{80,64},{96,112},{112,96},{1... | collective-permute-start | bytes 1769480 | tf_op jit(solution)/shard_map/ppermute | solution.py:387
  20.5 11.8 %collective-permute-start.7 = (bf16[128,1152]{1,0:T(8,128)(2,1)S(1)}, bf16[128,1152]{1,0:T(8,128)(2,1)S(1)}, u32[]{:S(2)}, u32[]{:S(2)}) collective-permute-start(bf16[128,1152]{1,0:T(8,128)(2,1)S(1)} %cut.3), channel_id=1, source_target_pairs={{0,192},{16,208},{32,224},{48,240},{64,0},{80,16},{96,32},{112,48}... | collective-permute-start | bytes 884744 | tf_op jit(solution)/shard_map/ppermute | solution.py:387
  24.3 9.5 %collective-permute-start.5 = (bf16[128,1152]{1,0:T(8,128)(2,1)S(1)}, bf16[128,1152]{1,0:T(8,128)(2,1)S(1)}, u32[]{:S(2)}, u32[]{:S(2)}) collective-permute-start(bf16[128,1152]{1,0:T(8,128)(2,1)S(1)} %cut.2), channel_id=1, source_target_pairs={{0,64},{16,80},{32,96},{48,112},{64,128},{80,144},{96,160},{112,17... | collective-permute-start | bytes 884744 | tf_op jit(solution)/shard_map/ppermute | solution.py:387
  38.9 7.2 %copy-start.3 = (bf16[512,1152]{1,0:T(8,128)(2,1)}, bf16[512,1152]{1,0:T(8,128)(2,1)S(1)}, u32[]{:S(2)}) copy-start(bf16[512,1152]{1,0:T(8,128)(2,1)S(1)} %get-tuple-element.48.own) | copy-start | bytes 3538948
  39.0 6.2 %collective-permute-start.11 = (bf16[512,1152]{1,0:T(8,128)(2,1)S(1)}, bf16[512,1152]{1,0:T(8,128)(2,1)S(1)}, u32[]{:S(2)}, u32[]{:S(2)}) collective-permute-start(bf16[512,1152]{1,0:T(8,128)(2,1)S(1)} %get-tuple-element.49), channel_id=1, source_target_pairs={{0,16},{16,0},{32,48},{48,32},{64,80},{80,64},{96,112},{112,96},{1... | collective-permute-start | bytes 3538952 | tf_op jit(solution)/shard_map/ppermute | solution.py:387
  39.1 2.8 %collective-permute-start.14 = (f32[8,128]{1,0:T(8,128)S(1)}, f32[8,128]{1,0:T(8,128)S(1)}, u32[]{:S(2)}, u32[]{:S(2)}) collective-permute-start(f32[8,128]{1,0:T(8,128)S(1)} %get-tuple-element.47.sums), channel_id=1, source_target_pairs={{0,16},{16,0},{32,48},{48,32},{64,80},{80,64},{96,112},{112,96},{1... | collective-permute-start | bytes 12296 | tf_op jit(solution)/shard_map/ppermute | solution.py:408
  39.6 4.0 %collective-permute-start.13 = (f32[8,128]{1,0:T(8,128)S(1)}, f32[8,128]{1,0:T(8,128)S(1)}, u32[]{:S(2)}, u32[]{:S(2)}) collective-permute-start(f32[8,128]{1,0:T(8,128)S(1)} %get-tuple-element.47.sums), channel_id=1, source_target_pairs={{0,32},{16,48},{32,0},{48,16},{64,96},{80,112},{96,64},{112,80},{1... | collective-permute-start | bytes 12296 | tf_op jit(solution)/shard_map/ppermute | solution.py:408
  41.1 4.0 %collective-permute-start.12 = (f32[8,128]{1,0:T(8,128)S(1)}, f32[8,128]{1,0:T(8,128)S(1)}, u32[]{:S(2)}, u32[]{:S(2)}) collective-permute-start(f32[8,128]{1,0:T(8,128)S(1)} %get-tuple-element.47.sums), channel_id=1, source_target_pairs={{0,48},{16,32},{32,16},{48,0},{64,112},{80,96},{96,80},{112,64},{1... | collective-permute-start | bytes 12296 | tf_op jit(solution)/shard_map/ppermute | solution.py:408
  41.1 27.8 %collective-permute-start.18 = (bf16[256,1152]{1,0:T(8,128)(2,1)}, bf16[256,1152]{1,0:T(8,128)(2,1)}, u32[]{:S(2)}, u32[]{:S(2)}) collective-permute-start(bf16[256,1152]{1,0:T(8,128)(2,1)} %get-tuple-element.55), channel_id=1, source_target_pairs={{0,128},{16,144},{32,160},{48,176},{64,192},{80,208},{96,224},{112... | collective-permute-start | bytes 1769480 | tf_op jit(solution)/shard_map/ppermute | solution.py:387
  41.9 29.6 %collective-permute-start.16 = (bf16[256,1152]{1,0:T(8,128)(2,1)}, bf16[256,1152]{1,0:T(8,128)(2,1)}, u32[]{:S(2)}, u32[]{:S(2)}) collective-permute-start(bf16[256,1152]{1,0:T(8,128)(2,1)} %get-tuple-element.53), channel_id=1, source_target_pairs={{0,64},{16,80},{32,96},{48,112},{64,128},{80,144},{96,160},{112,17... | collective-permute-start | bytes 1769480 | tf_op jit(solution)/shard_map/ppermute | solution.py:387
  43.5 29.4 %collective-permute-start.17 = (bf16[256,1152]{1,0:T(8,128)(2,1)}, bf16[256,1152]{1,0:T(8,128)(2,1)}, u32[]{:S(2)}, u32[]{:S(2)}) collective-permute-start(bf16[256,1152]{1,0:T(8,128)(2,1)} %get-tuple-element.54), channel_id=1, source_target_pairs={{0,192},{16,208},{32,224},{48,240},{64,0},{80,16},{96,32},{112,48}... | collective-permute-start | bytes 1769480 | tf_op jit(solution)/shard_map/ppermute | solution.py:387
  45.1 27.8 %copy-start.1 = (f32[256,1152]{1,0:T(8,128)S(1)}, f32[256,1152]{1,0:T(8,128)}, u32[]{:S(2)}) copy-start(f32[256,1152]{1,0:T(8,128)} %image_emb.1) | copy-start | bytes 3538948
  46.1 26.8 %collective-permute-start.15 = (bf16[256,1152]{1,0:T(8,128)(2,1)}, bf16[256,1152]{1,0:T(8,128)(2,1)}, u32[]{:S(2)}, u32[]{:S(2)}) collective-permute-start(bf16[256,1152]{1,0:T(8,128)(2,1)} %get-tuple-element.52), channel_id=1, source_target_pairs={{0,32},{16,48},{32,0},{48,16},{64,96},{80,112},{96,64},{112,80},{1... | collective-permute-start | bytes 1769480 | tf_op jit(solution)/shard_map/ppermute | solution.py:387
  48.4 3.7 %collective-permute-start = (f32[8,128]{1,0:T(8,128)S(1)}, f32[8,128]{1,0:T(8,128)S(1)}, u32[]{:S(2)}, u32[]{:S(2)}) collective-permute-start(f32[8,128]{1,0:T(8,128)S(1)} %param.1), channel_id=1, source_target_pairs={{0,1},{1,0},{2,3},{3,2},{4,5},{5,4},{6,7},{7,6},{8,9},{9,8},{10,11... | collective-permute-start | bytes 12296 | tf_op jit(solution)/shard_map/cond/branch_1_fun/ppermute | solution.py:408
  52.1 4.8 %collective-permute-start.1 = (f32[8,128]{1,0:T(8,128)S(1)}, f32[8,128]{1,0:T(8,128)S(1)}, u32[]{:S(2)}, u32[]{:S(2)}) collective-permute-start(f32[8,128]{1,0:T(8,128)S(1)} %add.9), channel_id=1, source_target_pairs={{0,2},{1,3},{2,0},{3,1},{4,6},{5,7},{6,4},{7,5},{8,10},{9,11},{10,... | collective-permute-start | bytes 12296 | tf_op jit(solution)/shard_map/cond/branch_1_fun/ppermute | solution.py:408
  56.9 7.1 %collective-permute-start.2 = (f32[8,128]{1,0:T(8,128)S(1)}, f32[8,128]{1,0:T(8,128)S(1)}, u32[]{:S(2)}, u32[]{:S(2)}) collective-permute-start(f32[8,128]{1,0:T(8,128)S(1)} %add.10), channel_id=1, source_target_pairs={{0,7},{1,6},{2,5},{3,4},{4,3},{5,2},{6,1},{7,0},{8,15},{9,14},{10,... | collective-permute-start | bytes 12296 | tf_op jit(solution)/shard_map/cond/branch_1_fun/ppermute | solution.py:408
  64.0 4.8 %collective-permute-start.3 = (f32[8,128]{1,0:T(8,128)S(1)}, f32[8,128]{1,0:T(8,128)S(1)}, u32[]{:S(2)}, u32[]{:S(2)}) collective-permute-start(f32[8,128]{1,0:T(8,128)S(1)} %add.11), channel_id=1, source_target_pairs={{0,40},{1,41},{2,42},{3,43},{4,44},{5,45},{6,46},{7,47},{8,32},{9,... | collective-permute-start | bytes 12296 | tf_op jit(solution)/shard_map/cond/branch_1_fun/ppermute | solution.py:408
  68.8 9.3 %collective-permute-start.21 = (f32[8,128]{1,0:T(8,128)S(1)}, f32[8,128]{1,0:T(8,128)S(1)}, u32[]{:S(2)}, u32[]{:S(2)}) collective-permute-start(f32[8,128]{1,0:T(8,128)S(1)} %get-tuple-element.64.sums), channel_id=1, source_target_pairs={{0,192},{16,208},{32,224},{48,240},{64,128},{80,144},{96,160},{112... | collective-permute-start | bytes 12296 | tf_op jit(solution)/shard_map/ppermute | solution.py:408
  68.9 9.3 %collective-permute-start.20 = (f32[8,128]{1,0:T(8,128)S(1)}, f32[8,128]{1,0:T(8,128)S(1)}, u32[]{:S(2)}, u32[]{:S(2)}) collective-permute-start(f32[8,128]{1,0:T(8,128)S(1)} %get-tuple-element.64.sums), channel_id=1, source_target_pairs={{0,128},{16,144},{32,160},{48,176},{64,192},{80,208},{96,224},{112... | collective-permute-start | bytes 12296 | tf_op jit(solution)/shard_map/ppermute | solution.py:408
  71.5 6.7 %collective-permute-start.19 = (f32[8,128]{1,0:T(8,128)S(1)}, f32[8,128]{1,0:T(8,128)S(1)}, u32[]{:S(2)}, u32[]{:S(2)}) collective-permute-start(f32[8,128]{1,0:T(8,128)S(1)} %get-tuple-element.64.sums), channel_id=1, source_target_pairs={{0,64},{16,80},{32,96},{48,112},{64,0},{80,16},{96,32},{112,48},{1... | collective-permute-start | bytes 12296 | tf_op jit(solution)/shard_map/ppermute | solution.py:408
  72.9 1.3 %copy-start.4 = (bf16[512,1152]{1,0:T(8,128)(2,1)S(1)}, bf16[512,1152]{1,0:T(8,128)(2,1)}, u32[]{:S(2)}) copy-start(bf16[512,1152]{1,0:T(8,128)(2,1)} %copy-done.3) | copy-start | bytes 3538948
